TPU v7x, 32 devices: a whole 2x2x4 slice. The times are simulated.
32 devices in a mesh: section: 4 (over y, x), expert: 4 (over z), mp: 2 (over core).
Axes of the slice: x: 2, y: 2, z: 4, core: 2. Of those that a mesh axis runs over, the one named last changes fastest.
Arguments:
- out_grad: bfloat16 [4, 512, 4096], P('section', 'expert', 'mp'), may hold values from -6 to 6
- expert_ids: int32 [4, 512, 2], P('section', 'expert'), may hold values from 0 to 3, all different within a row; in each aligned block of 128 rows (0 to 127, 128 to 255, ..., all dimensions but the last counted through in order) at most 128 rows name the same one
- gate_codes: int32 [4, 512, 2], P('section', 'expert'), may hold values from 1 to 255
- up_weight: bfloat16 [4, 4, 4096, 1024], P('section', 'expert', None, 'mp'), may hold values from -0.09375 to 0.09375
- down_weight: bfloat16 [4, 4, 1024, 4096], P('section', 'expert', 'mp'), may hold values from -0.1875 to 0.1875
- pre_act: bfloat16 [4, 4, 512, 1024], P('section', 'expert', None, 'mp'), may hold values from -6 to 6
- conv_grad: bfloat16 [4, 512, 4096], P('section', 'expert', 'mp'), may hold values from -6 to 6
- conv_input: bfloat16 [4, 512, 4096], P('section', 'expert', 'mp'), may hold values from -0.26367188 to 0.26367188
- conv_weight: float32 [4, 4, 4096], P('section', None, 'mp'), may hold values from -3 to 3
- in_proj: bfloat16 [4, 4096, 4096], P('section', 'expert', 'mp'), may hold values from -0.09375 to 0.09375
Outputs:
- residual_to_previous: bfloat16 [4, 512, 4096], P('section', 'expert', 'mp')
- kernel_grad: float32 [4, 4, 4096], P('section', None, 'mp')
Inputs may be any that keep to these rules, and one draw needn't show every extreme that they name: `expert_ids`: each token names two different experts; in every section, the tokens of one block of 128 name no expert more than 128 times, a bound that some block reaches.
All inputs are finite; a program needn't handle non-finite values.
Results may differ from a plain program's by a relative error of at most 0.0044.
Values may be sent and summed in bfloat16 or wider, within the bound.
No kernel may reach another device: no remote copies, remote signals or barrier semaphores. Data moves between devices by JAX's collectives and lax.ppermute only.
A program may use at most 128 MiB of HBM per device.

v0:
```python
import jax
import jax.numpy as jnp
from jax import lax
from jax.sharding import PartitionSpec as P


def shifted(array, axis, by):
    size = lax.axis_size(axis)
    pairs = [(i, i + by) for i in range(size) if 0 <= i + by < size]
    return lax.ppermute(array, axis, pairs)


def silu_slope(pre_value):
    sig = jax.nn.sigmoid(pre_value)
    return sig * (1.0 + pre_value * (1.0 - sig))


def gated_rows(gates, rows, tok_rows):
    scaled = (gates[:, :, None] * rows.astype(jnp.float32)[:, None, :]).astype(jnp.bfloat16)
    return scaled.reshape(tok_rows * 2, rows.shape[1])


def fill_buffer(scaled, target, experts, capacity):
    width = scaled.shape[1]
    buffer = jnp.zeros((experts * capacity, width), jnp.bfloat16).at[target].set(scaled)
    return buffer.reshape(experts, capacity, width)


def shards(
    out_grad,
    expert_ids,
    gate_codes,
    up_weight,
    down_weight,
    pre_act,
    conv_grad,
    conv_input,
    conv_weight,
    in_proj,
):
    grad_rows = out_grad[0]
    route_ids = expert_ids[0]
    tok_rows = grad_rows.shape[0]
    experts = lax.axis_size("expert")
    capacity = pre_act.shape[2] // experts
    gates = gate_codes[0].astype(jnp.float32) / 256.0
    flat_ids = route_ids.reshape(tok_rows * 2)
    onehot = (flat_ids[:, None] == jnp.arange(experts, dtype=jnp.int32)[None, :]).astype(jnp.int32)
    before = jnp.cumsum(onehot, axis=0) - onehot
    position = jnp.sum(before * onehot, axis=1)
    target = flat_ids * capacity + position
    whole_rows = lax.all_gather(grad_rows, "mp", axis=1, tiled=True)
    buffer = fill_buffer(gated_rows(gates, whole_rows, tok_rows), target, experts, capacity)
    arrived = lax.all_to_all(buffer, "expert", split_axis=0, concat_axis=0, tiled=True)
    slot_rows = arrived.reshape(experts * capacity, whole_rows.shape[1])
    w_down = down_weight[0, 0]
    w_up = up_weight[0, 0]
    pre_slots = pre_act[0, 0].astype(jnp.float32)
    hidden = lax.dot_general(
        slot_rows, w_down, (((1,), (1,)), ((), ())), preferred_element_type=jnp.float32
    )
    pre_grad = (hidden * silu_slope(pre_slots)).astype(jnp.bfloat16)
    partial_value = lax.dot_general(
        pre_grad, w_up, (((1,), (1,)), ((), ())), preferred_element_type=jnp.float32
    )
    share = lax.psum_scatter(partial_value, "mp", scatter_dimension=1, tiled=True).astype(
        jnp.bfloat16
    )
    returned = lax.all_to_all(
        share.reshape(experts, capacity, share.shape[1]),
        "expert",
        split_axis=0,
        concat_axis=0,
        tiled=True,
    )
    picked = returned.reshape(experts * capacity, grad_rows.shape[1])[target]
    picked = picked.astype(jnp.float32).reshape(tok_rows, 2, grad_rows.shape[1])
    moe_total = grad_rows.astype(jnp.float32) + picked[:, 0, :] + picked[:, 1, :]
    grads_here = conv_grad[0]
    inputs_here = conv_input[0]
    taps = conv_weight[0]
    kernel_size = taps.shape[0]
    next_rows = shifted(grads_here[: kernel_size - 1], "expert", -1)
    prev_rows = shifted(inputs_here[tok_rows - kernel_size + 1 :], "expert", 1)
    grad_ext = jnp.concatenate([grads_here, next_rows], axis=0).astype(jnp.float32)
    input_ext = jnp.concatenate([prev_rows, inputs_here], axis=0).astype(jnp.float32)
    grad_local = grads_here.astype(jnp.float32)
    conv_result = jnp.zeros(grads_here.shape, jnp.float32)
    tap_terms = []
    for tap in range(kernel_size):
        start = kernel_size - 1 - tap
        conv_result = conv_result + taps[tap][None, :] * grad_ext[start : start + tok_rows]
        tap_terms.append(jnp.sum(grad_local * input_ext[tap : tap + tok_rows], axis=0))
    input_grad = conv_result.astype(jnp.bfloat16)
    tap_grads = lax.psum(jnp.stack(tap_terms), "expert")
    w_proj = in_proj[0]
    proj_partial = lax.dot_general(
        input_grad,
        lax.all_gather(w_proj, "expert", axis=0, tiled=True),
        (((1,), (1,)), ((), ())),
        preferred_element_type=jnp.float32,
    )
    proj_share = lax.psum_scatter(proj_partial, "mp", scatter_dimension=1, tiled=True)
    residual = (moe_total + proj_share).astype(jnp.bfloat16)
    sent_residual = shifted(residual, "section", -1)
    return (sent_residual[None], tap_grads[None])


def solution(mesh):
    in_specs = (
        P("section", "expert", "mp"),
        P("section", "expert", None),
        P("section", "expert", None),
        P("section", "expert", None, "mp"),
        P("section", "expert", "mp", None),
        P("section", "expert", None, "mp"),
        P("section", "expert", "mp"),
        P("section", "expert", "mp"),
        P("section", None, "mp"),
        P("section", "expert", "mp"),
    )
    out_specs = (P("section", "expert", "mp"), P("section", None, "mp"))
    return jax.shard_map(shards, mesh=mesh, in_specs=in_specs, out_specs=out_specs, check_vma=False)
```

profile of v0, /device:TPU:0, one launch (start us, length us, event | category | flops | bytes accessed | tf_op | source)
XLA Modules:
  0.0 513.1 jit_solution(15405960011762926303)
XLA Ops:
  7.2 0.0 all-gather.5.cloned.1.call-start
  7.2 0.7 all-gather.5.cloned.1.call-update
  7.9 0.0 all-gather.7.cloned.1.call-start
  8.0 0.7 all-gather.7.cloned.1.call-update
  8.7 0.0 reduce-scatter.3.cloned.1.call-start
  8.7 0.1 copy.15
  8.8 0.1 eq.29
  9.0 0.1 eq.25
  9.1 0.1 copy.14
  9.2 0.1 mul.98
  9.4 1.2 reduce-window.6
  10.6 0.1 slice.86
  10.7 0.1 copy.17
  10.8 0.1 copy.18
  10.9 0.1 copy.19
  11.1 0.1 div.13
  11.2 0.1 add_bitcast_fusion
  11.3 10.1 %all-gather.5.cloned.1.call-done = bf16[1,128,4096]{2,1,0:T(8,128)(2,1)} async-done(((bf16[1,128,2048]{2,1,0:T(8,128)(2,1)}), bf16[1,128,4096]{2,1,0:T(8,128)(2,1)}) %all-gather.5.cloned.1.call-update) | async-done | bytes 1048592 | tf_op jit(solution)/shard_map/all_gather | solution.py:52
  21.4 1.4 bitcast_convert_fusion
  22.8 4.3 mul.101
  27.1 6.3 %mul.102 = f32[256,4096]{1,0:T(8,128)} reshape(f32[128,2,4096]{2,1,0:T(2,128)} %mul.101) | data formatting | bytes 8388608 | tf_op jit(solution)/shard_map/mul | solution.py:19
  33.4 8.5 %scatter_custom_fusion = bf16[512,4096]{1,0:T(8,128)(2,1)} fusion(s32[256]{0:T(256)S(1)} %bitcast.99, f32[256,4096]{1,0:T(8,128)} %mul.102, f32[256]{0:T(256)S(1)} %div.13, bf16[]{:T(256)} %constant.7.clone.1), kind=kCustom, calls=%fused_computation.9 | custom fusion | flops 2097152 | bytes 8389634 | tf_op jit(solution)/shard_map/scatter | solution.py:25
  41.9 201.0 %all_to_all.10 = bf16[4,128,4096]{2,1,0:T(8,128)(2,1)S(1)} all-to-all(bf16[4,128,4096]{2,1,0:T(8,128)(2,1)} %bitcast.85), channel_id=1, replica_groups=mesh['section'=4,'expert'=4,'mp'=2] {'expert'}, dimensions={0} | all-to-all | bytes 8388608 | tf_op jit(solution)/shard_map/all_to_all | solution.py:54
  242.9 2.5 fusion.12
  245.5 5.6 %fusion.2 = f32[512,4096]{1,0:T(8,128)} fusion(bf16[512,512]{1,0:T(8,128)(2,1)S(1)} %fusion.12, bf16[1,1,4096,512]{3,2,1,0:T(8,128)(2,1)S(1)} %copy-done), kind=kOutput, calls=%fused_computation.4 | convolution fusion | flops 2147483648 | bytes 13107200 | tf_op jit(solution)/shard_map/dot_general | solution.py:63
  251.1 0.0 reduce-scatter.5.cloned.1.call-start
  251.2 1.0 copy-done.1
  252.1 1.3 collective-permute-start
  253.5 12.8 %collective-permute-done = bf16[3,2048]{1,0:T(4,128)(2,1)S(1)} collective-permute-done((bf16[3,2048]{1,0:T(4,128)(2,1)S(1)}, bf16[3,2048]{1,0:T(4,128)(2,1)S(1)}, u32[]{:S(2)}, u32[]{:S(2)}) %collective-permute-start) | collective-permute-done | bytes 12320 | tf_op jit(solution)/shard_map/ppermute | solution.py:10
  266.3 0.1 maximum_convert_fusion
  266.4 134.3 %all-gather.7.cloned.1.call-done = bf16[1,4096,2048]{2,1,0:T(8,128)(2,1)} async-done(((bf16[1,1024,2048]{2,1,0:T(8,128)(2,1)}), bf16[1,4096,2048]{2,1,0:T(8,128)(2,1)}) %all-gather.7.cloned.1.call-update) | async-done | bytes 16777232 | tf_op jit(solution)/shard_map/all_gather | solution.py:99
  400.7 12.8 %fusion = f32[128,4096]{1,0:T(8,128)} fusion(bf16[1,4096,2048]{2,1,0:T(8,128)(2,1)} %all-gather.7.cloned.1.call-done, f32[131,2048]{1,0:T(8,128)S(1)} %maximum_convert_fusion, f32[2048]{0:T(1024)S(1)} %bitcast.93, f32[2048]{0:T(1024)S(1)} %bitcast.94, f32[2048]{0:T(1024)S(1)} %bitcast.92, f32[2048]{0:T(1024)S(1)} %bitcast.91), kind=kOutput, calls=%fused_computation.2 | convolution fusion | flops 2149580800 | bytes 23101440 | tf_op jit(solution)/shard_map/dot_general | solution.py:97
  413.5 4.5 reduce-scatter.3.cloned.1.call-done
  418.0 3.9 convert_element_type.68
  421.9 4.9 all-to-all-start.1
  426.8 0.8 slice_bitcast_fusion
  427.6 4.1 collective-permute-start.2
  431.8 29.7 %collective-permute-done.2 = bf16[3,2048]{1,0:T(4,128)(2,1)S(1)} collective-permute-done((bf16[3,2048]{1,0:T(4,128)(2,1)S(1)}, bf16[3,2048]{1,0:T(4,128)(2,1)S(1)}, u32[]{:S(2)}, u32[]{:S(2)}) %collective-permute-start.2) | collective-permute-done | bytes 12320 | tf_op jit(solution)/shard_map/ppermute | solution.py:10
  461.5 1.2 maximum_convert_fusion.1
  462.7 12.7 %all-to-all-done.1 = bf16[4,128,2048]{2,1,0:T(8,128)(2,1)S(1)} async-done(((bf16[4,128,2048]{2,1,0:T(8,128)(2,1)}), bf16[4,128,2048]{2,1,0:T(8,128)(2,1)S(1)}, u32[]{:S(2)}, u32[]{:S(2)}) %all-to-all-start.1) | async-done | bytes 2097184 | tf_op jit(solution)/shard_map/all_to_all | solution.py:69
  475.4 2.3 gather_fusion
  477.8 2.4 reshape.97
  480.1 3.0 fusion.40
  483.1 2.8 fusion.30
  485.9 1.3 collective-permute-start.1
  487.2 0.6 fusion.20
  487.8 17.9 %psum.7 = f32[1,4,2048]{2,1,0:T(4,128)} all-reduce(f32[1,4,2048]{2,1,0:T(4,128)S(1)} %maximum_bitcast_fusion), channel_id=1, replica_groups=mesh['section'=4,'expert'=4,'mp'=2] {'expert'}, use_global_device_ids=true, to_apply=%region_10.11 | all-reduce | flops 8192 | bytes 65536 | tf_op jit(solution)/shard_map/psum | solution.py:95
  505.7 0.8 copy.39
  (30 shorter events, 0.2 us)
Async XLA Ops:
  7.2 1.6 copy-start.4
  7.2 3.8 copy-start.5
  7.2 14.2 %all-gather.5.cloned.1.call-start = ((), (), s32[]{:S(2)}) async-start(), calls=%async_computation.6 | async-start | bytes 1572864 | tf_op jit(solution)/shard_map/all_gather | solution.py:52
  7.9 392.8 %all-gather.7.cloned.1.call-start = ((), (), s32[]{:S(2)}) async-start(), calls=%async_computation.7 | async-start | bytes 20971520 | tf_op jit(solution)/shard_map/all_gather | solution.py:99
  8.7 409.4 %reduce-scatter.3.cloned.1.call-start = ((), (), s32[]{:S(2)}) async-start(), calls=%async_computation.4 | async-start | bytes 12582912 | tf_op jit(solution)/shard_map/reduce_scatter | solution.py:66
  41.9 201.0 %copy-start.6 = (bf16[1,1,512,4096]{3,2,1,0:T(8,128)(2,1)S(1)}, bf16[1,1,512,4096]{3,2,1,0:T(8,128)(2,1)}, u32[]{:S(2)}) copy-start(bf16[1,1,512,4096]{3,2,1,0:T(8,128)(2,1)} %param.14) | copy-start | bytes 12582916
  41.9 201.0 %copy-start.7 = (bf16[1,1,512,512]{3,2,1,0:T(8,128)(2,1)S(1)}, bf16[1,1,512,512]{3,2,1,0:T(8,128)(2,1)}, u32[]{:S(2)}) copy-start(bf16[1,1,512,512]{3,2,1,0:T(8,128)(2,1)} %param.15) | copy-start | bytes 1572868
  242.9 2.6 copy-start
  251.1 1.0 copy-start.1
  251.1 2.4 copy-start.3
  251.1 232.0 %reduce-scatter.5.cloned.1.call-start = ((), (), s32[]{:S(2)}) async-start(), calls=%async_computation.5 | async-start | bytes 3145728 | tf_op jit(solution)/shard_map/reduce_scatter | solution.py:103
  252.1 14.2 %collective-permute-start = (bf16[3,2048]{1,0:T(4,128)(2,1)S(1)}, bf16[3,2048]{1,0:T(4,128)(2,1)S(1)}, u32[]{:S(2)}, u32[]{:S(2)}) collective-permute-start(bf16[3,2048]{1,0:T(4,128)(2,1)S(1)} %slice_bitcast_fusion.1), channel_id=1, source_target_pairs={{2,0},{4,2},{6,4},{3,1},{5,3},{7,5},{10,8},{12,10},{14,12},{11,9},... | collective-permute-start | bytes 36872 | tf_op jit(solution)/shard_map/ppermute | solution.py:10
  421.9 53.5 %all-to-all-start.1 = ((bf16[4,128,2048]{2,1,0:T(8,128)(2,1)}), bf16[4,128,2048]{2,1,0:T(8,128)(2,1)S(1)}, u32[]{:S(2)}, u32[]{:S(2)}) async-start(bf16[4,128,2048]{2,1,0:T(8,128)(2,1)} %bitcast.86), calls=%async_computation.2 | async-start | bytes 4194304 | tf_op jit(solution)/shard_map/all_to_all | solution.py:69
  427.6 33.9 %collective-permute-start.2 = (bf16[3,2048]{1,0:T(4,128)(2,1)S(1)}, bf16[3,2048]{1,0:T(4,128)(2,1)S(1)}, u32[]{:S(2)}, u32[]{:S(2)}) collective-permute-start(bf16[3,2048]{1,0:T(4,128)(2,1)S(1)} %slice_bitcast_fusion), channel_id=1, source_target_pairs={{0,2},{2,4},{4,6},{1,3},{3,5},{5,7},{8,10},{10,12},{12,14},{9,11},... | collective-permute-start | bytes 36872 | tf_op jit(solution)/shard_map/ppermute | solution.py:10
  483.1 4.1 copy-start.2
  485.9 19.8 %collective-permute-start.1 = (bf16[128,2048]{1,0:T(8,128)(2,1)S(1)}, bf16[128,2048]{1,0:T(8,128)(2,1)S(1)}, u32[]{:S(2)}, u32[]{:S(2)}) collective-permute-start(bf16[128,2048]{1,0:T(8,128)(2,1)S(1)} %fusion.30), channel_id=1, source_target_pairs={{8,0},{16,8},{24,16},{9,1},{17,9},{25,17},{10,2},{18,10},{26,18},{... | collective-permute-start | bytes 1572872 | tf_op jit(solution)/shard_map/ppermute | solution.py:10
Sparse Core Ops, SparseCore 0:
  9.6 11.7 all-gather.4
  22.9 377.7 all-gather.6
  403.0 14.9 reduce-scatter.2
  420.2 10.8 reduce-scatter.4
where the time goes:
time: 514 us; the launch traced here: 513 us
  blocking collectives  219 us (43%)
  waiting for transfers between devices  205 us (40%)
  local copies, waits for them, and re-layouts  22.1 us (4%)
  matrix products  21 us (4%)
  other arithmetic  19.8 us (4%)
  between operations  14 us (3%)
  starting transfers between devices  11.8 us (2%)
    all_to_all x1, blocking collectives, shards(): lax.all_to_all(buffer, 'expert', split_axis=0, concat_axis=0, tiled=True)  201 us
    all_gather x1, waiting for transfers between devices, shards(): lax.all_gather(w_proj, 'expert', axis=0, tiled=True)  134 us
    ppermute x3, waiting for transfers between devices, shifted(): return lax.ppermute(array, axis, pairs)  42.5 us
    psum x1, blocking collectives, shards(): tap_grads = lax.psum(jnp.stack(tap_terms), 'expert')  17.9 us
    dot_general x1, matrix products, shards(): lax.dot_general(input_grad, lax.all_gather(w_proj, 'expert', axis=0, tile...  12.8 us
    all_to_all x1, waiting for transfers between devices, shards(): lax.all_to_all(share.reshape(experts, capacity, share.shape[1]), 'expert'...  12.7 us
    mul x2, local copies, waits for them, and re-layouts, gated_rows(): gates[:, :, None] * rows.astype(jnp.float32)[:, None, :]  10.6 us
  transfers between devices with their start and end apart: 8, of which 6 were waited for; matrix products, arithmetic and copies ran while one was open for 11% of the time, Pallas kernels for 0%

commit v1 on v0

--- a/solution.py
+++ b/solution.py
@@ -26,7 +26,7 @@
     return buffer.reshape(experts, capacity, width)
 
 
-def shards(
+def slot_plan(
     out_grad,
     expert_ids,
     gate_codes,
@@ -106,6 +106,88 @@
     return (sent_residual[None], tap_grads[None])
 
 
+def token_plan(
+    out_grad,
+    expert_ids,
+    gate_codes,
+    up_weight,
+    down_weight,
+    pre_act,
+    conv_grad,
+    conv_input,
+    conv_weight,
+    in_proj,
+):
+    experts = lax.axis_size("expert")
+    halves = lax.axis_size("mp")
+    me = lax.axis_index("expert")
+    grad_rows = out_grad[0]
+    tok_rows, half_width = grad_rows.shape
+    tokens = experts * tok_rows
+    width = halves * half_width
+
+    pairs = (expert_ids[0] * 256 + gate_codes[0]).T
+    rows_here = lax.all_gather(grad_rows, "expert", axis=0, tiled=True)
+    all_rows = lax.all_gather(rows_here, "mp", axis=1, tiled=True)
+    all_pairs = lax.all_gather(pairs, "expert", axis=0)
+    all_conv = lax.all_gather(conv_grad[0], "expert", axis=0, tiled=True)
+
+    named = (all_pairs // 256 == me).astype(jnp.int32)
+    codes = jnp.sum(named * (all_pairs % 256), axis=1)
+    named = jnp.sum(named, axis=1)
+    gates = codes.reshape(tokens).astype(jnp.float32) / 256.0
+    earlier = jnp.triu(jnp.ones((tok_rows, tok_rows), jnp.bfloat16), 1)
+    rank = jnp.dot(named.astype(jnp.bfloat16), earlier, preferred_element_type=jnp.float32)
+    rank = jnp.where(named == 1, rank.astype(jnp.int32), -1)
+    pick = (rank[:, :, None] == jnp.arange(tok_rows, dtype=jnp.int32)).astype(jnp.bfloat16)
+    pre_blocks = pre_act[0, 0].reshape(experts, tok_rows, pre_act.shape[3])
+    pre_tokens = jnp.einsum("bts,bsf->btf", pick, pre_blocks, preferred_element_type=jnp.float32)
+    slope = silu_slope(pre_tokens.reshape(tokens, pre_act.shape[3]))
+
+    dispatched = (gates[:, None] * all_rows.astype(jnp.float32)).astype(jnp.bfloat16)
+    hidden = lax.dot_general(
+        dispatched, down_weight[0, 0], (((1,), (1,)), ((), ())), preferred_element_type=jnp.float32
+    )
+    pre_grad = (hidden * slope).astype(jnp.bfloat16)
+    partial = lax.dot_general(
+        pre_grad, up_weight[0, 0], (((1,), (1,)), ((), ())), preferred_element_type=jnp.float32
+    )
+
+    taps = conv_weight[0]
+    kernel_size = taps.shape[0]
+    padded = jnp.pad(all_conv, ((0, kernel_size - 1), (0, 0)))
+    window = lax.dynamic_slice_in_dim(padded, me * tok_rows, tok_rows + kernel_size - 1, 0)
+    window = window.astype(jnp.float32)
+    inputs_here = conv_input[0].astype(jnp.float32)
+    conv_result = jnp.zeros((tokens, half_width), jnp.float32)
+    tap_terms = []
+    for tap in range(kernel_size):
+        start = kernel_size - 1 - tap
+        conv_result = conv_result + taps[tap][None, :] * padded[start : start + tokens].astype(jnp.float32)
+        tap_terms.append(jnp.sum(inputs_here * window[start : start + tok_rows], axis=0))
+    tap_grads = lax.psum(jnp.stack(tap_terms), "expert")
+    proj = lax.dot_general(
+        conv_result.astype(jnp.bfloat16),
+        in_proj[0],
+        (((1,), (1,)), ((), ())),
+        preferred_element_type=jnp.float32,
+    )
+    block = width // experts
+    columns = partial.reshape(tokens, experts, block)
+    mine = (jnp.arange(experts) == me)[None, :, None]
+    total = columns + jnp.where(mine, proj[:, None, :], 0.0)
+    total = total.reshape(experts, tok_rows, halves, half_width).transpose(0, 2, 1, 3)
+    total = total.reshape(experts * halves, tok_rows, half_width).astype(jnp.bfloat16)
+    share = lax.psum_scatter(total, ("expert", "mp"), scatter_dimension=0, tiled=False)
+    residual = (grad_rows.astype(jnp.float32) + share.astype(jnp.float32)).astype(jnp.bfloat16)
+    return (shifted(residual, "section", -1)[None], tap_grads[None])
+
+
+def shards(*arrays):
+    tok_rows, capacity = arrays[0].shape[1], arrays[5].shape[2] // lax.axis_size("expert")
+    return (token_plan if capacity == tok_rows else slot_plan)(*arrays)
+
+
 def solution(mesh):
     in_specs = (
         P("section", "expert", "mp"),

time: 514 us -> 229 us (0.45)
  blocking collectives: 219 us -> 25.6 us
  waiting for transfers between devices: 205 us -> 141 us
  other arithmetic: 19.8 us -> 4.12 us
  starting transfers between devices: 11.8 us -> 1.44 us
    all_to_all x1 -> x0, blocking collectives: 201 us -> none  [shards(): lax.all_to_all(buffer, 'expert', split_axis=0, concat_axis=0, tiled=True)]
    all_gather x2 -> x3, waiting for transfers between devices: 144 us -> 89.1 us  [the longest x1 49.5 us: token_plan(): rows_here = lax.all_gather(grad_rows, 'expert', axis=0, tiled=True)]
    reduce_scatter x2 -> x1, waiting for transfers between devices: 4.49 us -> 50 us  [token_plan(): lax.psum_scatter(total, ('expert', 'mp'), scatter_dimension=0, tiled=False)]
    ppermute x3 -> x1, waiting for transfers between devices: 42.5 us -> 0.01 us  [shifted(): return lax.ppermute(array, axis, pairs)]
    convert_element_type x1 -> x3, local copies, waits for them, and re-layouts: 2.37 us -> 20.7 us  [token_plan(): total.reshape(experts * halves, tok_rows, half_width).astype(jnp.bfloat16)]
    all_to_all x1 -> x0, waiting for transfers between devices: 12.7 us -> none  [shards(): lax.all_to_all(share.reshape(experts, capacity, share.shape[1]), 'expert'...]
    mul x4 -> x0, local copies, waits for them, and re-layouts: 10.9 us -> none  [the longest x2 10.6 us: gated_rows(): gates[:, :, None] * rows.astype(jnp.float32)[:, None, :]]
    all_gather x0 -> x1, blocking collectives: none -> 8.69 us  [token_plan(): all_pairs = lax.all_gather(pairs, 'expert', axis=0)]
  transfers between devices with their start and end apart: 8 -> 5, of which waited for: 6 -> 4; matrix products, arithmetic and copies ran while one was open for 11% -> 6% of each run, Pallas kernels for 0% -> 0%
where the time goes in v1:
time: 229 us; the launch traced here: 228 us
  waiting for transfers between devices  141 us (62%)
  blocking collectives  25.6 us (11%)
  local copies, waits for them, and re-layouts  21.5 us (9%)
  matrix products  21.1 us (9%)
  between operations  13.9 us (6%)
  other arithmetic  4.12 us (2%)
    reduce_scatter x1, waiting for transfers between devices, token_plan(): lax.psum_scatter(total, ('expert', 'mp'), scatter_dimension=0, tiled=False)  50 us
    all_gather x1, waiting for transfers between devices, token_plan(): rows_here = lax.all_gather(grad_rows, 'expert', axis=0, tiled=True)  49.5 us
    all_gather x1, waiting for transfers between devices, token_plan(): all_conv = lax.all_gather(conv_grad[0], 'expert', axis=0, tiled=True)  35.9 us
    convert_element_type x3, local copies, waits for them, and re-layouts, token_plan(): total.reshape(experts * halves, tok_rows, half_width).astype(jnp.bfloat16)  20.7 us
    psum x1, blocking collectives, token_plan(): tap_grads = lax.psum(jnp.stack(tap_terms), 'expert')  16.9 us
    dot_general x1, matrix products, token_plan(): lax.dot_general(conv_result.astype(jnp.bfloat16), in_proj[0], (((1,), (1,...  10.3 us
    all_gather x1, blocking collectives, token_plan(): all_pairs = lax.all_gather(pairs, 'expert', axis=0)  8.69 us
    dot_general x1, matrix products, token_plan(): lax.dot_general(dispatched, down_weight[0, 0], (((1,), (1,)), ((), ())),...  5.97 us
  transfers between devices with their start and end apart: 5, of which 4 were waited for; matrix products, arithmetic and copies ran while one was open for 6% of the time, Pallas kernels for 0%

profile of v1, /device:TPU:0, one launch (start us, length us, event | category | flops | bytes accessed | tf_op | source)
XLA Modules:
  0.0 228.2 jit_solution(8711012415301170130)
XLA Ops:
  7.2 0.0 copy-start
  7.2 0.0 copy-start.3
  7.2 0.0 all-gather.9.cloned.1.call-start
  7.2 0.7 all-gather.9.cloned.1.call-update
  7.9 0.0 all-gather.13.cloned.1.call-start
  8.0 0.7 all-gather.13.cloned.1.call-update
  8.7 0.0 all-gather.11.cloned.1.call-start
  8.7 49.5 %all-gather.9.cloned.1.call-done = bf16[1,512,2048]{2,1,0:T(8,128)(2,1)} async-done(((bf16[1,128,2048]{2,1,0:T(8,128)(2,1)}), bf16[1,512,2048]{2,1,0:T(8,128)(2,1)}) %all-gather.9.cloned.1.call-update) | async-done | bytes 2097168 | tf_op jit(solution)/shard_map/all_gather | solution.py:130
  58.3 0.0 all-gather.11.cloned.1.call-update
  58.3 0.0 reduce-scatter.2.cloned.1.call-start
  58.3 0.7 add_bitcast_fusion
  59.0 8.7 %all-gather.4 = s32[4,2,128]{2,1,0:T(2,128)S(1)} all-gather(s32[1,2,128]{2,1,0:T(2,128)S(1)} %add_bitcast_fusion), channel_id=2, replica_groups=mesh['section'=4,'expert'=4,'mp'=2] {'expert'}, dimensions={0}, use_global_device_ids=true | all-gather | bytes 5120 | tf_op jit(solution)/shard_map/all_gather | solution.py:132
  67.8 0.1 fusion.30
  67.9 0.0 copy-done
  67.9 0.4 fusion.42
  68.3 0.3 fusion.39
  68.6 0.0 copy-done.3
  68.6 35.9 %all-gather.13.cloned.1.call-done = bf16[1,512,2048]{2,1,0:T(8,128)(2,1)} async-done(((bf16[1,128,2048]{2,1,0:T(8,128)(2,1)}), bf16[1,512,2048]{2,1,0:T(8,128)(2,1)}) %all-gather.13.cloned.1.call-update) | async-done | bytes 2097168 | tf_op jit(solution)/shard_map/all_gather | solution.py:133
  104.5 10.3 %fusion.4 = f32[512,1024]{1,0:T(8,128)} fusion(bf16[1,1024,2048]{2,1,0:T(8,128)(2,1)} %param.19, bf16[512,2048]{1,0:T(8,128)(2,1)} %bitcast.81, f32[2048]{0:T(1024)S(1)} %bitcast.90, f32[2048]{0:T(1024)S(1)} %bitcast.91, f32[2048]{0:T(1024)S(1)} %bitcast.89, f32[2048]{0:T(1024)S(1)} %bitcast.88), kind=kOutput, calls=%fused_computation.5 | convolution fusion | flops 2160066560 | bytes 8421376 | tf_op jit(solution)/shard_map/dot_general | solution.py:169
  114.8 3.7 %all-gather.11.cloned.1.call-done = bf16[1,512,4096]{2,1,0:T(8,128)(2,1)} async-done(((bf16[1,512,2048]{2,1,0:T(8,128)(2,1)}), bf16[1,512,4096]{2,1,0:T(8,128)(2,1)}) %all-gather.11.cloned.1.call-update) | async-done | bytes 4194320 | tf_op jit(solution)/shard_map/all_gather | solution.py:131
  118.5 0.0 copy-start.4
  118.5 0.0 copy-start.5
  118.5 6.0 %fusion.25 = bf16[512,512,1]{1,0,2:T(8,128)(2,1)S(1)} fusion(f32[512,512]{1,0:T(8,128)S(1)} %fusion.39, bf16[1,1,512,4096]{3,2,1,0:T(8,128)(2,1)} %param.14, bf16[1,512,4096]{2,1,0:T(8,128)(2,1)} %all-gather.11.cloned.1.call-done, f32[512]{0:T(512)S(1)} %multiply_bitcast_fusion), kind=kOutput, calls=%fused_computation.25 | convolution fusion | flops 2154299392 | bytes 9963520 | tf_op jit(solution)/shard_map/dot_general | solution.py:148
  124.4 0.0 copy-done.4
  124.5 0.0 copy-done.5
  124.5 4.4 %add_convert_fusion = bf16[512,4,1024]{2,0,1:T(8,128)(2,1)} fusion(f32[512,1024]{1,0:T(8,128)S(1)} %copy-done.5, pred[4]{0:T(512)(128)(4,1)S(1)} %iota_compare_fusion.3, bf16[512,512,1]{1,0,2:T(8,128)(2,1)S(1)} %fusion.25, bf16[4,1024,512]{2,1,0:T(8,128)(2,1)S(1)} %bitcast.92), kind=kOutput, calls=%fused_computation.2 | convolution fusion | flops 2153775104 | bytes 11010052 | tf_op jit(solution)/shard_map/dot_general | solution.py:152
  128.8 6.2 %copy.15 = bf16[512,4,1024]{0,2,1:T(8,128)(2,1)} copy(bf16[512,4,1024]{2,0,1:T(8,128)(2,1)} %add_convert_fusion) | data formatting | bytes 8388608 | tf_op jit(solution)/shard_map/convert_element_type | solution.py:180
  135.0 6.9 %convert_element_type.91 = bf16[4,128,2,2048]{1,0,3,2:T(4,128)(2,1)} reshape(bf16[512,4,1024]{0,2,1:T(8,128)(2,1)} %copy.15) | data formatting | bytes 8388608 | tf_op jit(solution)/shard_map/convert_element_type | solution.py:180
  141.9 7.6 %copy.16 = bf16[4,2,128,2048]{3,2,1,0:T(8,128)(2,1)} copy(bf16[4,2,128,2048]{2,0,3,1:T(4,128)(2,1)} %bitcast.80) | data formatting | bytes 8388608 | tf_op jit(solution)/shard_map/convert_element_type | solution.py:180
  149.5 0.0 copy-start.1
  149.5 0.0 copy-start.2
  149.5 0.0 reduce-scatter.2.cloned.1.call-update
  149.5 1.3 fusion.40
  150.8 50.0 %reduce-scatter.2.cloned.1.call-done = bf16[1,128,2048]{2,1,0:T(8,128)(2,1)} async-done(((bf16[8,128,2048]{2,1,0:T(8,128)(2,1)}), bf16[1,128,2048]{2,1,0:T(8,128)(2,1)}) %reduce-scatter.2.cloned.1.call-update) | async-done | bytes 524304 | tf_op jit(solution)/shard_map/reduce_scatter | solution.py:181
  200.9 0.0 copy-done.1
  200.9 1.2 fusion.41
  202.0 1.3 collective-permute-start
  203.3 0.0 copy-done.2
  203.3 0.6 fusion.31
  204.0 16.9 %psum.7 = f32[1,4,2048]{2,1,0:T(4,128)} all-reduce(f32[1,4,2048]{2,1,0:T(4,128)S(1)} %maximum_bitcast_fusion), channel_id=1, replica_groups=mesh['section'=4,'expert'=4,'mp'=2] {'expert'}, use_global_device_ids=true, to_apply=%region_7.8 | all-reduce | flops 8192 | bytes 65536 | tf_op jit(solution)/shard_map/psum | solution.py:168
  220.9 0.0 collective-permute-done
  220.9 0.8 copy.18
  (5 shorter events, 0.1 us)
Async XLA Ops:
  7.2 60.8 %copy-start = (bf16[1,1,512,512]{3,2,1,0:T(8,128)(2,1)S(1)}, bf16[1,1,512,512]{3,2,1,0:T(8,128)(2,1)}, u32[]{:S(2)}) copy-start(bf16[1,1,512,512]{3,2,1,0:T(8,128)(2,1)} %param.15) | copy-start | bytes 1572868
  7.2 61.4 %copy-start.3 = (f32[1,4,2048]{2,1,0:T(4,128)S(1)}, f32[1,4,2048]{2,1,0:T(4,128)}, u32[]{:S(2)}) copy-start(f32[1,4,2048]{2,1,0:T(4,128)} %param.18) | copy-start | bytes 98308
  7.2 51.1 %all-gather.9.cloned.1.call-start = ((), (), s32[]{:S(2)}) async-start(), calls=%async_computation.2 | async-start | bytes 2621440 | tf_op jit(solution)/shard_map/all_gather | solution.py:130
  7.9 96.6 %all-gather.13.cloned.1.call-start = ((), (), s32[]{:S(2)}) async-start(), calls=%async_computation.4 | async-start | bytes 2621440 | tf_op jit(solution)/shard_map/all_gather | solution.py:133
  8.7 109.8 %all-gather.11.cloned.1.call-start = ((), (), s32[]{:S(2)}) async-start(), calls=%async_computation.3 | async-start | bytes 6291456 | tf_op jit(solution)/shard_map/all_gather | solution.py:131
  58.3 142.6 %reduce-scatter.2.cloned.1.call-start = ((), (), s32[]{:S(2)}) async-start(), calls=%async_computation.1 | async-start | bytes 4718592 | tf_op jit(solution)/shard_map/reduce_scatter | solution.py:181
  118.5 6.0 %copy-start.4 = (bf16[1,1,4096,512]{3,2,1,0:T(8,128)(2,1)S(1)}, bf16[1,1,4096,512]{3,2,1,0:T(8,128)(2,1)}, u32[]{:S(2)}) copy-start(bf16[1,1,4096,512]{3,2,1,0:T(8,128)(2,1)} %param.13) | copy-start | bytes 12582916
  118.5 6.0 %copy-start.5 = (f32[512,1024]{1,0:T(8,128)S(1)}, f32[512,1024]{1,0:T(8,128)}, u32[]{:S(2)}) copy-start(f32[512,1024]{1,0:T(8,128)} %fusion.4) | copy-start | bytes 6291460
  149.5 51.4 %copy-start.1 = (bf16[1,128,2048]{2,1,0:T(8,128)(2,1)S(1)}, bf16[1,128,2048]{2,1,0:T(8,128)(2,1)}, u32[]{:S(2)}) copy-start(bf16[1,128,2048]{2,1,0:T(8,128)(2,1)} %param.10) | copy-start | bytes 1572868
  149.5 53.8 %copy-start.2 = (bf16[1,128,2048]{2,1,0:T(8,128)(2,1)S(1)}, bf16[1,128,2048]{2,1,0:T(8,128)(2,1)}, u32[]{:S(2)}) copy-start(bf16[1,128,2048]{2,1,0:T(8,128)(2,1)} %param.17) | copy-start | bytes 1572868
  202.0 18.9 %collective-permute-start = (bf16[128,2048]{1,0:T(8,128)(2,1)S(1)}, bf16[128,2048]{1,0:T(8,128)(2,1)S(1)}, u32[]{:S(2)}, u32[]{:S(2)}) collective-permute-start(bf16[128,2048]{1,0:T(8,128)(2,1)S(1)} %fusion.41), channel_id=1, source_target_pairs={{8,0},{16,8},{24,16},{9,1},{17,9},{25,17},{10,2},{18,10},{26,18},{... | collective-permute-start | bytes 1572872 | tf_op jit(solution)/shard_map/ppermute | solution.py:10
Sparse Core Ops, SparseCore 0:
  9.6 48.6 all-gather.8
  59.8 44.6 all-gather.12
  106.1 12.3 all-gather.10
  149.6 51.1 reduce-scatter.1

commit v2 on v0

--- a/solution.py
+++ b/solution.py
@@ -1,6 +1,10 @@
+import functools
+
 import jax
 import jax.numpy as jnp
 from jax import lax
+from jax.experimental import pallas as pl
+from jax.experimental.pallas import tpu as pltpu
 from jax.sharding import PartitionSpec as P
 
 
@@ -26,7 +30,7 @@
     return buffer.reshape(experts, capacity, width)
 
 
-def shards(
+def slot_plan(
     out_grad,
     expert_ids,
     gate_codes,
@@ -106,6 +110,275 @@
     return (sent_residual[None], tap_grads[None])
 
 
+F32, BF16 = jnp.float32, jnp.bfloat16
+VMEM_LIMIT = 40 * 1024 * 1024
+NT = (((1,), (1,)), ((), ()))
+TN = (((0,), (0,)), ((), ()))
+
+
+def whole(memory=pltpu.VMEM):
+    return pl.BlockSpec(memory_space=memory)
+
+
+def rotated(array, axis, by):
+    size = lax.axis_size(axis)
+    return lax.ppermute(array, axis, [(i, (i + by) % size) for i in range(size)])
+
+
+def around(array):
+    return [array] + [rotated(array, "expert", k) for k in range(1, lax.axis_size("expert"))]
+
+
+def doubling_sum(array, axis):
+    size, step = lax.axis_size(axis), 1
+    while step < size:
+        array = array + lax.ppermute(array, axis, [(i, i ^ step) for i in range(size)])
+        step *= 2
+    return array
+
+
+def expert_kernel(steps, place, *refs):
+    experts = len(refs) - 8
+    pairs = refs[:experts]
+    rows, down, up, pre, out, gates, slope, hidden = refs[experts:]
+    tok_rows = pre.shape[0] // experts
+    me, step = place[0], pl.program_id(0)
+
+    @pl.when(step == 0)
+    def _():
+        row = lax.broadcasted_iota(jnp.int32, (tok_rows, tok_rows), 0)
+        column = lax.broadcasted_iota(jnp.int32, (tok_rows, tok_rows), 1)
+
+        def upright(line):
+            return jnp.sum(jnp.where(row == column, line, 0.0), axis=1, keepdims=True)
+
+        for k in range(experts):
+            at = pl.ds(pl.multiple_of(lax.rem(me - k + experts, experts) * tok_rows, tok_rows), tok_rows)
+            pair = pairs[k][...]
+            named = (pair // 256) == me
+            code = jnp.sum(jnp.where(named, (pair % 256).astype(F32), 0.0), axis=0, keepdims=True)
+            named = jnp.sum(jnp.where(named, 1.0, 0.0), axis=0, keepdims=True)
+            gates[at, :] = upright(code) / 256.0
+            rank = jnp.sum(jnp.where(row < column, upright(named), 0.0), axis=0, keepdims=True)
+            pick = jnp.where(rank.astype(jnp.int32) == row, named, 0.0).astype(BF16)
+            p = lax.dot_general(pick, pre[at, :], TN, preferred_element_type=F32)
+            q = 1.0 / (1.0 + jnp.exp(-p))
+            slope[at, :] = q * (1.0 + p * (1.0 - q))
+        hidden[...] = jnp.zeros_like(hidden)
+
+    @pl.when(step < steps)
+    def _():
+        values = rows[...].reshape(experts * tok_rows, rows.shape[-1]).astype(F32)
+        scaled = (gates[...] * values).astype(BF16)
+        hidden[...] += lax.dot_general(scaled, down[...], NT, preferred_element_type=F32)
+
+    @pl.when(step >= steps)
+    def _():
+        pre_grad = (hidden[...] * slope[...]).astype(BF16)
+        result = lax.dot_general(pre_grad, up[...], NT, preferred_element_type=F32)
+        out[...] = result.astype(BF16).reshape(out.shape)
+
+
+def expert_sums(place, pairs, rows, down, up, pre):
+    experts, halves, tok_rows, half_width = rows.shape
+    units, width = down.shape
+    tokens = experts * tok_rows
+    chunk = half_width // 2
+    per_half = half_width // chunk
+    steps = width // chunk
+
+    def first(i):
+        return jnp.minimum(i, steps - 1)
+
+    def second(i):
+        return jnp.maximum(i - steps, 0)
+
+    block = (experts, 1, tok_rows, chunk)
+    return pl.pallas_call(
+        functools.partial(expert_kernel, steps),
+        grid=(2 * steps,),
+        in_specs=[whole(pltpu.SMEM)]
+        + [whole()] * experts
+        + [
+            pl.BlockSpec(block, lambda i: (0, first(i) // per_half, 0, first(i) % per_half)),
+            pl.BlockSpec((units, chunk), lambda i: (0, first(i))),
+            pl.BlockSpec((chunk, units), lambda i: (second(i), 0)),
+            whole(),
+        ],
+        out_specs=pl.BlockSpec(block, lambda i: (0, second(i) // per_half, 0, second(i) % per_half)),
+        out_shape=jax.ShapeDtypeStruct(rows.shape, BF16),
+        scratch_shapes=[
+            pltpu.VMEM((tokens, 1), F32),
+            pltpu.VMEM((tokens, units), F32),
+            pltpu.VMEM((tokens, units), F32),
+        ],
+        compiler_params=pltpu.CompilerParams(vmem_limit_bytes=VMEM_LIMIT),
+        cost_estimate=pl.CostEstimate(
+            flops=4 * tokens * width * units, bytes_accessed=8 * width * units + 4 * tokens * width, transcendentals=0
+        ),
+        name="experts",
+    )(place, *pairs, rows, down, up, pre)
+
+
+def proj_kernel(place, *refs):
+    experts = len(refs) - 8
+    grads = refs[:experts]
+    inputs, taps, weight, keep, send, tap_out, ext, total = refs[experts:]
+    tok_rows, chunk = inputs.shape
+    tokens = experts * tok_rows
+    kernel_size = taps.shape[0]
+    me, half, step = place[0], place[1], pl.program_id(0)
+
+    for k in range(experts):
+        at = pl.ds(pl.multiple_of(lax.rem(me - k + experts, experts) * tok_rows, tok_rows), tok_rows)
+        ext[at, :] = grads[k][...].astype(F32)
+    ext[tokens:, :] = jnp.zeros((ext.shape[0] - tokens, chunk), F32)
+
+    tap = taps[...]
+    result = jnp.zeros((tokens, chunk), F32)
+    for j in range(kernel_size):
+        start = kernel_size - 1 - j
+        result = result + tap[j : j + 1, :] * ext[start : start + tokens, :]
+    window = ext[pl.ds(pl.multiple_of(me * tok_rows, tok_rows), tok_rows + 8), :]
+    values = inputs[...].astype(F32)
+    for j in range(kernel_size):
+        start = kernel_size - 1 - j
+        tap_out[j : j + 1, :] = jnp.sum(values * window[start : start + tok_rows, :], axis=0, keepdims=True)
+
+    product = lax.dot_general(result.astype(BF16), weight[...], NT, preferred_element_type=F32)
+
+    @pl.when(step == 0)
+    def _():
+        total[...] = product
+
+    @pl.when(step > 0)
+    def _():
+        total[...] += product
+
+    @pl.when(step == pl.num_programs(0) - 1)
+    def _():
+        part = keep.shape[1]
+        keep[...] = total[:, pl.ds(pl.multiple_of(half * part, part), part)]
+        send[...] = total[:, pl.ds(pl.multiple_of((1 - half) * part, part), part)].astype(BF16)
+
+
+def proj_sums(place, grads, inputs, taps, weight):
+    experts = len(grads)
+    tok_rows, half_width = inputs.shape
+    block = weight.shape[0]
+    part = block // 2
+    tokens = experts * tok_rows
+    chunk = half_width // 4
+
+    def wide(rows):
+        return pl.BlockSpec((rows, chunk), lambda i: (0, i))
+
+    return pl.pallas_call(
+        proj_kernel,
+        grid=(half_width // chunk,),
+        in_specs=[whole(pltpu.SMEM)]
+        + [wide(tok_rows)] * (experts + 1)
+        + [wide(taps.shape[0]), wide(block)],
+        out_specs=[
+            pl.BlockSpec((tokens, part), lambda i: (0, 0)),
+            pl.BlockSpec((tokens, part), lambda i: (0, 0)),
+            wide(taps.shape[0]),
+        ],
+        out_shape=[
+            jax.ShapeDtypeStruct((tokens, part), F32),
+            jax.ShapeDtypeStruct((tokens, part), BF16),
+            jax.ShapeDtypeStruct(taps.shape, F32),
+        ],
+        scratch_shapes=[pltpu.VMEM((tokens + 8, chunk), F32), pltpu.VMEM((tokens, block), F32)],
+        compiler_params=pltpu.CompilerParams(vmem_limit_bytes=VMEM_LIMIT),
+        cost_estimate=pl.CostEstimate(
+            flops=2 * tokens * half_width * block,
+            bytes_accessed=2 * (block + tokens) * half_width + 6 * tokens * part,
+            transcendentals=0,
+        ),
+        name="projection",
+    )(place, *grads, inputs, taps, weight)
+
+
+def final_kernel(place, grad, share, *refs):
+    pieces, out = refs[:-1], refs[-1]
+    count, part = len(pieces), pieces[0].shape[1]
+    for r in range(count):
+        at = pl.ds(pl.multiple_of(lax.rem(place[0] - r + count, count) * part, part), part)
+        value = grad[:, at].astype(F32) + share[:, at].astype(F32) + pieces[r][...].astype(F32)
+        out[:, at] = value.astype(BF16)
+
+
+def final_sum(place, grad, share, pieces):
+    return pl.pallas_call(
+        final_kernel,
+        in_specs=[whole(pltpu.SMEM)] + [whole()] * (2 + len(pieces)),
+        out_specs=whole(),
+        out_shape=jax.ShapeDtypeStruct(grad.shape, BF16),
+        compiler_params=pltpu.CompilerParams(vmem_limit_bytes=VMEM_LIMIT),
+        cost_estimate=pl.CostEstimate(flops=2 * grad.size, bytes_accessed=8 * grad.size, transcendentals=0),
+        name="residual",
+    )(place, grad, share, *pieces)
+
+
+def returned_pieces(keep, received, me, half):
+    experts, halves = lax.axis_size("expert"), lax.axis_size("mp")
+    tok_rows = keep.shape[0] // experts
+    pieces = []
+    for r in range(experts):
+        owner = (2 * (me % 2) + half + r) % experts
+        at = owner * tok_rows
+        piece = lax.dynamic_slice_in_dim(keep, at, tok_rows, 0)
+        piece = piece + lax.dynamic_slice_in_dim(received, at, tok_rows, 0).astype(F32)
+        pairs = []
+        for e in range(experts):
+            for m in range(halves):
+                pairs.append((e * halves + m, (2 * (e % 2) + m + r) % experts * halves + e // 2))
+        pieces.append(lax.ppermute(piece.astype(BF16), ("expert", "mp"), pairs))
+    return pieces
+
+
+def token_plan(
+    out_grad,
+    expert_ids,
+    gate_codes,
+    up_weight,
+    down_weight,
+    pre_act,
+    conv_grad,
+    conv_input,
+    conv_weight,
+    in_proj,
+):
+    me, half = lax.axis_index("expert"), lax.axis_index("mp")
+    place = jnp.stack([me, half]).astype(jnp.int32)
+    grad_rows = out_grad[0]
+    experts, halves = lax.axis_size("expert"), lax.axis_size("mp")
+    tok_rows, half_width = grad_rows.shape
+
+    rows = lax.all_gather(grad_rows, ("expert", "mp"), axis=0)
+    rows = rows.reshape(experts, halves, tok_rows, half_width)
+    pairs = around((expert_ids[0] * 256 + gate_codes[0]).T)
+    grads = around(conv_grad[0])
+    sums = expert_sums(place, pairs, rows, down_weight[0, 0], up_weight[0, 0], pre_act[0, 0])
+    sums = sums.reshape(experts * halves, tok_rows, half_width)
+    share = lax.psum_scatter(sums, ("expert", "mp"), scatter_dimension=0, tiled=False)
+
+    keep, send, tap_terms = proj_sums(place, grads, conv_input[0], conv_weight[0], in_proj[0])
+    received = rotated(send, "mp", 1)
+    pieces = returned_pieces(keep, received, me, half)
+    tap_grads = doubling_sum(tap_terms, "expert")
+    residual = final_sum(place, grad_rows, share, pieces)
+    return (shifted(residual, "section", -1)[None], tap_grads[None])
+
+
+def shards(*arrays):
+    experts, halves = lax.axis_size("expert"), lax.axis_size("mp")
+    capacity = arrays[5].shape[2] // experts
+    dense = capacity == arrays[0].shape[1] and experts == 4 and halves == 2
+    return (token_plan if dense else slot_plan)(*arrays)
+
+
 def solution(mesh):
     in_specs = (
         P("section", "expert", "mp"),

time: 514 us -> 206 us (0.40)
  blocking collectives: 219 us -> 0 us
  waiting for transfers between devices: 205 us -> 108 us
  starting transfers between devices: 11.8 us -> 48.1 us
  matrix products: 21 us -> 0 us
  other arithmetic: 19.8 us -> 1.6 us
  Pallas kernels: 0 us -> 18 us
  local copies, waits for them, and re-layouts: 22.1 us -> 12.5 us
    all_to_all x1 -> x0, blocking collectives: 201 us -> none  [shards(): lax.all_to_all(buffer, 'expert', split_axis=0, concat_axis=0, tiled=True)]
    all_gather x2 -> x1, waiting for transfers between devices: 144 us -> 41.7 us  [token_plan(): rows = lax.all_gather(grad_rows, ('expert', 'mp'), axis=0)]
    ppermute x0 -> x13, waiting for transfers between devices: none -> 65.1 us  [the longest x7 55.9 us: rotated(): lax.ppermute(array, axis, [(i, (i + by) % size) for i in range(size)])]
    ppermute x0 -> x13, starting transfers between devices: none -> 46.8 us  [the longest x4 31.3 us: returned_pieces(): pieces.append(lax.ppermute(piece.astype(BF16), ('expert', 'mp'), pairs))]
    ppermute x3 -> x1, waiting for transfers between devices: 42.5 us -> 0.78 us  [shifted(): return lax.ppermute(array, axis, pairs)]
    dot_general x3 -> x0, matrix products: 21 us -> none  [the longest x1 12.8 us: shards(): lax.dot_general(input_grad, lax.all_gather(w_proj, 'expert', axis=0, tile...]
    pallas_call x0 -> x3, Pallas kernels: none -> 18 us  [the longest x1 9.92 us: expert_sums(): pl.pallas_call(functools.partial(expert_kernel, steps), grid=(2 * steps,)...]
    psum x1 -> x0, blocking collectives: 17.9 us -> none  [shards(): tap_grads = lax.psum(jnp.stack(tap_terms), 'expert')]
  transfers between devices with their start and end apart: 8 -> 16, of which waited for: 6 -> 11; matrix products, arithmetic and copies ran while one was open for 11% -> 1% of each run, Pallas kernels for 0% -> 4%
where the time goes in v2:
time: 206 us; the launch traced here: 203 us
  waiting for transfers between devices  108 us (52%)
  starting transfers between devices  48.1 us (23%)
  Pallas kernels  18 us (9%)
  between operations  14.2 us (7%)
  local copies, waits for them, and re-layouts  12.5 us (6%)
    ppermute x7, waiting for transfers between devices, rotated(): lax.ppermute(array, axis, [(i, (i + by) % size) for i in range(size)])  55.9 us
    all_gather x1, waiting for transfers between devices, token_plan(): rows = lax.all_gather(grad_rows, ('expert', 'mp'), axis=0)  41.7 us
    ppermute x4, starting transfers between devices, returned_pieces(): pieces.append(lax.ppermute(piece.astype(BF16), ('expert', 'mp'), pairs))  31.3 us
    unnamed x21, local copies, waits for them, and re-layouts  12.5 us
    ppermute x7, starting transfers between devices, rotated(): lax.ppermute(array, axis, [(i, (i + by) % size) for i in range(size)])  11 us
    pallas_call x1, Pallas kernels, expert_sums(): pl.pallas_call(functools.partial(expert_kernel, steps), grid=(2 * steps,)...  9.92 us
    pallas_call x1, Pallas kernels, proj_sums(): pl.pallas_call(proj_kernel, grid=(half_width // chunk,), in_specs=[whole(...  7.37 us
    ppermute x2, waiting for transfers between devices, doubling_sum(): lax.ppermute(array, axis, [(i, i ^ step) for i in range(size)])  6.67 us
  transfers between devices with their start and end apart: 16, of which 11 were waited for; matrix products, arithmetic and copies ran while one was open for 1% of the time, Pallas kernels for 4%

profile of v2, /device:TPU:0, one launch (start us, length us, event | category | flops | bytes accessed | tf_op | source)
XLA Modules:
  0.0 202.7 jit_solution(7105899234657838687)
XLA Ops:
  7.2 0.0 all-gather.2.cloned.1.call-start
  7.2 0.7 all-gather.2.cloned.1.call-update
  7.9 0.0 reduce-scatter.2.cloned.1.call-start
  7.9 0.7 add_bitcast_fusion.1.refs_0_
  8.6 3.0 %collective-permute-start = (s32[2,128]{1,0:T(2,128)S(1)}, s32[2,128]{1,0:T(2,128)S(1)}, u32[]{:S(2)}, u32[]{:S(2)}) collective-permute-start(s32[2,128]{1,0:T(2,128)S(1)} %add_bitcast_fusion.1.refs_0_), channel_id=1, source_target_pairs={{0,2},{2,4},{4,6},{6,0},{1,3},{3,5},{5,7},{7,1},{8,10},{10,12},{12... | collective-permute-start | bytes 3080 | tf_op jit(solution)/shard_map/ppermute | solution.py:125
  11.7 2.6 %collective-permute-start.1 = (s32[2,128]{1,0:T(2,128)S(1)}, s32[2,128]{1,0:T(2,128)S(1)}, u32[]{:S(2)}, u32[]{:S(2)}) collective-permute-start(s32[2,128]{1,0:T(2,128)S(1)} %add_bitcast_fusion.1.refs_0_), channel_id=1, source_target_pairs={{0,4},{2,6},{4,0},{6,2},{1,5},{3,7},{5,1},{7,3},{8,12},{10,14},{12... | collective-permute-start | bytes 3080 | tf_op jit(solution)/shard_map/ppermute | solution.py:125
  14.3 1.3 collective-permute-start.2
  15.6 0.1 pad_add_fusion.place
  15.7 0.0 collective-permute-done.refs_1_
  15.7 0.5 collective-permute-done.1.refs_2_
  16.1 1.7 collective-permute-done.2.refs_3_
  17.8 41.7 %all-gather.2.cloned.1.call-done = bf16[8,128,2048]{2,1,0:T(8,128)(2,1)} async-done(((bf16[1,128,2048]{2,1,0:T(8,128)(2,1)}), bf16[8,128,2048]{2,1,0:T(8,128)(2,1)}) %all-gather.2.cloned.1.call-update) | async-done | bytes 4194320 | tf_op jit(solution)/shard_map/all_gather | solution.py:359
  59.5 2.2 %copy-done.1 = bf16[1,1,512,4096]{3,2,1,0:T(8,128)(2,1)S(1)} copy-done((bf16[1,1,512,4096]{3,2,1,0:T(8,128)(2,1)S(1)}, bf16[1,1,512,4096]{3,2,1,0:T(8,128)(2,1)}, u32[]{:S(2)}) %copy-start.1) | copy-done | bytes 4194328
  61.7 2.2 %copy-done.2 = bf16[8,128,2048]{2,1,0:T(8,128)(2,1)S(1)} copy-done((bf16[8,128,2048]{2,1,0:T(8,128)(2,1)S(1)}, bf16[8,128,2048]{2,1,0:T(8,128)(2,1)}, u32[]{:S(2)}) %copy-start.2) | copy-done | bytes 4194328
  63.9 1.0 copy-done.4
  64.9 9.9 %experts.1 = bf16[4,2,128,2048]{3,2,1,0:T(8,128)(2,1)S(1)} custom-call(s32[2]{0:T(128)S(1)} %pad_add_fusion.place, s32[2,128]{1,0:T(2,128)S(1)} %add_bitcast_fusion.1.refs_0_, s32[2,128]{1,0:T(2,128)S(1)} %collective-permute-done.refs_1_, s32[2,128]{1,0:T(2,128)S(1)} %collective-permute-done.1.refs_2_, s32[2,128]{1,0:T(2,128)S(1)} %collective-permute-done.2.refs_3_, ...), custom_call_target="tpu_custom_call" | custom-call | flops 4294967296 | bytes 25165824 | tf_op jit(solution)/shard_map/experts/pallas_call | solution.py:197
  74.8 1.9 copy-done
  76.8 0.0 reduce-scatter.2.cloned.1.call-update
  76.8 1.0 copy-done.7
  77.8 0.0 collective-permute-start.3
  77.8 1.7 collective-permute-start.4
  79.5 2.3 %collective-permute-start.5 = (bf16[128,2048]{1,0:T(8,128)(2,1)S(1)}, bf16[128,2048]{1,0:T(8,128)(2,1)S(1)}, u32[]{:S(2)}, u32[]{:S(2)}) collective-permute-start(bf16[128,2048]{1,0:T(8,128)(2,1)S(1)} %bitcast.29), channel_id=1, source_target_pairs={{0,6},{2,0},{4,2},{6,4},{1,7},{3,1},{5,3},{7,5},{8,14},{10,8},{12,... | collective-permute-start | bytes 1572872 | tf_op jit(solution)/shard_map/ppermute | solution.py:125
  81.8 21.5 %collective-permute-done.3.refs_1_ = bf16[128,2048]{1,0:T(8,128)(2,1)S(1)} collective-permute-done((bf16[128,2048]{1,0:T(8,128)(2,1)S(1)}, bf16[128,2048]{1,0:T(8,128)(2,1)S(1)}, u32[]{:S(2)}, u32[]{:S(2)}) %collective-permute-start.3) | collective-permute-done | bytes 524320 | tf_op jit(solution)/shard_map/ppermute | solution.py:125
  103.3 30.5 %collective-permute-done.4.refs_2_ = bf16[128,2048]{1,0:T(8,128)(2,1)S(1)} collective-permute-done((bf16[128,2048]{1,0:T(8,128)(2,1)S(1)}, bf16[128,2048]{1,0:T(8,128)(2,1)S(1)}, u32[]{:S(2)}, u32[]{:S(2)}) %collective-permute-start.4) | collective-permute-done | bytes 524320 | tf_op jit(solution)/shard_map/ppermute | solution.py:125
  133.8 0.0 collective-permute-done.5.refs_3_
  133.8 0.0 copy-start.6
  133.8 2.2 %copy-done.6 = bf16[1,1024,2048]{2,1,0:T(8,128)(2,1)S(1)} copy-done((bf16[1,1024,2048]{2,1,0:T(8,128)(2,1)S(1)}, bf16[1,1024,2048]{2,1,0:T(8,128)(2,1)}, u32[]{:S(2)}) %copy-start.6) | copy-done | bytes 4194328
  136.0 7.4 %projection.1 = (f32[512,512]{1,0:T(8,128)S(1)}, bf16[512,512]{1,0:T(8,128)(2,1)S(1)}, f32[4,2048]{1,0:T(4,128)S(1)}) custom-call(s32[2]{0:T(128)S(1)} %pad_add_fusion.place, bf16[128,2048]{1,0:T(8,128)(2,1)S(1)} %bitcast.30, bf16[128,2048]{1,0:T(8,128)(2,1)S(1)} %collective-permute-done.3.refs_1_, bf16[128,2048]{1,0:T(8,128)(2,1)S(1)} %collective-permute-done.4.refs_2_, ...), custom_call_target="tpu_custom_call" | custom-call | flops 2147483648 | bytes 7864320 | tf_op jit(solution)/shard_map/projection/pallas_call | solution.py:276
  143.4 0.1 collective-permute-start.6
  143.6 1.8 collective-permute-done.6
  145.4 0.2 add_convert_fusion
  145.6 0.7 collective-permute-start.7
  146.2 25.1 %collective-permute-start.8 = (bf16[128,512]{1,0:T(8,128)(2,1)S(1)}, bf16[128,512]{1,0:T(8,128)(2,1)S(1)}, u32[]{:S(2)}, u32[]{:S(2)}) collective-permute-start(bf16[128,512]{1,0:T(8,128)(2,1)S(1)} %get-tuple-element.10), channel_id=1, source_target_pairs={{0,2},{1,4},{2,6},{3,0},{4,3},{5,5},{6,7},{7,1},{8,10},{9,12},{10,... | collective-permute-start | bytes 393224 | tf_op jit(solution)/shard_map/ppermute | solution.py:337
  171.4 2.1 %collective-permute-start.9 = (bf16[128,512]{1,0:T(8,128)(2,1)S(1)}, bf16[128,512]{1,0:T(8,128)(2,1)S(1)}, u32[]{:S(2)}, u32[]{:S(2)}) collective-permute-start(bf16[128,512]{1,0:T(8,128)(2,1)S(1)} %get-tuple-element.9), channel_id=1, source_target_pairs={{0,4},{1,6},{2,0},{3,2},{4,5},{5,7},{6,1},{7,3},{8,12},{9,14},{10,... | collective-permute-start | bytes 393224 | tf_op jit(solution)/shard_map/ppermute | solution.py:337
  173.5 3.4 %collective-permute-start.10 = (bf16[128,512]{1,0:T(8,128)(2,1)S(1)}, bf16[128,512]{1,0:T(8,128)(2,1)S(1)}, u32[]{:S(2)}, u32[]{:S(2)}) collective-permute-start(bf16[128,512]{1,0:T(8,128)(2,1)S(1)} %get-tuple-element.8), channel_id=1, source_target_pairs={{0,6},{1,0},{2,2},{3,4},{4,7},{5,1},{6,3},{7,5},{8,14},{9,8},{10,1... | collective-permute-start | bytes 393224 | tf_op jit(solution)/shard_map/ppermute | solution.py:337
  176.9 0.0 collective-permute-done.7.refs_0_
  176.9 2.1 %collective-permute-done.9.refs_2_ = bf16[128,512]{1,0:T(8,128)(2,1)S(1)} collective-permute-done((bf16[128,512]{1,0:T(8,128)(2,1)S(1)}, bf16[128,512]{1,0:T(8,128)(2,1)S(1)}, u32[]{:S(2)}, u32[]{:S(2)}) %collective-permute-start.9) | collective-permute-done | bytes 131104 | tf_op jit(solution)/shard_map/ppermute | solution.py:337
  179.1 0.3 collective-permute-done.10.refs_3_
  179.4 1.0 copy-done.5
  180.5 0.7 residual.1
  181.2 1.3 collective-permute-start.11
  182.5 0.1 collective-permute-start.12
  182.6 3.9 %collective-permute-done.12 = f32[4,2048]{1,0:T(4,128)S(1)} collective-permute-done((f32[4,2048]{1,0:T(4,128)S(1)}, f32[4,2048]{1,0:T(4,128)S(1)}, u32[]{:S(2)}, u32[]{:S(2)}) %collective-permute-start.12) | collective-permute-done | bytes 32800 | tf_op jit(solution)/shard_map/ppermute | solution.py:135
  186.5 4.4 %collective-permute-start.13 = (f32[4,2048]{1,0:T(4,128)S(1)}, f32[4,2048]{1,0:T(4,128)S(1)}, u32[]{:S(2)}, u32[]{:S(2)}) collective-permute-start(f32[4,2048]{1,0:T(4,128)S(1)} %add.95), channel_id=1, source_target_pairs={{0,4},{2,6},{4,0},{6,2},{1,5},{3,7},{5,1},{7,3},{8,12},{10,14},{12... | collective-permute-start | bytes 98312 | tf_op jit(solution)/shard_map/ppermute | solution.py:135
  190.9 2.8 %collective-permute-done.13 = f32[4,2048]{1,0:T(4,128)S(1)} collective-permute-done((f32[4,2048]{1,0:T(4,128)S(1)}, f32[4,2048]{1,0:T(4,128)S(1)}, u32[]{:S(2)}, u32[]{:S(2)}) %collective-permute-start.13) | collective-permute-done | bytes 32800 | tf_op jit(solution)/shard_map/ppermute | solution.py:135
  193.6 0.6 add_bitcast_fusion
  194.3 0.8 collective-permute-done.11
  195.0 0.8 copy.13
  (15 shorter events, 0.0 us)
Async XLA Ops:
  7.2 52.3 %all-gather.2.cloned.1.call-start = ((), (), s32[]{:S(2)}) async-start(), calls=%async_computation.1 | async-start | bytes 4718592 | tf_op jit(solution)/shard_map/all_gather | solution.py:359
  7.9 171.5 %reduce-scatter.2.cloned.1.call-start = ((), (), s32[]{:S(2)}) async-start(), calls=%async_computation.2 | async-start | bytes 4718592 | tf_op jit(solution)/shard_map/reduce_scatter | solution.py:365
  8.6 7.0 %collective-permute-start = (s32[2,128]{1,0:T(2,128)S(1)}, s32[2,128]{1,0:T(2,128)S(1)}, u32[]{:S(2)}, u32[]{:S(2)}) collective-permute-start(s32[2,128]{1,0:T(2,128)S(1)} %add_bitcast_fusion.1.refs_0_), channel_id=1, source_target_pairs={{0,2},{2,4},{4,6},{6,0},{1,3},{3,5},{5,7},{7,1},{8,10},{10,12},{12... | collective-permute-start | bytes 3080 | tf_op jit(solution)/shard_map/ppermute | solution.py:125
  11.7 4.5 %collective-permute-start.1 = (s32[2,128]{1,0:T(2,128)S(1)}, s32[2,128]{1,0:T(2,128)S(1)}, u32[]{:S(2)}, u32[]{:S(2)}) collective-permute-start(s32[2,128]{1,0:T(2,128)S(1)} %add_bitcast_fusion.1.refs_0_), channel_id=1, source_target_pairs={{0,4},{2,6},{4,0},{6,2},{1,5},{3,7},{5,1},{7,3},{8,12},{10,14},{12... | collective-permute-start | bytes 3080 | tf_op jit(solution)/shard_map/ppermute | solution.py:125
  14.3 3.6 %collective-permute-start.2 = (s32[2,128]{1,0:T(2,128)S(1)}, s32[2,128]{1,0:T(2,128)S(1)}, u32[]{:S(2)}, u32[]{:S(2)}) collective-permute-start(s32[2,128]{1,0:T(2,128)S(1)} %add_bitcast_fusion.1.refs_0_), channel_id=1, source_target_pairs={{0,6},{2,0},{4,2},{6,4},{1,7},{3,1},{5,3},{7,5},{8,14},{10,8},{12,... | collective-permute-start | bytes 3080 | tf_op jit(solution)/shard_map/ppermute | solution.py:125
  59.5 2.2 %copy-start.1 = (bf16[1,1,512,4096]{3,2,1,0:T(8,128)(2,1)S(1)}, bf16[1,1,512,4096]{3,2,1,0:T(8,128)(2,1)}, u32[]{:S(2)}) copy-start(bf16[1,1,512,4096]{3,2,1,0:T(8,128)(2,1)} %param.14) | copy-start | bytes 12582916
  61.7 2.2 %copy-start.2 = (bf16[8,128,2048]{2,1,0:T(8,128)(2,1)S(1)}, bf16[8,128,2048]{2,1,0:T(8,128)(2,1)}, u32[]{:S(2)}) copy-start(bf16[8,128,2048]{2,1,0:T(8,128)(2,1)} %all-gather.2.cloned.1.call-done) | copy-start | bytes 12582916
  63.9 1.0 copy-start.4
  74.8 2.0 copy-start
  76.8 1.0 copy-start.7
  76.8 57.0 %copy-start.8 = (bf16[1,128,2048]{2,1,0:T(8,128)(2,1)S(1)}, bf16[1,128,2048]{2,1,0:T(8,128)(2,1)}, u32[]{:S(2)}) copy-start(bf16[1,128,2048]{2,1,0:T(8,128)(2,1)} %param.17) | copy-start | bytes 1572868
  76.8 57.0 %copy-start.9 = (f32[1,4,2048]{2,1,0:T(4,128)S(1)}, f32[1,4,2048]{2,1,0:T(4,128)}, u32[]{:S(2)}) copy-start(f32[1,4,2048]{2,1,0:T(4,128)} %param.18) | copy-start | bytes 98308
  77.8 25.5 %collective-permute-start.3 = (bf16[128,2048]{1,0:T(8,128)(2,1)S(1)}, bf16[128,2048]{1,0:T(8,128)(2,1)S(1)}, u32[]{:S(2)}, u32[]{:S(2)}) collective-permute-start(bf16[128,2048]{1,0:T(8,128)(2,1)S(1)} %bitcast.27), channel_id=1, source_target_pairs={{0,2},{2,4},{4,6},{6,0},{1,3},{3,5},{5,7},{7,1},{8,10},{10,12},{12... | collective-permute-start | bytes 1572872 | tf_op jit(solution)/shard_map/ppermute | solution.py:125
  77.8 55.9 %collective-permute-start.4 = (bf16[128,2048]{1,0:T(8,128)(2,1)S(1)}, bf16[128,2048]{1,0:T(8,128)(2,1)S(1)}, u32[]{:S(2)}, u32[]{:S(2)}) collective-permute-start(bf16[128,2048]{1,0:T(8,128)(2,1)S(1)} %bitcast.28), channel_id=1, source_target_pairs={{0,4},{2,6},{4,0},{6,2},{1,5},{3,7},{5,1},{7,3},{8,12},{10,14},{12... | collective-permute-start | bytes 1572872 | tf_op jit(solution)/shard_map/ppermute | solution.py:125
  79.5 54.2 %collective-permute-start.5 = (bf16[128,2048]{1,0:T(8,128)(2,1)S(1)}, bf16[128,2048]{1,0:T(8,128)(2,1)S(1)}, u32[]{:S(2)}, u32[]{:S(2)}) collective-permute-start(bf16[128,2048]{1,0:T(8,128)(2,1)S(1)} %bitcast.29), channel_id=1, source_target_pairs={{0,6},{2,0},{4,2},{6,4},{1,7},{3,1},{5,3},{7,5},{8,14},{10,8},{12,... | collective-permute-start | bytes 1572872 | tf_op jit(solution)/shard_map/ppermute | solution.py:125
  133.8 2.2 %copy-start.6 = (bf16[1,1024,2048]{2,1,0:T(8,128)(2,1)S(1)}, bf16[1,1024,2048]{2,1,0:T(8,128)(2,1)}, u32[]{:S(2)}) copy-start(bf16[1,1024,2048]{2,1,0:T(8,128)(2,1)} %param.19) | copy-start | bytes 12582916
  136.0 43.4 %copy-start.3 = (bf16[1,128,2048]{2,1,0:T(8,128)(2,1)S(1)}, bf16[1,128,2048]{2,1,0:T(8,128)(2,1)}, u32[]{:S(2)}) copy-start(bf16[1,128,2048]{2,1,0:T(8,128)(2,1)} %param.10) | copy-start | bytes 1572868
  143.4 2.0 collective-permute-start.6
  145.6 31.3 %collective-permute-start.7 = (bf16[128,512]{1,0:T(8,128)(2,1)S(1)}, bf16[128,512]{1,0:T(8,128)(2,1)S(1)}, u32[]{:S(2)}, u32[]{:S(2)}) collective-permute-start(bf16[128,512]{1,0:T(8,128)(2,1)S(1)} %get-tuple-element.11), channel_id=1, source_target_pairs={{0,0},{1,2},{2,4},{3,6},{4,1},{5,3},{6,5},{7,7},{8,8},{9,10},{10,1... | collective-permute-start | bytes 393224 | tf_op jit(solution)/shard_map/ppermute | solution.py:337
  146.2 30.7 %collective-permute-start.8 = (bf16[128,512]{1,0:T(8,128)(2,1)S(1)}, bf16[128,512]{1,0:T(8,128)(2,1)S(1)}, u32[]{:S(2)}, u32[]{:S(2)}) collective-permute-start(bf16[128,512]{1,0:T(8,128)(2,1)S(1)} %get-tuple-element.10), channel_id=1, source_target_pairs={{0,2},{1,4},{2,6},{3,0},{4,3},{5,5},{6,7},{7,1},{8,10},{9,12},{10,... | collective-permute-start | bytes 393224 | tf_op jit(solution)/shard_map/ppermute | solution.py:337
  171.4 7.7 %collective-permute-start.9 = (bf16[128,512]{1,0:T(8,128)(2,1)S(1)}, bf16[128,512]{1,0:T(8,128)(2,1)S(1)}, u32[]{:S(2)}, u32[]{:S(2)}) collective-permute-start(bf16[128,512]{1,0:T(8,128)(2,1)S(1)} %get-tuple-element.9), channel_id=1, source_target_pairs={{0,4},{1,6},{2,0},{3,2},{4,5},{5,7},{6,1},{7,3},{8,12},{9,14},{10,... | collective-permute-start | bytes 393224 | tf_op jit(solution)/shard_map/ppermute | solution.py:337
  173.5 6.0 %collective-permute-start.10 = (bf16[128,512]{1,0:T(8,128)(2,1)S(1)}, bf16[128,512]{1,0:T(8,128)(2,1)S(1)}, u32[]{:S(2)}, u32[]{:S(2)}) collective-permute-start(bf16[128,512]{1,0:T(8,128)(2,1)S(1)} %get-tuple-element.8), channel_id=1, source_target_pairs={{0,6},{1,0},{2,2},{3,4},{4,7},{5,1},{6,3},{7,5},{8,14},{9,8},{10,1... | collective-permute-start | bytes 393224 | tf_op jit(solution)/shard_map/ppermute | solution.py:337
  179.4 1.0 copy-start.5
  181.2 13.8 %collective-permute-start.11 = (bf16[128,2048]{1,0:T(8,128)(2,1)S(1)}, bf16[128,2048]{1,0:T(8,128)(2,1)S(1)}, u32[]{:S(2)}, u32[]{:S(2)}) collective-permute-start(bf16[128,2048]{1,0:T(8,128)(2,1)S(1)} %residual.1), channel_id=1, source_target_pairs={{8,0},{16,8},{24,16},{9,1},{17,9},{25,17},{10,2},{18,10},{26,18},{... | collective-permute-start | bytes 1572872 | tf_op jit(solution)/shard_map/ppermute | solution.py:14
  182.5 4.0 %collective-permute-start.12 = (f32[4,2048]{1,0:T(4,128)S(1)}, f32[4,2048]{1,0:T(4,128)S(1)}, u32[]{:S(2)}, u32[]{:S(2)}) collective-permute-start(f32[4,2048]{1,0:T(4,128)S(1)} %get-tuple-element.7), channel_id=1, source_target_pairs={{0,2},{2,0},{4,6},{6,4},{1,3},{3,1},{5,7},{7,5},{8,10},{10,8},{12,... | collective-permute-start | bytes 98312 | tf_op jit(solution)/shard_map/ppermute | solution.py:135
  186.5 7.1 %collective-permute-start.13 = (f32[4,2048]{1,0:T(4,128)S(1)}, f32[4,2048]{1,0:T(4,128)S(1)}, u32[]{:S(2)}, u32[]{:S(2)}) collective-permute-start(f32[4,2048]{1,0:T(4,128)S(1)} %add.95), channel_id=1, source_target_pairs={{0,4},{2,6},{4,0},{6,2},{1,5},{3,7},{5,1},{7,3},{8,12},{10,14},{12... | collective-permute-start | bytes 98312 | tf_op jit(solution)/shard_map/ppermute | solution.py:135
Sparse Core Ops, SparseCore 0:
  9.6 49.8 all-gather.1
  76.9 85.0 reduce-scatter.1

commit v3 on v0

--- a/solution.py
+++ b/solution.py
@@ -1,6 +1,10 @@
+import functools
+
 import jax
 import jax.numpy as jnp
 from jax import lax
+from jax.experimental import pallas as pl
+from jax.experimental.pallas import tpu as pltpu
 from jax.sharding import PartitionSpec as P
 
 
@@ -26,7 +30,7 @@
     return buffer.reshape(experts, capacity, width)
 
 
-def shards(
+def slot_plan(
     out_grad,
     expert_ids,
     gate_codes,
@@ -106,6 +110,388 @@
     return (sent_residual[None], tap_grads[None])
 
 
+F32, BF16 = jnp.float32, jnp.bfloat16
+VMEM_LIMIT = 40 * 1024 * 1024
+HEAD = 16
+NT = (((1,), (1,)), ((), ()))
+TN = (((0,), (0,)), ((), ()))
+
+
+def whole(memory=pltpu.VMEM):
+    return pl.BlockSpec(memory_space=memory)
+
+
+def rotated(array, axis, by):
+    size = lax.axis_size(axis)
+    return lax.ppermute(array, axis, [(i, (i + by) % size) for i in range(size)])
+
+
+def around(array):
+    return [array] + [rotated(array, "expert", k) for k in range(1, lax.axis_size("expert"))]
+
+
+def doubling_sum(array, axis):
+    size, step = lax.axis_size(axis), 1
+    while step < size:
+        array = array + lax.ppermute(array, axis, [(i, i ^ step) for i in range(size)])
+        step *= 2
+    return array
+
+
+def expert_kernel(count, place, *refs):
+    pairs, mine, other = refs[:count], refs[count : 2 * count], refs[2 * count : 3 * count]
+    down, up, pre, send, keep, gates, slope, hidden, scaled = refs[3 * count :]
+    tok_rows = mine[0].shape[0]
+    me, step = place[1], pl.program_id(0)
+
+    @pl.when(step == 0)
+    def _():
+        row = lax.broadcasted_iota(jnp.int32, (tok_rows, tok_rows), 0)
+        column = lax.broadcasted_iota(jnp.int32, (tok_rows, tok_rows), 1)
+
+        def upright(line):
+            return jnp.sum(jnp.where(row == column, line, 0.0), axis=1, keepdims=True)
+
+        for k in range(count):
+            at = pl.ds(k * tok_rows, tok_rows)
+            pair = pairs[k][...]
+            named = (pair // 256) == me
+            code = jnp.sum(jnp.where(named, (pair % 256).astype(F32), 0.0), axis=0, keepdims=True)
+            named = jnp.sum(jnp.where(named, 1.0, 0.0), axis=0, keepdims=True)
+            gates[at, :] = upright(code) / 256.0
+            rank = jnp.sum(jnp.where(row < column, upright(named), 0.0), axis=0, keepdims=True)
+            pick = jnp.where(rank.astype(jnp.int32) == row, named, 0.0).astype(BF16)
+            slots = pl.ds(pl.multiple_of(place[2 + k] * tok_rows, tok_rows), tok_rows)
+            p = lax.dot_general(pick, pre[slots, :], TN, preferred_element_type=F32)
+            q = 1.0 / (1.0 + jnp.exp(-p))
+            slope[at, :] = q * (1.0 + p * (1.0 - q))
+        hidden[...] = jnp.zeros_like(hidden)
+
+    def add(blocks):
+        for k in range(count):
+            at = pl.ds(k * tok_rows, tok_rows)
+            scaled[at, :] = (gates[at, :] * blocks[k][...].astype(F32)).astype(BF16)
+        hidden[...] += lax.dot_general(scaled[...], down[...], NT, preferred_element_type=F32)
+
+    @pl.when(step < 2)
+    def _():
+        add(mine)
+
+    @pl.when((step >= 2) & (step < 4))
+    def _():
+        add(other)
+
+    def result():
+        pre_grad = (hidden[...] * slope[...]).astype(BF16)
+        return lax.dot_general(pre_grad, up[...], NT, preferred_element_type=F32)
+
+    @pl.when((step >= 4) & (step < 6))
+    def _():
+        send[...] = result().astype(BF16)
+
+    @pl.when(step >= 6)
+    def _():
+        keep[...] = result()
+
+
+def expert_sums(place, pairs, mine, other, down, up, pre):
+    count = len(mine)
+    tok_rows, half_width = mine[0].shape
+    units, width = down.shape
+    tokens = count * tok_rows
+    chunk = half_width // 2
+
+    def clip(i, low):
+        return jnp.clip(i - low, 0, 1)
+
+    def down_at(i, place):
+        return (0, jnp.where(i < 2, 2 * place[0] + clip(i, 0), 2 * (1 - place[0]) + clip(i, 2)))
+
+    def up_at(i, place):
+        return (jnp.where(i < 6, 2 * (1 - place[0]) + clip(i, 4), 2 * place[0] + clip(i, 6)), 0)
+
+    return pl.pallas_call(
+        functools.partial(expert_kernel, count),
+        grid_spec=pltpu.PrefetchScalarGridSpec(
+            num_scalar_prefetch=1,
+            grid=(8,),
+            in_specs=[whole()] * count
+            + [pl.BlockSpec((tok_rows, chunk), lambda i, place: (0, clip(i, 0)))] * count
+            + [pl.BlockSpec((tok_rows, chunk), lambda i, place: (0, clip(i, 2)))] * count
+            + [pl.BlockSpec((units, chunk), down_at), pl.BlockSpec((chunk, units), up_at), whole()],
+            out_specs=[
+                pl.BlockSpec((tokens, chunk), lambda i, place: (0, clip(i, 4))),
+                pl.BlockSpec((tokens, chunk), lambda i, place: (0, clip(i, 6))),
+            ],
+            scratch_shapes=[
+                pltpu.VMEM((tokens, 1), F32),
+                pltpu.VMEM((tokens, units), F32),
+                pltpu.VMEM((tokens, units), F32),
+                pltpu.VMEM((tokens, chunk), BF16),
+            ],
+        ),
+        out_shape=[
+            jax.ShapeDtypeStruct((tokens, half_width), BF16),
+            jax.ShapeDtypeStruct((tokens, half_width), F32),
+        ],
+        compiler_params=pltpu.CompilerParams(vmem_limit_bytes=VMEM_LIMIT),
+        cost_estimate=pl.CostEstimate(
+            flops=4 * tokens * width * units, bytes_accessed=4 * width * units + 10 * tokens * width, transcendentals=0
+        ),
+        name="experts",
+    )(place, *pairs, *mine, *other, down, up, pre)
+
+
+def proj_kernel(count, with_taps, place, *refs):
+    grads, heads = refs[:count], refs[count : 2 * count]
+    taps, weight = refs[2 * count : 2 * count + 2]
+    refs = refs[2 * count + 2 :]
+    if with_taps:
+        inputs, send, keep, tap_out, ext, scaled = refs
+    else:
+        send, keep, ext, scaled = refs
+    tok_rows, chunk = grads[0].shape
+    kernel_size = taps.shape[0]
+    step = pl.program_id(0)
+
+    tap = taps[...]
+    for k in range(count):
+        ext[:tok_rows, :] = grads[k][...].astype(F32)
+        follows = (place[2 + k] < lax.axis_size("expert") - 1).astype(F32)
+        ext[tok_rows:, :] = heads[k][...].astype(F32) * follows
+        result = jnp.zeros((tok_rows, chunk), F32)
+        for j in range(kernel_size):
+            start = kernel_size - 1 - j
+            result = result + tap[j : j + 1, :] * ext[start : start + tok_rows, :]
+        scaled[k * tok_rows : (k + 1) * tok_rows, :] = result.astype(BF16)
+        if with_taps and k == 0:
+            values = inputs[...].astype(F32)
+            for j in range(kernel_size):
+                start = kernel_size - 1 - j
+                terms = values * ext[start : start + tok_rows, :]
+                tap_out[j : j + 1, :] = jnp.sum(terms, axis=0, keepdims=True)
+
+    product = lax.dot_general(scaled[...], weight[...], NT, preferred_element_type=F32)
+
+    @pl.when(step == 0)
+    def _():
+        keep[...] = product
+
+    @pl.when(step > 0)
+    def _():
+        keep[...] += product
+
+    @pl.when(step == pl.num_programs(0) - 1)
+    def _():
+        send[...] = keep[...].astype(BF16)
+
+
+def proj_sums(place, grads, heads, taps, weight, inputs=None):
+    count = len(grads)
+    tok_rows, half_width = grads[0].shape
+    block = weight.shape[0]
+    tokens = count * tok_rows
+    chunk = half_width // 4
+    with_taps = inputs is not None
+
+    def wide(rows):
+        return pl.BlockSpec((rows, chunk), lambda i: (0, i))
+
+    last = [wide(tok_rows)] if with_taps else []
+    out_specs = [pl.BlockSpec((tokens, block), lambda i: (0, 0))] * 2
+    out_shape = [jax.ShapeDtypeStruct((tokens, block), BF16), jax.ShapeDtypeStruct((tokens, block), F32)]
+    if with_taps:
+        out_specs = out_specs + [wide(taps.shape[0])]
+        out_shape = out_shape + [jax.ShapeDtypeStruct(taps.shape, F32)]
+    return pl.pallas_call(
+        functools.partial(proj_kernel, count, with_taps),
+        grid=(half_width // chunk,),
+        in_specs=[whole(pltpu.SMEM)]
+        + [wide(tok_rows)] * count
+        + [wide(HEAD)] * count
+        + [wide(taps.shape[0]), wide(block)]
+        + last,
+        out_specs=out_specs,
+        out_shape=out_shape,
+        scratch_shapes=[pltpu.VMEM((tok_rows + HEAD, chunk), F32), pltpu.VMEM((tokens, chunk), BF16)],
+        compiler_params=pltpu.CompilerParams(vmem_limit_bytes=VMEM_LIMIT),
+        cost_estimate=pl.CostEstimate(
+            flops=2 * tokens * half_width * block,
+            bytes_accessed=2 * (block + tokens) * half_width + 6 * tokens * block,
+            transcendentals=0,
+        ),
+        name="projection",
+    )(place, *grads, *heads, taps, weight, *([inputs] if with_taps else []))
+
+
+def final_kernel(place, grad, keep, received, right, left, own_proj, own_received, *refs):
+    pieces, out, total = refs[:-2], refs[-2], refs[-1]
+    half, me = place[0], place[1]
+    experts = lax.axis_size("expert")
+    part = own_proj.shape[1]
+    total[...] = (
+        grad[...].astype(F32)
+        + (keep[...] + received[...].astype(F32))
+        + right[...].astype(F32)
+        + left[...].astype(F32)
+    )
+
+    def add(source, value):
+        @pl.when((source >= 0) & (source < experts) & (source // 2 == half))
+        def _():
+            at = pl.ds(pl.multiple_of(lax.rem(source, 2) * part, part), part)
+            total[:, at] += value()
+
+    add(me, lambda: own_proj[...] + own_received[...].astype(F32))
+    sources = (me + 1, me - 1, lax.rem(me + 2, experts), experts - 1 - me + jnp.where(me % 3 == 0, 0, experts))
+    for source, piece in zip(sources, pieces):
+        add(source, lambda piece=piece: piece[...].astype(F32))
+    out[...] = total[...].astype(BF16)
+
+
+def final_sum(place, grad, *arrays):
+    return pl.pallas_call(
+        final_kernel,
+        in_specs=[whole(pltpu.SMEM)] + [whole()] * (1 + len(arrays)),
+        out_specs=whole(),
+        out_shape=jax.ShapeDtypeStruct(grad.shape, BF16),
+        scratch_shapes=[pltpu.VMEM(grad.shape, F32)],
+        compiler_params=pltpu.CompilerParams(vmem_limit_bytes=VMEM_LIMIT),
+        cost_estimate=pl.CostEstimate(flops=8 * grad.size, bytes_accessed=24 * grad.size, transcendentals=0),
+        name="residual",
+    )(place, grad, *arrays)
+
+
+RIGHT = [(0, 1), (1, 2), (2, 3)]
+LEFT = [(3, 2), (2, 1), (1, 0)]
+
+
+def moved(array, pairs):
+    return lax.ppermute(array, "expert", pairs)
+
+
+def swapped(array):
+    return rotated(array, "mp", 1)
+
+
+def together(*arrays):
+    return lax.optimization_barrier(arrays)
+
+
+def token_plan(
+    out_grad,
+    expert_ids,
+    gate_codes,
+    up_weight,
+    down_weight,
+    pre_act,
+    conv_grad,
+    conv_input,
+    conv_weight,
+    in_proj,
+):
+    me, half = lax.axis_index("expert"), lax.axis_index("mp")
+    experts = lax.axis_size("expert")
+    far_block = (me + 2) % experts
+    end_block = jnp.where(me == 0, experts - 1, 0)
+    near = jnp.stack([half, me, me, jnp.maximum(me - 1, 0), jnp.minimum(me + 1, experts - 1), far_block])
+    near, last = near.astype(jnp.int32), jnp.stack([half, me, end_block]).astype(jnp.int32)
+    rows_own, conv_own = out_grad[0], conv_grad[0]
+    tok_rows = rows_own.shape[0]
+    w_down, w_up, pre = down_weight[0, 0], up_weight[0, 0], pre_act[0, 0]
+    taps, w_proj = conv_weight[0], in_proj[0]
+
+    def block(array, k):
+        return array[k * tok_rows : (k + 1) * tok_rows]
+
+    rows_left, rows_right = moved(rows_own, RIGHT), moved(rows_own, LEFT)
+    pairs = around((expert_ids[0] * 256 + gate_codes[0]).T)
+    heads = around(conv_own[:HEAD])
+    other_own = swapped(rows_own)
+    rows_left, rows_right, other_own, *tiny = together(rows_left, rows_right, other_own, *pairs, *heads)
+    pairs, heads = tiny[:experts], tiny[experts:]
+
+    from_left, from_right = moved(rows_left, RIGHT[1:]), moved(rows_right, LEFT[1:])
+    other_left, other_right = swapped(rows_left), swapped(rows_right)
+    from_left, from_right, other_left, other_right = together(from_left, from_right, other_left, other_right)
+
+    rows_far = jnp.where(me >= 2, from_left, from_right)
+    rows_end = moved(rows_far, [(2, 3), (1, 0)])
+    other_far = swapped(rows_far)
+    send, keep = expert_sums(
+        near,
+        [pairs[0], pairs[1], pairs[3], pairs[2]],
+        [rows_own, rows_left, rows_right, rows_far],
+        [other_own, other_left, other_right, other_far],
+        w_down,
+        w_up,
+        pre,
+    )
+    rows_end, send, keep, conv_own = together(rows_end, send, keep, conv_own)
+
+    conv_left, conv_right = moved(conv_own, RIGHT), moved(conv_own, LEFT)
+    other_end = swapped(rows_end)
+    got = swapped(send)
+    send_end, keep_end = expert_sums(
+        last, [jnp.where(me == 0, pairs[1], pairs[3])], [rows_end], [other_end], w_down, w_up, pre
+    )
+    conv_left, conv_right, got, send_end, keep_end = together(conv_left, conv_right, got, send_end, keep_end)
+
+    from_left, from_right = moved(conv_left, RIGHT[1:]), moved(conv_right, LEFT[1:])
+    back_end = (keep_end + swapped(send_end).astype(F32)).astype(BF16)
+    back_end = moved(back_end, [(0, 1), (3, 2)])
+    from_left, from_right, back_end = together(from_left, from_right, back_end)
+
+    conv_far = jnp.where(me >= 2, from_left, from_right)
+    conv_end = moved(conv_far, [(2, 3), (1, 0)])
+    back = (block(keep, 3) + block(got, 3).astype(F32) + back_end.astype(F32)).astype(BF16)
+    back_right, back_left = moved(back, RIGHT[:2]), moved(back, LEFT[:2])
+    proj_send, proj_keep, tap_terms = proj_sums(
+        near,
+        [conv_own, conv_left, conv_right, conv_far],
+        [heads[3], heads[0], heads[2], heads[1]],
+        taps,
+        w_proj,
+        conv_input[0],
+    )
+    conv_end, back_right, back_left, proj_send, proj_keep = together(
+        conv_end, back_right, back_left, proj_send, proj_keep
+    )
+
+    to_right = (block(keep, 2) + block(got, 2).astype(F32) + back_right.astype(F32)).astype(BF16)
+    to_left = (block(keep, 1) + block(got, 1).astype(F32) + back_left.astype(F32)).astype(BF16)
+    to_right, to_left = moved(to_right, RIGHT), moved(to_left, LEFT)
+    proj_send_end, proj_keep_end = proj_sums(last, [conv_end], [heads[2]], taps, w_proj)
+
+    gather = [(e * 2 + 1 - e // 2, e * 2 + e // 2) for e in range(experts)]
+    both = ("expert", "mp")
+    proj_got = lax.ppermute(proj_send, both, gather)
+    proj_got_end = lax.ppermute(proj_send_end, both, gather)
+
+    def deliver(kept, got, pairs):
+        value = (kept + got.astype(F32)).astype(BF16)
+        return lax.ppermute(value, both, [(e * 2 + e // 2, d * 2 + e // 2) for e, d in pairs])
+
+    pieces = [
+        deliver(block(proj_keep, 1), block(proj_got, 1), LEFT),
+        deliver(block(proj_keep, 2), block(proj_got, 2), RIGHT),
+        deliver(block(proj_keep, 3), block(proj_got, 3), [(e, (e + 2) % 4) for e in range(experts)]),
+        deliver(proj_keep_end, proj_got_end, [(0, 3), (3, 0)]),
+    ]
+    tap_grads = doubling_sum(tap_terms, "expert")
+    residual = final_sum(
+        near, rows_own, block(keep, 0), block(got, 0), to_right, to_left, block(proj_keep, 0), block(proj_got, 0), *pieces
+    )
+    return (shifted(residual, "section", -1)[None], tap_grads[None])
+
+
+def shards(*arrays):
+    experts, halves = lax.axis_size("expert"), lax.axis_size("mp")
+    capacity = arrays[5].shape[2] // experts
+    dense = capacity == arrays[0].shape[1] and experts == 4 and halves == 2
+    return (token_plan if dense else slot_plan)(*arrays)
+
+
 def solution(mesh):
     in_specs = (
         P("section", "expert", "mp"),

time: 514 us -> 193 us (0.38)
  the two profiles are of different devices: /device:TPU:0 before, /device:TPU:10 now
where the time goes in v3:
time: 193 us; the launch traced here: 192 us
  starting transfers between devices  76.1 us (39%)
  waiting for transfers between devices  64.3 us (33%)
  Pallas kernels  30.2 us (16%)
  local copies, waits for them, and re-layouts  15.6 us (8%)
  other arithmetic  5.08 us (3%)
    ppermute x15, starting transfers between devices, moved(): return lax.ppermute(array, 'expert', pairs)  39.8 us
    ppermute x15, waiting for transfers between devices, moved(): return lax.ppermute(array, 'expert', pairs)  34.6 us
    pallas_call x2, Pallas kernels, expert_sums(): pl.pallas_call(functools.partial(expert_kernel, count), grid_spec=pltpu.P...  18.7 us
    ppermute x13, starting transfers between devices, rotated(): lax.ppermute(array, axis, [(i, (i + by) % size) for i in range(size)])  15.9 us
    ppermute x13, waiting for transfers between devices, rotated(): lax.ppermute(array, axis, [(i, (i + by) % size) for i in range(size)])  15.4 us
    unnamed x37, local copies, waits for them, and re-layouts  13.5 us
    ppermute x4, starting transfers between devices, deliver(): lax.ppermute(value, both, [(e * 2 + e // 2, d * 2 + e // 2) for e, d in p...  11.9 us
    pallas_call x2, Pallas kernels, proj_sums(): pl.pallas_call(functools.partial(proj_kernel, count, with_taps), grid=(ha...  10.4 us
  transfers between devices with their start and end apart: 37, of which 20 were waited for; matrix products, arithmetic and copies ran while one was open for 3% of the time, Pallas kernels for 15%

profile of v3, /device:TPU:10, one launch (start us, length us, event | category | flops | bytes accessed | tf_op | source)
XLA Modules:
  0.0 192.3 jit_solution(2123054906236089211)
XLA Ops:
  0.6 3.5 %collective-permute-start = (bf16[128,2048]{1,0:T(8,128)(2,1)}, bf16[128,2048]{1,0:T(8,128)(2,1)S(1)}, u32[]{:S(2)}, u32[]{:S(2)}) collective-permute-start(bf16[128,2048]{1,0:T(8,128)(2,1)} %bitcast.29), channel_id=1, source_target_pairs={{0,2},{2,4},{4,6},{1,3},{3,5},{5,7},{8,10},{10,12},{12,14},{9,11},... | collective-permute-start | bytes 1572872 | tf_op jit(solution)/shard_map/ppermute | solution.py:370
  4.1 2.4 %collective-permute-start.1 = (bf16[128,2048]{1,0:T(8,128)(2,1)}, bf16[128,2048]{1,0:T(8,128)(2,1)S(1)}, u32[]{:S(2)}, u32[]{:S(2)}) collective-permute-start(bf16[128,2048]{1,0:T(8,128)(2,1)} %bitcast.30), channel_id=1, source_target_pairs={{6,4},{4,2},{2,0},{7,5},{5,3},{3,1},{14,12},{12,10},{10,8},{15,13}... | collective-permute-start | bytes 1572872 | tf_op jit(solution)/shard_map/ppermute | solution.py:370
  7.4 1.5 collective-permute-start.6
  9.7 1.6 collective-permute-start.3
  11.3 6.6 %collective-permute-done.3.refs_1_ = s32[2,128]{1,0:T(2,128)S(1)} collective-permute-done((s32[2,128]{1,0:T(2,128)S(1)}, s32[2,128]{1,0:T(2,128)S(1)}, u32[]{:S(2)}, u32[]{:S(2)}) %collective-permute-start.3) | collective-permute-done | bytes 1056 | tf_op jit(solution)/shard_map/ppermute | solution.py:126
  17.9 3.8 %collective-permute-start.4 = (s32[2,128]{1,0:T(2,128)S(1)}, s32[2,128]{1,0:T(2,128)S(1)}, u32[]{:S(2)}, u32[]{:S(2)}) collective-permute-start(s32[2,128]{1,0:T(2,128)S(1)} %add_bitcast_fusion.1.refs_0_), channel_id=1, source_target_pairs={{0,4},{2,6},{4,0},{6,2},{1,5},{3,7},{5,1},{7,3},{8,12},{10,14},{12... | collective-permute-start | bytes 3080 | tf_op jit(solution)/shard_map/ppermute | solution.py:126
  21.6 1.5 collective-permute-done.4.refs_3_
  23.2 4.9 %collective-permute-start.5 = (s32[2,128]{1,0:T(2,128)S(1)}, s32[2,128]{1,0:T(2,128)S(1)}, u32[]{:S(2)}, u32[]{:S(2)}) collective-permute-start(s32[2,128]{1,0:T(2,128)S(1)} %add_bitcast_fusion.1.refs_0_), channel_id=1, source_target_pairs={{0,6},{2,0},{4,2},{6,4},{1,7},{3,1},{5,3},{7,5},{8,14},{10,8},{12,... | collective-permute-start | bytes 3080 | tf_op jit(solution)/shard_map/ppermute | solution.py:126
  28.0 1.3 collective-permute-done.5.refs_2_
  29.3 2.6 %collective-permute-start.7 = (bf16[16,2048]{1,0:T(8,128)(2,1)S(1)}, bf16[16,2048]{1,0:T(8,128)(2,1)S(1)}, u32[]{:S(2)}, u32[]{:S(2)}) collective-permute-start(bf16[16,2048]{1,0:T(8,128)(2,1)S(1)} %slice_bitcast_fusion.refs_5_), channel_id=1, source_target_pairs={{0,4},{2,6},{4,0},{6,2},{1,5},{3,7},{5,1},{7,3},{8,12},{10,14},{12... | collective-permute-start | bytes 196616 | tf_op jit(solution)/shard_map/ppermute | solution.py:126
  32.2 2.2 %collective-permute-done.7.refs_6_.refs_1_ = bf16[16,2048]{1,0:T(8,128)(2,1)S(1)} collective-permute-done((bf16[16,2048]{1,0:T(8,128)(2,1)S(1)}, bf16[16,2048]{1,0:T(8,128)(2,1)S(1)}, u32[]{:S(2)}, u32[]{:S(2)}) %collective-permute-start.7) | collective-permute-done | bytes 65568 | tf_op jit(solution)/shard_map/ppermute | solution.py:126
  34.5 3.2 %collective-permute-done.8.refs_4_ = bf16[16,2048]{1,0:T(8,128)(2,1)S(1)} collective-permute-done((bf16[16,2048]{1,0:T(8,128)(2,1)S(1)}, bf16[16,2048]{1,0:T(8,128)(2,1)S(1)}, u32[]{:S(2)}, u32[]{:S(2)}) %collective-permute-start.8) | collective-permute-done | bytes 65568 | tf_op jit(solution)/shard_map/ppermute | solution.py:126
  37.7 2.0 %collective-permute-start.10 = (bf16[128,2048]{1,0:T(8,128)(2,1)S(1)}, bf16[128,2048]{1,0:T(8,128)(2,1)S(1)}, u32[]{:S(2)}, u32[]{:S(2)}) collective-permute-start(bf16[128,2048]{1,0:T(8,128)(2,1)S(1)} %collective-permute-done.1.refs_6_), channel_id=1, source_target_pairs={{4,2},{2,0},{5,3},{3,1},{12,10},{10,8},{13,11},{11,9},{20,18},{18,... | collective-permute-start | bytes 1572872 | tf_op jit(solution)/shard_map/ppermute | solution.py:370
  40.2 4.7 %collective-permute-start.9 = (bf16[128,2048]{1,0:T(8,128)(2,1)S(1)}, bf16[128,2048]{1,0:T(8,128)(2,1)}, u32[]{:S(2)}, u32[]{:S(2)}) collective-permute-start(bf16[128,2048]{1,0:T(8,128)(2,1)S(1)} %collective-permute-done.refs_5_), channel_id=1, source_target_pairs={{2,4},{4,6},{3,5},{5,7},{10,12},{12,14},{11,13},{13,15},{18,20},{2... | collective-permute-start | bytes 1572872 | tf_op jit(solution)/shard_map/ppermute | solution.py:370
  44.9 3.8 %collective-permute-done.10 = bf16[128,2048]{1,0:T(8,128)(2,1)S(1)} collective-permute-done((bf16[128,2048]{1,0:T(8,128)(2,1)S(1)}, bf16[128,2048]{1,0:T(8,128)(2,1)S(1)}, u32[]{:S(2)}, u32[]{:S(2)}) %collective-permute-start.10) | collective-permute-done | bytes 524320 | tf_op jit(solution)/shard_map/ppermute | solution.py:370
  49.6 6.0 %collective-permute-done.9 = bf16[128,2048]{1,0:T(8,128)(2,1)} collective-permute-done((bf16[128,2048]{1,0:T(8,128)(2,1)S(1)}, bf16[128,2048]{1,0:T(8,128)(2,1)}, u32[]{:S(2)}, u32[]{:S(2)}) %collective-permute-start.9) | collective-permute-done | bytes 524320 | tf_op jit(solution)/shard_map/ppermute | solution.py:370
  55.7 1.3 collective-permute-start.13
  62.9 12.7 %experts.2 = (bf16[512,2048]{1,0:T(8,128)(2,1)}, f32[512,2048]{1,0:T(8,128)S(1)}) custom-call(s32[6]{0:T(128)S(1)} %stack.32.place, s32[2,128]{1,0:T(2,128)S(1)} %add_bitcast_fusion.1.refs_0_, s32[2,128]{1,0:T(2,128)S(1)} %collective-permute-done.3.refs_1_, s32[2,128]{1,0:T(2,128)S(1)} %collective-permute-done.5.refs_2_, ...), custom_call_target="tpu_custom_call" | custom-call | flops 4294967296 | bytes 29360128 | tf_op jit(solution)/shard_map/experts/pallas_call | solution.py:213
  75.6 2.0 %copy-done = f32[512,2048]{1,0:T(8,128)} copy-done((f32[512,2048]{1,0:T(8,128)}, f32[512,2048]{1,0:T(8,128)S(1)}, u32[]{:S(2)}) %copy-start) | copy-done | bytes 4194328
  78.1 5.8 %collective-permute-start.15 = (bf16[128,2048]{1,0:T(8,128)(2,1)S(1)}, bf16[128,2048]{1,0:T(8,128)(2,1)S(1)}, u32[]{:S(2)}, u32[]{:S(2)}) collective-permute-start(bf16[128,2048]{1,0:T(8,128)(2,1)S(1)} %bitcast.38), channel_id=1, source_target_pairs={{0,2},{2,4},{4,6},{1,3},{3,5},{5,7},{8,10},{10,12},{12,14},{9,11},... | collective-permute-start | bytes 1572872 | tf_op jit(solution)/shard_map/ppermute | solution.py:370
  84.0 1.9 collective-permute-start.16
  86.0 2.3 %copy-done.3 = bf16[1,1,512,4096]{3,2,1,0:T(8,128)(2,1)S(1)} copy-done((bf16[1,1,512,4096]{3,2,1,0:T(8,128)(2,1)S(1)}, bf16[1,1,512,4096]{3,2,1,0:T(8,128)(2,1)}, u32[]{:S(2)}) %copy-start.3) | copy-done | bytes 4194328
  88.4 2.3 %copy-done.4 = bf16[1,1,4096,512]{3,2,1,0:T(8,128)(2,1)S(1)} copy-done((bf16[1,1,4096,512]{3,2,1,0:T(8,128)(2,1)S(1)}, bf16[1,1,4096,512]{3,2,1,0:T(8,128)(2,1)}, u32[]{:S(2)}) %copy-start.4) | copy-done | bytes 4194328
  90.7 6.0 %experts.3 = (bf16[128,2048]{1,0:T(8,128)(2,1)S(1)}, f32[128,2048]{1,0:T(8,128)S(1)}) custom-call(s32[3]{0:T(128)S(1)} %pad_add_fusion.place, s32[2,128]{1,0:T(2,128)S(1)} %broadcast_select_fusion.2.refs_0_, bf16[128,2048]{1,0:T(8,128)(2,1)S(1)} %collective-permute-done.13.refs_1_, bf16[128,2048]{1,0:T(8,128)(2,1)S(1)} %collective-permute-done.18.refs_2_, ...), custom_call_target="tpu_custom_call" | custom-call | flops 1073741824 | bytes 13631488 | tf_op jit(solution)/shard_map/experts/pallas_call | solution.py:213
  96.8 2.8 %collective-permute-done.16.refs_2_ = bf16[128,2048]{1,0:T(8,128)(2,1)S(1)} collective-permute-done((bf16[128,2048]{1,0:T(8,128)(2,1)S(1)}, bf16[128,2048]{1,0:T(8,128)(2,1)S(1)}, u32[]{:S(2)}, u32[]{:S(2)}) %collective-permute-start.16) | collective-permute-done | bytes 524320 | tf_op jit(solution)/shard_map/ppermute | solution.py:370
  99.6 2.4 %collective-permute-start.19 = (bf16[128,2048]{1,0:T(8,128)(2,1)S(1)}, bf16[128,2048]{1,0:T(8,128)(2,1)S(1)}, u32[]{:S(2)}, u32[]{:S(2)}) collective-permute-start(bf16[128,2048]{1,0:T(8,128)(2,1)S(1)} %collective-permute-done.15.refs_1_), channel_id=1, source_target_pairs={{2,4},{4,6},{3,5},{5,7},{10,12},{12,14},{11,13},{13,15},{18,20},{2... | collective-permute-start | bytes 1572872 | tf_op jit(solution)/shard_map/ppermute | solution.py:370
  102.0 1.9 collective-permute-start.20
  105.4 8.3 %collective-permute-done.19 = bf16[128,2048]{1,0:T(8,128)(2,1)S(1)} collective-permute-done((bf16[128,2048]{1,0:T(8,128)(2,1)S(1)}, bf16[128,2048]{1,0:T(8,128)(2,1)S(1)}, u32[]{:S(2)}, u32[]{:S(2)}) %collective-permute-start.19) | collective-permute-done | bytes 524320 | tf_op jit(solution)/shard_map/ppermute | solution.py:370
  113.7 4.1 %collective-permute-done.20 = bf16[128,2048]{1,0:T(8,128)(2,1)S(1)} collective-permute-done((bf16[128,2048]{1,0:T(8,128)(2,1)S(1)}, bf16[128,2048]{1,0:T(8,128)(2,1)S(1)}, u32[]{:S(2)}, u32[]{:S(2)}) %collective-permute-start.20) | collective-permute-done | bytes 524320 | tf_op jit(solution)/shard_map/ppermute | solution.py:370
  117.8 2.1 %collective-permute-done.22 = bf16[128,2048]{1,0:T(8,128)(2,1)S(1)} collective-permute-done((bf16[128,2048]{1,0:T(8,128)(2,1)S(1)}, bf16[128,2048]{1,0:T(8,128)(2,1)S(1)}, u32[]{:S(2)}, u32[]{:S(2)}) %collective-permute-start.22) | collective-permute-done | bytes 524320 | tf_op jit(solution)/shard_map/ppermute | solution.py:370
  121.1 3.7 %collective-permute-start.24 = (bf16[128,2048]{1,0:T(8,128)(2,1)S(1)}, bf16[128,2048]{1,0:T(8,128)(2,1)S(1)}, u32[]{:S(2)}, u32[]{:S(2)}) collective-permute-start(bf16[128,2048]{1,0:T(8,128)(2,1)S(1)} %add_convert_fusion.2), channel_id=1, source_target_pairs={{0,2},{2,4},{1,3},{3,5},{8,10},{10,12},{9,11},{11,13},{16,18},{18,... | collective-permute-start | bytes 1572872 | tf_op jit(solution)/shard_map/ppermute | solution.py:370
  126.2 1.6 collective-permute-start.23
  127.9 7.4 %projection.2 = (bf16[512,1024]{1,0:T(8,128)(2,1)S(1)}, f32[512,1024]{1,0:T(8,128)S(1)}, f32[4,2048]{1,0:T(4,128)S(1)}) custom-call(s32[6]{0:T(128)S(1)} %stack.32.place, bf16[128,2048]{1,0:T(8,128)(2,1)S(1)} %bitcast.40, bf16[128,2048]{1,0:T(8,128)(2,1)S(1)} %collective-permute-done.15.refs_1_, bf16[128,2048]{1,0:T(8,128)(2,1)S(1)} %collective-permute-done.16.refs_2_, ...), custom_call_target="tpu_custom_call" | custom-call | flops 2147483648 | bytes 9437184 | tf_op jit(solution)/shard_map/projection/pallas_call | solution.py:306
  136.1 3.1 %collective-permute-done.25 = bf16[128,2048]{1,0:T(8,128)(2,1)S(1)} collective-permute-done((bf16[128,2048]{1,0:T(8,128)(2,1)S(1)}, bf16[128,2048]{1,0:T(8,128)(2,1)S(1)}, u32[]{:S(2)}, u32[]{:S(2)}) %collective-permute-start.25) | collective-permute-done | bytes 524320 | tf_op jit(solution)/shard_map/ppermute | solution.py:370
  140.5 3.0 %projection.3 = (bf16[128,1024]{1,0:T(8,128)(2,1)S(1)}, f32[128,1024]{1,0:T(8,128)S(1)}) custom-call(s32[3]{0:T(128)S(1)} %pad_add_fusion.place, bf16[128,2048]{1,0:T(8,128)(2,1)S(1)} %collective-permute-done.23.refs_0_, bf16[16,2048]{1,0:T(8,128)(2,1)S(1)} %collective-permute-done.7.refs_6_.refs_1_, f32[4,2048]{1,0:T(4,128)S(1)} %bitcast.37, ...), custom_call_target="tpu_custom_call" | custom-call | flops 536870912 | bytes 5505024 | tf_op jit(solution)/shard_map/projection/pallas_call | solution.py:306
  144.8 1.8 add_convert_fusion
  146.6 3.1 %collective-permute-start.26 = (bf16[128,2048]{1,0:T(8,128)(2,1)S(1)}, bf16[128,2048]{1,0:T(8,128)(2,1)S(1)}, u32[]{:S(2)}, u32[]{:S(2)}) collective-permute-start(bf16[128,2048]{1,0:T(8,128)(2,1)S(1)} %get-tuple-element.85), channel_id=1, source_target_pairs={{0,2},{2,4},{4,6},{1,3},{3,5},{5,7},{8,10},{10,12},{12,14},{9,11},... | collective-permute-start | bytes 1572872 | tf_op jit(solution)/shard_map/ppermute | solution.py:370
  149.6 3.0 %collective-permute-start.27 = (bf16[128,2048]{1,0:T(8,128)(2,1)S(1)}, bf16[128,2048]{1,0:T(8,128)(2,1)S(1)}, u32[]{:S(2)}, u32[]{:S(2)}) collective-permute-start(bf16[128,2048]{1,0:T(8,128)(2,1)S(1)} %get-tuple-element.84), channel_id=1, source_target_pairs={{6,4},{4,2},{2,0},{7,5},{5,3},{3,1},{14,12},{12,10},{10,8},{15,13}... | collective-permute-start | bytes 1572872 | tf_op jit(solution)/shard_map/ppermute | solution.py:370
  153.7 7.6 %collective-permute-start.29 = (bf16[128,1024]{1,0:T(8,128)(2,1)S(1)}, bf16[128,1024]{1,0:T(8,128)(2,1)S(1)}, u32[]{:S(2)}, u32[]{:S(2)}) collective-permute-start(bf16[128,1024]{1,0:T(8,128)(2,1)S(1)} %get-tuple-element.89), channel_id=1, source_target_pairs={{7,5},{5,3},{2,0},{15,13},{13,11},{10,8},{23,21},{21,19},{18,16},{... | collective-permute-start | bytes 786440 | tf_op jit(solution)/shard_map/ppermute | solution.py:473
  161.3 1.9 collective-permute-start.30
  163.2 1.7 collective-permute-start.31
  166.0 3.6 %collective-permute-done.27.left = bf16[128,2048]{1,0:T(8,128)(2,1)S(1)} collective-permute-done((bf16[128,2048]{1,0:T(8,128)(2,1)S(1)}, bf16[128,2048]{1,0:T(8,128)(2,1)S(1)}, u32[]{:S(2)}, u32[]{:S(2)}) %collective-permute-start.27) | collective-permute-done | bytes 524320 | tf_op jit(solution)/shard_map/ppermute | solution.py:370
  170.5 3.2 %collective-permute-done.31.refs_2_ = bf16[128,1024]{1,0:T(8,128)(2,1)S(1)} collective-permute-done((bf16[128,1024]{1,0:T(8,128)(2,1)S(1)}, bf16[128,1024]{1,0:T(8,128)(2,1)S(1)}, u32[]{:S(2)}, u32[]{:S(2)}) %collective-permute-start.31) | collective-permute-done | bytes 262176 | tf_op jit(solution)/shard_map/ppermute | solution.py:473
  174.7 2.4 %collective-permute-start.34 = (bf16[128,2048]{1,0:T(8,128)(2,1)S(1)}, bf16[128,2048]{1,0:T(8,128)(2,1)S(1)}, u32[]{:S(2)}, u32[]{:S(2)}) collective-permute-start(bf16[128,2048]{1,0:T(8,128)(2,1)S(1)} %residual.1), channel_id=1, source_target_pairs={{8,0},{16,8},{24,16},{9,1},{17,9},{25,17},{10,2},{18,10},{26,18},{... | collective-permute-start | bytes 1572872 | tf_op jit(solution)/shard_map/ppermute | solution.py:14
  177.2 3.9 %collective-permute-done.35 = f32[4,2048]{1,0:T(4,128)S(1)} collective-permute-done((f32[4,2048]{1,0:T(4,128)S(1)}, f32[4,2048]{1,0:T(4,128)S(1)}, u32[]{:S(2)}, u32[]{:S(2)}) %collective-permute-start.35) | collective-permute-done | bytes 32800 | tf_op jit(solution)/shard_map/ppermute | solution.py:136
  181.2 3.4 %collective-permute-start.36 = (f32[4,2048]{1,0:T(4,128)S(1)}, f32[4,2048]{1,0:T(4,128)S(1)}, u32[]{:S(2)}, u32[]{:S(2)}) collective-permute-start(f32[4,2048]{1,0:T(4,128)S(1)} %add.72), channel_id=1, source_target_pairs={{0,4},{2,6},{4,0},{6,2},{1,5},{3,7},{5,1},{7,3},{8,12},{10,14},{12... | collective-permute-start | bytes 98312 | tf_op jit(solution)/shard_map/ppermute | solution.py:136
  184.6 2.2 %collective-permute-done.36 = f32[4,2048]{1,0:T(4,128)S(1)} collective-permute-done((f32[4,2048]{1,0:T(4,128)S(1)}, f32[4,2048]{1,0:T(4,128)S(1)}, u32[]{:S(2)}, u32[]{:S(2)}) %collective-permute-start.36) | collective-permute-done | bytes 32800 | tf_op jit(solution)/shard_map/ppermute | solution.py:136
  187.4 4.1 %collective-permute-done.34 = bf16[128,2048]{1,0:T(8,128)(2,1)S(1)} collective-permute-done((bf16[128,2048]{1,0:T(8,128)(2,1)S(1)}, bf16[128,2048]{1,0:T(8,128)(2,1)S(1)}, u32[]{:S(2)}, u32[]{:S(2)}) %collective-permute-start.34) | collective-permute-done | bytes 524320 | tf_op jit(solution)/shard_map/ppermute | solution.py:14
  (84 shorter events, 22.9 us)
Async XLA Ops:
  0.6 37.0 %collective-permute-start = (bf16[128,2048]{1,0:T(8,128)(2,1)}, bf16[128,2048]{1,0:T(8,128)(2,1)S(1)}, u32[]{:S(2)}, u32[]{:S(2)}) collective-permute-start(bf16[128,2048]{1,0:T(8,128)(2,1)} %bitcast.29), channel_id=1, source_target_pairs={{0,2},{2,4},{4,6},{1,3},{3,5},{5,7},{8,10},{10,12},{12,14},{9,11},... | collective-permute-start | bytes 1572872 | tf_op jit(solution)/shard_map/ppermute | solution.py:370
  4.1 33.5 %collective-permute-start.1 = (bf16[128,2048]{1,0:T(8,128)(2,1)}, bf16[128,2048]{1,0:T(8,128)(2,1)S(1)}, u32[]{:S(2)}, u32[]{:S(2)}) collective-permute-start(bf16[128,2048]{1,0:T(8,128)(2,1)} %bitcast.30), channel_id=1, source_target_pairs={{6,4},{4,2},{2,0},{7,5},{5,3},{3,1},{14,12},{12,10},{10,8},{15,13}... | collective-permute-start | bytes 1572872 | tf_op jit(solution)/shard_map/ppermute | solution.py:370
  6.5 31.1 %collective-permute-start.2 = (bf16[128,2048]{1,0:T(8,128)(2,1)}, bf16[128,2048]{1,0:T(8,128)(2,1)S(1)}, u32[]{:S(2)}, u32[]{:S(2)}) collective-permute-start(bf16[128,2048]{1,0:T(8,128)(2,1)} %bitcast.31), channel_id=1, source_target_pairs={{0,1},{1,0},{2,3},{3,2},{4,5},{5,4},{6,7},{7,6},{8,9},{9,8},{10,11... | collective-permute-start | bytes 1572872 | tf_op jit(solution)/shard_map/ppermute | solution.py:126
  7.4 24.5 %collective-permute-start.6 = (bf16[16,2048]{1,0:T(8,128)(2,1)S(1)}, bf16[16,2048]{1,0:T(8,128)(2,1)S(1)}, u32[]{:S(2)}, u32[]{:S(2)}) collective-permute-start(bf16[16,2048]{1,0:T(8,128)(2,1)S(1)} %slice_bitcast_fusion.refs_5_), channel_id=1, source_target_pairs={{0,2},{2,4},{4,6},{6,0},{1,3},{3,5},{5,7},{7,1},{8,10},{10,12},{12... | collective-permute-start | bytes 196616 | tf_op jit(solution)/shard_map/ppermute | solution.py:126
  9.7 8.2 %collective-permute-start.3 = (s32[2,128]{1,0:T(2,128)S(1)}, s32[2,128]{1,0:T(2,128)S(1)}, u32[]{:S(2)}, u32[]{:S(2)}) collective-permute-start(s32[2,128]{1,0:T(2,128)S(1)} %add_bitcast_fusion.1.refs_0_), channel_id=1, source_target_pairs={{0,2},{2,4},{4,6},{6,0},{1,3},{3,5},{5,7},{7,1},{8,10},{10,12},{12... | collective-permute-start | bytes 3080 | tf_op jit(solution)/shard_map/ppermute | solution.py:126
  17.9 5.3 %collective-permute-start.4 = (s32[2,128]{1,0:T(2,128)S(1)}, s32[2,128]{1,0:T(2,128)S(1)}, u32[]{:S(2)}, u32[]{:S(2)}) collective-permute-start(s32[2,128]{1,0:T(2,128)S(1)} %add_bitcast_fusion.1.refs_0_), channel_id=1, source_target_pairs={{0,4},{2,6},{4,0},{6,2},{1,5},{3,7},{5,1},{7,3},{8,12},{10,14},{12... | collective-permute-start | bytes 3080 | tf_op jit(solution)/shard_map/ppermute | solution.py:126
  23.2 6.2 %collective-permute-start.5 = (s32[2,128]{1,0:T(2,128)S(1)}, s32[2,128]{1,0:T(2,128)S(1)}, u32[]{:S(2)}, u32[]{:S(2)}) collective-permute-start(s32[2,128]{1,0:T(2,128)S(1)} %add_bitcast_fusion.1.refs_0_), channel_id=1, source_target_pairs={{0,6},{2,0},{4,2},{6,4},{1,7},{3,1},{5,3},{7,5},{8,14},{10,8},{12,... | collective-permute-start | bytes 3080 | tf_op jit(solution)/shard_map/ppermute | solution.py:126
  29.3 5.2 %collective-permute-start.7 = (bf16[16,2048]{1,0:T(8,128)(2,1)S(1)}, bf16[16,2048]{1,0:T(8,128)(2,1)S(1)}, u32[]{:S(2)}, u32[]{:S(2)}) collective-permute-start(bf16[16,2048]{1,0:T(8,128)(2,1)S(1)} %slice_bitcast_fusion.refs_5_), channel_id=1, source_target_pairs={{0,4},{2,6},{4,0},{6,2},{1,5},{3,7},{5,1},{7,3},{8,12},{10,14},{12... | collective-permute-start | bytes 196616 | tf_op jit(solution)/shard_map/ppermute | solution.py:126
  31.9 5.7 %collective-permute-start.8 = (bf16[16,2048]{1,0:T(8,128)(2,1)S(1)}, bf16[16,2048]{1,0:T(8,128)(2,1)S(1)}, u32[]{:S(2)}, u32[]{:S(2)}) collective-permute-start(bf16[16,2048]{1,0:T(8,128)(2,1)S(1)} %slice_bitcast_fusion.refs_5_), channel_id=1, source_target_pairs={{0,6},{2,0},{4,2},{6,4},{1,7},{3,1},{5,3},{7,5},{8,14},{10,8},{12,... | collective-permute-start | bytes 196616 | tf_op jit(solution)/shard_map/ppermute | solution.py:126
  37.7 20.0 %copy-start.12 = (bf16[128,2048]{1,0:T(8,128)(2,1)}, bf16[128,2048]{1,0:T(8,128)(2,1)S(1)}, u32[]{:S(2)}) copy-start(bf16[128,2048]{1,0:T(8,128)(2,1)S(1)} %collective-permute-done.2.refs_8_) | copy-start | bytes 1572868
  37.7 11.1 %collective-permute-start.10 = (bf16[128,2048]{1,0:T(8,128)(2,1)S(1)}, bf16[128,2048]{1,0:T(8,128)(2,1)S(1)}, u32[]{:S(2)}, u32[]{:S(2)}) collective-permute-start(bf16[128,2048]{1,0:T(8,128)(2,1)S(1)} %collective-permute-done.1.refs_6_), channel_id=1, source_target_pairs={{4,2},{2,0},{5,3},{3,1},{12,10},{10,8},{13,11},{11,9},{20,18},{18,... | collective-permute-start | bytes 1572872 | tf_op jit(solution)/shard_map/ppermute | solution.py:370
  39.7 9.1 %collective-permute-start.11 = (bf16[128,2048]{1,0:T(8,128)(2,1)S(1)}, bf16[128,2048]{1,0:T(8,128)(2,1)S(1)}, u32[]{:S(2)}, u32[]{:S(2)}) collective-permute-start(bf16[128,2048]{1,0:T(8,128)(2,1)S(1)} %collective-permute-done.refs_5_), channel_id=1, source_target_pairs={{0,1},{1,0},{2,3},{3,2},{4,5},{5,4},{6,7},{7,6},{8,9},{9,8},{10,11... | collective-permute-start | bytes 1572872 | tf_op jit(solution)/shard_map/ppermute | solution.py:126
  39.7 9.8 %collective-permute-start.12 = (bf16[128,2048]{1,0:T(8,128)(2,1)S(1)}, bf16[128,2048]{1,0:T(8,128)(2,1)S(1)}, u32[]{:S(2)}, u32[]{:S(2)}) collective-permute-start(bf16[128,2048]{1,0:T(8,128)(2,1)S(1)} %collective-permute-done.1.refs_6_), channel_id=1, source_target_pairs={{0,1},{1,0},{2,3},{3,2},{4,5},{5,4},{6,7},{7,6},{8,9},{9,8},{10,11... | collective-permute-start | bytes 1572872 | tf_op jit(solution)/shard_map/ppermute | solution.py:126
  40.2 15.3 %collective-permute-start.9 = (bf16[128,2048]{1,0:T(8,128)(2,1)S(1)}, bf16[128,2048]{1,0:T(8,128)(2,1)}, u32[]{:S(2)}, u32[]{:S(2)}) collective-permute-start(bf16[128,2048]{1,0:T(8,128)(2,1)S(1)} %collective-permute-done.refs_5_), channel_id=1, source_target_pairs={{2,4},{4,6},{3,5},{5,7},{10,12},{12,14},{11,13},{13,15},{18,20},{2... | collective-permute-start | bytes 1572872 | tf_op jit(solution)/shard_map/ppermute | solution.py:370
  49.6 8.1 %copy-start.16 = (bf16[128,2048]{1,0:T(8,128)(2,1)}, bf16[128,2048]{1,0:T(8,128)(2,1)S(1)}, u32[]{:S(2)}) copy-start(bf16[128,2048]{1,0:T(8,128)(2,1)S(1)} %collective-permute-done.12.refs_10_) | copy-start | bytes 1572868
  55.6 2.1 %collective-permute-start.14 = (bf16[128,2048]{1,0:T(8,128)(2,1)S(1)}, bf16[128,2048]{1,0:T(8,128)(2,1)}, u32[]{:S(2)}, u32[]{:S(2)}) collective-permute-start(bf16[128,2048]{1,0:T(8,128)(2,1)S(1)} %broadcast_select_fusion.1.refs_7_), channel_id=1, source_target_pairs={{0,1},{1,0},{2,3},{3,2},{4,5},{5,4},{6,7},{7,6},{8,9},{9,8},{10,11... | collective-permute-start | bytes 1572872 | tf_op jit(solution)/shard_map/ppermute | solution.py:126
  55.7 21.9 %collective-permute-start.13 = (bf16[128,2048]{1,0:T(8,128)(2,1)S(1)}, bf16[128,2048]{1,0:T(8,128)(2,1)S(1)}, u32[]{:S(2)}, u32[]{:S(2)}) collective-permute-start(bf16[128,2048]{1,0:T(8,128)(2,1)S(1)} %broadcast_select_fusion.1.refs_7_), channel_id=1, source_target_pairs={{4,6},{2,0},{5,7},{3,1},{12,14},{10,8},{13,15},{11,9},{20,22},{18,... | collective-permute-start | bytes 1572872 | tf_op jit(solution)/shard_map/ppermute | solution.py:370
  62.9 15.2 %copy-start.10 = (bf16[1,128,2048]{2,1,0:T(8,128)(2,1)S(1)}, bf16[1,128,2048]{2,1,0:T(8,128)(2,1)}, u32[]{:S(2)}) copy-start(bf16[1,128,2048]{2,1,0:T(8,128)(2,1)} %param.16) | copy-start | bytes 1572868
  62.9 23.1 %copy-start.8 = (bf16[1,1,512,512]{3,2,1,0:T(8,128)(2,1)S(1)}, bf16[1,1,512,512]{3,2,1,0:T(8,128)(2,1)}, u32[]{:S(2)}) copy-start(bf16[1,1,512,512]{3,2,1,0:T(8,128)(2,1)} %param.15) | copy-start | bytes 1572868
  77.6 22.0 %collective-permute-start.17 = (bf16[512,2048]{1,0:T(8,128)(2,1)}, bf16[512,2048]{1,0:T(8,128)(2,1)}, u32[]{:S(2)}, u32[]{:S(2)}) collective-permute-start(bf16[512,2048]{1,0:T(8,128)(2,1)} %get-tuple-element.58), channel_id=1, source_target_pairs={{0,1},{1,0},{2,3},{3,2},{4,5},{5,4},{6,7},{7,6},{8,9},{9,8},{10,11... | collective-permute-start | bytes 6291464 | tf_op jit(solution)/shard_map/ppermute | solution.py:126
  77.8 8.3 %collective-permute-start.18 = (bf16[128,2048]{1,0:T(8,128)(2,1)S(1)}, bf16[128,2048]{1,0:T(8,128)(2,1)S(1)}, u32[]{:S(2)}, u32[]{:S(2)}) collective-permute-start(bf16[128,2048]{1,0:T(8,128)(2,1)S(1)} %collective-permute-done.13.refs_1_), channel_id=1, source_target_pairs={{0,1},{1,0},{2,3},{3,2},{4,5},{5,4},{6,7},{7,6},{8,9},{9,8},{10,11... | collective-permute-start | bytes 1572872 | tf_op jit(solution)/shard_map/ppermute | solution.py:126
  78.1 18.7 %collective-permute-start.15 = (bf16[128,2048]{1,0:T(8,128)(2,1)S(1)}, bf16[128,2048]{1,0:T(8,128)(2,1)S(1)}, u32[]{:S(2)}, u32[]{:S(2)}) collective-permute-start(bf16[128,2048]{1,0:T(8,128)(2,1)S(1)} %bitcast.38), channel_id=1, source_target_pairs={{0,2},{2,4},{4,6},{1,3},{3,5},{5,7},{8,10},{10,12},{12,14},{9,11},... | collective-permute-start | bytes 1572872 | tf_op jit(solution)/shard_map/ppermute | solution.py:370
  84.0 15.7 %collective-permute-start.16 = (bf16[128,2048]{1,0:T(8,128)(2,1)S(1)}, bf16[128,2048]{1,0:T(8,128)(2,1)S(1)}, u32[]{:S(2)}, u32[]{:S(2)}) collective-permute-start(bf16[128,2048]{1,0:T(8,128)(2,1)S(1)} %bitcast.39), channel_id=1, source_target_pairs={{6,4},{4,2},{2,0},{7,5},{5,3},{3,1},{14,12},{12,10},{10,8},{15,13}... | collective-permute-start | bytes 1572872 | tf_op jit(solution)/shard_map/ppermute | solution.py:370
  86.0 33.9 %copy-start.1 = (f32[512,2048]{1,0:T(8,128)S(1)}, f32[512,2048]{1,0:T(8,128)}, u32[]{:S(2)}) copy-start(f32[512,2048]{1,0:T(8,128)} %copy-done) | copy-start | bytes 12582916
  86.0 2.3 %copy-start.3 = (bf16[1,1,512,4096]{3,2,1,0:T(8,128)(2,1)S(1)}, bf16[1,1,512,4096]{3,2,1,0:T(8,128)(2,1)}, u32[]{:S(2)}) copy-start(bf16[1,1,512,4096]{3,2,1,0:T(8,128)(2,1)} %param.14) | copy-start | bytes 12582916
  88.4 2.4 %copy-start.4 = (bf16[1,1,4096,512]{3,2,1,0:T(8,128)(2,1)S(1)}, bf16[1,1,4096,512]{3,2,1,0:T(8,128)(2,1)}, u32[]{:S(2)}) copy-start(bf16[1,1,4096,512]{3,2,1,0:T(8,128)(2,1)} %param.13) | copy-start | bytes 12582916
  96.8 31.1 %copy-start.2 = (bf16[1,1024,2048]{2,1,0:T(8,128)(2,1)S(1)}, bf16[1,1024,2048]{2,1,0:T(8,128)(2,1)}, u32[]{:S(2)}) copy-start(bf16[1,1024,2048]{2,1,0:T(8,128)(2,1)} %param.19) | copy-start | bytes 12582916
  96.8 31.1 %copy-start.9 = (f32[1,4,2048]{2,1,0:T(4,128)S(1)}, f32[1,4,2048]{2,1,0:T(4,128)}, u32[]{:S(2)}) copy-start(f32[1,4,2048]{2,1,0:T(4,128)} %param.18) | copy-start | bytes 98308
  96.8 31.1 %copy-start.11 = (bf16[1,128,2048]{2,1,0:T(8,128)(2,1)S(1)}, bf16[1,128,2048]{2,1,0:T(8,128)(2,1)}, u32[]{:S(2)}) copy-start(bf16[1,128,2048]{2,1,0:T(8,128)(2,1)} %param.17) | copy-start | bytes 1572868
  99.6 4.3 %collective-permute-start.21 = (bf16[128,2048]{1,0:T(8,128)(2,1)S(1)}, bf16[128,2048]{1,0:T(8,128)(2,1)S(1)}, u32[]{:S(2)}, u32[]{:S(2)}) collective-permute-start(bf16[128,2048]{1,0:T(8,128)(2,1)S(1)} %get-tuple-element.66), channel_id=1, source_target_pairs={{0,1},{1,0},{2,3},{3,2},{4,5},{5,4},{6,7},{7,6},{8,9},{9,8},{10,11... | collective-permute-start | bytes 1572872 | tf_op jit(solution)/shard_map/ppermute | solution.py:126
  99.6 14.0 %collective-permute-start.19 = (bf16[128,2048]{1,0:T(8,128)(2,1)S(1)}, bf16[128,2048]{1,0:T(8,128)(2,1)S(1)}, u32[]{:S(2)}, u32[]{:S(2)}) collective-permute-start(bf16[128,2048]{1,0:T(8,128)(2,1)S(1)} %collective-permute-done.15.refs_1_), channel_id=1, source_target_pairs={{2,4},{4,6},{3,5},{5,7},{10,12},{12,14},{11,13},{13,15},{18,20},{2... | collective-permute-start | bytes 1572872 | tf_op jit(solution)/shard_map/ppermute | solution.py:370
  102.0 15.8 %collective-permute-start.20 = (bf16[128,2048]{1,0:T(8,128)(2,1)S(1)}, bf16[128,2048]{1,0:T(8,128)(2,1)S(1)}, u32[]{:S(2)}, u32[]{:S(2)}) collective-permute-start(bf16[128,2048]{1,0:T(8,128)(2,1)S(1)} %collective-permute-done.16.refs_2_), channel_id=1, source_target_pairs={{4,2},{2,0},{5,3},{3,1},{12,10},{10,8},{13,11},{11,9},{20,18},{18,... | collective-permute-start | bytes 1572872 | tf_op jit(solution)/shard_map/ppermute | solution.py:370
  104.1 15.8 %collective-permute-start.22 = (bf16[128,2048]{1,0:T(8,128)(2,1)S(1)}, bf16[128,2048]{1,0:T(8,128)(2,1)S(1)}, u32[]{:S(2)}, u32[]{:S(2)}) collective-permute-start(bf16[128,2048]{1,0:T(8,128)(2,1)S(1)} %add_convert_fusion.3), channel_id=1, source_target_pairs={{0,2},{6,4},{1,3},{7,5},{8,10},{14,12},{9,11},{15,13},{16,18},{22,... | collective-permute-start | bytes 1572872 | tf_op jit(solution)/shard_map/ppermute | solution.py:370
  121.1 15.0 %collective-permute-start.24 = (bf16[128,2048]{1,0:T(8,128)(2,1)S(1)}, bf16[128,2048]{1,0:T(8,128)(2,1)S(1)}, u32[]{:S(2)}, u32[]{:S(2)}) collective-permute-start(bf16[128,2048]{1,0:T(8,128)(2,1)S(1)} %add_convert_fusion.2), channel_id=1, source_target_pairs={{0,2},{2,4},{1,3},{3,5},{8,10},{10,12},{9,11},{11,13},{16,18},{18,... | collective-permute-start | bytes 1572872 | tf_op jit(solution)/shard_map/ppermute | solution.py:370
  124.8 14.4 %collective-permute-start.25 = (bf16[128,2048]{1,0:T(8,128)(2,1)S(1)}, bf16[128,2048]{1,0:T(8,128)(2,1)S(1)}, u32[]{:S(2)}, u32[]{:S(2)}) collective-permute-start(bf16[128,2048]{1,0:T(8,128)(2,1)S(1)} %add_convert_fusion.2), channel_id=1, source_target_pairs={{6,4},{4,2},{7,5},{5,3},{14,12},{12,10},{15,13},{13,11},{22,20},{2... | collective-permute-start | bytes 1572872 | tf_op jit(solution)/shard_map/ppermute | solution.py:370
  126.2 13.0 %collective-permute-start.23 = (bf16[128,2048]{1,0:T(8,128)(2,1)S(1)}, bf16[128,2048]{1,0:T(8,128)(2,1)S(1)}, u32[]{:S(2)}, u32[]{:S(2)}) collective-permute-start(bf16[128,2048]{1,0:T(8,128)(2,1)S(1)} %broadcast_select_fusion.refs_3_), channel_id=1, source_target_pairs={{4,6},{2,0},{5,7},{3,1},{12,14},{10,8},{13,15},{11,9},{20,22},{18,... | collective-permute-start | bytes 1572872 | tf_op jit(solution)/shard_map/ppermute | solution.py:370
  139.2 14.2 %collective-permute-start.28 = (bf16[512,1024]{1,0:T(8,128)(2,1)S(1)}, bf16[512,1024]{1,0:T(8,128)(2,1)S(1)}, u32[]{:S(2)}, u32[]{:S(2)}) collective-permute-start(bf16[512,1024]{1,0:T(8,128)(2,1)S(1)} %get-tuple-element.79), channel_id=1, source_target_pairs={{1,0},{3,2},{4,5},{6,7},{9,8},{11,10},{12,13},{14,15},{17,16},{19,... | collective-permute-start | bytes 3145736 | tf_op jit(solution)/shard_map/ppermute | solution.py:468
  143.5 9.1 %collective-permute-start.32 = (bf16[128,1024]{1,0:T(8,128)(2,1)S(1)}, bf16[128,1024]{1,0:T(8,128)(2,1)S(1)}, u32[]{:S(2)}, u32[]{:S(2)}) collective-permute-start(bf16[128,1024]{1,0:T(8,128)(2,1)S(1)} %get-tuple-element.82), channel_id=1, source_target_pairs={{1,0},{3,2},{4,5},{6,7},{9,8},{11,10},{12,13},{14,15},{17,16},{19,... | collective-permute-start | bytes 786440 | tf_op jit(solution)/shard_map/ppermute | solution.py:469
  146.6 27.1 %copy-start.6 = (bf16[1,128,2048]{2,1,0:T(8,128)(2,1)S(1)}, bf16[1,128,2048]{2,1,0:T(8,128)(2,1)}, u32[]{:S(2)}) copy-start(bf16[1,128,2048]{2,1,0:T(8,128)(2,1)} %param.10) | copy-start | bytes 1572868
  146.6 16.6 %collective-permute-start.26 = (bf16[128,2048]{1,0:T(8,128)(2,1)S(1)}, bf16[128,2048]{1,0:T(8,128)(2,1)S(1)}, u32[]{:S(2)}, u32[]{:S(2)}) collective-permute-start(bf16[128,2048]{1,0:T(8,128)(2,1)S(1)} %get-tuple-element.85), channel_id=1, source_target_pairs={{0,2},{2,4},{4,6},{1,3},{3,5},{5,7},{8,10},{10,12},{12,14},{9,11},... | collective-permute-start | bytes 1572872 | tf_op jit(solution)/shard_map/ppermute | solution.py:370
  149.6 20.0 %collective-permute-start.27 = (bf16[128,2048]{1,0:T(8,128)(2,1)S(1)}, bf16[128,2048]{1,0:T(8,128)(2,1)S(1)}, u32[]{:S(2)}, u32[]{:S(2)}) collective-permute-start(bf16[128,2048]{1,0:T(8,128)(2,1)S(1)} %get-tuple-element.84), channel_id=1, source_target_pairs={{6,4},{4,2},{2,0},{7,5},{5,3},{3,1},{14,12},{12,10},{10,8},{15,13}... | collective-permute-start | bytes 1572872 | tf_op jit(solution)/shard_map/ppermute | solution.py:370
  152.7 17.0 %collective-permute-start.33 = (bf16[128,1024]{1,0:T(8,128)(2,1)S(1)}, bf16[128,1024]{1,0:T(8,128)(2,1)S(1)}, u32[]{:S(2)}, u32[]{:S(2)}) collective-permute-start(bf16[128,1024]{1,0:T(8,128)(2,1)S(1)} %add_convert_fusion.4), channel_id=1, source_target_pairs={{0,6},{7,1},{8,14},{15,9},{16,22},{23,17},{24,30},{31,25}} | collective-permute-start | bytes 786440 | tf_op jit(solution)/shard_map/ppermute | solution.py:473
  153.7 16.7 %collective-permute-start.29 = (bf16[128,1024]{1,0:T(8,128)(2,1)S(1)}, bf16[128,1024]{1,0:T(8,128)(2,1)S(1)}, u32[]{:S(2)}, u32[]{:S(2)}) collective-permute-start(bf16[128,1024]{1,0:T(8,128)(2,1)S(1)} %get-tuple-element.89), channel_id=1, source_target_pairs={{7,5},{5,3},{2,0},{15,13},{13,11},{10,8},{23,21},{21,19},{18,16},{... | collective-permute-start | bytes 786440 | tf_op jit(solution)/shard_map/ppermute | solution.py:473
  161.3 9.2 %collective-permute-start.30 = (bf16[128,1024]{1,0:T(8,128)(2,1)S(1)}, bf16[128,1024]{1,0:T(8,128)(2,1)S(1)}, u32[]{:S(2)}, u32[]{:S(2)}) collective-permute-start(bf16[128,1024]{1,0:T(8,128)(2,1)S(1)} %get-tuple-element.88), channel_id=1, source_target_pairs={{0,2},{2,4},{5,7},{8,10},{10,12},{13,15},{16,18},{18,20},{21,23},{... | collective-permute-start | bytes 786440 | tf_op jit(solution)/shard_map/ppermute | solution.py:473
  163.2 10.5 %collective-permute-start.31 = (bf16[128,1024]{1,0:T(8,128)(2,1)S(1)}, bf16[128,1024]{1,0:T(8,128)(2,1)S(1)}, u32[]{:S(2)}, u32[]{:S(2)}) collective-permute-start(bf16[128,1024]{1,0:T(8,128)(2,1)S(1)} %get-tuple-element.87), channel_id=1, source_target_pairs={{0,4},{2,6},{5,1},{7,3},{8,12},{10,14},{13,9},{15,11},{16,20},{18,... | collective-permute-start | bytes 786440 | tf_op jit(solution)/shard_map/ppermute | solution.py:473
  174.7 16.7 %collective-permute-start.34 = (bf16[128,2048]{1,0:T(8,128)(2,1)S(1)}, bf16[128,2048]{1,0:T(8,128)(2,1)S(1)}, u32[]{:S(2)}, u32[]{:S(2)}) collective-permute-start(bf16[128,2048]{1,0:T(8,128)(2,1)S(1)} %residual.1), channel_id=1, source_target_pairs={{8,0},{16,8},{24,16},{9,1},{17,9},{25,17},{10,2},{18,10},{26,18},{... | collective-permute-start | bytes 1572872 | tf_op jit(solution)/shard_map/ppermute | solution.py:14
  177.2 4.0 %collective-permute-start.35 = (f32[4,2048]{1,0:T(4,128)S(1)}, f32[4,2048]{1,0:T(4,128)S(1)}, u32[]{:S(2)}, u32[]{:S(2)}) collective-permute-start(f32[4,2048]{1,0:T(4,128)S(1)} %get-tuple-element.83), channel_id=1, source_target_pairs={{0,2},{2,0},{4,6},{6,4},{1,3},{3,1},{5,7},{7,5},{8,10},{10,8},{12,... | collective-permute-start | bytes 98312 | tf_op jit(solution)/shard_map/ppermute | solution.py:136
  181.2 5.6 %collective-permute-start.36 = (f32[4,2048]{1,0:T(4,128)S(1)}, f32[4,2048]{1,0:T(4,128)S(1)}, u32[]{:S(2)}, u32[]{:S(2)}) collective-permute-start(f32[4,2048]{1,0:T(4,128)S(1)} %add.72), channel_id=1, source_target_pairs={{0,4},{2,6},{4,0},{6,2},{1,5},{3,7},{5,1},{7,3},{8,12},{10,14},{12... | collective-permute-start | bytes 98312 | tf_op jit(solution)/shard_map/ppermute | solution.py:136
  (7 other events, 8.0 us)

commit v4 on v0

--- a/solution.py
+++ b/solution.py
@@ -1,6 +1,10 @@
+import functools
+
 import jax
 import jax.numpy as jnp
 from jax import lax
+from jax.experimental import pallas as pl
+from jax.experimental.pallas import tpu as pltpu
 from jax.sharding import PartitionSpec as P
 
 
@@ -26,7 +30,7 @@
     return buffer.reshape(experts, capacity, width)
 
 
-def shards(
+def slot_plan(
     out_grad,
     expert_ids,
     gate_codes,
@@ -106,6 +110,437 @@
     return (sent_residual[None], tap_grads[None])
 
 
+F32, BF16 = jnp.float32, jnp.bfloat16
+VMEM_LIMIT = 14 * 1024 * 1024
+HEAD = 16
+RIGHT = [(0, 1), (1, 2), (2, 3)]
+LEFT = [(3, 2), (2, 1), (1, 0)]
+NT = (((1,), (1,)), ((), ()))
+TN = (((0,), (0,)), ((), ()))
+
+
+def whole(memory=pltpu.VMEM):
+    return pl.BlockSpec(memory_space=memory)
+
+
+def rotated(array, axis, by):
+    size = lax.axis_size(axis)
+    return lax.ppermute(array, axis, [(i, (i + by) % size) for i in range(size)])
+
+
+def around(array):
+    return [array] + [rotated(array, "expert", k) for k in range(1, lax.axis_size("expert"))]
+
+
+def doubling_sum(array, axis):
+    size, step = lax.axis_size(axis), 1
+    while step < size:
+        array = array + lax.ppermute(array, axis, [(i, i ^ step) for i in range(size)])
+        step *= 2
+    return array
+
+
+def params():
+    return pltpu.CompilerParams(vmem_limit_bytes=VMEM_LIMIT)
+
+
+def cost(flops, bytes_accessed):
+    return pl.CostEstimate(flops=8 * flops, bytes_accessed=8 * bytes_accessed, transcendentals=0)
+
+
+def square(size):
+    row = lax.broadcasted_iota(jnp.int32, (size, size), 0)
+    return row, lax.broadcasted_iota(jnp.int32, (size, size), 1)
+
+
+def upright(line, row, column):
+    return jnp.sum(jnp.where(row == column, line, 0.0), axis=1, keepdims=True)
+
+
+def hidden_kernel(count, place, *refs):
+    pairs, rows = refs[:count], refs[count : 2 * count]
+    down_own, down_other, send, keep, gates, scaled = refs[2 * count :]
+    tok_rows = rows[0].shape[0]
+    units = down_own.shape[0]
+    step = pl.program_id(0)
+
+    @pl.when(step == 0)
+    def _():
+        row, column = square(tok_rows)
+        for k in range(count):
+            pair = pairs[k][...]
+            named = (pair // 256) == place[1]
+            code = jnp.sum(jnp.where(named, (pair % 256).astype(F32), 0.0), axis=0, keepdims=True)
+            gates[k * tok_rows : (k + 1) * tok_rows, :] = upright(code, row, column) / 256.0
+        keep[...] = jnp.zeros_like(keep)
+
+    for k in range(count):
+        at = pl.ds(k * tok_rows, tok_rows)
+        scaled[at, :] = (gates[at, :] * rows[k][...].astype(F32)).astype(BF16)
+    keep[:, :units] += lax.dot_general(scaled[...], down_own[...], NT, preferred_element_type=F32)
+    keep[:, units:] += lax.dot_general(scaled[...], down_other[...], NT, preferred_element_type=F32)
+
+    @pl.when(step == pl.num_programs(0) - 1)
+    def _():
+        send[...] = keep[...].astype(BF16)
+
+
+def hidden_sums(place, pairs, rows, down, down_other):
+    count = len(rows)
+    tok_rows, half_width = rows[0].shape
+    units = down.shape[0]
+    tokens = count * tok_rows
+    chunk = half_width // 4
+    return pl.pallas_call(
+        functools.partial(hidden_kernel, count),
+        grid_spec=pltpu.PrefetchScalarGridSpec(
+            num_scalar_prefetch=1,
+            grid=(4,),
+            in_specs=[whole()] * count
+            + [pl.BlockSpec((tok_rows, chunk), lambda i, place: (0, i))] * count
+            + [
+                pl.BlockSpec((units, chunk), lambda i, place: (0, 4 * place[0] + i)),
+                pl.BlockSpec((units, chunk), lambda i, place: (0, i)),
+            ],
+            out_specs=[pl.BlockSpec((tokens, 2 * units), lambda i, place: (0, 0))] * 2,
+            scratch_shapes=[pltpu.VMEM((tokens, 1), F32), pltpu.VMEM((tokens, chunk), BF16)],
+        ),
+        out_shape=[jax.ShapeDtypeStruct((tokens, 2 * units), dtype) for dtype in (BF16, F32)],
+        compiler_params=params(),
+        cost_estimate=cost(4 * tokens * half_width * units, 4 * units * half_width + 2 * tokens * half_width),
+        name="hidden",
+    )(place, *pairs, *rows, down, down_other)
+
+
+def finish_kernel(count, place, *refs):
+    pairs = refs[:count]
+    keep, got, pre_own, pre_other, up_own, up_other, out, pre_grad = refs[count:]
+    tok_rows = keep.shape[0] // count
+    units = pre_own.shape[1]
+
+    @pl.when(pl.program_id(0) == 0)
+    def _():
+        row, column = square(tok_rows)
+        for k in range(count):
+            at = pl.ds(k * tok_rows, tok_rows)
+            named = jnp.where((pairs[k][...] // 256) == place[1], 1.0, 0.0)
+            named = jnp.sum(named, axis=0, keepdims=True)
+            rank = jnp.where(row < column, upright(named, row, column), 0.0)
+            rank = jnp.sum(rank, axis=0, keepdims=True).astype(jnp.int32)
+            pick = jnp.where(rank == row, named, 0.0).astype(BF16)
+            slots = pl.ds(pl.multiple_of(place[2 + k] * tok_rows, tok_rows), tok_rows)
+            for side, pre in enumerate((pre_own, pre_other)):
+                here = pl.ds(side * units, units)
+                p = lax.dot_general(pick, pre[slots, :], TN, preferred_element_type=F32)
+                q = 1.0 / (1.0 + jnp.exp(-p))
+                hidden = keep[at, here] + got[at, pl.ds((1 - side) * units, units)].astype(F32)
+                pre_grad[at, here] = (hidden * (q * (1.0 + p * (1.0 - q)))).astype(BF16)
+
+    value = lax.dot_general(pre_grad[:, :units], up_own[...], NT, preferred_element_type=F32)
+    value += lax.dot_general(pre_grad[:, units:], up_other[...], NT, preferred_element_type=F32)
+    out[...] = value.astype(out.dtype)
+
+
+def expert_sums(place, pairs, keep, got, pre, pre_other, up, up_other, dtype):
+    count = len(pairs)
+    tokens = keep.shape[0]
+    units = pre.shape[1]
+    half_width = up_other.shape[0]
+    chunk = half_width // 4
+    return pl.pallas_call(
+        functools.partial(finish_kernel, count),
+        grid_spec=pltpu.PrefetchScalarGridSpec(
+            num_scalar_prefetch=1,
+            grid=(4,),
+            in_specs=[whole()] * (count + 4)
+            + [
+                pl.BlockSpec((chunk, units), lambda i, place: (4 * place[0] + i, 0)),
+                pl.BlockSpec((chunk, units), lambda i, place: (i, 0)),
+            ],
+            out_specs=pl.BlockSpec((tokens, chunk), lambda i, place: (0, i)),
+            scratch_shapes=[pltpu.VMEM((tokens, 2 * units), BF16)],
+        ),
+        out_shape=jax.ShapeDtypeStruct((tokens, half_width), dtype),
+        compiler_params=params(),
+        cost_estimate=cost(4 * tokens * half_width * units, 4 * units * half_width + 4 * tokens * half_width),
+        name="experts",
+    )(place, *pairs, keep, got, pre, pre_other, up, up_other)
+
+
+def proj_kernel(count, with_taps, place, *refs):
+    grads, heads = refs[:count], refs[count : 2 * count]
+    taps, weight = refs[2 * count : 2 * count + 2]
+    refs = refs[2 * count + 2 :]
+    if with_taps:
+        inputs, send, keep, tap_out, ext, scaled = refs
+    else:
+        send, keep, ext, scaled = refs
+    tok_rows, chunk = grads[0].shape
+    kernel_size = taps.shape[0]
+    step = pl.program_id(0)
+
+    tap = taps[...]
+    for k in range(count):
+        ext[:tok_rows, :] = grads[k][...].astype(F32)
+        follows = (place[2 + k] < lax.axis_size("expert") - 1).astype(F32)
+        ext[tok_rows:, :] = heads[k][...].astype(F32) * follows
+        result = jnp.zeros((tok_rows, chunk), F32)
+        for j in range(kernel_size):
+            start = kernel_size - 1 - j
+            result = result + tap[j : j + 1, :] * ext[start : start + tok_rows, :]
+        scaled[k * tok_rows : (k + 1) * tok_rows, :] = result.astype(BF16)
+        if with_taps and k == 0:
+            values = inputs[...].astype(F32)
+            for j in range(kernel_size):
+                start = kernel_size - 1 - j
+                terms = values * ext[start : start + tok_rows, :]
+                tap_out[j : j + 1, :] = jnp.sum(terms, axis=0, keepdims=True)
+
+    product = lax.dot_general(scaled[...], weight[...], NT, preferred_element_type=F32)
+
+    @pl.when(step == 0)
+    def _():
+        keep[...] = product
+
+    @pl.when(step > 0)
+    def _():
+        keep[...] += product
+
+    @pl.when(step == pl.num_programs(0) - 1)
+    def _():
+        send[...] = keep[...].astype(BF16)
+
+
+def proj_sums(place, grads, heads, taps, weight, inputs=None):
+    count = len(grads)
+    tok_rows, half_width = grads[0].shape
+    block = weight.shape[0]
+    tokens = count * tok_rows
+    chunk = half_width // 4
+    with_taps = inputs is not None
+
+    def wide(rows):
+        return pl.BlockSpec((rows, chunk), lambda i: (0, i))
+
+    last = [wide(tok_rows)] if with_taps else []
+    out_specs = [pl.BlockSpec((tokens, block), lambda i: (0, 0))] * 2
+    out_shape = [jax.ShapeDtypeStruct((tokens, block), BF16), jax.ShapeDtypeStruct((tokens, block), F32)]
+    if with_taps:
+        out_specs = out_specs + [wide(taps.shape[0])]
+        out_shape = out_shape + [jax.ShapeDtypeStruct(taps.shape, F32)]
+    return pl.pallas_call(
+        functools.partial(proj_kernel, count, with_taps),
+        grid=(half_width // chunk,),
+        in_specs=[whole(pltpu.SMEM)]
+        + [wide(tok_rows)] * count
+        + [wide(HEAD)] * count
+        + [wide(taps.shape[0]), wide(block)]
+        + last,
+        out_specs=out_specs,
+        out_shape=out_shape,
+        scratch_shapes=[pltpu.VMEM((tok_rows + HEAD, chunk), F32), pltpu.VMEM((tokens, chunk), BF16)],
+        compiler_params=params(),
+        cost_estimate=cost(
+            2 * tokens * half_width * block, 2 * (block + tokens) * half_width + 6 * tokens * block
+        ),
+        name="projection",
+    )(place, *grads, *heads, taps, weight, *([inputs] if with_taps else []))
+
+
+def combine_kernel(place, grad, sums, back_right, back_left, proj_keep, proj_got, to_right, to_left, own, total):
+    half, me = place[0], place[1]
+    rows, part = grad.shape[0], proj_keep.shape[1]
+    total[0:rows, :] = grad[...].astype(F32) + sums[0:rows, :]
+    total[rows : 2 * rows, :] = sums[rows : 2 * rows, :] + back_left[...].astype(F32)
+    total[2 * rows :, :] = sums[2 * rows :, :] + back_right[...].astype(F32)
+
+    @pl.when(me // 2 == half)
+    def _():
+        at = pl.ds(pl.multiple_of(lax.rem(me, 2) * part, part), part)
+        total[:, at] += proj_keep[...] + proj_got[...].astype(F32)
+
+    own[...] = total[0:rows, :]
+    to_left[...] = total[rows : 2 * rows, :].astype(BF16)
+    to_right[...] = total[2 * rows :, :].astype(BF16)
+
+
+def combined(place, grad, sums, *arrays):
+    outs = [jax.ShapeDtypeStruct(grad.shape, dtype) for dtype in (BF16, BF16, F32)]
+    return pl.pallas_call(
+        combine_kernel,
+        in_specs=[whole(pltpu.SMEM)] + [whole()] * (2 + len(arrays)),
+        out_specs=[whole()] * 3,
+        out_shape=outs,
+        scratch_shapes=[pltpu.VMEM(sums.shape, F32)],
+        compiler_params=params(),
+        cost_estimate=cost(8 * grad.size, 40 * grad.size),
+        name="combine",
+    )(place, grad, sums, *arrays)
+
+
+def final_kernel(place, residual, far, end, out, total):
+    half, me = place[0], place[1]
+    experts = lax.axis_size("expert")
+    part = far.shape[1]
+    total[...] = residual[...].astype(F32)
+
+    def add(source, value):
+        @pl.when((source < experts) & (source // 2 == half))
+        def _():
+            at = pl.ds(pl.multiple_of(lax.rem(source, 2) * part, part), part)
+            total[:, at] += value[...].astype(F32)
+
+    add(lax.rem(me + 2, experts), far)
+    add(jnp.where(lax.rem(me, experts - 1) == 0, experts - 1 - me, experts), end)
+    out[...] = total[...].astype(BF16)
+
+
+def final_sum(place, residual, far, end):
+    return pl.pallas_call(
+        final_kernel,
+        in_specs=[whole(pltpu.SMEM)] + [whole()] * 3,
+        out_specs=whole(),
+        out_shape=jax.ShapeDtypeStruct(residual.shape, BF16),
+        scratch_shapes=[pltpu.VMEM(residual.shape, F32)],
+        compiler_params=params(),
+        cost_estimate=cost(4 * residual.size, 8 * residual.size),
+        name="residual",
+    )(place, residual, far, end)
+
+
+def moved(array, pairs):
+    return lax.ppermute(array, "expert", pairs)
+
+
+def swapped(array):
+    return rotated(array, "mp", 1)
+
+
+def together(*arrays):
+    return lax.optimization_barrier(arrays)
+
+
+def token_plan(
+    out_grad,
+    expert_ids,
+    gate_codes,
+    up_weight,
+    down_weight,
+    pre_act,
+    conv_grad,
+    conv_input,
+    conv_weight,
+    in_proj,
+):
+    me, half = lax.axis_index("expert"), lax.axis_index("mp")
+    experts = lax.axis_size("expert")
+
+    def place(*blocks):
+        return jnp.stack([half, me, *blocks]).astype(jnp.int32)
+
+    far_block, end_block = (me + 2) % experts, jnp.where(me == 0, experts - 1, 0)
+    near = place(me, jnp.maximum(me - 1, 0), jnp.minimum(me + 1, experts - 1))
+    rows_own, conv_own = out_grad[0], conv_grad[0]
+    tok_rows, half_width = rows_own.shape
+    w_down, w_up, pre = down_weight[0, 0], up_weight[0, 0], pre_act[0, 0]
+    taps, w_proj = conv_weight[0], in_proj[0]
+
+    pairs = around((expert_ids[0] * 256 + gate_codes[0]).T)
+    down_send = lax.dynamic_slice_in_dim(w_down, (1 - half) * half_width, half_width, 1)
+    up_send = lax.dynamic_slice_in_dim(w_up, (1 - half) * half_width, half_width, 0)
+    rows_own, down_send, *pairs = together(rows_own, down_send, *pairs)
+
+    rows_left, rows_right = moved(rows_own, RIGHT), moved(rows_own, LEFT)
+    down_other = swapped(down_send)
+    rows_left, rows_right, down_other, up_send, pre_send = together(rows_left, rows_right, down_other, up_send, pre)
+
+    def hidden(where, routes, rows):
+        send, keep = hidden_sums(where, routes, rows, w_down, down_other)
+        return keep, swapped(send)
+
+    def finish(where, routes, keep, got, dtype):
+        return expert_sums(where, routes, keep, got, pre, pre_other, w_up, up_other, dtype)
+
+    near_pairs = [pairs[0], pairs[1], pairs[3]]
+    from_left, from_right = moved(rows_left, RIGHT[1:]), moved(rows_right, LEFT[1:])
+    up_other, pre_other = swapped(up_send), swapped(pre_send)
+    near_keep, near_got = hidden(near, near_pairs, [rows_own, rows_left, rows_right])
+    from_left, from_right, near_keep, up_other, pre_other = together(
+        from_left, from_right, near_keep, up_other, pre_other
+    )
+
+    far, end = place(far_block), place(end_block)
+    end_pairs = [jnp.where(me == 0, pairs[1], pairs[3])]
+    rows_far = jnp.where(me >= 2, from_left, from_right)
+    rows_end = moved(rows_far, [(2, 3), (1, 0)])
+    near_sums = finish(near, near_pairs, near_keep, near_got, F32)
+    far_keep, far_got = hidden(far, [pairs[2]], [rows_far])
+    rows_end, near_sums, far_keep, conv_own = together(rows_end, near_sums, far_keep, conv_own)
+
+    conv_left, conv_right = moved(conv_own, RIGHT), moved(conv_own, LEFT)
+    end_keep, end_got = hidden(end, end_pairs, [rows_end])
+    far_sums = finish(far, [pairs[2]], far_keep, far_got, F32)
+    end_sums = finish(end, end_pairs, end_keep, end_got, BF16)
+    next_head = moved(conv_own[:HEAD], [(2, 0), (3, 1)])
+    last_head = moved(conv_own[:HEAD], [(3, 0)])
+    conv_left, conv_right, end_sums, far_sums, next_head, last_head = together(
+        conv_left, conv_right, end_sums, far_sums, next_head, last_head
+    )
+
+    from_left, from_right = moved(conv_left, RIGHT[1:]), moved(conv_right, LEFT[1:])
+    back_end = moved(end_sums, [(0, 1), (3, 2)])
+    gather = [(e * 2 + 1 - e // 2, e * 2 + e // 2) for e in range(experts)]
+
+    def proj(where, grads, heads, *inputs):
+        send, keep, *tap_terms = proj_sums(where, grads, heads, taps, w_proj, *inputs)
+        return keep, lax.ppermute(send, ("expert", "mp"), gather), *tap_terms
+
+    near_proj, near_proj_got, tap_terms = proj(
+        near, [conv_own, conv_left, conv_right], [conv_right, conv_own, next_head], conv_input[0]
+    )
+    from_left, from_right, back_end, near_proj, conv_left = together(
+        from_left, from_right, back_end, near_proj, conv_left
+    )
+
+    conv_far = jnp.where(me >= 2, from_left, from_right)
+    conv_end = moved(conv_far, [(2, 3), (1, 0)])
+    back = (far_sums + back_end.astype(F32)).astype(BF16)
+    back_right, back_left = moved(back, RIGHT[:2]), moved(back, LEFT[:2])
+    far_head = jnp.where(me >= 2, conv_left[:HEAD], last_head)
+    far_proj, far_proj_got = proj(far, [conv_far], [far_head])
+    conv_end, back_right, back_left, far_proj = together(conv_end, back_right, back_left, far_proj)
+
+    to_right, to_left, own = combined(near, rows_own, near_sums, back_right, back_left, near_proj, near_proj_got)
+    to_right, to_left, conv_end = together(to_right, to_left, conv_end)
+    to_right, to_left = moved(to_right, RIGHT), moved(to_left, LEFT)
+    end_proj, end_proj_got = proj(end, [conv_end], [conv_far])
+    to_right, to_left, end_proj = together(to_right, to_left, end_proj)
+
+    residual = (own + to_right.astype(F32) + to_left.astype(F32)).astype(BF16)
+    sections, halves = lax.axis_size("section"), lax.axis_size("mp")
+
+    def deliver(keep, got, pairs):
+        def at(s, e, m):
+            return (s * experts + e) * halves + m
+
+        moves = [(at(s, e, e // 2), at(s - 1, d, e // 2)) for s in range(1, sections) for e, d in pairs]
+        return lax.ppermute((keep + got.astype(F32)).astype(BF16), ("section", "expert", "mp"), moves)
+
+    residual = shifted(residual, "section", -1)
+    far_piece = deliver(far_proj, far_proj_got, [(e, (e + 2) % experts) for e in range(experts)])
+    end_piece = deliver(end_proj, end_proj_got, [(0, experts - 1), (experts - 1, 0)])
+    tap_grads = doubling_sum(tap_terms, "expert")
+    residual = final_sum(near, residual, far_piece, end_piece)
+    return (residual[None], tap_grads[None])
+
+
+def shards(*arrays):
+    experts, halves = lax.axis_size("expert"), lax.axis_size("mp")
+    capacity = arrays[5].shape[2] // experts
+    dense = capacity == arrays[0].shape[1] and experts == 4 and halves == 2
+    return (token_plan if dense else slot_plan)(*arrays)
+
+
 def solution(mesh):
     in_specs = (
         P("section", "expert", "mp"),

time: 514 us -> 165 us (0.32)
  blocking collectives: 219 us -> 0 us
  waiting for transfers between devices: 205 us -> 65 us
  Pallas kernels: 0 us -> 40.9 us
  starting transfers between devices: 11.8 us -> 48.5 us
  matrix products: 21 us -> 0 us
  other arithmetic: 19.8 us -> 2.06 us
  local copies, waits for them, and re-layouts: 22.1 us -> 6.75 us
  between operations: 14 us -> 1.29 us
    all_to_all x1 -> x0, blocking collectives: 201 us -> none  [shards(): lax.all_to_all(buffer, 'expert', split_axis=0, concat_axis=0, tiled=True)]
    all_gather x2 -> x0, waiting for transfers between devices: 144 us -> none  [the longest x1 134 us: shards(): lax.all_gather(w_proj, 'expert', axis=0, tiled=True)]
    ppermute x0 -> x33, waiting for transfers between devices: none -> 50.2 us  [the longest x17 49.9 us: moved(): return lax.ppermute(array, 'expert', pairs)]
    ppermute x0 -> x33, starting transfers between devices: none -> 47.2 us  [the longest x17 32.8 us: moved(): return lax.ppermute(array, 'expert', pairs)]
    pallas_call x0 -> x11, Pallas kernels: none -> 40.9 us  [the longest x3 15.6 us: expert_sums(): pl.pallas_call(functools.partial(finish_kernel, count), grid_spec=pltpu.P...]
    ppermute x3 -> x1, waiting for transfers between devices: 42.5 us -> 14.8 us  [shifted(): return lax.ppermute(array, axis, pairs)]
    dot_general x3 -> x0, matrix products: 21 us -> none  [the longest x1 12.8 us: shards(): lax.dot_general(input_grad, lax.all_gather(w_proj, 'expert', axis=0, tile...]
    psum x1 -> x0, blocking collectives: 17.9 us -> none  [shards(): tap_grads = lax.psum(jnp.stack(tap_terms), 'expert')]
  transfers between devices with their start and end apart: 8 -> 34, of which waited for: 6 -> 12; matrix products, arithmetic and copies ran while one was open for 11% -> 3% of each run, Pallas kernels for 0% -> 24%
where the time goes in v4:
time: 165 us
  waiting for transfers between devices  65 us (39%)
  starting transfers between devices  48.5 us (29%)
  Pallas kernels  40.9 us (25%)
  local copies, waits for them, and re-layouts  6.75 us (4%)
  other arithmetic  2.06 us (1%)
    ppermute x17, waiting for transfers between devices, moved(): return lax.ppermute(array, 'expert', pairs)  49.9 us
    ppermute x17, starting transfers between devices, moved(): return lax.ppermute(array, 'expert', pairs)  32.8 us
    pallas_call x3, Pallas kernels, expert_sums(): pl.pallas_call(functools.partial(finish_kernel, count), grid_spec=pltpu.P...  15.6 us
    ppermute x1, waiting for transfers between devices, shifted(): return lax.ppermute(array, axis, pairs)  14.8 us
    pallas_call x3, Pallas kernels, proj_sums(): pl.pallas_call(functools.partial(proj_kernel, count, with_taps), grid=(ha...  11.8 us
    pallas_call x3, Pallas kernels, hidden_sums(): pl.pallas_call(functools.partial(hidden_kernel, count), grid_spec=pltpu.P...  10.9 us
    ppermute x9, starting transfers between devices, rotated(): lax.ppermute(array, axis, [(i, (i + by) % size) for i in range(size)])  7.75 us
    ppermute x3, starting transfers between devices, proj(): return (keep, lax.ppermute(send, ('expert', 'mp'), gather), *tap_terms)  3.88 us
  transfers between devices with their start and end apart: 34, of which 12 were waited for; matrix products, arithmetic and copies ran while one was open for 3% of the time, Pallas kernels for 24%

profile of v4, /device:TPU:0, one launch (start us, length us, event | category | flops | bytes accessed | tf_op | source)
XLA Modules:
  0.0 164.6 jit_solution(14297431284265781963)
XLA Ops:
  1.3 3.0 %collective-permute-start = (s32[2,128]{1,0:T(2,128)S(1)}, s32[2,128]{1,0:T(2,128)S(1)}, u32[]{:S(2)}, u32[]{:S(2)}) collective-permute-start(s32[2,128]{1,0:T(2,128)S(1)} %add_bitcast_fusion.1.refs_0_), channel_id=1, source_target_pairs={{0,2},{2,4},{4,6},{6,0},{1,3},{3,5},{5,7},{7,1},{8,10},{10,12},{12... | collective-permute-start | bytes 3080 | tf_op jit(solution)/shard_map/ppermute | solution.py:128
  4.4 2.6 %collective-permute-start.1 = (s32[2,128]{1,0:T(2,128)S(1)}, s32[2,128]{1,0:T(2,128)S(1)}, u32[]{:S(2)}, u32[]{:S(2)}) collective-permute-start(s32[2,128]{1,0:T(2,128)S(1)} %add_bitcast_fusion.1.refs_0_), channel_id=1, source_target_pairs={{0,4},{2,6},{4,0},{6,2},{1,5},{3,7},{5,1},{7,3},{8,12},{10,14},{12... | collective-permute-start | bytes 3080 | tf_op jit(solution)/shard_map/ppermute | solution.py:128
  6.9 1.3 collective-permute-start.2
  8.3 1.9 %dynamic-slice_bitcast_fusion.1 = bf16[512,2048]{1,0:T(8,128)(2,1)S(1)} fusion(bf16[1,1,512,4096]{3,2,1,0:T(8,128)(2,1)} %param.14, s32[]{:T(128)S(6)} %select_n.43), kind=kLoop, calls=%fused_computation.1 | loop fusion | bytes 4194308 | tf_op jit(solution)/shard_map/dynamic_slice | solution.py:449
  10.5 2.5 %collective-permute-start.3 = (bf16[128,2048]{1,0:T(8,128)(2,1)}, bf16[128,2048]{1,0:T(8,128)(2,1)S(1)}, u32[]{:S(2)}, u32[]{:S(2)}) collective-permute-start(bf16[128,2048]{1,0:T(8,128)(2,1)} %bitcast.31), channel_id=1, source_target_pairs={{0,2},{2,4},{4,6},{1,3},{3,5},{5,7},{8,10},{10,12},{12,14},{9,11},... | collective-permute-start | bytes 1572872 | tf_op jit(solution)/shard_map/ppermute | solution.py:412
  13.1 1.3 collective-permute-start.4
  14.4 1.5 dynamic-slice_bitcast_fusion
  15.9 9.2 %collective-permute-done.3.refs_4_ = bf16[128,2048]{1,0:T(8,128)(2,1)S(1)} collective-permute-done((bf16[128,2048]{1,0:T(8,128)(2,1)}, bf16[128,2048]{1,0:T(8,128)(2,1)S(1)}, u32[]{:S(2)}, u32[]{:S(2)}) %collective-permute-start.3) | collective-permute-done | bytes 524320 | tf_op jit(solution)/shard_map/ppermute | solution.py:412
  25.0 4.1 %collective-permute-done.4.refs_5_ = bf16[128,2048]{1,0:T(8,128)(2,1)} collective-permute-done((bf16[128,2048]{1,0:T(8,128)(2,1)}, bf16[128,2048]{1,0:T(8,128)(2,1)}, u32[]{:S(2)}, u32[]{:S(2)}) %collective-permute-start.4) | collective-permute-done | bytes 524320 | tf_op jit(solution)/shard_map/ppermute | solution.py:412
  30.2 1.3 collective-permute-start.7
  32.0 2.2 %copy-done = bf16[1,1,512,4096]{3,2,1,0:T(8,128)(2,1)S(1)} copy-done((bf16[1,1,512,4096]{3,2,1,0:T(8,128)(2,1)S(1)}, bf16[1,1,512,4096]{3,2,1,0:T(8,128)(2,1)}, u32[]{:S(2)}) %copy-start) | copy-done | bytes 4194328
  34.2 1.0 copy-done.4
  35.2 4.7 %hidden.3 = (bf16[384,1024]{1,0:T(8,128)(2,1)S(1)}, f32[384,1024]{1,0:T(8,128)S(1)}) custom-call(s32[5]{0:T(128)S(1)} %stack.36.place, s32[2,128]{1,0:T(2,128)S(1)} %add_bitcast_fusion.1.refs_0_, s32[2,128]{1,0:T(2,128)S(1)} %collective-permute-done.refs_1_, s32[2,128]{1,0:T(2,128)S(1)} %collective-permute-done.2.refs_2_, bf16[128,2048]{1,0:T(8,128)(2,1)S(1)} %bitcast.33, ...), custom_call_target="tpu_custom_call" | custom-call | flops 12884901888 | bytes 46137344 | tf_op jit(solution)/shard_map/hidden/pallas_call | solution.py:194
  40.1 9.5 %collective-permute-done.7 = bf16[128,2048]{1,0:T(8,128)(2,1)S(1)} collective-permute-done((bf16[128,2048]{1,0:T(8,128)(2,1)}, bf16[128,2048]{1,0:T(8,128)(2,1)S(1)}, u32[]{:S(2)}, u32[]{:S(2)}) %collective-permute-start.7) | collective-permute-done | bytes 524320 | tf_op jit(solution)/shard_map/ppermute | solution.py:412
  49.7 1.6 collective-permute-start.10
  51.2 3.1 %hidden.4 = (bf16[128,1024]{1,0:T(8,128)(2,1)S(1)}, f32[128,1024]{1,0:T(8,128)S(1)}) custom-call(s32[3]{0:T(128)S(1)} %pad_add_fusion.place, s32[2,128]{1,0:T(2,128)S(1)} %collective-permute-done.1.refs_0_, bf16[128,2048]{1,0:T(8,128)(2,1)S(1)} %broadcast_select_fusion.1.refs_1_, bf16[512,4096]{1,0:T(8,128)(2,1)S(1)} %bitcast.26, ...), custom_call_target="tpu_custom_call" | custom-call | flops 4294967296 | bytes 37748736 | tf_op jit(solution)/shard_map/hidden/pallas_call | solution.py:194
  54.5 5.9 %experts.3.sums = f32[384,2048]{1,0:T(8,128)S(1)} custom-call(s32[5]{0:T(128)S(1)} %stack.36.place, s32[2,128]{1,0:T(2,128)S(1)} %add_bitcast_fusion.1.refs_0_, s32[2,128]{1,0:T(2,128)S(1)} %collective-permute-done.refs_1_, s32[2,128]{1,0:T(2,128)S(1)} %collective-permute-done.2.refs_2_, f32[384,1024]{1,0:T(8,128)S(1)} %get-tuple-element.72.refs_3_, ...), custom_call_target="tpu_custom_call" | custom-call | flops 12884901888 | bytes 58720256 | tf_op jit(solution)/shard_map/experts/pallas_call | solution.py:250
  60.4 5.0 %collective-permute-done.10.refs_1_ = bf16[128,2048]{1,0:T(8,128)(2,1)S(1)} collective-permute-done((bf16[128,2048]{1,0:T(8,128)(2,1)S(1)}, bf16[128,2048]{1,0:T(8,128)(2,1)S(1)}, u32[]{:S(2)}, u32[]{:S(2)}) %collective-permute-start.10) | collective-permute-done | bytes 524320 | tf_op jit(solution)/shard_map/ppermute | solution.py:412
  65.3 1.5 collective-permute-start.12
  66.8 1.3 collective-permute-start.13
  68.1 1.3 collective-permute-start.16
  69.4 1.3 collective-permute-start.17
  70.8 3.1 %hidden.5 = (bf16[128,1024]{1,0:T(8,128)(2,1)S(1)}, f32[128,1024]{1,0:T(8,128)S(1)}) custom-call(s32[3]{0:T(128)S(1)} %pad_add_fusion.2.place, s32[2,128]{1,0:T(2,128)S(1)} %broadcast_select_fusion.2.refs_0_, bf16[128,2048]{1,0:T(8,128)(2,1)S(1)} %collective-permute-done.10.refs_1_, bf16[512,4096]{1,0:T(8,128)(2,1)S(1)} %bitcast.27, ...), custom_call_target="tpu_custom_call" | custom-call | flops 4294967296 | bytes 37748736 | tf_op jit(solution)/shard_map/hidden/pallas_call | solution.py:194
  73.9 4.7 %experts.5 = f32[128,2048]{1,0:T(8,128)S(1)} custom-call(s32[3]{0:T(128)S(1)} %pad_add_fusion.place, s32[2,128]{1,0:T(2,128)S(1)} %collective-permute-done.1.refs_0_, f32[128,1024]{1,0:T(8,128)S(1)} %get-tuple-element.83.refs_1_, bf16[128,1024]{1,0:T(8,128)(2,1)S(1)} %collective-permute-done.15.refs_2_, bf16[512,512]{1,0:T(8,128)(2,1)S(1)} %bitcast.45, ...), custom_call_target="tpu_custom_call" | custom-call | flops 4294967296 | bytes 41943040 | tf_op jit(solution)/shard_map/experts/pallas_call | solution.py:250
  78.7 5.0 %experts.4 = bf16[128,2048]{1,0:T(8,128)(2,1)S(1)} custom-call(s32[3]{0:T(128)S(1)} %pad_add_fusion.2.place, s32[2,128]{1,0:T(2,128)S(1)} %broadcast_select_fusion.2.refs_0_, f32[128,1024]{1,0:T(8,128)S(1)} %get-tuple-element.81.refs_1_, bf16[128,1024]{1,0:T(8,128)(2,1)S(1)} %collective-permute-done.14.refs_2_, bf16[512,512]{1,0:T(8,128)(2,1)S(1)} %bitcast.46, ...), custom_call_target="tpu_custom_call" | custom-call | flops 4294967296 | bytes 41943040 | tf_op jit(solution)/shard_map/experts/pallas_call | solution.py:250
  83.7 1.3 collective-permute-done.16.refs_5_
  85.7 1.3 collective-permute-start.19
  87.0 6.0 %collective-permute-start.20 = (bf16[128,2048]{1,0:T(8,128)(2,1)S(1)}, bf16[128,2048]{1,0:T(8,128)(2,1)S(1)}, u32[]{:S(2)}, u32[]{:S(2)}) collective-permute-start(bf16[128,2048]{1,0:T(8,128)(2,1)S(1)} %experts.4), channel_id=1, source_target_pairs={{0,2},{6,4},{1,3},{7,5},{8,10},{14,12},{9,11},{15,13},{16,18},{22,... | collective-permute-start | bytes 1572872 | tf_op jit(solution)/shard_map/ppermute | solution.py:412
  93.0 5.9 %projection.3 = (bf16[384,1024]{1,0:T(8,128)(2,1)S(1)}, f32[384,1024]{1,0:T(8,128)S(1)}, f32[4,2048]{1,0:T(4,128)S(1)}) custom-call(s32[5]{0:T(128)S(1)} %stack.36.place, bf16[128,2048]{1,0:T(8,128)(2,1)S(1)} %bitcast.38, bf16[128,2048]{1,0:T(8,128)(2,1)S(1)} %collective-permute-done.12.refs_1_, ...), custom_call_target="tpu_custom_call" | custom-call | flops 12884901888 | bytes 65011712 | tf_op jit(solution)/shard_map/projection/pallas_call | solution.py:331
  98.9 1.3 collective-permute-start.24
  100.3 3.0 %collective-permute-done.19 = bf16[128,2048]{1,0:T(8,128)(2,1)S(1)} collective-permute-done((bf16[128,2048]{1,0:T(8,128)(2,1)S(1)}, bf16[128,2048]{1,0:T(8,128)(2,1)S(1)}, u32[]{:S(2)}, u32[]{:S(2)}) %collective-permute-start.19) | collective-permute-done | bytes 524320 | tf_op jit(solution)/shard_map/ppermute | solution.py:412
  103.3 1.5 collective-permute-done.20
  105.0 4.4 %collective-permute-start.22 = (bf16[128,2048]{1,0:T(8,128)(2,1)S(1)}, bf16[128,2048]{1,0:T(8,128)(2,1)S(1)}, u32[]{:S(2)}, u32[]{:S(2)}) collective-permute-start(bf16[128,2048]{1,0:T(8,128)(2,1)S(1)} %add_convert_fusion.1), channel_id=1, source_target_pairs={{0,2},{2,4},{1,3},{3,5},{8,10},{10,12},{9,11},{11,13},{16,18},{18,... | collective-permute-start | bytes 1572872 | tf_op jit(solution)/shard_map/ppermute | solution.py:412
  110.2 1.3 collective-permute-start.21
  111.5 3.0 %projection.4 = (bf16[128,1024]{1,0:T(8,128)(2,1)S(1)}, f32[128,1024]{1,0:T(8,128)S(1)}) custom-call(s32[3]{0:T(128)S(1)} %pad_add_fusion.place, bf16[128,2048]{1,0:T(8,128)(2,1)S(1)} %broadcast_select_fusion.refs_0_.refs_1_, bf16[16,2048]{1,0:T(8,128)(2,1)S(1)} %slice_select_fusion.refs_1_, f32[4,2048]{1,0:T(4,128)S(1)} %bitcast.49, ...), custom_call_target="tpu_custom_call" | custom-call | flops 4294967296 | bytes 44040192 | tf_op jit(solution)/shard_map/projection/pallas_call | solution.py:331
  114.5 1.3 collective-permute-start.28
  115.8 9.7 %collective-permute-done.21.refs_0_ = bf16[128,2048]{1,0:T(8,128)(2,1)S(1)} collective-permute-done((bf16[128,2048]{1,0:T(8,128)(2,1)S(1)}, bf16[128,2048]{1,0:T(8,128)(2,1)S(1)}, u32[]{:S(2)}, u32[]{:S(2)}) %collective-permute-start.21) | collective-permute-done | bytes 524320 | tf_op jit(solution)/shard_map/ppermute | solution.py:412
  125.5 1.4 collective-permute-start.33
  126.9 1.2 combine.1
  128.1 4.4 %collective-permute-start.25 = (bf16[128,2048]{1,0:T(8,128)(2,1)S(1)}, bf16[128,2048]{1,0:T(8,128)(2,1)S(1)}, u32[]{:S(2)}, u32[]{:S(2)}) collective-permute-start(bf16[128,2048]{1,0:T(8,128)(2,1)S(1)} %get-tuple-element.105), channel_id=1, source_target_pairs={{0,2},{2,4},{4,6},{1,3},{3,5},{5,7},{8,10},{10,12},{12,14},{9,11},... | collective-permute-start | bytes 1572872 | tf_op jit(solution)/shard_map/ppermute | solution.py:412
  132.5 1.3 collective-permute-start.26
  134.6 3.0 %projection.5 = (bf16[128,1024]{1,0:T(8,128)(2,1)S(1)}, f32[128,1024]{1,0:T(8,128)S(1)}) custom-call(s32[3]{0:T(128)S(1)} %pad_add_fusion.2.place, bf16[128,2048]{1,0:T(8,128)(2,1)S(1)} %collective-permute-done.21.refs_0_, bf16[128,2048]{1,0:T(8,128)(2,1)S(1)} %broadcast_select_fusion.refs_0_.refs_1_, f32[4,2048]{1,0:T(4,128)S(1)} %bitcast.50, ...), custom_call_target="tpu_custom_call" | custom-call | flops 4294967296 | bytes 44040192 | tf_op jit(solution)/shard_map/projection/pallas_call | solution.py:331
  137.5 1.3 collective-permute-start.30
  138.8 2.4 %collective-permute-done.25 = bf16[128,2048]{1,0:T(8,128)(2,1)S(1)} collective-permute-done((bf16[128,2048]{1,0:T(8,128)(2,1)S(1)}, bf16[128,2048]{1,0:T(8,128)(2,1)S(1)}, u32[]{:S(2)}, u32[]{:S(2)}) %collective-permute-start.25) | collective-permute-done | bytes 524320 | tf_op jit(solution)/shard_map/ppermute | solution.py:412
  141.2 4.1 %collective-permute-done.26 = bf16[128,2048]{1,0:T(8,128)(2,1)S(1)} collective-permute-done((bf16[128,2048]{1,0:T(8,128)(2,1)S(1)}, bf16[128,2048]{1,0:T(8,128)(2,1)S(1)}, u32[]{:S(2)}, u32[]{:S(2)}) %collective-permute-start.26) | collective-permute-done | bytes 524320 | tf_op jit(solution)/shard_map/ppermute | solution.py:412
  145.5 1.3 collective-permute-start.27
  148.3 14.8 %collective-permute-done.27.residual = bf16[128,2048]{1,0:T(8,128)(2,1)S(1)} collective-permute-done((bf16[128,2048]{1,0:T(8,128)(2,1)S(1)}, bf16[128,2048]{1,0:T(8,128)(2,1)S(1)}, u32[]{:S(2)}, u32[]{:S(2)}) %collective-permute-start.27) | collective-permute-done | bytes 524320 | tf_op jit(solution)/shard_map/ppermute | solution.py:14
  163.1 1.5 residual.1
  (76 shorter events, 6.9 us)
Async XLA Ops:
  1.3 8.8 %collective-permute-start = (s32[2,128]{1,0:T(2,128)S(1)}, s32[2,128]{1,0:T(2,128)S(1)}, u32[]{:S(2)}, u32[]{:S(2)}) collective-permute-start(s32[2,128]{1,0:T(2,128)S(1)} %add_bitcast_fusion.1.refs_0_), channel_id=1, source_target_pairs={{0,2},{2,4},{4,6},{6,0},{1,3},{3,5},{5,7},{7,1},{8,10},{10,12},{12... | collective-permute-start | bytes 3080 | tf_op jit(solution)/shard_map/ppermute | solution.py:128
  4.4 5.8 %collective-permute-start.1 = (s32[2,128]{1,0:T(2,128)S(1)}, s32[2,128]{1,0:T(2,128)S(1)}, u32[]{:S(2)}, u32[]{:S(2)}) collective-permute-start(s32[2,128]{1,0:T(2,128)S(1)} %add_bitcast_fusion.1.refs_0_), channel_id=1, source_target_pairs={{0,4},{2,6},{4,0},{6,2},{1,5},{3,7},{5,1},{7,3},{8,12},{10,14},{12... | collective-permute-start | bytes 3080 | tf_op jit(solution)/shard_map/ppermute | solution.py:128
  6.9 3.6 %collective-permute-start.2 = (s32[2,128]{1,0:T(2,128)S(1)}, s32[2,128]{1,0:T(2,128)S(1)}, u32[]{:S(2)}, u32[]{:S(2)}) collective-permute-start(s32[2,128]{1,0:T(2,128)S(1)} %add_bitcast_fusion.1.refs_0_), channel_id=1, source_target_pairs={{0,6},{2,0},{4,2},{6,4},{1,7},{3,1},{5,3},{7,5},{8,14},{10,8},{12,... | collective-permute-start | bytes 3080 | tf_op jit(solution)/shard_map/ppermute | solution.py:128
  8.3 6.1 %copy-start.2 = (bf16[1,1,4096,512]{3,2,1,0:T(8,128)(2,1)S(1)}, bf16[1,1,4096,512]{3,2,1,0:T(8,128)(2,1)}, u32[]{:S(2)}) copy-start(bf16[1,1,4096,512]{3,2,1,0:T(8,128)(2,1)} %param.13) | copy-start | bytes 12582916
  10.5 20.9 %copy-start.10 = (bf16[1,1,512,512]{3,2,1,0:T(8,128)(2,1)S(1)}, bf16[1,1,512,512]{3,2,1,0:T(8,128)(2,1)}, u32[]{:S(2)}) copy-start(bf16[1,1,512,512]{3,2,1,0:T(8,128)(2,1)} %param.15) | copy-start | bytes 1572868
  10.5 18.7 %collective-permute-start.5 = (bf16[512,2048]{1,0:T(8,128)(2,1)S(1)}, bf16[512,2048]{1,0:T(8,128)(2,1)S(1)}, u32[]{:S(2)}, u32[]{:S(2)}) collective-permute-start(bf16[512,2048]{1,0:T(8,128)(2,1)S(1)} %dynamic-slice_bitcast_fusion.1), channel_id=1, source_target_pairs={{0,1},{1,0},{2,3},{3,2},{4,5},{5,4},{6,7},{7,6},{8,9},{9,8},{10,11... | collective-permute-start | bytes 6291464 | tf_op jit(solution)/shard_map/ppermute | solution.py:128
  10.5 14.5 %collective-permute-start.3 = (bf16[128,2048]{1,0:T(8,128)(2,1)}, bf16[128,2048]{1,0:T(8,128)(2,1)S(1)}, u32[]{:S(2)}, u32[]{:S(2)}) collective-permute-start(bf16[128,2048]{1,0:T(8,128)(2,1)} %bitcast.31), channel_id=1, source_target_pairs={{0,2},{2,4},{4,6},{1,3},{3,5},{5,7},{8,10},{10,12},{12,14},{9,11},... | collective-permute-start | bytes 1572872 | tf_op jit(solution)/shard_map/ppermute | solution.py:412
  13.1 16.1 %collective-permute-start.4 = (bf16[128,2048]{1,0:T(8,128)(2,1)}, bf16[128,2048]{1,0:T(8,128)(2,1)}, u32[]{:S(2)}, u32[]{:S(2)}) collective-permute-start(bf16[128,2048]{1,0:T(8,128)(2,1)} %bitcast.32), channel_id=1, source_target_pairs={{6,4},{4,2},{2,0},{7,5},{5,3},{3,1},{14,12},{12,10},{10,8},{15,13}... | collective-permute-start | bytes 1572872 | tf_op jit(solution)/shard_map/ppermute | solution.py:412
  29.2 22.1 %copy-start.8 = (bf16[512,2048]{1,0:T(8,128)(2,1)}, bf16[512,2048]{1,0:T(8,128)(2,1)S(1)}, u32[]{:S(2)}) copy-start(bf16[512,2048]{1,0:T(8,128)(2,1)S(1)} %collective-permute-done.5.refs_7_.refs_3_) | copy-start | bytes 6291460
  29.2 20.4 %collective-permute-start.8 = (bf16[2048,512]{1,0:T(8,128)(2,1)}, bf16[2048,512]{1,0:T(8,128)(2,1)}, u32[]{:S(2)}, u32[]{:S(2)}) collective-permute-start(bf16[2048,512]{1,0:T(8,128)(2,1)} %dynamic-slice_bitcast_fusion), channel_id=1, source_target_pairs={{0,1},{1,0},{2,3},{3,2},{4,5},{5,4},{6,7},{7,6},{8,9},{9,8},{10,11... | collective-permute-start | bytes 6291464 | tf_op jit(solution)/shard_map/ppermute | solution.py:128
  29.5 10.6 %collective-permute-start.6 = (bf16[128,2048]{1,0:T(8,128)(2,1)S(1)}, bf16[128,2048]{1,0:T(8,128)(2,1)S(1)}, u32[]{:S(2)}, u32[]{:S(2)}) collective-permute-start(bf16[128,2048]{1,0:T(8,128)(2,1)S(1)} %collective-permute-done.3.refs_4_), channel_id=1, source_target_pairs={{2,4},{4,6},{3,5},{5,7},{10,12},{12,14},{11,13},{13,15},{18,20},{2... | collective-permute-start | bytes 1572872 | tf_op jit(solution)/shard_map/ppermute | solution.py:412
  30.2 19.4 %collective-permute-start.7 = (bf16[128,2048]{1,0:T(8,128)(2,1)}, bf16[128,2048]{1,0:T(8,128)(2,1)S(1)}, u32[]{:S(2)}, u32[]{:S(2)}) collective-permute-start(bf16[128,2048]{1,0:T(8,128)(2,1)} %collective-permute-done.4.refs_5_), channel_id=1, source_target_pairs={{4,2},{2,0},{5,3},{3,1},{12,10},{10,8},{13,11},{11,9},{20,18},{18,... | collective-permute-start | bytes 1572872 | tf_op jit(solution)/shard_map/ppermute | solution.py:412
  31.5 18.1 %collective-permute-start.9 = (bf16[512,512]{1,0:T(8,128)(2,1)S(1)}, bf16[512,512]{1,0:T(8,128)(2,1)S(1)}, u32[]{:S(2)}, u32[]{:S(2)}) collective-permute-start(bf16[512,512]{1,0:T(8,128)(2,1)S(1)} %bitcast.43), channel_id=1, source_target_pairs={{0,1},{1,0},{2,3},{3,2},{4,5},{5,4},{6,7},{7,6},{8,9},{9,8},{10,11... | collective-permute-start | bytes 1572872 | tf_op jit(solution)/shard_map/ppermute | solution.py:128
  32.0 2.2 %copy-start = (bf16[1,1,512,4096]{3,2,1,0:T(8,128)(2,1)S(1)}, bf16[1,1,512,4096]{3,2,1,0:T(8,128)(2,1)}, u32[]{:S(2)}) copy-start(bf16[1,1,512,4096]{3,2,1,0:T(8,128)(2,1)} %param.14) | copy-start | bytes 12582916
  34.2 1.0 copy-start.4
  40.0 14.5 %collective-permute-start.11 = (bf16[384,1024]{1,0:T(8,128)(2,1)S(1)}, bf16[384,1024]{1,0:T(8,128)(2,1)S(1)}, u32[]{:S(2)}, u32[]{:S(2)}) collective-permute-start(bf16[384,1024]{1,0:T(8,128)(2,1)S(1)} %get-tuple-element.73), channel_id=1, source_target_pairs={{0,1},{1,0},{2,3},{3,2},{4,5},{5,4},{6,7},{7,6},{8,9},{9,8},{10,11... | collective-permute-start | bytes 2359304 | tf_op jit(solution)/shard_map/ppermute | solution.py:128
  49.6 4.8 %copy-start.3 = (bf16[1,1,4096,512]{3,2,1,0:T(8,128)(2,1)S(1)}, bf16[1,1,4096,512]{3,2,1,0:T(8,128)(2,1)}, u32[]{:S(2)}) copy-start(bf16[1,1,4096,512]{3,2,1,0:T(8,128)(2,1)} %param.13) | copy-start | bytes 12582916
  49.7 4.8 %copy-start.11 = (bf16[1,1,512,512]{3,2,1,0:T(8,128)(2,1)S(1)}, bf16[1,1,512,512]{3,2,1,0:T(8,128)(2,1)}, u32[]{:S(2)}) copy-start(bf16[1,1,512,512]{3,2,1,0:T(8,128)(2,1)} %param.15) | copy-start | bytes 1572868
  49.7 15.7 %collective-permute-start.10 = (bf16[128,2048]{1,0:T(8,128)(2,1)S(1)}, bf16[128,2048]{1,0:T(8,128)(2,1)S(1)}, u32[]{:S(2)}, u32[]{:S(2)}) collective-permute-start(bf16[128,2048]{1,0:T(8,128)(2,1)S(1)} %broadcast_select_fusion.1.refs_1_), channel_id=1, source_target_pairs={{4,6},{2,0},{5,7},{3,1},{12,14},{10,8},{13,15},{11,9},{20,22},{18,... | collective-permute-start | bytes 1572872 | tf_op jit(solution)/shard_map/ppermute | solution.py:412
  54.3 19.5 %collective-permute-start.15 = (bf16[128,1024]{1,0:T(8,128)(2,1)S(1)}, bf16[128,1024]{1,0:T(8,128)(2,1)S(1)}, u32[]{:S(2)}, u32[]{:S(2)}) collective-permute-start(bf16[128,1024]{1,0:T(8,128)(2,1)S(1)} %get-tuple-element.84), channel_id=1, source_target_pairs={{0,1},{1,0},{2,3},{3,2},{4,5},{5,4},{6,7},{7,6},{8,9},{9,8},{10,11... | collective-permute-start | bytes 786440 | tf_op jit(solution)/shard_map/ppermute | solution.py:128
  54.4 10.9 %copy-start.6 = (bf16[1,128,2048]{2,1,0:T(8,128)(2,1)S(1)}, bf16[1,128,2048]{2,1,0:T(8,128)(2,1)}, u32[]{:S(2)}) copy-start(bf16[1,128,2048]{2,1,0:T(8,128)(2,1)} %param.16) | copy-start | bytes 1572868
  54.5 16.3 %copy-start.1 = (bf16[1,1,512,4096]{3,2,1,0:T(8,128)(2,1)S(1)}, bf16[1,1,512,4096]{3,2,1,0:T(8,128)(2,1)}, u32[]{:S(2)}) copy-start(bf16[1,1,512,4096]{3,2,1,0:T(8,128)(2,1)} %param.14) | copy-start | bytes 12582916
  54.5 16.3 %copy-start.9 = (bf16[512,2048]{1,0:T(8,128)(2,1)S(1)}, bf16[512,2048]{1,0:T(8,128)(2,1)}, u32[]{:S(2)}) copy-start(bf16[512,2048]{1,0:T(8,128)(2,1)} %copy-done.8) | copy-start | bytes 6291460
  65.3 19.6 %collective-permute-start.12 = (bf16[128,2048]{1,0:T(8,128)(2,1)S(1)}, bf16[128,2048]{1,0:T(8,128)(2,1)S(1)}, u32[]{:S(2)}, u32[]{:S(2)}) collective-permute-start(bf16[128,2048]{1,0:T(8,128)(2,1)S(1)} %bitcast.35), channel_id=1, source_target_pairs={{0,2},{2,4},{4,6},{1,3},{3,5},{5,7},{8,10},{10,12},{12,14},{9,11},... | collective-permute-start | bytes 1572872 | tf_op jit(solution)/shard_map/ppermute | solution.py:412
  66.8 18.2 %collective-permute-start.13 = (bf16[128,2048]{1,0:T(8,128)(2,1)S(1)}, bf16[128,2048]{1,0:T(8,128)(2,1)S(1)}, u32[]{:S(2)}, u32[]{:S(2)}) collective-permute-start(bf16[128,2048]{1,0:T(8,128)(2,1)S(1)} %bitcast.36), channel_id=1, source_target_pairs={{6,4},{4,2},{2,0},{7,5},{5,3},{3,1},{14,12},{12,10},{10,8},{15,13}... | collective-permute-start | bytes 1572872 | tf_op jit(solution)/shard_map/ppermute | solution.py:412
  68.1 16.8 %collective-permute-start.16 = (bf16[16,2048]{1,0:T(8,128)(2,1)S(1)}, bf16[16,2048]{1,0:T(8,128)(2,1)S(1)}, u32[]{:S(2)}, u32[]{:S(2)}) collective-permute-start(bf16[16,2048]{1,0:T(8,128)(2,1)S(1)} %slice.7), channel_id=1, source_target_pairs={{4,0},{6,2},{5,1},{7,3},{12,8},{14,10},{13,9},{15,11},{20,16},{22,... | collective-permute-start | bytes 196616 | tf_op jit(solution)/shard_map/ppermute | solution.py:412
  69.4 15.5 %collective-permute-start.17 = (bf16[16,2048]{1,0:T(8,128)(2,1)S(1)}, bf16[16,2048]{1,0:T(8,128)(2,1)S(1)}, u32[]{:S(2)}, u32[]{:S(2)}) collective-permute-start(bf16[16,2048]{1,0:T(8,128)(2,1)S(1)} %slice.7), channel_id=1, source_target_pairs={{6,0},{7,1},{14,8},{15,9},{22,16},{23,17},{30,24},{31,25}} | collective-permute-start | bytes 196616 | tf_op jit(solution)/shard_map/ppermute | solution.py:412
  73.8 4.8 %collective-permute-start.14 = (bf16[128,1024]{1,0:T(8,128)(2,1)S(1)}, bf16[128,1024]{1,0:T(8,128)(2,1)S(1)}, u32[]{:S(2)}, u32[]{:S(2)}) collective-permute-start(bf16[128,1024]{1,0:T(8,128)(2,1)S(1)} %get-tuple-element.82), channel_id=1, source_target_pairs={{0,1},{1,0},{2,3},{3,2},{4,5},{5,4},{6,7},{7,6},{8,9},{9,8},{10,11... | collective-permute-start | bytes 786440 | tf_op jit(solution)/shard_map/ppermute | solution.py:128
  78.6 14.4 %copy-start.7 = (bf16[1,1024,2048]{2,1,0:T(8,128)(2,1)S(1)}, bf16[1,1024,2048]{2,1,0:T(8,128)(2,1)}, u32[]{:S(2)}) copy-start(bf16[1,1024,2048]{2,1,0:T(8,128)(2,1)} %param.19) | copy-start | bytes 12582916
  78.6 14.4 %copy-start.12 = (bf16[1,128,2048]{2,1,0:T(8,128)(2,1)S(1)}, bf16[1,128,2048]{2,1,0:T(8,128)(2,1)}, u32[]{:S(2)}) copy-start(bf16[1,128,2048]{2,1,0:T(8,128)(2,1)} %param.17) | copy-start | bytes 1572868
  78.7 14.4 %copy-start.13 = (f32[1,4,2048]{2,1,0:T(4,128)S(1)}, f32[1,4,2048]{2,1,0:T(4,128)}, u32[]{:S(2)}) copy-start(f32[1,4,2048]{2,1,0:T(4,128)} %param.18) | copy-start | bytes 98308
  85.0 15.3 %collective-permute-start.18 = (bf16[128,2048]{1,0:T(8,128)(2,1)S(1)}, bf16[128,2048]{1,0:T(8,128)(2,1)S(1)}, u32[]{:S(2)}, u32[]{:S(2)}) collective-permute-start(bf16[128,2048]{1,0:T(8,128)(2,1)S(1)} %collective-permute-done.12.refs_1_), channel_id=1, source_target_pairs={{2,4},{4,6},{3,5},{5,7},{10,12},{12,14},{11,13},{13,15},{18,20},{2... | collective-permute-start | bytes 1572872 | tf_op jit(solution)/shard_map/ppermute | solution.py:412
  85.7 17.6 %collective-permute-start.19 = (bf16[128,2048]{1,0:T(8,128)(2,1)S(1)}, bf16[128,2048]{1,0:T(8,128)(2,1)S(1)}, u32[]{:S(2)}, u32[]{:S(2)}) collective-permute-start(bf16[128,2048]{1,0:T(8,128)(2,1)S(1)} %collective-permute-done.13.refs_2_.refs_3_), channel_id=1, source_target_pairs={{4,2},{2,0},{5,3},{3,1},{12,10},{10,8},{13,11},{11,9},{20,18},{18,... | collective-permute-start | bytes 1572872 | tf_op jit(solution)/shard_map/ppermute | solution.py:412
  87.0 17.9 %collective-permute-start.20 = (bf16[128,2048]{1,0:T(8,128)(2,1)S(1)}, bf16[128,2048]{1,0:T(8,128)(2,1)S(1)}, u32[]{:S(2)}, u32[]{:S(2)}) collective-permute-start(bf16[128,2048]{1,0:T(8,128)(2,1)S(1)} %experts.4), channel_id=1, source_target_pairs={{0,2},{6,4},{1,3},{7,5},{8,10},{14,12},{9,11},{15,13},{16,18},{22,... | collective-permute-start | bytes 1572872 | tf_op jit(solution)/shard_map/ppermute | solution.py:412
  98.9 28.0 %collective-permute-start.24 = (bf16[384,1024]{1,0:T(8,128)(2,1)S(1)}, bf16[384,1024]{1,0:T(8,128)(2,1)S(1)}, u32[]{:S(2)}, u32[]{:S(2)}) collective-permute-start(bf16[384,1024]{1,0:T(8,128)(2,1)S(1)} %get-tuple-element.100), channel_id=1, source_target_pairs={{1,0},{3,2},{4,5},{6,7},{9,8},{11,10},{12,13},{14,15},{17,16},{19,... | collective-permute-start | bytes 2359304 | tf_op jit(solution)/shard_map/ppermute | solution.py:496
  100.2 14.3 %collective-permute-start.32 = (f32[4,2048]{1,0:T(4,128)S(1)}, f32[4,2048]{1,0:T(4,128)S(1)}, u32[]{:S(2)}, u32[]{:S(2)}) collective-permute-start(f32[4,2048]{1,0:T(4,128)S(1)} %get-tuple-element.115), channel_id=1, source_target_pairs={{0,2},{2,0},{4,6},{6,4},{1,3},{3,1},{5,7},{7,5},{8,10},{10,8},{12,... | collective-permute-start | bytes 98312 | tf_op jit(solution)/shard_map/ppermute | solution.py:138
  105.0 21.9 %collective-permute-start.22 = (bf16[128,2048]{1,0:T(8,128)(2,1)S(1)}, bf16[128,2048]{1,0:T(8,128)(2,1)S(1)}, u32[]{:S(2)}, u32[]{:S(2)}) collective-permute-start(bf16[128,2048]{1,0:T(8,128)(2,1)S(1)} %add_convert_fusion.1), channel_id=1, source_target_pairs={{0,2},{2,4},{1,3},{3,5},{8,10},{10,12},{9,11},{11,13},{16,18},{18,... | collective-permute-start | bytes 1572872 | tf_op jit(solution)/shard_map/ppermute | solution.py:412
  109.4 17.5 %collective-permute-start.23 = (bf16[128,2048]{1,0:T(8,128)(2,1)S(1)}, bf16[128,2048]{1,0:T(8,128)(2,1)S(1)}, u32[]{:S(2)}, u32[]{:S(2)}) collective-permute-start(bf16[128,2048]{1,0:T(8,128)(2,1)S(1)} %add_convert_fusion.1), channel_id=1, source_target_pairs={{6,4},{4,2},{7,5},{5,3},{14,12},{12,10},{15,13},{13,11},{22,20},{2... | collective-permute-start | bytes 1572872 | tf_op jit(solution)/shard_map/ppermute | solution.py:412
  110.2 15.3 %collective-permute-start.21 = (bf16[128,2048]{1,0:T(8,128)(2,1)S(1)}, bf16[128,2048]{1,0:T(8,128)(2,1)S(1)}, u32[]{:S(2)}, u32[]{:S(2)}) collective-permute-start(bf16[128,2048]{1,0:T(8,128)(2,1)S(1)} %broadcast_select_fusion.refs_0_.refs_1_), channel_id=1, source_target_pairs={{4,6},{2,0},{5,7},{3,1},{12,14},{10,8},{13,15},{11,9},{20,22},{18,... | collective-permute-start | bytes 1572872 | tf_op jit(solution)/shard_map/ppermute | solution.py:412
  111.5 15.4 %copy-start.5 = (bf16[1,128,2048]{2,1,0:T(8,128)(2,1)S(1)}, bf16[1,128,2048]{2,1,0:T(8,128)(2,1)}, u32[]{:S(2)}) copy-start(bf16[1,128,2048]{2,1,0:T(8,128)(2,1)} %param.10) | copy-start | bytes 1572868
  114.5 19.3 %collective-permute-start.28 = (bf16[128,1024]{1,0:T(8,128)(2,1)S(1)}, bf16[128,1024]{1,0:T(8,128)(2,1)S(1)}, u32[]{:S(2)}, u32[]{:S(2)}) collective-permute-start(bf16[128,1024]{1,0:T(8,128)(2,1)S(1)} %get-tuple-element.112), channel_id=1, source_target_pairs={{1,0},{3,2},{4,5},{6,7},{9,8},{11,10},{12,13},{14,15},{17,16},{19,... | collective-permute-start | bytes 786440 | tf_op jit(solution)/shard_map/ppermute | solution.py:496
  125.5 22.1 %collective-permute-start.33 = (f32[4,2048]{1,0:T(4,128)S(1)}, f32[4,2048]{1,0:T(4,128)S(1)}, u32[]{:S(2)}, u32[]{:S(2)}) collective-permute-start(f32[4,2048]{1,0:T(4,128)S(1)} %add.53), channel_id=1, source_target_pairs={{0,4},{2,6},{4,0},{6,2},{1,5},{3,7},{5,1},{7,3},{8,12},{10,14},{12... | collective-permute-start | bytes 98312 | tf_op jit(solution)/shard_map/ppermute | solution.py:138
  128.1 13.1 %collective-permute-start.25 = (bf16[128,2048]{1,0:T(8,128)(2,1)S(1)}, bf16[128,2048]{1,0:T(8,128)(2,1)S(1)}, u32[]{:S(2)}, u32[]{:S(2)}) collective-permute-start(bf16[128,2048]{1,0:T(8,128)(2,1)S(1)} %get-tuple-element.105), channel_id=1, source_target_pairs={{0,2},{2,4},{4,6},{1,3},{3,5},{5,7},{8,10},{10,12},{12,14},{9,11},... | collective-permute-start | bytes 1572872 | tf_op jit(solution)/shard_map/ppermute | solution.py:412
  132.5 12.8 %collective-permute-start.26 = (bf16[128,2048]{1,0:T(8,128)(2,1)S(1)}, bf16[128,2048]{1,0:T(8,128)(2,1)S(1)}, u32[]{:S(2)}, u32[]{:S(2)}) collective-permute-start(bf16[128,2048]{1,0:T(8,128)(2,1)S(1)} %get-tuple-element.106), channel_id=1, source_target_pairs={{6,4},{4,2},{2,0},{7,5},{5,3},{3,1},{14,12},{12,10},{10,8},{15,13}... | collective-permute-start | bytes 1572872 | tf_op jit(solution)/shard_map/ppermute | solution.py:412
  133.9 14.4 %collective-permute-start.29 = (bf16[128,1024]{1,0:T(8,128)(2,1)S(1)}, bf16[128,1024]{1,0:T(8,128)(2,1)S(1)}, u32[]{:S(2)}, u32[]{:S(2)}) collective-permute-start(bf16[128,1024]{1,0:T(8,128)(2,1)S(1)} %add_convert_fusion.3), channel_id=1, source_target_pairs={{8,4},{10,6},{13,1},{15,3},{16,12},{18,14},{21,9},{23,11},{24,20},... | collective-permute-start | bytes 786440 | tf_op jit(solution)/shard_map/ppermute | solution.py:527
  137.5 9.3 %collective-permute-start.30 = (bf16[128,1024]{1,0:T(8,128)(2,1)S(1)}, bf16[128,1024]{1,0:T(8,128)(2,1)S(1)}, u32[]{:S(2)}, u32[]{:S(2)}) collective-permute-start(bf16[128,1024]{1,0:T(8,128)(2,1)S(1)} %get-tuple-element.114), channel_id=1, source_target_pairs={{1,0},{3,2},{4,5},{6,7},{9,8},{11,10},{12,13},{14,15},{17,16},{19,... | collective-permute-start | bytes 786440 | tf_op jit(solution)/shard_map/ppermute | solution.py:496
  145.5 17.5 %collective-permute-start.27 = (bf16[128,2048]{1,0:T(8,128)(2,1)S(1)}, bf16[128,2048]{1,0:T(8,128)(2,1)S(1)}, u32[]{:S(2)}, u32[]{:S(2)}) collective-permute-start(bf16[128,2048]{1,0:T(8,128)(2,1)S(1)} %add_convert_fusion), channel_id=1, source_target_pairs={{8,0},{16,8},{24,16},{9,1},{17,9},{25,17},{10,2},{18,10},{26,18},{... | collective-permute-start | bytes 1572872 | tf_op jit(solution)/shard_map/ppermute | solution.py:14
  146.9 1.3 collective-permute-start.31

commit v5 on v4

v5 whole, which is shorter than its diff:
```python
import functools

import jax
import jax.numpy as jnp
from jax import lax
from jax.experimental import pallas as pl
from jax.experimental.pallas import tpu as pltpu
from jax.sharding import PartitionSpec as P


def shifted(array, axis, by):
    size = lax.axis_size(axis)
    pairs = [(i, i + by) for i in range(size) if 0 <= i + by < size]
    return lax.ppermute(array, axis, pairs)


def silu_slope(pre_value):
    sig = jax.nn.sigmoid(pre_value)
    return sig * (1.0 + pre_value * (1.0 - sig))


def gated_rows(gates, rows, tok_rows):
    scaled = (gates[:, :, None] * rows.astype(jnp.float32)[:, None, :]).astype(jnp.bfloat16)
    return scaled.reshape(tok_rows * 2, rows.shape[1])


def fill_buffer(scaled, target, experts, capacity):
    width = scaled.shape[1]
    buffer = jnp.zeros((experts * capacity, width), jnp.bfloat16).at[target].set(scaled)
    return buffer.reshape(experts, capacity, width)


def slot_plan(
    out_grad,
    expert_ids,
    gate_codes,
    up_weight,
    down_weight,
    pre_act,
    conv_grad,
    conv_input,
    conv_weight,
    in_proj,
):
    grad_rows = out_grad[0]
    route_ids = expert_ids[0]
    tok_rows = grad_rows.shape[0]
    experts = lax.axis_size("expert")
    capacity = pre_act.shape[2] // experts
    gates = gate_codes[0].astype(jnp.float32) / 256.0
    flat_ids = route_ids.reshape(tok_rows * 2)
    onehot = (flat_ids[:, None] == jnp.arange(experts, dtype=jnp.int32)[None, :]).astype(jnp.int32)
    before = jnp.cumsum(onehot, axis=0) - onehot
    position = jnp.sum(before * onehot, axis=1)
    target = flat_ids * capacity + position
    whole_rows = lax.all_gather(grad_rows, "mp", axis=1, tiled=True)
    buffer = fill_buffer(gated_rows(gates, whole_rows, tok_rows), target, experts, capacity)
    arrived = lax.all_to_all(buffer, "expert", split_axis=0, concat_axis=0, tiled=True)
    slot_rows = arrived.reshape(experts * capacity, whole_rows.shape[1])
    w_down = down_weight[0, 0]
    w_up = up_weight[0, 0]
    pre_slots = pre_act[0, 0].astype(jnp.float32)
    hidden = lax.dot_general(
        slot_rows, w_down, (((1,), (1,)), ((), ())), preferred_element_type=jnp.float32
    )
    pre_grad = (hidden * silu_slope(pre_slots)).astype(jnp.bfloat16)
    partial_value = lax.dot_general(
        pre_grad, w_up, (((1,), (1,)), ((), ())), preferred_element_type=jnp.float32
    )
    share = lax.psum_scatter(partial_value, "mp", scatter_dimension=1, tiled=True).astype(
        jnp.bfloat16
    )
    returned = lax.all_to_all(
        share.reshape(experts, capacity, share.shape[1]),
        "expert",
        split_axis=0,
        concat_axis=0,
        tiled=True,
    )
    picked = returned.reshape(experts * capacity, grad_rows.shape[1])[target]
    picked = picked.astype(jnp.float32).reshape(tok_rows, 2, grad_rows.shape[1])
    moe_total = grad_rows.astype(jnp.float32) + picked[:, 0, :] + picked[:, 1, :]
    grads_here = conv_grad[0]
    inputs_here = conv_input[0]
    taps = conv_weight[0]
    kernel_size = taps.shape[0]
    next_rows = shifted(grads_here[: kernel_size - 1], "expert", -1)
    prev_rows = shifted(inputs_here[tok_rows - kernel_size + 1 :], "expert", 1)
    grad_ext = jnp.concatenate([grads_here, next_rows], axis=0).astype(jnp.float32)
    input_ext = jnp.concatenate([prev_rows, inputs_here], axis=0).astype(jnp.float32)
    grad_local = grads_here.astype(jnp.float32)
    conv_result = jnp.zeros(grads_here.shape, jnp.float32)
    tap_terms = []
    for tap in range(kernel_size):
        start = kernel_size - 1 - tap
        conv_result = conv_result + taps[tap][None, :] * grad_ext[start : start + tok_rows]
        tap_terms.append(jnp.sum(grad_local * input_ext[tap : tap + tok_rows], axis=0))
    input_grad = conv_result.astype(jnp.bfloat16)
    tap_grads = lax.psum(jnp.stack(tap_terms), "expert")
    w_proj = in_proj[0]
    proj_partial = lax.dot_general(
        input_grad,
        lax.all_gather(w_proj, "expert", axis=0, tiled=True),
        (((1,), (1,)), ((), ())),
        preferred_element_type=jnp.float32,
    )
    proj_share = lax.psum_scatter(proj_partial, "mp", scatter_dimension=1, tiled=True)
    residual = (moe_total + proj_share).astype(jnp.bfloat16)
    sent_residual = shifted(residual, "section", -1)
    return (sent_residual[None], tap_grads[None])


F32, BF16 = jnp.float32, jnp.bfloat16
VMEM_LIMIT = 14 * 1024 * 1024
RIGHT = [(0, 1), (1, 2), (2, 3)]
LEFT = [(3, 2), (2, 1), (1, 0)]
NT = (((1,), (1,)), ((), ()))
TN = (((0,), (0,)), ((), ()))


def whole(memory=pltpu.VMEM):
    return pl.BlockSpec(memory_space=memory)


def rotated(array, axis, by):
    size = lax.axis_size(axis)
    return lax.ppermute(array, axis, [(i, (i + by) % size) for i in range(size)])


def around(array):
    return [array] + [rotated(array, "expert", k) for k in range(1, lax.axis_size("expert"))]


def doubling_sum(array, axis):
    size, step = lax.axis_size(axis), 1
    while step < size:
        array = array + lax.ppermute(array, axis, [(i, i ^ step) for i in range(size)])
        step *= 2
    return array


def params(limit=VMEM_LIMIT):
    return pltpu.CompilerParams(vmem_limit_bytes=limit)


def cost(flops, bytes_accessed):
    return pl.CostEstimate(flops=flops, bytes_accessed=bytes_accessed, transcendentals=0)


def streamed(source, buffer, sems, step):
    count, _, chunk = buffer.shape

    def copy(i):
        columns = pl.ds(pl.multiple_of(i * chunk, chunk), chunk)
        return pltpu.make_async_copy(source.at[:, columns], buffer.at[i], sems.at[i])

    @pl.when(step == 0)
    def _():
        for i in range(count):
            copy(i).start()

    copy(step).wait()
    return buffer[step]


def stream_scratch(array, count):
    shape = (count, array.shape[0], array.shape[1] // count)
    return [pltpu.VMEM(shape, array.dtype), pltpu.SemaphoreType.DMA((count,))]


def square(size):
    row = lax.broadcasted_iota(jnp.int32, (size, size), 0)
    return row, lax.broadcasted_iota(jnp.int32, (size, size), 1)


def upright(line, row, column):
    return jnp.sum(jnp.where(row == column, line, 0.0), axis=1, keepdims=True)


def rows_of(place, k, experts, tok_rows):
    block = lax.rem(place[1] - k + experts, experts)
    return pl.ds(pl.multiple_of(block * tok_rows, tok_rows), tok_rows)


def hidden_kernel(experts, place, *refs):
    pairs = refs[:experts]
    rows, down_own, down_other, send, keep, gates, buffer, sems = refs[experts:]
    tok_rows = rows.shape[0] // experts
    units = down_own.shape[0]
    step = pl.program_id(0)
    values = streamed(rows, buffer, sems, step).astype(F32)

    @pl.when(step == 0)
    def _():
        row, column = square(tok_rows)
        for k in range(experts):
            pair = pairs[k][...]
            named = (pair // 256) == place[1]
            code = jnp.sum(jnp.where(named, (pair % 256).astype(F32), 0.0), axis=0, keepdims=True)
            gates[rows_of(place, k, experts, tok_rows), :] = upright(code, row, column) / 256.0
        keep[...] = jnp.zeros_like(keep)

    scaled = (gates[...] * values).astype(BF16)
    keep[:, :units] += lax.dot_general(scaled, down_own[...], NT, preferred_element_type=F32)
    keep[:, units:] += lax.dot_general(scaled, down_other[...], NT, preferred_element_type=F32)

    @pl.when(step == pl.num_programs(0) - 1)
    def _():
        send[...] = keep[...].astype(BF16)


def hidden_sums(place, pairs, rows, down, down_other):
    experts = len(pairs)
    tokens, half_width = rows.shape
    units = down.shape[0]
    chunk = half_width // 4
    return pl.pallas_call(
        functools.partial(hidden_kernel, experts),
        grid_spec=pltpu.PrefetchScalarGridSpec(
            num_scalar_prefetch=1,
            grid=(4,),
            in_specs=[whole()] * experts
            + [
                whole(pltpu.HBM),
                pl.BlockSpec((units, chunk), lambda i, place: (0, 4 * place[0] + i)),
                pl.BlockSpec((units, chunk), lambda i, place: (0, i)),
            ],
            out_specs=[pl.BlockSpec((tokens, 2 * units), lambda i, place: (0, 0))] * 2,
            scratch_shapes=[pltpu.VMEM((tokens, 1), F32)] + stream_scratch(rows, 4),
        ),
        out_shape=[jax.ShapeDtypeStruct((tokens, 2 * units), dtype) for dtype in (BF16, F32)],
        compiler_params=params(),
        cost_estimate=cost(4 * tokens * half_width * units, 4 * units * half_width + 2 * tokens * half_width),
        name="hidden",
    )(place, *pairs, rows, down, down_other)


def finish_kernel(experts, place, *refs):
    pairs = refs[:experts]
    keep, got, pre_own, pre_other, up_own, up_other, out, pre_grad = refs[experts:]
    tok_rows = keep.shape[0] // experts
    units = pre_own.shape[1]

    @pl.when(pl.program_id(0) == 0)
    def _():
        row, column = square(tok_rows)
        for k in range(experts):
            at = rows_of(place, k, experts, tok_rows)
            named = jnp.where((pairs[k][...] // 256) == place[1], 1.0, 0.0)
            named = jnp.sum(named, axis=0, keepdims=True)
            rank = jnp.where(row < column, upright(named, row, column), 0.0)
            rank = jnp.sum(rank, axis=0, keepdims=True).astype(jnp.int32)
            pick = jnp.where(rank == row, named, 0.0).astype(BF16)
            for side, pre in enumerate((pre_own, pre_other)):
                here = pl.ds(side * units, units)
                p = lax.dot_general(pick, pre[at, :], TN, preferred_element_type=F32)
                q = 1.0 / (1.0 + jnp.exp(-p))
                hidden = keep[at, here] + got[at, pl.ds((1 - side) * units, units)].astype(F32)
                pre_grad[at, here] = (hidden * (q * (1.0 + p * (1.0 - q)))).astype(BF16)

    value = lax.dot_general(pre_grad[:, :units], up_own[...], NT, preferred_element_type=F32)
    value += lax.dot_general(pre_grad[:, units:], up_other[...], NT, preferred_element_type=F32)
    out[...] = value


def expert_sums(place, pairs, keep, got, pre, pre_other, up, up_other):
    experts = len(pairs)
    tokens = keep.shape[0]
    units = pre.shape[1]
    half_width = up_other.shape[0]
    chunk = half_width // 4
    return pl.pallas_call(
        functools.partial(finish_kernel, experts),
        grid_spec=pltpu.PrefetchScalarGridSpec(
            num_scalar_prefetch=1,
            grid=(4,),
            in_specs=[whole()] * (experts + 4)
            + [
                pl.BlockSpec((chunk, units), lambda i, place: (4 * place[0] + i, 0)),
                pl.BlockSpec((chunk, units), lambda i, place: (i, 0)),
            ],
            out_specs=pl.BlockSpec((tokens, chunk), lambda i, place: (0, i)),
            scratch_shapes=[pltpu.VMEM((tokens, 2 * units), BF16)],
        ),
        out_shape=jax.ShapeDtypeStruct((tokens, half_width), F32),
        compiler_params=params(),
        cost_estimate=cost(4 * tokens * half_width * units, 4 * units * half_width + 4 * tokens * half_width),
        name="experts",
    )(place, *pairs, keep, got, pre, pre_other, up, up_other)


def proj_kernel(place, grads, taps, weight, inputs, send, keep, tap_out, ext, buffer, sems):
    tokens = grads.shape[0]
    tok_rows, chunk = inputs.shape
    kernel_size = taps.shape[0]
    step = pl.program_id(0)

    ext[:tokens, :] = streamed(grads, buffer, sems, step).astype(F32)
    ext[tokens:, :] = jnp.zeros((ext.shape[0] - tokens, chunk), F32)
    tap = taps[...]
    result = jnp.zeros((tokens, chunk), F32)
    for j in range(kernel_size):
        start = kernel_size - 1 - j
        result = result + tap[j : j + 1, :] * ext[start : start + tokens, :]
    window = ext[pl.ds(pl.multiple_of(place[1] * tok_rows, tok_rows), tok_rows + 8), :]
    values = inputs[...].astype(F32)
    for j in range(kernel_size):
        start = kernel_size - 1 - j
        tap_out[j : j + 1, :] = jnp.sum(values * window[start : start + tok_rows, :], axis=0, keepdims=True)
    product = lax.dot_general(result.astype(BF16), weight[...], NT, preferred_element_type=F32)

    @pl.when(step == 0)
    def _():
        keep[...] = product

    @pl.when(step > 0)
    def _():
        keep[...] += product

    @pl.when(step == pl.num_programs(0) - 1)
    def _():
        send[...] = keep[...].astype(BF16)


def proj_sums(place, grads, taps, weight, inputs):
    tokens, half_width = grads.shape
    block = weight.shape[0]
    chunk = half_width // 4

    def wide(array):
        return pl.BlockSpec((array.shape[0], chunk), lambda i: (0, i))

    return pl.pallas_call(
        proj_kernel,
        grid=(half_width // chunk,),
        in_specs=[whole(pltpu.SMEM), whole(pltpu.HBM), wide(taps), wide(weight), wide(inputs)],
        out_specs=[pl.BlockSpec((tokens, block), lambda i: (0, 0))] * 2 + [wide(taps)],
        out_shape=[
            jax.ShapeDtypeStruct((tokens, block), BF16),
            jax.ShapeDtypeStruct((tokens, block), F32),
            jax.ShapeDtypeStruct(taps.shape, F32),
        ],
        scratch_shapes=[pltpu.VMEM((tokens + 8, chunk), F32)] + stream_scratch(grads, 4),
        compiler_params=params(),
        cost_estimate=cost(
            2 * tokens * half_width * block, 2 * (block + tokens) * half_width + 6 * tokens * block
        ),
        name="projection",
    )(place, grads, taps, weight, inputs)


def combine_kernel(place, grad, sums, back_right, back_left, proj_keep, proj_got, to_right, to_left, own, total):
    half, me = place[0], place[1]
    rows, part = grad.shape[0], proj_keep.shape[1]
    experts = sums.shape[0] // rows
    blocks = (me, jnp.maximum(me - 1, 0), jnp.minimum(me + 1, experts - 1))
    places = [pl.ds(pl.multiple_of(block * rows, rows), rows) for block in blocks]
    for k, other in enumerate((grad, back_left, back_right)):
        total[k * rows : (k + 1) * rows, :] = sums[places[k], :] + other[...].astype(F32)

    @pl.when(me // 2 == half)
    def _():
        at = pl.ds(pl.multiple_of(lax.rem(me, 2) * part, part), part)
        for k in range(3):
            total[k * rows : (k + 1) * rows, at] += proj_keep[places[k], :] + proj_got[places[k], :].astype(F32)

    own[...] = total[0:rows, :]
    to_left[...] = total[rows : 2 * rows, :].astype(BF16)
    to_right[...] = total[2 * rows :, :].astype(BF16)


def combined(place, grad, *arrays):
    outs = [jax.ShapeDtypeStruct(grad.shape, dtype) for dtype in (BF16, BF16, F32)]
    return pl.pallas_call(
        combine_kernel,
        in_specs=[whole(pltpu.SMEM)] + [whole()] * (1 + len(arrays)),
        out_specs=[whole()] * 3,
        out_shape=outs,
        scratch_shapes=[pltpu.VMEM((3 * grad.shape[0], grad.shape[1]), F32)],
        compiler_params=params(),
        cost_estimate=cost(8 * grad.size, 40 * grad.size),
        name="combine",
    )(place, grad, *arrays)


def final_kernel(place, residual, far, end, out, total):
    half, me = place[0], place[1]
    experts = lax.axis_size("expert")
    part = far.shape[1]
    total[...] = residual[...].astype(F32)

    def add(source, value):
        @pl.when((source < experts) & (source // 2 == half))
        def _():
            at = pl.ds(pl.multiple_of(lax.rem(source, 2) * part, part), part)
            total[:, at] += value[...].astype(F32)

    add(lax.rem(me + 2, experts), far)
    add(jnp.where(lax.rem(me, experts - 1) == 0, experts - 1 - me, experts), end)
    out[...] = total[...].astype(BF16)


def final_sum(place, residual, far, end):
    return pl.pallas_call(
        final_kernel,
        in_specs=[whole(pltpu.SMEM)] + [whole()] * 3,
        out_specs=whole(),
        out_shape=jax.ShapeDtypeStruct(residual.shape, BF16),
        scratch_shapes=[pltpu.VMEM(residual.shape, F32)],
        compiler_params=params(),
        cost_estimate=cost(4 * residual.size, 8 * residual.size),
        name="residual",
    )(place, residual, far, end)


def moved(array, pairs):
    return lax.ppermute(array, "expert", pairs)


def swapped(array):
    return rotated(array, "mp", 1)


def together(*arrays):
    return lax.optimization_barrier(arrays)


def token_plan(
    out_grad,
    expert_ids,
    gate_codes,
    up_weight,
    down_weight,
    pre_act,
    conv_grad,
    conv_input,
    conv_weight,
    in_proj,
):
    me, half = lax.axis_index("expert"), lax.axis_index("mp")
    experts = lax.axis_size("expert")
    place = jnp.stack([half, me]).astype(jnp.int32)
    far_block, end_block = (me + 2) % experts, jnp.where(me == 0, experts - 1, 0)
    rows_own = out_grad[0]
    tok_rows, half_width = rows_own.shape
    w_down, w_up, pre = down_weight[0, 0], up_weight[0, 0], pre_act[0, 0]

    def block(array, k):
        return lax.dynamic_slice_in_dim(array, k * tok_rows, tok_rows, 0)

    all_rows = lax.all_gather(rows_own, "expert", axis=0, tiled=True)
    all_conv = lax.all_gather(conv_grad[0], "expert", axis=0, tiled=True)

    pairs = around((expert_ids[0] * 256 + gate_codes[0]).T)
    down_other = swapped(lax.dynamic_slice_in_dim(w_down, (1 - half) * half_width, half_width, 1))
    up_other = swapped(lax.dynamic_slice_in_dim(w_up, (1 - half) * half_width, half_width, 0))
    pre_other = swapped(pre)
    down_other, up_other, pre_other, all_rows, *pairs = together(down_other, up_other, pre_other, all_rows, *pairs)

    send, keep = hidden_sums(place, pairs, all_rows, w_down, down_other)
    sums = expert_sums(place, pairs, keep, swapped(send), pre, pre_other, w_up, up_other)
    back_end = moved(block(sums, end_block).astype(BF16), [(0, 1), (3, 2)])
    back = (block(sums, far_block) + back_end.astype(F32)).astype(BF16)
    back_right, back_left = moved(back, RIGHT[:2]), moved(back, LEFT[:2])
    back_right, back_left, all_conv = together(back_right, back_left, all_conv)

    proj_send, proj, tap_terms = proj_sums(place, all_conv, conv_weight[0], in_proj[0], conv_input[0])
    gather = [(e * 2 + 1 - e // 2, e * 2 + e // 2) for e in range(experts)]
    proj_got = lax.ppermute(proj_send, ("expert", "mp"), gather)
    to_right, to_left, own = combined(place, rows_own, sums, back_right, back_left, proj, proj_got)
    to_right, to_left = moved(to_right, RIGHT), moved(to_left, LEFT)

    residual = (own + to_right.astype(F32) + to_left.astype(F32)).astype(BF16)
    sections, halves = lax.axis_size("section"), lax.axis_size("mp")

    def deliver(keep, got, pairs):
        def at(s, e, m):
            return (s * experts + e) * halves + m

        moves = [(at(s, e, e // 2), at(s - 1, d, e // 2)) for s in range(1, sections) for e, d in pairs]
        return lax.ppermute((keep + got.astype(F32)).astype(BF16), ("section", "expert", "mp"), moves)

    residual = shifted(residual, "section", -1)
    far_piece = deliver(block(proj, far_block), block(proj_got, far_block), [(e, (e + 2) % experts) for e in range(experts)])
    end_piece = deliver(block(proj, end_block), block(proj_got, end_block), [(0, experts - 1), (experts - 1, 0)])
    tap_grads = doubling_sum(tap_terms, "expert")
    residual = final_sum(place, residual, far_piece, end_piece)
    return (residual[None], tap_grads[None])


def shards(*arrays):
    experts, halves = lax.axis_size("expert"), lax.axis_size("mp")
    capacity = arrays[5].shape[2] // experts
    dense = capacity == arrays[0].shape[1] and experts == 4 and halves == 2
    return (token_plan if dense else slot_plan)(*arrays)


def solution(mesh):
    in_specs = (
        P("section", "expert", "mp"),
        P("section", "expert", None),
        P("section", "expert", None),
        P("section", "expert", None, "mp"),
        P("section", "expert", "mp", None),
        P("section", "expert", None, "mp"),
        P("section", "expert", "mp"),
        P("section", "expert", "mp"),
        P("section", None, "mp"),
        P("section", "expert", "mp"),
    )
    out_specs = (P("section", "expert", "mp"), P("section", None, "mp"))
    return jax.shard_map(shards, mesh=mesh, in_specs=in_specs, out_specs=out_specs, check_vma=False)
```

time: 165 us -> 198 us (1.20)
  waiting for transfers between devices: 65 us -> 103 us
  Pallas kernels: 40.9 us -> 22.1 us
  starting transfers between devices: 48.5 us -> 32.5 us
  local copies, waits for them, and re-layouts: 6.75 us -> 22.7 us
  between operations: 1.29 us -> 14.3 us
    all_gather x0 -> x2, waiting for transfers between devices: none -> 34.7 us  [the longest x1 34.7 us: token_plan(): all_rows = lax.all_gather(rows_own, 'expert', axis=0, tiled=True)]
    pallas_call x9 -> x3, Pallas kernels: 38.3 us -> 19.3 us  [the longest x1 7.32 us: proj_sums(): pl.pallas_call(proj_kernel, grid=(half_width // chunk,), in_specs=[whole(...]
    ppermute x17 -> x5, waiting for transfers between devices: 49.9 us -> 33 us  [moved(): return lax.ppermute(array, 'expert', pairs)]
    ppermute x17 -> x5, starting transfers between devices: 32.8 us -> 16.6 us  [moved(): return lax.ppermute(array, 'expert', pairs)]
    unnamed x28 -> x38, local copies, waits for them, and re-layouts: 3.29 us -> 17.8 us
    ppermute x2, waiting for transfers between devices: 0.01 us -> 10.3 us  [doubling_sum(): lax.ppermute(array, axis, [(i, i ^ step) for i in range(size)])]
    ppermute x9 -> x7, waiting for transfers between devices: 0.34 us -> 5.31 us  [rotated(): lax.ppermute(array, axis, [(i, (i + by) % size) for i in range(size)])]
    ppermute x3 -> x1, waiting for transfers between devices: 0.01 us -> 3.25 us  [token_plan(): proj_got = lax.ppermute(proj_send, ('expert', 'mp'), gather)]
  transfers between devices with their start and end apart: 34 -> 20, of which waited for: 12 -> 10; matrix products, arithmetic and copies ran while one was open for 3% -> 4% of each run, Pallas kernels for 24% -> 6%
where the time goes in v5:
time: 198 us; the launch traced here: 197 us
  waiting for transfers between devices  103 us (52%)
  starting transfers between devices  32.5 us (16%)
  local copies, waits for them, and re-layouts  22.7 us (11%)
  Pallas kernels  22.1 us (11%)
  between operations  14.3 us (7%)
  other arithmetic  2.41 us (1%)
    all_gather x1, waiting for transfers between devices, token_plan(): all_rows = lax.all_gather(rows_own, 'expert', axis=0, tiled=True)  34.7 us
    ppermute x5, waiting for transfers between devices, moved(): return lax.ppermute(array, 'expert', pairs)  33 us
    unnamed x38, local copies, waits for them, and re-layouts  17.8 us
    ppermute x5, starting transfers between devices, moved(): return lax.ppermute(array, 'expert', pairs)  16.6 us
    ppermute x1, waiting for transfers between devices, shifted(): return lax.ppermute(array, axis, pairs)  16 us
    ppermute x2, waiting for transfers between devices, doubling_sum(): lax.ppermute(array, axis, [(i, i ^ step) for i in range(size)])  10.3 us
    ppermute x7, starting transfers between devices, rotated(): lax.ppermute(array, axis, [(i, (i + by) % size) for i in range(size)])  8.22 us
    pallas_call x1, Pallas kernels, proj_sums(): pl.pallas_call(proj_kernel, grid=(half_width // chunk,), in_specs=[whole(...  7.32 us
  transfers between devices with their start and end apart: 20, of which 10 were waited for; matrix products, arithmetic and copies ran while one was open for 4% of the time, Pallas kernels for 6%

profile of v5, /device:TPU:0, one launch (start us, length us, event | category | flops | bytes accessed | tf_op | source)
XLA Modules:
  0.0 197.2 jit_solution(8266038595472610847)
XLA Ops:
  7.2 0.7 all-gather.5.cloned.1.call-update
  8.0 3.4 %dynamic-slice_bitcast_fusion.1 = bf16[512,2048]{1,0:T(8,128)(2,1)} fusion(bf16[1,1,512,4096]{3,2,1,0:T(8,128)(2,1)} %param.14, s32[]{:T(128)S(6)} %select_n.25), kind=kLoop, calls=%fused_computation.1 | loop fusion | bytes 4194308 | tf_op jit(solution)/shard_map/dynamic_slice | solution.py:455
  11.4 0.5 collective-permute-start
  11.8 1.5 dynamic-slice_bitcast_fusion
  13.3 0.5 collective-permute-start.2
  13.8 2.6 %collective-permute-start.3 = (s32[2,128]{1,0:T(2,128)S(1)}, s32[2,128]{1,0:T(2,128)S(1)}, u32[]{:S(2)}, u32[]{:S(2)}) collective-permute-start(s32[2,128]{1,0:T(2,128)S(1)} %add_bitcast_fusion.1.refs_0_), channel_id=1, source_target_pairs={{0,2},{2,4},{4,6},{6,0},{1,3},{3,5},{5,7},{7,1},{8,10},{10,12},{12... | collective-permute-start | bytes 3080 | tf_op jit(solution)/shard_map/ppermute | solution.py:127
  16.4 2.6 %collective-permute-start.4 = (s32[2,128]{1,0:T(2,128)S(1)}, s32[2,128]{1,0:T(2,128)S(1)}, u32[]{:S(2)}, u32[]{:S(2)}) collective-permute-start(s32[2,128]{1,0:T(2,128)S(1)} %add_bitcast_fusion.1.refs_0_), channel_id=1, source_target_pairs={{0,4},{2,6},{4,0},{6,2},{1,5},{3,7},{5,1},{7,3},{8,12},{10,14},{12... | collective-permute-start | bytes 3080 | tf_op jit(solution)/shard_map/ppermute | solution.py:127
  19.1 1.0 collective-permute-done.3.refs_1_
  20.0 2.0 %collective-permute-start.5 = (s32[2,128]{1,0:T(2,128)S(1)}, s32[2,128]{1,0:T(2,128)S(1)}, u32[]{:S(2)}, u32[]{:S(2)}) collective-permute-start(s32[2,128]{1,0:T(2,128)S(1)} %add_bitcast_fusion.1.refs_0_), channel_id=1, source_target_pairs={{0,6},{2,0},{4,2},{6,4},{1,7},{3,1},{5,3},{7,5},{8,14},{10,8},{12,... | collective-permute-start | bytes 3080 | tf_op jit(solution)/shard_map/ppermute | solution.py:127
  22.1 1.5 collective-permute-done.5.refs_3_
  23.6 34.7 %all-gather.5.cloned.1.call-done = bf16[1,512,2048]{2,1,0:T(8,128)(2,1)} async-done(((bf16[1,128,2048]{2,1,0:T(8,128)(2,1)}), bf16[1,512,2048]{2,1,0:T(8,128)(2,1)}) %all-gather.5.cloned.1.call-update) | async-done | bytes 2097168 | tf_op jit(solution)/shard_map/all_gather | solution.py:451
  58.3 2.2 %copy-done.4 = bf16[1,1,512,4096]{3,2,1,0:T(8,128)(2,1)S(1)} copy-done((bf16[1,1,512,4096]{3,2,1,0:T(8,128)(2,1)S(1)}, bf16[1,1,512,4096]{3,2,1,0:T(8,128)(2,1)}, u32[]{:S(2)}) %copy-start.4) | copy-done | bytes 4194328
  60.5 1.6 copy-done.8
  62.1 7.0 %hidden.1 = (bf16[512,1024]{1,0:T(8,128)(2,1)}, f32[512,1024]{1,0:T(8,128)S(1)}) custom-call(s32[2]{0:T(128)S(1)} %pad_add_fusion.place, s32[2,128]{1,0:T(2,128)S(1)} %add_bitcast_fusion.1.refs_0_, s32[2,128]{1,0:T(2,128)S(1)} %collective-permute-done.3.refs_1_, s32[2,128]{1,0:T(2,128)S(1)} %collective-permute-done.4.refs_2_, ...), custom_call_target="tpu_custom_call" | custom-call | flops 2147483648 | bytes 6291456 | tf_op jit(solution)/shard_map/hidden/pallas_call | solution.py:217
  69.1 1.3 copy-done.5
  70.4 2.9 %collective-permute-done.6.refs_5_ = bf16[512,1024]{1,0:T(8,128)(2,1)S(1)} collective-permute-done((bf16[512,1024]{1,0:T(8,128)(2,1)}, bf16[512,1024]{1,0:T(8,128)(2,1)S(1)}, u32[]{:S(2)}, u32[]{:S(2)}) %collective-permute-start.6) | collective-permute-done | bytes 1048608 | tf_op jit(solution)/shard_map/ppermute | solution.py:127
  73.3 2.2 %copy-done.3 = bf16[1,1,4096,512]{3,2,1,0:T(8,128)(2,1)S(1)} copy-done((bf16[1,1,4096,512]{3,2,1,0:T(8,128)(2,1)S(1)}, bf16[1,1,4096,512]{3,2,1,0:T(8,128)(2,1)}, u32[]{:S(2)}) %copy-start.3) | copy-done | bytes 4194328
  75.5 1.6 copy-done.6
  77.1 1.0 copy-done.10
  78.1 1.0 copy-done.12
  79.2 5.0 %experts.1.sums = f32[512,2048]{1,0:T(8,128)S(1)} custom-call(s32[2]{0:T(128)S(1)} %pad_add_fusion.place, s32[2,128]{1,0:T(2,128)S(1)} %add_bitcast_fusion.1.refs_0_, s32[2,128]{1,0:T(2,128)S(1)} %collective-permute-done.3.refs_1_, s32[2,128]{1,0:T(2,128)S(1)} %collective-permute-done.4.refs_2_, s32[2,128]{1,0:T(2,128)S(1)} %collective-permute-done.5.refs_3_, ...), custom_call_target="tpu_custom_call" | custom-call | flops 2147483648 | bytes 8388608 | tf_op jit(solution)/shard_map/experts/pallas_call | solution.py:272
  84.2 1.9 copy-done
  86.2 1.8 collective-permute-start.7
  88.0 23.2 %collective-permute-done.7 = bf16[128,2048]{1,0:T(8,128)(2,1)S(1)} collective-permute-done((bf16[128,2048]{1,0:T(8,128)(2,1)S(1)}, bf16[128,2048]{1,0:T(8,128)(2,1)S(1)}, u32[]{:S(2)}, u32[]{:S(2)}) %collective-permute-start.7) | collective-permute-done | bytes 524320 | tf_op jit(solution)/shard_map/ppermute | solution.py:417
  111.2 1.3 add_convert_fusion.1
  112.5 4.4 %collective-permute-start.8 = (bf16[128,2048]{1,0:T(8,128)(2,1)S(1)}, bf16[128,2048]{1,0:T(8,128)(2,1)S(1)}, u32[]{:S(2)}, u32[]{:S(2)}) collective-permute-start(bf16[128,2048]{1,0:T(8,128)(2,1)S(1)} %add_convert_fusion.1), channel_id=1, source_target_pairs={{0,2},{2,4},{1,3},{3,5},{8,10},{10,12},{9,11},{11,13},{16,18},{18,... | collective-permute-start | bytes 1572872 | tf_op jit(solution)/shard_map/ppermute | solution.py:417
  116.9 0.7 collective-permute-start.9
  117.6 9.9 %collective-permute-done.8.back_right = bf16[128,2048]{1,0:T(8,128)(2,1)S(1)} collective-permute-done((bf16[128,2048]{1,0:T(8,128)(2,1)S(1)}, bf16[128,2048]{1,0:T(8,128)(2,1)S(1)}, u32[]{:S(2)}, u32[]{:S(2)}) %collective-permute-start.8) | collective-permute-done | bytes 524320 | tf_op jit(solution)/shard_map/ppermute | solution.py:417
  127.5 2.2 %copy-done.13 = bf16[1,1024,2048]{2,1,0:T(8,128)(2,1)S(1)} copy-done((bf16[1,1024,2048]{2,1,0:T(8,128)(2,1)S(1)}, bf16[1,1024,2048]{2,1,0:T(8,128)(2,1)}, u32[]{:S(2)}) %copy-start.13) | copy-done | bytes 4194328
  129.7 1.6 copy-done.14
  131.3 1.0 copy-done.15
  132.3 7.3 %projection.1 = (bf16[512,1024]{1,0:T(8,128)(2,1)S(1)}, f32[512,1024]{1,0:T(8,128)S(1)}, f32[4,2048]{1,0:T(4,128)S(1)}) custom-call(s32[2]{0:T(128)S(1)} %pad_add_fusion.place, bf16[512,2048]{1,0:T(8,128)(2,1)S(1)} %bitcast.29, f32[4,2048]{1,0:T(4,128)S(1)} %bitcast.31, bf16[1024,2048]{1,0:T(8,128)(2,1)S(1)} %bitcast.28, bf16[128,2048]{1,0:T(8,128)(2,1)S(1)} %bitcast.30), custom_call_target="tpu_custom_call" | custom-call | flops 2147483648 | bytes 9437184 | tf_op jit(solution)/shard_map/projection/pallas_call | solution.py:333
  139.7 1.3 collective-permute-start.10
  141.0 3.3 %collective-permute-done.10.proj_got = bf16[512,1024]{1,0:T(8,128)(2,1)S(1)} collective-permute-done((bf16[512,1024]{1,0:T(8,128)(2,1)S(1)}, bf16[512,1024]{1,0:T(8,128)(2,1)S(1)}, u32[]{:S(2)}, u32[]{:S(2)}) %collective-permute-start.10) | collective-permute-done | bytes 1048608 | tf_op jit(solution)/shard_map/ppermute | solution.py:469
  144.2 1.3 combine.1
  145.6 1.3 collective-permute-start.12
  146.9 8.5 %collective-permute-start.11 = (bf16[128,2048]{1,0:T(8,128)(2,1)S(1)}, bf16[128,2048]{1,0:T(8,128)(2,1)S(1)}, u32[]{:S(2)}, u32[]{:S(2)}) collective-permute-start(bf16[128,2048]{1,0:T(8,128)(2,1)S(1)} %get-tuple-element.37), channel_id=1, source_target_pairs={{0,2},{2,4},{4,6},{1,3},{3,5},{5,7},{8,10},{10,12},{12,14},{9,11},... | collective-permute-start | bytes 1572872 | tf_op jit(solution)/shard_map/ppermute | solution.py:417
  155.3 2.1 %collective-permute-start.16 = (f32[4,2048]{1,0:T(4,128)S(1)}, f32[4,2048]{1,0:T(4,128)S(1)}, u32[]{:S(2)}, u32[]{:S(2)}) collective-permute-start(f32[4,2048]{1,0:T(4,128)S(1)} %get-tuple-element.39), channel_id=1, source_target_pairs={{0,2},{2,0},{4,6},{6,4},{1,3},{3,1},{5,7},{7,5},{8,10},{10,8},{12,... | collective-permute-start | bytes 98312 | tf_op jit(solution)/shard_map/ppermute | solution.py:137
  157.4 9.8 %collective-permute-done.16 = f32[4,2048]{1,0:T(4,128)S(1)} collective-permute-done((f32[4,2048]{1,0:T(4,128)S(1)}, f32[4,2048]{1,0:T(4,128)S(1)}, u32[]{:S(2)}, u32[]{:S(2)}) %collective-permute-start.16) | collective-permute-done | bytes 32800 | tf_op jit(solution)/shard_map/ppermute | solution.py:137
  167.2 1.5 collective-permute-start.17
  168.7 0.2 add_convert_fusion
  168.9 1.3 collective-permute-start.13
  170.4 0.7 collective-permute-start.14
  171.1 0.7 collective-permute-start.15
  171.8 0.5 collective-permute-done.17
  172.3 0.6 add_bitcast_fusion
  172.9 16.0 %collective-permute-done.13.residual = bf16[128,2048]{1,0:T(8,128)(2,1)S(1)} collective-permute-done((bf16[128,2048]{1,0:T(8,128)(2,1)S(1)}, bf16[128,2048]{1,0:T(8,128)(2,1)S(1)}, u32[]{:S(2)}, u32[]{:S(2)}) %collective-permute-start.13) | collective-permute-done | bytes 524320 | tf_op jit(solution)/shard_map/ppermute | solution.py:14
  188.9 1.5 residual.1
  (47 shorter events, 0.6 us)
Async XLA Ops:
  7.2 51.1 %all-gather.5.cloned.1.call-start = ((), (), s32[]{:S(2)}) async-start(), calls=%async_computation | async-start | bytes 2621440 | tf_op jit(solution)/shard_map/all_gather | solution.py:451
  7.9 109.7 %all-gather.7.cloned.1.call-start = ((), (), s32[]{:S(2)}) async-start(), calls=%async_computation.1 | async-start | bytes 2621440 | tf_op jit(solution)/shard_map/all_gather | solution.py:452
  7.9 3.9 %copy-start.2 = (bf16[1,1,4096,512]{3,2,1,0:T(8,128)(2,1)S(1)}, bf16[1,1,4096,512]{3,2,1,0:T(8,128)(2,1)}, u32[]{:S(2)}) copy-start(bf16[1,1,4096,512]{3,2,1,0:T(8,128)(2,1)} %param.13) | copy-start | bytes 12582916
  11.3 2.0 %copy-start.9 = (bf16[1,1,512,512]{3,2,1,0:T(8,128)(2,1)S(1)}, bf16[1,1,512,512]{3,2,1,0:T(8,128)(2,1)}, u32[]{:S(2)}) copy-start(bf16[1,1,512,512]{3,2,1,0:T(8,128)(2,1)} %param.15) | copy-start | bytes 1572868
  11.3 2.4 %copy-start.17 = (s32[1,128,2]{1,2,0:T(2,128)S(1)}, s32[1,128,2]{1,2,0:T(2,128)}, u32[]{:S(2)}) copy-start(s32[1,128,2]{1,2,0:T(2,128)} %param.12) | copy-start | bytes 3076
  11.4 2.4 %copy-start.18 = (s32[1,128,2]{1,2,0:T(2,128)S(1)}, s32[1,128,2]{1,2,0:T(2,128)}, u32[]{:S(2)}) copy-start(s32[1,128,2]{1,2,0:T(2,128)} %param.11) | copy-start | bytes 3076
  11.4 12.2 %collective-permute-start = (bf16[512,2048]{1,0:T(8,128)(2,1)}, bf16[512,2048]{1,0:T(8,128)(2,1)}, u32[]{:S(2)}, u32[]{:S(2)}) collective-permute-start(bf16[512,2048]{1,0:T(8,128)(2,1)} %dynamic-slice_bitcast_fusion.1), channel_id=1, source_target_pairs={{0,1},{1,0},{2,3},{3,2},{4,5},{5,4},{6,7},{7,6},{8,9},{9,8},{10,11... | collective-permute-start | bytes 6291464 | tf_op jit(solution)/shard_map/ppermute | solution.py:127
  13.3 10.3 %collective-permute-start.1 = (bf16[2048,512]{1,0:T(8,128)(2,1)}, bf16[2048,512]{1,0:T(8,128)(2,1)S(1)}, u32[]{:S(2)}, u32[]{:S(2)}) collective-permute-start(bf16[2048,512]{1,0:T(8,128)(2,1)} %dynamic-slice_bitcast_fusion), channel_id=1, source_target_pairs={{0,1},{1,0},{2,3},{3,2},{4,5},{5,4},{6,7},{7,6},{8,9},{9,8},{10,11... | collective-permute-start | bytes 6291464 | tf_op jit(solution)/shard_map/ppermute | solution.py:127
  13.3 10.3 %collective-permute-start.2 = (bf16[512,512]{1,0:T(8,128)(2,1)S(1)}, bf16[512,512]{1,0:T(8,128)(2,1)S(1)}, u32[]{:S(2)}, u32[]{:S(2)}) collective-permute-start(bf16[512,512]{1,0:T(8,128)(2,1)S(1)} %bitcast.26), channel_id=1, source_target_pairs={{0,1},{1,0},{2,3},{3,2},{4,5},{5,4},{6,7},{7,6},{8,9},{9,8},{10,11... | collective-permute-start | bytes 1572872 | tf_op jit(solution)/shard_map/ppermute | solution.py:127
  13.8 6.2 %collective-permute-start.3 = (s32[2,128]{1,0:T(2,128)S(1)}, s32[2,128]{1,0:T(2,128)S(1)}, u32[]{:S(2)}, u32[]{:S(2)}) collective-permute-start(s32[2,128]{1,0:T(2,128)S(1)} %add_bitcast_fusion.1.refs_0_), channel_id=1, source_target_pairs={{0,2},{2,4},{4,6},{6,0},{1,3},{3,5},{5,7},{7,1},{8,10},{10,12},{12... | collective-permute-start | bytes 3080 | tf_op jit(solution)/shard_map/ppermute | solution.py:127
  16.4 5.7 %collective-permute-start.4 = (s32[2,128]{1,0:T(2,128)S(1)}, s32[2,128]{1,0:T(2,128)S(1)}, u32[]{:S(2)}, u32[]{:S(2)}) collective-permute-start(s32[2,128]{1,0:T(2,128)S(1)} %add_bitcast_fusion.1.refs_0_), channel_id=1, source_target_pairs={{0,4},{2,6},{4,0},{6,2},{1,5},{3,7},{5,1},{7,3},{8,12},{10,14},{12... | collective-permute-start | bytes 3080 | tf_op jit(solution)/shard_map/ppermute | solution.py:127
  20.0 3.6 %collective-permute-start.5 = (s32[2,128]{1,0:T(2,128)S(1)}, s32[2,128]{1,0:T(2,128)S(1)}, u32[]{:S(2)}, u32[]{:S(2)}) collective-permute-start(s32[2,128]{1,0:T(2,128)S(1)} %add_bitcast_fusion.1.refs_0_), channel_id=1, source_target_pairs={{0,6},{2,0},{4,2},{6,4},{1,7},{3,1},{5,3},{7,5},{8,14},{10,8},{12,... | collective-permute-start | bytes 3080 | tf_op jit(solution)/shard_map/ppermute | solution.py:127
  23.6 45.4 %copy-start.11 = (bf16[512,512]{1,0:T(8,128)(2,1)}, bf16[512,512]{1,0:T(8,128)(2,1)S(1)}, u32[]{:S(2)}) copy-start(bf16[512,512]{1,0:T(8,128)(2,1)S(1)} %collective-permute-done.2.refs_7_) | copy-start | bytes 1572868
  58.3 2.2 %copy-start.4 = (bf16[1,1,512,4096]{3,2,1,0:T(8,128)(2,1)S(1)}, bf16[1,1,512,4096]{3,2,1,0:T(8,128)(2,1)}, u32[]{:S(2)}) copy-start(bf16[1,1,512,4096]{3,2,1,0:T(8,128)(2,1)} %param.14) | copy-start | bytes 12582916
  60.5 1.6 copy-start.8
  69.0 1.3 copy-start.5
  70.4 2.9 %collective-permute-start.6 = (bf16[512,1024]{1,0:T(8,128)(2,1)}, bf16[512,1024]{1,0:T(8,128)(2,1)S(1)}, u32[]{:S(2)}, u32[]{:S(2)}) collective-permute-start(bf16[512,1024]{1,0:T(8,128)(2,1)} %get-tuple-element.28), channel_id=1, source_target_pairs={{0,1},{1,0},{2,3},{3,2},{4,5},{5,4},{6,7},{7,6},{8,9},{9,8},{10,11... | collective-permute-start | bytes 3145736 | tf_op jit(solution)/shard_map/ppermute | solution.py:127
  73.3 2.2 %copy-start.3 = (bf16[1,1,4096,512]{3,2,1,0:T(8,128)(2,1)S(1)}, bf16[1,1,4096,512]{3,2,1,0:T(8,128)(2,1)}, u32[]{:S(2)}) copy-start(bf16[1,1,4096,512]{3,2,1,0:T(8,128)(2,1)} %param.13) | copy-start | bytes 12582916
  75.5 1.6 copy-start.6
  77.1 1.0 copy-start.10
  78.1 1.0 copy-start.12
  84.2 2.0 copy-start
  86.1 41.4 %copy-start.16 = (f32[1,4,2048]{2,1,0:T(4,128)S(1)}, f32[1,4,2048]{2,1,0:T(4,128)}, u32[]{:S(2)}) copy-start(f32[1,4,2048]{2,1,0:T(4,128)} %param.18) | copy-start | bytes 98308
  86.2 25.0 %collective-permute-start.7 = (bf16[128,2048]{1,0:T(8,128)(2,1)S(1)}, bf16[128,2048]{1,0:T(8,128)(2,1)S(1)}, u32[]{:S(2)}, u32[]{:S(2)}) collective-permute-start(bf16[128,2048]{1,0:T(8,128)(2,1)S(1)} %dynamic-slice_convert_fusion), channel_id=1, source_target_pairs={{0,2},{6,4},{1,3},{7,5},{8,10},{14,12},{9,11},{15,13},{16,18},{22,... | collective-permute-start | bytes 1572872 | tf_op jit(solution)/shard_map/ppermute | solution.py:417
  112.5 15.0 %collective-permute-start.8 = (bf16[128,2048]{1,0:T(8,128)(2,1)S(1)}, bf16[128,2048]{1,0:T(8,128)(2,1)S(1)}, u32[]{:S(2)}, u32[]{:S(2)}) collective-permute-start(bf16[128,2048]{1,0:T(8,128)(2,1)S(1)} %add_convert_fusion.1), channel_id=1, source_target_pairs={{0,2},{2,4},{1,3},{3,5},{8,10},{10,12},{9,11},{11,13},{16,18},{18,... | collective-permute-start | bytes 1572872 | tf_op jit(solution)/shard_map/ppermute | solution.py:417
  116.9 10.6 %collective-permute-start.9 = (bf16[128,2048]{1,0:T(8,128)(2,1)S(1)}, bf16[128,2048]{1,0:T(8,128)(2,1)S(1)}, u32[]{:S(2)}, u32[]{:S(2)}) collective-permute-start(bf16[128,2048]{1,0:T(8,128)(2,1)S(1)} %add_convert_fusion.1), channel_id=1, source_target_pairs={{6,4},{4,2},{7,5},{5,3},{14,12},{12,10},{15,13},{13,11},{22,20},{2... | collective-permute-start | bytes 1572872 | tf_op jit(solution)/shard_map/ppermute | solution.py:417
  127.5 2.2 %copy-start.13 = (bf16[1,1024,2048]{2,1,0:T(8,128)(2,1)S(1)}, bf16[1,1024,2048]{2,1,0:T(8,128)(2,1)}, u32[]{:S(2)}) copy-start(bf16[1,1024,2048]{2,1,0:T(8,128)(2,1)} %param.19) | copy-start | bytes 12582916
  129.7 1.6 copy-start.14
  131.3 1.0 copy-start.15
  132.3 11.9 %copy-start.1 = (f32[512,2048]{1,0:T(8,128)S(1)}, f32[512,2048]{1,0:T(8,128)}, u32[]{:S(2)}) copy-start(f32[512,2048]{1,0:T(8,128)} %copy-done) | copy-start | bytes 12582916
  132.3 11.9 %copy-start.7 = (bf16[1,128,2048]{2,1,0:T(8,128)(2,1)S(1)}, bf16[1,128,2048]{2,1,0:T(8,128)(2,1)}, u32[]{:S(2)}) copy-start(bf16[1,128,2048]{2,1,0:T(8,128)(2,1)} %param.10) | copy-start | bytes 1572868
  139.7 4.6 %collective-permute-start.10 = (bf16[512,1024]{1,0:T(8,128)(2,1)S(1)}, bf16[512,1024]{1,0:T(8,128)(2,1)S(1)}, u32[]{:S(2)}, u32[]{:S(2)}) collective-permute-start(bf16[512,1024]{1,0:T(8,128)(2,1)S(1)} %get-tuple-element.35), channel_id=1, source_target_pairs={{1,0},{3,2},{4,5},{6,7},{9,8},{11,10},{12,13},{14,15},{17,16},{19,... | collective-permute-start | bytes 3145736 | tf_op jit(solution)/shard_map/ppermute | solution.py:469
  145.6 23.1 %collective-permute-start.12 = (bf16[128,2048]{1,0:T(8,128)(2,1)S(1)}, bf16[128,2048]{1,0:T(8,128)(2,1)S(1)}, u32[]{:S(2)}, u32[]{:S(2)}) collective-permute-start(bf16[128,2048]{1,0:T(8,128)(2,1)S(1)} %get-tuple-element.38), channel_id=1, source_target_pairs={{6,4},{4,2},{2,0},{7,5},{5,3},{3,1},{14,12},{12,10},{10,8},{15,13}... | collective-permute-start | bytes 1572872 | tf_op jit(solution)/shard_map/ppermute | solution.py:417
  146.9 21.8 %collective-permute-start.11 = (bf16[128,2048]{1,0:T(8,128)(2,1)S(1)}, bf16[128,2048]{1,0:T(8,128)(2,1)S(1)}, u32[]{:S(2)}, u32[]{:S(2)}) collective-permute-start(bf16[128,2048]{1,0:T(8,128)(2,1)S(1)} %get-tuple-element.37), channel_id=1, source_target_pairs={{0,2},{2,4},{4,6},{1,3},{3,5},{5,7},{8,10},{10,12},{12,14},{9,11},... | collective-permute-start | bytes 1572872 | tf_op jit(solution)/shard_map/ppermute | solution.py:417
  155.3 11.8 %collective-permute-start.16 = (f32[4,2048]{1,0:T(4,128)S(1)}, f32[4,2048]{1,0:T(4,128)S(1)}, u32[]{:S(2)}, u32[]{:S(2)}) collective-permute-start(f32[4,2048]{1,0:T(4,128)S(1)} %get-tuple-element.39), channel_id=1, source_target_pairs={{0,2},{2,0},{4,6},{6,4},{1,3},{3,1},{5,7},{7,5},{8,10},{10,8},{12,... | collective-permute-start | bytes 98312 | tf_op jit(solution)/shard_map/ppermute | solution.py:137
  167.2 5.1 %collective-permute-start.17 = (f32[4,2048]{1,0:T(4,128)S(1)}, f32[4,2048]{1,0:T(4,128)S(1)}, u32[]{:S(2)}, u32[]{:S(2)}) collective-permute-start(f32[4,2048]{1,0:T(4,128)S(1)} %add.60), channel_id=1, source_target_pairs={{0,4},{2,6},{4,0},{6,2},{1,5},{3,7},{5,1},{7,3},{8,12},{10,14},{12... | collective-permute-start | bytes 98312 | tf_op jit(solution)/shard_map/ppermute | solution.py:137
  168.9 20.0 %collective-permute-start.13 = (bf16[128,2048]{1,0:T(8,128)(2,1)S(1)}, bf16[128,2048]{1,0:T(8,128)(2,1)S(1)}, u32[]{:S(2)}, u32[]{:S(2)}) collective-permute-start(bf16[128,2048]{1,0:T(8,128)(2,1)S(1)} %add_convert_fusion), channel_id=1, source_target_pairs={{8,0},{16,8},{24,16},{9,1},{17,9},{25,17},{10,2},{18,10},{26,18},{... | collective-permute-start | bytes 1572872 | tf_op jit(solution)/shard_map/ppermute | solution.py:14
  170.4 2.5 %collective-permute-start.14 = (bf16[128,1024]{1,0:T(8,128)(2,1)S(1)}, bf16[128,1024]{1,0:T(8,128)(2,1)S(1)}, u32[]{:S(2)}, u32[]{:S(2)}) collective-permute-start(bf16[128,1024]{1,0:T(8,128)(2,1)S(1)} %get-tuple-element.41), channel_id=1, source_target_pairs={{8,4},{10,6},{13,1},{15,3},{16,12},{18,14},{21,9},{23,11},{24,20},... | collective-permute-start | bytes 786440 | tf_op jit(solution)/shard_map/ppermute | solution.py:481
  171.1 1.8 collective-permute-start.15
Sparse Core Ops, SparseCore 0:
  9.6 48.6 all-gather.4
  59.9 52.2 all-gather.6

commit v6 on v4

--- a/solution.py
+++ b/solution.py
@@ -113,6 +113,7 @@
 F32, BF16 = jnp.float32, jnp.bfloat16
 VMEM_LIMIT = 14 * 1024 * 1024
 HEAD = 16
+LANES = 128
 RIGHT = [(0, 1), (1, 2), (2, 3)]
 LEFT = [(3, 2), (2, 1), (1, 0)]
 NT = (((1,), (1,)), ((), ()))
@@ -153,12 +154,15 @@
     return row, lax.broadcasted_iota(jnp.int32, (size, size), 1)
 
 
-def upright(line, row, column):
-    return jnp.sum(jnp.where(row == column, line, 0.0), axis=1, keepdims=True)
+def routing(columns, me):
+    values = columns[...].astype(F32)
+    named = jnp.where(values[:, 0:2] == me.astype(F32), 1.0, 0.0)
+    gate = jnp.sum(named * values[:, 2:4], axis=1, keepdims=True) / 256.0
+    return jnp.sum(named, axis=1, keepdims=True), gate
 
 
 def hidden_kernel(count, place, *refs):
-    pairs, rows = refs[:count], refs[count : 2 * count]
+    routes, rows = refs[:count], refs[count : 2 * count]
     down_own, down_other, send, keep, gates, scaled = refs[2 * count :]
     tok_rows = rows[0].shape[0]
     units = down_own.shape[0]
@@ -166,12 +170,8 @@
 
     @pl.when(step == 0)
     def _():
-        row, column = square(tok_rows)
         for k in range(count):
-            pair = pairs[k][...]
-            named = (pair // 256) == place[1]
-            code = jnp.sum(jnp.where(named, (pair % 256).astype(F32), 0.0), axis=0, keepdims=True)
-            gates[k * tok_rows : (k + 1) * tok_rows, :] = upright(code, row, column) / 256.0
+            gates[k * tok_rows : (k + 1) * tok_rows, :] = routing(routes[k], place[1])[1]
         keep[...] = jnp.zeros_like(keep)
 
     for k in range(count):
@@ -185,10 +185,15 @@
         send[...] = keep[...].astype(BF16)
 
 
-def hidden_sums(place, pairs, rows, down, down_other):
+def route_columns(rows):
+    tok_rows, width = rows.shape
+    return pl.BlockSpec((tok_rows, LANES), lambda i, place: (0, width // LANES - 1))
+
+
+def hidden_sums(place, rows, down, down_other):
     count = len(rows)
-    tok_rows, half_width = rows[0].shape
-    units = down.shape[0]
+    tok_rows = rows[0].shape[0]
+    units, half_width = down_other.shape
     tokens = count * tok_rows
     chunk = half_width // 4
     return pl.pallas_call(
@@ -196,7 +201,7 @@
         grid_spec=pltpu.PrefetchScalarGridSpec(
             num_scalar_prefetch=1,
             grid=(4,),
-            in_specs=[whole()] * count
+            in_specs=[route_columns(rows[0])] * count
             + [pl.BlockSpec((tok_rows, chunk), lambda i, place: (0, i))] * count
             + [
                 pl.BlockSpec((units, chunk), lambda i, place: (0, 4 * place[0] + i)),
@@ -209,11 +214,11 @@
         compiler_params=params(),
         cost_estimate=cost(4 * tokens * half_width * units, 4 * units * half_width + 2 * tokens * half_width),
         name="hidden",
-    )(place, *pairs, *rows, down, down_other)
+    )(place, *rows, *rows, down, down_other)
 
 
 def finish_kernel(count, place, *refs):
-    pairs = refs[:count]
+    routes = refs[:count]
     keep, got, pre_own, pre_other, up_own, up_other, out, pre_grad = refs[count:]
     tok_rows = keep.shape[0] // count
     units = pre_own.shape[1]
@@ -223,10 +228,9 @@
         row, column = square(tok_rows)
         for k in range(count):
             at = pl.ds(k * tok_rows, tok_rows)
-            named = jnp.where((pairs[k][...] // 256) == place[1], 1.0, 0.0)
-            named = jnp.sum(named, axis=0, keepdims=True)
-            rank = jnp.where(row < column, upright(named, row, column), 0.0)
-            rank = jnp.sum(rank, axis=0, keepdims=True).astype(jnp.int32)
+            named, _ = routing(routes[k], place[1])
+            rank = jnp.sum(jnp.where(row < column, named, 0.0), axis=0, keepdims=True).astype(jnp.int32)
+            named = jnp.sum(jnp.where(row == column, named, 0.0), axis=0, keepdims=True)
             pick = jnp.where(rank == row, named, 0.0).astype(BF16)
             slots = pl.ds(pl.multiple_of(place[2 + k] * tok_rows, tok_rows), tok_rows)
             for side, pre in enumerate((pre_own, pre_other)):
@@ -241,8 +245,8 @@
     out[...] = value.astype(out.dtype)
 
 
-def expert_sums(place, pairs, keep, got, pre, pre_other, up, up_other, dtype):
-    count = len(pairs)
+def expert_sums(place, rows, keep, got, pre, pre_other, up, up_other, dtype):
+    count = len(rows)
     tokens = keep.shape[0]
     units = pre.shape[1]
     half_width = up_other.shape[0]
@@ -252,7 +256,8 @@
         grid_spec=pltpu.PrefetchScalarGridSpec(
             num_scalar_prefetch=1,
             grid=(4,),
-            in_specs=[whole()] * (count + 4)
+            in_specs=[route_columns(rows[0])] * count
+            + [whole()] * 4
             + [
                 pl.BlockSpec((chunk, units), lambda i, place: (4 * place[0] + i, 0)),
                 pl.BlockSpec((chunk, units), lambda i, place: (i, 0)),
@@ -264,7 +269,7 @@
         compiler_params=params(),
         cost_estimate=cost(4 * tokens * half_width * units, 4 * units * half_width + 4 * tokens * half_width),
         name="experts",
-    )(place, *pairs, keep, got, pre, pre_other, up, up_other)
+    )(place, *rows, keep, got, pre, pre_other, up, up_other)
 
 
 def proj_kernel(count, with_taps, place, *refs):
@@ -445,47 +450,42 @@
     w_down, w_up, pre = down_weight[0, 0], up_weight[0, 0], pre_act[0, 0]
     taps, w_proj = conv_weight[0], in_proj[0]
 
-    pairs = around((expert_ids[0] * 256 + gate_codes[0]).T)
+    routes = jnp.concatenate([expert_ids[0], gate_codes[0]], axis=1).astype(BF16)
+    rows_own = jnp.concatenate([rows_own, jnp.pad(routes, ((0, 0), (0, LANES - routes.shape[1])))], axis=1)
     down_send = lax.dynamic_slice_in_dim(w_down, (1 - half) * half_width, half_width, 1)
-    up_send = lax.dynamic_slice_in_dim(w_up, (1 - half) * half_width, half_width, 0)
-    rows_own, down_send, *pairs = together(rows_own, down_send, *pairs)
-
     rows_left, rows_right = moved(rows_own, RIGHT), moved(rows_own, LEFT)
     down_other = swapped(down_send)
-    rows_left, rows_right, down_other, up_send, pre_send = together(rows_left, rows_right, down_other, up_send, pre)
-
-    def hidden(where, routes, rows):
-        send, keep = hidden_sums(where, routes, rows, w_down, down_other)
+    up_send = lax.dynamic_slice_in_dim(w_up, (1 - half) * half_width, half_width, 0)
+    rows_left, rows_right, down_other, up_send = together(rows_left, rows_right, down_other, up_send)
+
+    def hidden(where, rows):
+        send, keep = hidden_sums(where, rows, w_down, down_other)
         return keep, swapped(send)
 
-    def finish(where, routes, keep, got, dtype):
-        return expert_sums(where, routes, keep, got, pre, pre_other, w_up, up_other, dtype)
-
-    near_pairs = [pairs[0], pairs[1], pairs[3]]
+    def finish(where, rows, keep, got, dtype):
+        return expert_sums(where, rows, keep, got, pre, pre_other, w_up, up_other, dtype)
+
+    near_rows = [rows_own, rows_left, rows_right]
     from_left, from_right = moved(rows_left, RIGHT[1:]), moved(rows_right, LEFT[1:])
-    up_other, pre_other = swapped(up_send), swapped(pre_send)
-    near_keep, near_got = hidden(near, near_pairs, [rows_own, rows_left, rows_right])
-    from_left, from_right, near_keep, up_other, pre_other = together(
-        from_left, from_right, near_keep, up_other, pre_other
-    )
+    near_keep, near_got = hidden(near, near_rows)
+    from_left, from_right, near_keep, up_send, pre_send = together(from_left, from_right, near_keep, up_send, pre)
 
     far, end = place(far_block), place(end_block)
-    end_pairs = [jnp.where(me == 0, pairs[1], pairs[3])]
     rows_far = jnp.where(me >= 2, from_left, from_right)
     rows_end = moved(rows_far, [(2, 3), (1, 0)])
-    near_sums = finish(near, near_pairs, near_keep, near_got, F32)
-    far_keep, far_got = hidden(far, [pairs[2]], [rows_far])
-    rows_end, near_sums, far_keep, conv_own = together(rows_end, near_sums, far_keep, conv_own)
-
-    conv_left, conv_right = moved(conv_own, RIGHT), moved(conv_own, LEFT)
-    end_keep, end_got = hidden(end, end_pairs, [rows_end])
-    far_sums = finish(far, [pairs[2]], far_keep, far_got, F32)
-    end_sums = finish(end, end_pairs, end_keep, end_got, BF16)
+    up_other, pre_other = swapped(up_send), swapped(pre_send)
+    far_keep, far_got = hidden(far, [rows_far])
     next_head = moved(conv_own[:HEAD], [(2, 0), (3, 1)])
     last_head = moved(conv_own[:HEAD], [(3, 0)])
-    conv_left, conv_right, end_sums, far_sums, next_head, last_head = together(
-        conv_left, conv_right, end_sums, far_sums, next_head, last_head
-    )
+    rows_end, far_keep, up_other, pre_other, next_head, last_head, conv_own = together(
+        rows_end, far_keep, up_other, pre_other, next_head, last_head, conv_own
+    )
+
+    conv_left, conv_right = moved(conv_own, RIGHT), moved(conv_own, LEFT)
+    end_keep, end_got = hidden(end, [rows_end])
+    far_sums = finish(far, [rows_far], far_keep, far_got, F32)
+    end_sums = finish(end, [rows_end], end_keep, end_got, BF16)
+    conv_left, conv_right, end_sums, far_sums = together(conv_left, conv_right, end_sums, far_sums)
 
     from_left, from_right = moved(conv_left, RIGHT[1:]), moved(conv_right, LEFT[1:])
     back_end = moved(end_sums, [(0, 1), (3, 2)])
@@ -498,30 +498,35 @@
     near_proj, near_proj_got, tap_terms = proj(
         near, [conv_own, conv_left, conv_right], [conv_right, conv_own, next_head], conv_input[0]
     )
-    from_left, from_right, back_end, near_proj, conv_left = together(
-        from_left, from_right, back_end, near_proj, conv_left
+    from_left, from_right, near_proj, conv_left, near_keep = together(
+        from_left, from_right, near_proj, conv_left, near_keep
     )
 
     conv_far = jnp.where(me >= 2, from_left, from_right)
+    conv_far, back_end = together(conv_far, back_end)
     conv_end = moved(conv_far, [(2, 3), (1, 0)])
     back = (far_sums + back_end.astype(F32)).astype(BF16)
     back_right, back_left = moved(back, RIGHT[:2]), moved(back, LEFT[:2])
     far_head = jnp.where(me >= 2, conv_left[:HEAD], last_head)
+    near_sums = finish(near, near_rows, near_keep, near_got, F32)
+    near_sums, conv_far = together(near_sums, conv_far)
     far_proj, far_proj_got = proj(far, [conv_far], [far_head])
-    conv_end, back_right, back_left, far_proj = together(conv_end, back_right, back_left, far_proj)
-
-    to_right, to_left, own = combined(near, rows_own, near_sums, back_right, back_left, near_proj, near_proj_got)
+    conv_end, back_right, back_left, far_proj, near_sums = together(
+        conv_end, back_right, back_left, far_proj, near_sums
+    )
+
+    to_right, to_left, own = combined(near, out_grad[0], near_sums, back_right, back_left, near_proj, near_proj_got)
     to_right, to_left, conv_end = together(to_right, to_left, conv_end)
     to_right, to_left = moved(to_right, RIGHT), moved(to_left, LEFT)
     end_proj, end_proj_got = proj(end, [conv_end], [conv_far])
     to_right, to_left, end_proj = together(to_right, to_left, end_proj)
 
     residual = (own + to_right.astype(F32) + to_left.astype(F32)).astype(BF16)
-    sections, halves = lax.axis_size("section"), lax.axis_size("mp")
+    sections, cores = lax.axis_size("section"), lax.axis_size("mp")
 
     def deliver(keep, got, pairs):
         def at(s, e, m):
-            return (s * experts + e) * halves + m
+            return (s * experts + e) * cores + m
 
         moves = [(at(s, e, e // 2), at(s - 1, d, e // 2)) for s in range(1, sections) for e, d in pairs]
         return lax.ppermute((keep + got.astype(F32)).astype(BF16), ("section", "expert", "mp"), moves)

time: 165 us -> 168 us (1.018)
  local copies, waits for them, and re-layouts: 6.75 us -> 11.6 us
  waiting for transfers between devices: 65 us -> 60.4 us
  Pallas kernels: 40.9 us -> 45.4 us
  starting transfers between devices: 48.5 us -> 44.6 us
    ppermute x9 -> x6, starting transfers between devices: 7.75 us -> 1.67 us  [rotated(): lax.ppermute(array, axis, [(i, (i + by) % size) for i in range(size)])]
    ppermute x17, waiting for transfers between devices: 49.9 us -> 44.2 us  [moved(): return lax.ppermute(array, 'expert', pairs)]
    ppermute x2, starting transfers between devices: 1.44 us -> 6.22 us  [doubling_sum(): lax.ppermute(array, axis, [(i, i ^ step) for i in range(size)])]
    pallas_call x3, Pallas kernels: 10.9 us -> 14.7 us  [hidden_sums(): pl.pallas_call(functools.partial(hidden_kernel, count), grid_spec=pltpu.P...]
    ppermute x17, starting transfers between devices: 32.8 us -> 30.2 us  [moved(): return lax.ppermute(array, 'expert', pairs)]
    dynamic_slice x1, local copies, waits for them, and re-layouts: 1.49 us -> 3.24 us  [token_plan(): lax.dynamic_slice_in_dim(w_up, (1 - half) * half_width, half_width, 0)]
    unnamed x28 -> x34, local copies, waits for them, and re-layouts: 3.29 us -> 4.26 us
  transfers between devices with their start and end apart: 34 -> 31, of which waited for: 12 -> 9; matrix products, arithmetic and copies ran while one was open for 3% -> 4% of each run, Pallas kernels for 24% -> 26%
where the time goes in v6:
time: 168 us; the launch traced here: 167 us
  waiting for transfers between devices  60.4 us (36%)
  Pallas kernels  45.4 us (27%)
  starting transfers between devices  44.6 us (27%)
  local copies, waits for them, and re-layouts  11.6 us (7%)
  other arithmetic  3.29 us (2%)
    ppermute x17, waiting for transfers between devices, moved(): return lax.ppermute(array, 'expert', pairs)  44.2 us
    ppermute x17, starting transfers between devices, moved(): return lax.ppermute(array, 'expert', pairs)  30.2 us
    ppermute x1, waiting for transfers between devices, shifted(): return lax.ppermute(array, axis, pairs)  16.1 us
    pallas_call x3, Pallas kernels, expert_sums(): pl.pallas_call(functools.partial(finish_kernel, count), grid_spec=pltpu.P...  15.8 us
    pallas_call x3, Pallas kernels, hidden_sums(): pl.pallas_call(functools.partial(hidden_kernel, count), grid_spec=pltpu.P...  14.7 us
    pallas_call x3, Pallas kernels, proj_sums(): pl.pallas_call(functools.partial(proj_kernel, count, with_taps), grid=(ha...  12.1 us
    ppermute x2, starting transfers between devices, doubling_sum(): lax.ppermute(array, axis, [(i, i ^ step) for i in range(size)])  6.22 us
    unnamed x34, local copies, waits for them, and re-layouts  4.26 us
  transfers between devices with their start and end apart: 31, of which 9 were waited for; matrix products, arithmetic and copies ran while one was open for 4% of the time, Pallas kernels for 26%

profile of v6, /device:TPU:0, one launch (start us, length us, event | category | flops | bytes accessed | tf_op | source)
XLA Modules:
  0.0 166.6 jit_solution(8321055701607438123)
XLA Ops:
  0.7 3.3 %dynamic-slice_bitcast_fusion.1 = bf16[512,2048]{1,0:T(8,128)(2,1)} fusion(bf16[1,1,512,4096]{3,2,1,0:T(8,128)(2,1)} %param.14, s32[]{:T(128)S(6)} %select_n.41), kind=kLoop, calls=%fused_computation.1 | loop fusion | bytes 4194308 | tf_op jit(solution)/shard_map/dynamic_slice | solution.py:455
  4.6 1.3 collective-permute-start.1
  5.9 5.1 %collective-permute-start = (bf16[128,2176]{1,0:T(8,128)(2,1)S(1)}, bf16[128,2176]{1,0:T(8,128)(2,1)S(1)}, u32[]{:S(2)}, u32[]{:S(2)}) collective-permute-start(bf16[128,2176]{1,0:T(8,128)(2,1)S(1)} %fusion.1.refs_0_.refs_3_), channel_id=1, source_target_pairs={{0,2},{2,4},{4,6},{1,3},{3,5},{5,7},{8,10},{10,12},{12,14},{9,11},... | collective-permute-start | bytes 1671176 | tf_op jit(solution)/shard_map/ppermute | solution.py:417
  11.2 3.2 %dynamic-slice_bitcast_fusion = bf16[2048,512]{1,0:T(8,128)(2,1)} fusion(bf16[1,1,4096,512]{3,2,1,0:T(8,128)(2,1)} %param.13, s32[]{:T(128)S(6)} %select_n.41), kind=kLoop, calls=%fused_computation | loop fusion | bytes 4194308 | tf_op jit(solution)/shard_map/dynamic_slice | solution.py:458
  14.4 8.0 %collective-permute-done.1.refs_2_.refs_5_ = bf16[128,2176]{1,0:T(8,128)(2,1)S(1)} collective-permute-done((bf16[128,2176]{1,0:T(8,128)(2,1)S(1)}, bf16[128,2176]{1,0:T(8,128)(2,1)S(1)}, u32[]{:S(2)}, u32[]{:S(2)}) %collective-permute-start.1) | collective-permute-done | bytes 557088 | tf_op jit(solution)/shard_map/ppermute | solution.py:417
  22.4 1.2 collective-permute-done.refs_1_.refs_4_
  24.3 1.3 collective-permute-start.4
  25.6 5.5 %hidden.3 = (bf16[384,1024]{1,0:T(8,128)(2,1)S(1)}, f32[384,1024]{1,0:T(8,128)S(1)}) custom-call(s32[5]{0:T(128)S(1)} %stack.36.place, bf16[128,2176]{1,0:T(8,128)(2,1)S(1)} %fusion.1.refs_0_.refs_3_, bf16[128,2176]{1,0:T(8,128)(2,1)S(1)} %collective-permute-done.refs_1_.refs_4_, bf16[128,2176]{1,0:T(8,128)(2,1)S(1)} %collective-permute-done.1.refs_2_.refs_5_, ...), custom_call_target="tpu_custom_call" | custom-call | flops 12884901888 | bytes 46137344 | tf_op jit(solution)/shard_map/hidden/pallas_call | solution.py:199
  31.1 1.2 copy-done.11
  32.3 11.3 %collective-permute-done.4 = bf16[128,2176]{1,0:T(8,128)(2,1)S(1)} collective-permute-done((bf16[128,2176]{1,0:T(8,128)(2,1)S(1)}, bf16[128,2176]{1,0:T(8,128)(2,1)S(1)}, u32[]{:S(2)}, u32[]{:S(2)}) %collective-permute-start.4) | collective-permute-done | bytes 557088 | tf_op jit(solution)/shard_map/ppermute | solution.py:417
  43.5 0.8 copy-done.14
  45.0 1.3 collective-permute-start.9
  46.3 1.3 collective-permute-start.8
  48.1 1.1 broadcast_select_fusion.refs_0_.refs_1_
  49.3 1.3 collective-permute-start.5
  50.7 2.2 %copy-done.2 = bf16[1,1,512,4096]{3,2,1,0:T(8,128)(2,1)S(1)} copy-done((bf16[1,1,512,4096]{3,2,1,0:T(8,128)(2,1)S(1)}, bf16[1,1,512,4096]{3,2,1,0:T(8,128)(2,1)}, u32[]{:S(2)}) %copy-start.2) | copy-done | bytes 4194328
  52.9 4.7 %hidden.4 = (bf16[128,1024]{1,0:T(8,128)(2,1)S(1)}, f32[128,1024]{1,0:T(8,128)S(1)}) custom-call(s32[3]{0:T(128)S(1)} %pad_add_fusion.place, bf16[128,2176]{1,0:T(8,128)(2,1)S(1)} %broadcast_select_fusion.refs_0_.refs_1_, bf16[128,2176]{1,0:T(8,128)(2,1)S(1)} %broadcast_select_fusion.refs_0_.refs_1_, bf16[512,4096]{1,0:T(8,128)(2,1)S(1)} %bitcast.30, ...), custom_call_target="tpu_custom_call" | custom-call | flops 4294967296 | bytes 37748736 | tf_op jit(solution)/shard_map/hidden/pallas_call | solution.py:199
  58.2 8.6 %collective-permute-done.5.refs_0_.refs_1_ = bf16[128,2176]{1,0:T(8,128)(2,1)} collective-permute-done((bf16[128,2176]{1,0:T(8,128)(2,1)S(1)}, bf16[128,2176]{1,0:T(8,128)(2,1)}, u32[]{:S(2)}, u32[]{:S(2)}) %collective-permute-start.5) | collective-permute-done | bytes 557088 | tf_op jit(solution)/shard_map/ppermute | solution.py:417
  66.8 1.6 collective-permute-start.11
  68.4 4.6 %collective-permute-start.10 = (bf16[128,2048]{1,0:T(8,128)(2,1)S(1)}, bf16[128,2048]{1,0:T(8,128)(2,1)S(1)}, u32[]{:S(2)}, u32[]{:S(2)}) collective-permute-start(bf16[128,2048]{1,0:T(8,128)(2,1)S(1)} %bitcast.36), channel_id=1, source_target_pairs={{0,2},{2,4},{4,6},{1,3},{3,5},{5,7},{8,10},{10,12},{12,14},{9,11},... | collective-permute-start | bytes 1572872 | tf_op jit(solution)/shard_map/ppermute | solution.py:417
  73.0 4.6 %hidden.5 = (bf16[128,1024]{1,0:T(8,128)(2,1)S(1)}, f32[128,1024]{1,0:T(8,128)S(1)}) custom-call(s32[3]{0:T(128)S(1)} %pad_add_fusion.2.place, bf16[128,2176]{1,0:T(8,128)(2,1)} %collective-permute-done.5.refs_0_.refs_1_, bf16[128,2176]{1,0:T(8,128)(2,1)} %collective-permute-done.5.refs_0_.refs_1_, bf16[512,4096]{1,0:T(8,128)(2,1)S(1)} %bitcast.31, ...), custom_call_target="tpu_custom_call" | custom-call | flops 4294967296 | bytes 37748736 | tf_op jit(solution)/shard_map/hidden/pallas_call | solution.py:199
  77.7 4.9 %experts.4 = f32[128,2048]{1,0:T(8,128)S(1)} custom-call(s32[3]{0:T(128)S(1)} %pad_add_fusion.place, bf16[128,2176]{1,0:T(8,128)(2,1)S(1)} %broadcast_select_fusion.refs_0_.refs_1_, f32[128,1024]{1,0:T(8,128)S(1)} %get-tuple-element.74.refs_1_, bf16[128,1024]{1,0:T(8,128)(2,1)S(1)} %collective-permute-done.13.refs_2_, bf16[512,512]{1,0:T(8,128)(2,1)S(1)} %bitcast.44, ...), custom_call_target="tpu_custom_call" | custom-call | flops 4294967296 | bytes 41943040 | tf_op jit(solution)/shard_map/experts/pallas_call | solution.py:254
  82.6 5.2 %experts.3 = bf16[128,2048]{1,0:T(8,128)(2,1)S(1)} custom-call(s32[3]{0:T(128)S(1)} %pad_add_fusion.2.place, bf16[128,2176]{1,0:T(8,128)(2,1)} %collective-permute-done.5.refs_0_.refs_1_, f32[128,1024]{1,0:T(8,128)S(1)} %get-tuple-element.70.refs_1_, bf16[128,1024]{1,0:T(8,128)(2,1)S(1)} %collective-permute-done.12.refs_2_, bf16[512,512]{1,0:T(8,128)(2,1)S(1)} %bitcast.45, ...), custom_call_target="tpu_custom_call" | custom-call | flops 4294967296 | bytes 41943040 | tf_op jit(solution)/shard_map/experts/pallas_call | solution.py:254
  87.8 3.0 %collective-permute-start.16 = (bf16[128,2048]{1,0:T(8,128)(2,1)S(1)}, bf16[128,2048]{1,0:T(8,128)(2,1)S(1)}, u32[]{:S(2)}, u32[]{:S(2)}) collective-permute-start(bf16[128,2048]{1,0:T(8,128)(2,1)S(1)} %experts.3), channel_id=1, source_target_pairs={{0,2},{6,4},{1,3},{7,5},{8,10},{14,12},{9,11},{15,13},{16,18},{22,... | collective-permute-start | bytes 1572872 | tf_op jit(solution)/shard_map/ppermute | solution.py:417
  90.8 1.3 collective-permute-start.15
  92.8 6.1 %projection.3 = (bf16[384,1024]{1,0:T(8,128)(2,1)S(1)}, f32[384,1024]{1,0:T(8,128)S(1)}, f32[4,2048]{1,0:T(4,128)S(1)}) custom-call(s32[5]{0:T(128)S(1)} %stack.36.place, bf16[128,2048]{1,0:T(8,128)(2,1)S(1)} %bitcast.37, bf16[128,2048]{1,0:T(8,128)(2,1)S(1)} %collective-permute-done.10.refs_1_, ...), custom_call_target="tpu_custom_call" | custom-call | flops 12884901888 | bytes 65011712 | tf_op jit(solution)/shard_map/projection/pallas_call | solution.py:336
  99.0 3.3 %collective-permute-start.29 = (f32[4,2048]{1,0:T(4,128)S(1)}, f32[4,2048]{1,0:T(4,128)S(1)}, u32[]{:S(2)}, u32[]{:S(2)}) collective-permute-start(f32[4,2048]{1,0:T(4,128)S(1)} %get-tuple-element.113), channel_id=1, source_target_pairs={{0,2},{2,0},{4,6},{6,4},{1,3},{3,1},{5,7},{7,5},{8,10},{10,8},{12,... | collective-permute-start | bytes 98312 | tf_op jit(solution)/shard_map/ppermute | solution.py:139
  102.3 4.7 %collective-permute-done.15 = bf16[128,2048]{1,0:T(8,128)(2,1)S(1)} collective-permute-done((bf16[128,2048]{1,0:T(8,128)(2,1)S(1)}, bf16[128,2048]{1,0:T(8,128)(2,1)S(1)}, u32[]{:S(2)}, u32[]{:S(2)}) %collective-permute-start.15) | collective-permute-done | bytes 524320 | tf_op jit(solution)/shard_map/ppermute | solution.py:417
  107.1 1.3 collective-permute-start.21
  108.5 0.7 collective-permute-start.19
  109.2 2.1 %collective-permute-start.18 = (bf16[128,2048]{1,0:T(8,128)(2,1)S(1)}, bf16[128,2048]{1,0:T(8,128)(2,1)S(1)}, u32[]{:S(2)}, u32[]{:S(2)}) collective-permute-start(bf16[128,2048]{1,0:T(8,128)(2,1)S(1)} %add_convert_fusion.1), channel_id=1, source_target_pairs={{0,2},{2,4},{1,3},{3,5},{8,10},{10,12},{9,11},{11,13},{16,18},{18,... | collective-permute-start | bytes 1572872 | tf_op jit(solution)/shard_map/ppermute | solution.py:417
  111.3 1.3 collective-permute-start.17
  112.7 5.8 %experts.5.sums = f32[384,2048]{1,0:T(8,128)S(1)} custom-call(s32[5]{0:T(128)S(1)} %stack.36.place, bf16[128,2176]{1,0:T(8,128)(2,1)S(1)} %fusion.1.refs_0_.refs_3_, bf16[128,2176]{1,0:T(8,128)(2,1)S(1)} %copy-done.7, bf16[128,2176]{1,0:T(8,128)(2,1)S(1)} %collective-permute-done.1.refs_2_.refs_5_, f32[384,1024]{1,0:T(8,128)S(1)} %copy-done.12, ...), custom_call_target="tpu_custom_call" | custom-call | flops 12884901888 | bytes 58720256 | tf_op jit(solution)/shard_map/experts/pallas_call | solution.py:254
  118.5 0.9 slice_select_fusion.refs_1_
  119.3 3.0 %projection.4 = (bf16[128,1024]{1,0:T(8,128)(2,1)S(1)}, f32[128,1024]{1,0:T(8,128)S(1)}) custom-call(s32[3]{0:T(128)S(1)} %pad_add_fusion.place, bf16[128,2048]{1,0:T(8,128)(2,1)S(1)} %broadcast_select_fusion.1.refs_0_.refs_1_, bf16[16,2048]{1,0:T(8,128)(2,1)S(1)} %slice_select_fusion.refs_1_, f32[4,2048]{1,0:T(4,128)S(1)} %bitcast.48, ...), custom_call_target="tpu_custom_call" | custom-call | flops 4294967296 | bytes 44040192 | tf_op jit(solution)/shard_map/projection/pallas_call | solution.py:336
  122.3 1.3 collective-permute-start.25
  123.7 2.9 %collective-permute-start.30 = (f32[4,2048]{1,0:T(4,128)S(1)}, f32[4,2048]{1,0:T(4,128)S(1)}, u32[]{:S(2)}, u32[]{:S(2)}) collective-permute-start(f32[4,2048]{1,0:T(4,128)S(1)} %add.47), channel_id=1, source_target_pairs={{0,4},{2,6},{4,0},{6,2},{1,5},{3,7},{5,1},{7,3},{8,12},{10,14},{12... | collective-permute-start | bytes 98312 | tf_op jit(solution)/shard_map/ppermute | solution.py:139
  126.6 1.4 collective-permute-done.17.refs_0_
  128.0 1.3 combine.1
  129.3 1.5 collective-permute-start.22
  130.8 1.3 collective-permute-start.23
  132.8 3.0 %projection.5 = (bf16[128,1024]{1,0:T(8,128)(2,1)S(1)}, f32[128,1024]{1,0:T(8,128)S(1)}) custom-call(s32[3]{0:T(128)S(1)} %pad_add_fusion.2.place, bf16[128,2048]{1,0:T(8,128)(2,1)S(1)} %collective-permute-done.17.refs_0_, bf16[128,2048]{1,0:T(8,128)(2,1)S(1)} %broadcast_select_fusion.1.refs_0_.refs_1_, f32[4,2048]{1,0:T(4,128)S(1)} %bitcast.49, ...), custom_call_target="tpu_custom_call" | custom-call | flops 4294967296 | bytes 44040192 | tf_op jit(solution)/shard_map/projection/pallas_call | solution.py:336
  135.8 1.3 collective-permute-start.27
  137.1 4.8 %collective-permute-done.22 = bf16[128,2048]{1,0:T(8,128)(2,1)S(1)} collective-permute-done((bf16[128,2048]{1,0:T(8,128)(2,1)S(1)}, bf16[128,2048]{1,0:T(8,128)(2,1)S(1)}, u32[]{:S(2)}, u32[]{:S(2)}) %collective-permute-start.22) | collective-permute-done | bytes 524320 | tf_op jit(solution)/shard_map/ppermute | solution.py:417
  142.0 4.1 %collective-permute-done.23 = bf16[128,2048]{1,0:T(8,128)(2,1)S(1)} collective-permute-done((bf16[128,2048]{1,0:T(8,128)(2,1)S(1)}, bf16[128,2048]{1,0:T(8,128)(2,1)S(1)}, u32[]{:S(2)}, u32[]{:S(2)}) %collective-permute-start.23) | collective-permute-done | bytes 524320 | tf_op jit(solution)/shard_map/ppermute | solution.py:417
  146.3 1.3 collective-permute-start.24
  149.0 16.1 %collective-permute-done.24.residual = bf16[128,2048]{1,0:T(8,128)(2,1)S(1)} collective-permute-done((bf16[128,2048]{1,0:T(8,128)(2,1)S(1)}, bf16[128,2048]{1,0:T(8,128)(2,1)S(1)}, u32[]{:S(2)}, u32[]{:S(2)}) %collective-permute-start.24) | collective-permute-done | bytes 524320 | tf_op jit(solution)/shard_map/ppermute | solution.py:14
  165.1 1.5 residual.1
  (78 shorter events, 6.7 us)
Async XLA Ops:
  0.6 3.8 %copy-start.15 = (s32[1,128,2]{1,2,0:T(2,128)S(1)}, s32[1,128,2]{1,2,0:T(2,128)}, u32[]{:S(2)}) copy-start(s32[1,128,2]{1,2,0:T(2,128)} %param.12) | copy-start | bytes 3076
  0.6 3.7 %copy-start.16 = (s32[1,128,2]{1,2,0:T(2,128)S(1)}, s32[1,128,2]{1,2,0:T(2,128)}, u32[]{:S(2)}) copy-start(s32[1,128,2]{1,2,0:T(2,128)} %param.11) | copy-start | bytes 3076
  0.7 3.9 %copy-start = (bf16[1,128,2048]{2,1,0:T(8,128)(2,1)S(1)}, bf16[1,128,2048]{2,1,0:T(8,128)(2,1)}, u32[]{:S(2)}) copy-start(bf16[1,128,2048]{2,1,0:T(8,128)(2,1)} %param.10) | copy-start | bytes 1572868
  3.9 19.6 %collective-permute-start.2 = (bf16[512,2048]{1,0:T(8,128)(2,1)}, bf16[512,2048]{1,0:T(8,128)(2,1)}, u32[]{:S(2)}, u32[]{:S(2)}) collective-permute-start(bf16[512,2048]{1,0:T(8,128)(2,1)} %dynamic-slice_bitcast_fusion.1), channel_id=1, source_target_pairs={{0,1},{1,0},{2,3},{3,2},{4,5},{5,4},{6,7},{7,6},{8,9},{9,8},{10,11... | collective-permute-start | bytes 6291464 | tf_op jit(solution)/shard_map/ppermute | solution.py:129
  4.6 17.8 %collective-permute-start.1 = (bf16[128,2176]{1,0:T(8,128)(2,1)S(1)}, bf16[128,2176]{1,0:T(8,128)(2,1)S(1)}, u32[]{:S(2)}, u32[]{:S(2)}) collective-permute-start(bf16[128,2176]{1,0:T(8,128)(2,1)S(1)} %fusion.1.refs_0_.refs_3_), channel_id=1, source_target_pairs={{6,4},{4,2},{2,0},{7,5},{5,3},{3,1},{14,12},{12,10},{10,8},{15,13}... | collective-permute-start | bytes 1671176 | tf_op jit(solution)/shard_map/ppermute | solution.py:417
  5.9 17.7 %collective-permute-start = (bf16[128,2176]{1,0:T(8,128)(2,1)S(1)}, bf16[128,2176]{1,0:T(8,128)(2,1)S(1)}, u32[]{:S(2)}, u32[]{:S(2)}) collective-permute-start(bf16[128,2176]{1,0:T(8,128)(2,1)S(1)} %fusion.1.refs_0_.refs_3_), channel_id=1, source_target_pairs={{0,2},{2,4},{4,6},{1,3},{3,5},{5,7},{8,10},{10,12},{12,14},{9,11},... | collective-permute-start | bytes 1671176 | tf_op jit(solution)/shard_map/ppermute | solution.py:417
  11.2 14.4 %copy-start.1 = (bf16[1,1,512,4096]{3,2,1,0:T(8,128)(2,1)S(1)}, bf16[1,1,512,4096]{3,2,1,0:T(8,128)(2,1)}, u32[]{:S(2)}) copy-start(bf16[1,1,512,4096]{3,2,1,0:T(8,128)(2,1)} %param.14) | copy-start | bytes 12582916
  23.6 7.5 %copy-start.6 = (bf16[128,2176]{1,0:T(8,128)(2,1)}, bf16[128,2176]{1,0:T(8,128)(2,1)S(1)}, u32[]{:S(2)}) copy-start(bf16[128,2176]{1,0:T(8,128)(2,1)S(1)} %collective-permute-done.refs_1_.refs_4_) | copy-start | bytes 1671172
  23.6 8.7 %collective-permute-start.3 = (bf16[128,2176]{1,0:T(8,128)(2,1)S(1)}, bf16[128,2176]{1,0:T(8,128)(2,1)S(1)}, u32[]{:S(2)}, u32[]{:S(2)}) collective-permute-start(bf16[128,2176]{1,0:T(8,128)(2,1)S(1)} %collective-permute-done.refs_1_.refs_4_), channel_id=1, source_target_pairs={{2,4},{4,6},{3,5},{5,7},{10,12},{12,14},{11,13},{13,15},{18,20},{2... | collective-permute-start | bytes 1671176 | tf_op jit(solution)/shard_map/ppermute | solution.py:417
  24.3 19.3 %collective-permute-start.4 = (bf16[128,2176]{1,0:T(8,128)(2,1)S(1)}, bf16[128,2176]{1,0:T(8,128)(2,1)S(1)}, u32[]{:S(2)}, u32[]{:S(2)}) collective-permute-start(bf16[128,2176]{1,0:T(8,128)(2,1)S(1)} %collective-permute-done.1.refs_2_.refs_5_), channel_id=1, source_target_pairs={{4,2},{2,0},{5,3},{3,1},{12,10},{10,8},{13,11},{11,9},{20,18},{18,... | collective-permute-start | bytes 1671176 | tf_op jit(solution)/shard_map/ppermute | solution.py:417
  25.6 18.8 %copy-start.4 = (bf16[1,128,2048]{2,1,0:T(8,128)(2,1)S(1)}, bf16[1,128,2048]{2,1,0:T(8,128)(2,1)}, u32[]{:S(2)}) copy-start(bf16[1,128,2048]{2,1,0:T(8,128)(2,1)} %param.16) | copy-start | bytes 1572868
  31.1 1.2 copy-start.11
  32.3 11.3 %copy-start.13 = (bf16[128,2176]{1,0:T(8,128)(2,1)}, bf16[128,2176]{1,0:T(8,128)(2,1)S(1)}, u32[]{:S(2)}) copy-start(bf16[128,2176]{1,0:T(8,128)(2,1)S(1)} %collective-permute-done.3) | copy-start | bytes 1671172
  43.5 0.8 copy-start.14
  44.3 22.5 %collective-permute-start.6 = (bf16[2048,512]{1,0:T(8,128)(2,1)}, bf16[2048,512]{1,0:T(8,128)(2,1)}, u32[]{:S(2)}, u32[]{:S(2)}) collective-permute-start(bf16[2048,512]{1,0:T(8,128)(2,1)} %dynamic-slice_bitcast_fusion), channel_id=1, source_target_pairs={{0,1},{1,0},{2,3},{3,2},{4,5},{5,4},{6,7},{7,6},{8,9},{9,8},{10,11... | collective-permute-start | bytes 6291464 | tf_op jit(solution)/shard_map/ppermute | solution.py:129
  45.0 12.6 %collective-permute-start.9 = (bf16[16,2048]{1,0:T(8,128)(2,1)}, bf16[16,2048]{1,0:T(8,128)(2,1)}, u32[]{:S(2)}, u32[]{:S(2)}) collective-permute-start(bf16[16,2048]{1,0:T(8,128)(2,1)} %slice_bitcast_fusion), channel_id=1, source_target_pairs={{6,0},{7,1},{14,8},{15,9},{22,16},{23,17},{30,24},{31,25}} | collective-permute-start | bytes 196616 | tf_op jit(solution)/shard_map/ppermute | solution.py:417
  46.3 11.4 %collective-permute-start.8 = (bf16[16,2048]{1,0:T(8,128)(2,1)}, bf16[16,2048]{1,0:T(8,128)(2,1)}, u32[]{:S(2)}, u32[]{:S(2)}) collective-permute-start(bf16[16,2048]{1,0:T(8,128)(2,1)} %slice_bitcast_fusion), channel_id=1, source_target_pairs={{4,0},{6,2},{5,1},{7,3},{12,8},{14,10},{13,9},{15,11},{20,16},{22,... | collective-permute-start | bytes 196616 | tf_op jit(solution)/shard_map/ppermute | solution.py:417
  47.6 10.6 %collective-permute-start.7 = (bf16[512,512]{1,0:T(8,128)(2,1)}, bf16[512,512]{1,0:T(8,128)(2,1)}, u32[]{:S(2)}, u32[]{:S(2)}) collective-permute-start(bf16[512,512]{1,0:T(8,128)(2,1)} %bitcast.43), channel_id=1, source_target_pairs={{0,1},{1,0},{2,3},{3,2},{4,5},{5,4},{6,7},{7,6},{8,9},{9,8},{10,11... | collective-permute-start | bytes 1572872 | tf_op jit(solution)/shard_map/ppermute | solution.py:129
  49.3 17.6 %collective-permute-start.5 = (bf16[128,2176]{1,0:T(8,128)(2,1)S(1)}, bf16[128,2176]{1,0:T(8,128)(2,1)}, u32[]{:S(2)}, u32[]{:S(2)}) collective-permute-start(bf16[128,2176]{1,0:T(8,128)(2,1)S(1)} %broadcast_select_fusion.refs_0_.refs_1_), channel_id=1, source_target_pairs={{4,6},{2,0},{5,7},{3,1},{12,14},{10,8},{13,15},{11,9},{20,22},{18,... | collective-permute-start | bytes 1671176 | tf_op jit(solution)/shard_map/ppermute | solution.py:417
  50.7 2.2 %copy-start.2 = (bf16[1,1,512,4096]{3,2,1,0:T(8,128)(2,1)S(1)}, bf16[1,1,512,4096]{3,2,1,0:T(8,128)(2,1)}, u32[]{:S(2)}) copy-start(bf16[1,1,512,4096]{3,2,1,0:T(8,128)(2,1)} %param.14) | copy-start | bytes 12582916
  57.6 53.8 %collective-permute-start.20 = (bf16[384,1024]{1,0:T(8,128)(2,1)S(1)}, bf16[384,1024]{1,0:T(8,128)(2,1)S(1)}, u32[]{:S(2)}, u32[]{:S(2)}) collective-permute-start(bf16[384,1024]{1,0:T(8,128)(2,1)S(1)} %get-tuple-element.88), channel_id=1, source_target_pairs={{0,1},{1,0},{2,3},{3,2},{4,5},{5,4},{6,7},{7,6},{8,9},{9,8},{10,11... | collective-permute-start | bytes 2359304 | tf_op jit(solution)/shard_map/ppermute | solution.py:129
  57.7 20.0 %collective-permute-start.13 = (bf16[128,1024]{1,0:T(8,128)(2,1)S(1)}, bf16[128,1024]{1,0:T(8,128)(2,1)S(1)}, u32[]{:S(2)}, u32[]{:S(2)}) collective-permute-start(bf16[128,1024]{1,0:T(8,128)(2,1)S(1)} %get-tuple-element.75), channel_id=1, source_target_pairs={{0,1},{1,0},{2,3},{3,2},{4,5},{5,4},{6,7},{7,6},{8,9},{9,8},{10,11... | collective-permute-start | bytes 786440 | tf_op jit(solution)/shard_map/ppermute | solution.py:129
  66.8 10.8 %copy-start.3 = (bf16[1,1,4096,512]{3,2,1,0:T(8,128)(2,1)S(1)}, bf16[1,1,4096,512]{3,2,1,0:T(8,128)(2,1)}, u32[]{:S(2)}) copy-start(bf16[1,1,4096,512]{3,2,1,0:T(8,128)(2,1)} %param.13) | copy-start | bytes 12582916
  66.8 10.8 %copy-start.9 = (bf16[1,1,512,512]{3,2,1,0:T(8,128)(2,1)S(1)}, bf16[1,1,512,512]{3,2,1,0:T(8,128)(2,1)}, u32[]{:S(2)}) copy-start(bf16[1,1,512,512]{3,2,1,0:T(8,128)(2,1)} %param.15) | copy-start | bytes 1572868
  66.8 21.0 %collective-permute-start.11 = (bf16[128,2048]{1,0:T(8,128)(2,1)S(1)}, bf16[128,2048]{1,0:T(8,128)(2,1)S(1)}, u32[]{:S(2)}, u32[]{:S(2)}) collective-permute-start(bf16[128,2048]{1,0:T(8,128)(2,1)S(1)} %bitcast.35), channel_id=1, source_target_pairs={{6,4},{4,2},{2,0},{7,5},{5,3},{3,1},{14,12},{12,10},{10,8},{15,13}... | collective-permute-start | bytes 1572872 | tf_op jit(solution)/shard_map/ppermute | solution.py:417
  68.4 19.4 %collective-permute-start.10 = (bf16[128,2048]{1,0:T(8,128)(2,1)S(1)}, bf16[128,2048]{1,0:T(8,128)(2,1)S(1)}, u32[]{:S(2)}, u32[]{:S(2)}) collective-permute-start(bf16[128,2048]{1,0:T(8,128)(2,1)S(1)} %bitcast.36), channel_id=1, source_target_pairs={{0,2},{2,4},{4,6},{1,3},{3,5},{5,7},{8,10},{10,12},{12,14},{9,11},... | collective-permute-start | bytes 1572872 | tf_op jit(solution)/shard_map/ppermute | solution.py:417
  77.6 5.0 %collective-permute-start.12 = (bf16[128,1024]{1,0:T(8,128)(2,1)S(1)}, bf16[128,1024]{1,0:T(8,128)(2,1)S(1)}, u32[]{:S(2)}, u32[]{:S(2)}) collective-permute-start(bf16[128,1024]{1,0:T(8,128)(2,1)S(1)} %get-tuple-element.71), channel_id=1, source_target_pairs={{0,1},{1,0},{2,3},{3,2},{4,5},{5,4},{6,7},{7,6},{8,9},{9,8},{10,11... | collective-permute-start | bytes 786440 | tf_op jit(solution)/shard_map/ppermute | solution.py:129
  82.6 10.2 %copy-start.5 = (bf16[1,1024,2048]{2,1,0:T(8,128)(2,1)S(1)}, bf16[1,1024,2048]{2,1,0:T(8,128)(2,1)}, u32[]{:S(2)}) copy-start(bf16[1,1024,2048]{2,1,0:T(8,128)(2,1)} %param.19) | copy-start | bytes 12582916
  82.6 10.2 %copy-start.8 = (bf16[1,128,2048]{2,1,0:T(8,128)(2,1)S(1)}, bf16[1,128,2048]{2,1,0:T(8,128)(2,1)}, u32[]{:S(2)}) copy-start(bf16[1,128,2048]{2,1,0:T(8,128)(2,1)} %param.17) | copy-start | bytes 1572868
  82.6 10.2 %copy-start.10 = (f32[1,4,2048]{2,1,0:T(4,128)S(1)}, f32[1,4,2048]{2,1,0:T(4,128)}, u32[]{:S(2)}) copy-start(f32[1,4,2048]{2,1,0:T(4,128)} %param.18) | copy-start | bytes 98308
  87.8 20.6 %collective-permute-start.16 = (bf16[128,2048]{1,0:T(8,128)(2,1)S(1)}, bf16[128,2048]{1,0:T(8,128)(2,1)S(1)}, u32[]{:S(2)}, u32[]{:S(2)}) collective-permute-start(bf16[128,2048]{1,0:T(8,128)(2,1)S(1)} %experts.3), channel_id=1, source_target_pairs={{0,2},{6,4},{1,3},{7,5},{8,10},{14,12},{9,11},{15,13},{16,18},{22,... | collective-permute-start | bytes 1572872 | tf_op jit(solution)/shard_map/ppermute | solution.py:417
  90.8 16.3 %collective-permute-start.15 = (bf16[128,2048]{1,0:T(8,128)(2,1)S(1)}, bf16[128,2048]{1,0:T(8,128)(2,1)S(1)}, u32[]{:S(2)}, u32[]{:S(2)}) collective-permute-start(bf16[128,2048]{1,0:T(8,128)(2,1)S(1)} %collective-permute-done.11.refs_2_.refs_3_), channel_id=1, source_target_pairs={{4,2},{2,0},{5,3},{3,1},{12,10},{10,8},{13,11},{11,9},{20,18},{18,... | collective-permute-start | bytes 1572872 | tf_op jit(solution)/shard_map/ppermute | solution.py:417
  92.1 16.3 %collective-permute-start.14 = (bf16[128,2048]{1,0:T(8,128)(2,1)S(1)}, bf16[128,2048]{1,0:T(8,128)(2,1)S(1)}, u32[]{:S(2)}, u32[]{:S(2)}) collective-permute-start(bf16[128,2048]{1,0:T(8,128)(2,1)S(1)} %collective-permute-done.10.refs_1_), channel_id=1, source_target_pairs={{2,4},{4,6},{3,5},{5,7},{10,12},{12,14},{11,13},{13,15},{18,20},{2... | collective-permute-start | bytes 1572872 | tf_op jit(solution)/shard_map/ppermute | solution.py:417
  99.0 13.7 %copy-start.7 = (bf16[128,2176]{1,0:T(8,128)(2,1)S(1)}, bf16[128,2176]{1,0:T(8,128)(2,1)}, u32[]{:S(2)}) copy-start(bf16[128,2176]{1,0:T(8,128)(2,1)} %copy-done.6) | copy-start | bytes 1671172
  99.0 13.7 %copy-start.12 = (f32[384,1024]{1,0:T(8,128)S(1)}, f32[384,1024]{1,0:T(8,128)}, u32[]{:S(2)}) copy-start(f32[384,1024]{1,0:T(8,128)} %copy-done.11) | copy-start | bytes 4718596
  99.0 23.3 %collective-permute-start.29 = (f32[4,2048]{1,0:T(4,128)S(1)}, f32[4,2048]{1,0:T(4,128)S(1)}, u32[]{:S(2)}, u32[]{:S(2)}) collective-permute-start(f32[4,2048]{1,0:T(4,128)S(1)} %get-tuple-element.113), channel_id=1, source_target_pairs={{0,2},{2,0},{4,6},{6,4},{1,3},{3,1},{5,7},{7,5},{8,10},{10,8},{12,... | collective-permute-start | bytes 98312 | tf_op jit(solution)/shard_map/ppermute | solution.py:139
  107.1 20.9 %collective-permute-start.21 = (bf16[384,1024]{1,0:T(8,128)(2,1)S(1)}, bf16[384,1024]{1,0:T(8,128)(2,1)S(1)}, u32[]{:S(2)}, u32[]{:S(2)}) collective-permute-start(bf16[384,1024]{1,0:T(8,128)(2,1)S(1)} %get-tuple-element.98), channel_id=1, source_target_pairs={{1,0},{3,2},{4,5},{6,7},{9,8},{11,10},{12,13},{14,15},{17,16},{19,... | collective-permute-start | bytes 2359304 | tf_op jit(solution)/shard_map/ppermute | solution.py:496
  108.5 15.1 %collective-permute-start.19 = (bf16[128,2048]{1,0:T(8,128)(2,1)S(1)}, bf16[128,2048]{1,0:T(8,128)(2,1)S(1)}, u32[]{:S(2)}, u32[]{:S(2)}) collective-permute-start(bf16[128,2048]{1,0:T(8,128)(2,1)S(1)} %add_convert_fusion.1), channel_id=1, source_target_pairs={{6,4},{4,2},{7,5},{5,3},{14,12},{12,10},{15,13},{13,11},{22,20},{2... | collective-permute-start | bytes 1572872 | tf_op jit(solution)/shard_map/ppermute | solution.py:417
  109.2 17.3 %collective-permute-start.18 = (bf16[128,2048]{1,0:T(8,128)(2,1)S(1)}, bf16[128,2048]{1,0:T(8,128)(2,1)S(1)}, u32[]{:S(2)}, u32[]{:S(2)}) collective-permute-start(bf16[128,2048]{1,0:T(8,128)(2,1)S(1)} %add_convert_fusion.1), channel_id=1, source_target_pairs={{0,2},{2,4},{1,3},{3,5},{8,10},{10,12},{9,11},{11,13},{16,18},{18,... | collective-permute-start | bytes 1572872 | tf_op jit(solution)/shard_map/ppermute | solution.py:417
  111.3 16.6 %collective-permute-start.17 = (bf16[128,2048]{1,0:T(8,128)(2,1)S(1)}, bf16[128,2048]{1,0:T(8,128)(2,1)S(1)}, u32[]{:S(2)}, u32[]{:S(2)}) collective-permute-start(bf16[128,2048]{1,0:T(8,128)(2,1)S(1)} %broadcast_select_fusion.1.refs_0_.refs_1_), channel_id=1, source_target_pairs={{4,6},{2,0},{5,7},{3,1},{12,14},{10,8},{13,15},{11,9},{20,22},{18,... | collective-permute-start | bytes 1572872 | tf_op jit(solution)/shard_map/ppermute | solution.py:417
  122.3 9.7 %collective-permute-start.25 = (bf16[128,1024]{1,0:T(8,128)(2,1)S(1)}, bf16[128,1024]{1,0:T(8,128)(2,1)S(1)}, u32[]{:S(2)}, u32[]{:S(2)}) collective-permute-start(bf16[128,1024]{1,0:T(8,128)(2,1)S(1)} %get-tuple-element.110), channel_id=1, source_target_pairs={{1,0},{3,2},{4,5},{6,7},{9,8},{11,10},{12,13},{14,15},{17,16},{19,... | collective-permute-start | bytes 786440 | tf_op jit(solution)/shard_map/ppermute | solution.py:496
  123.7 24.7 %collective-permute-start.30 = (f32[4,2048]{1,0:T(4,128)S(1)}, f32[4,2048]{1,0:T(4,128)S(1)}, u32[]{:S(2)}, u32[]{:S(2)}) collective-permute-start(f32[4,2048]{1,0:T(4,128)S(1)} %add.47), channel_id=1, source_target_pairs={{0,4},{2,6},{4,0},{6,2},{1,5},{3,7},{5,1},{7,3},{8,12},{10,14},{12... | collective-permute-start | bytes 98312 | tf_op jit(solution)/shard_map/ppermute | solution.py:139
  129.3 12.7 %collective-permute-start.22 = (bf16[128,2048]{1,0:T(8,128)(2,1)S(1)}, bf16[128,2048]{1,0:T(8,128)(2,1)S(1)}, u32[]{:S(2)}, u32[]{:S(2)}) collective-permute-start(bf16[128,2048]{1,0:T(8,128)(2,1)S(1)} %get-tuple-element.103), channel_id=1, source_target_pairs={{0,2},{2,4},{4,6},{1,3},{3,5},{5,7},{8,10},{10,12},{12,14},{9,11},... | collective-permute-start | bytes 1572872 | tf_op jit(solution)/shard_map/ppermute | solution.py:417
  130.8 15.3 %collective-permute-start.23 = (bf16[128,2048]{1,0:T(8,128)(2,1)S(1)}, bf16[128,2048]{1,0:T(8,128)(2,1)S(1)}, u32[]{:S(2)}, u32[]{:S(2)}) collective-permute-start(bf16[128,2048]{1,0:T(8,128)(2,1)S(1)} %get-tuple-element.104), channel_id=1, source_target_pairs={{6,4},{4,2},{2,0},{7,5},{5,3},{3,1},{14,12},{12,10},{10,8},{15,13}... | collective-permute-start | bytes 1572872 | tf_op jit(solution)/shard_map/ppermute | solution.py:417
  132.1 16.8 %collective-permute-start.26 = (bf16[128,1024]{1,0:T(8,128)(2,1)S(1)}, bf16[128,1024]{1,0:T(8,128)(2,1)S(1)}, u32[]{:S(2)}, u32[]{:S(2)}) collective-permute-start(bf16[128,1024]{1,0:T(8,128)(2,1)S(1)} %add_convert_fusion.3), channel_id=1, source_target_pairs={{8,4},{10,6},{13,1},{15,3},{16,12},{18,14},{21,9},{23,11},{24,20},... | collective-permute-start | bytes 786440 | tf_op jit(solution)/shard_map/ppermute | solution.py:532
  135.8 11.8 %collective-permute-start.27 = (bf16[128,1024]{1,0:T(8,128)(2,1)S(1)}, bf16[128,1024]{1,0:T(8,128)(2,1)S(1)}, u32[]{:S(2)}, u32[]{:S(2)}) collective-permute-start(bf16[128,1024]{1,0:T(8,128)(2,1)S(1)} %get-tuple-element.112), channel_id=1, source_target_pairs={{1,0},{3,2},{4,5},{6,7},{9,8},{11,10},{12,13},{14,15},{17,16},{19,... | collective-permute-start | bytes 786440 | tf_op jit(solution)/shard_map/ppermute | solution.py:496
  146.3 18.8 %collective-permute-start.24 = (bf16[128,2048]{1,0:T(8,128)(2,1)S(1)}, bf16[128,2048]{1,0:T(8,128)(2,1)S(1)}, u32[]{:S(2)}, u32[]{:S(2)}) collective-permute-start(bf16[128,2048]{1,0:T(8,128)(2,1)S(1)} %add_convert_fusion), channel_id=1, source_target_pairs={{8,0},{16,8},{24,16},{9,1},{17,9},{25,17},{10,2},{18,10},{26,18},{... | collective-permute-start | bytes 1572872 | tf_op jit(solution)/shard_map/ppermute | solution.py:14
  147.7 1.3 collective-permute-start.28

commit v7 on v6

--- a/solution.py
+++ b/solution.py
@@ -220,7 +220,7 @@
 def finish_kernel(count, place, *refs):
     routes = refs[:count]
     keep, got, pre_own, pre_other, up_own, up_other, out, pre_grad = refs[count:]
-    tok_rows = keep.shape[0] // count
+    tok_rows = pre_grad.shape[0] // count
     units = pre_own.shape[1]
 
     @pl.when(pl.program_id(0) == 0)
@@ -247,7 +247,7 @@
 
 def expert_sums(place, rows, keep, got, pre, pre_other, up, up_other, dtype):
     count = len(rows)
-    tokens = keep.shape[0]
+    tokens = count * rows[0].shape[0]
     units = pre.shape[1]
     half_width = up_other.shape[0]
     chunk = half_width // 4
@@ -452,40 +452,40 @@
 
     routes = jnp.concatenate([expert_ids[0], gate_codes[0]], axis=1).astype(BF16)
     rows_own = jnp.concatenate([rows_own, jnp.pad(routes, ((0, 0), (0, LANES - routes.shape[1])))], axis=1)
+    rows_left, rows_right = moved(rows_own, RIGHT), moved(rows_own, LEFT)
     down_send = lax.dynamic_slice_in_dim(w_down, (1 - half) * half_width, half_width, 1)
-    rows_left, rows_right = moved(rows_own, RIGHT), moved(rows_own, LEFT)
-    down_other = swapped(down_send)
     up_send = lax.dynamic_slice_in_dim(w_up, (1 - half) * half_width, half_width, 0)
-    rows_left, rows_right, down_other, up_send = together(rows_left, rows_right, down_other, up_send)
+    rows_left, rows_right, down_send, up_send, pre_send, head = together(
+        rows_left, rows_right, down_send, up_send, pre, conv_own[:HEAD]
+    )
+
+    from_left, from_right = moved(rows_left, RIGHT[1:]), moved(rows_right, LEFT[1:])
+    down_other, pre_other = swapped(down_send), swapped(pre_send)
+    next_head = moved(head, [(2, 0), (3, 1)])
+    from_left, from_right, down_other, pre_other, up_send, next_head = together(
+        from_left, from_right, down_other, pre_other, up_send, next_head
+    )
 
     def hidden(where, rows):
         send, keep = hidden_sums(where, rows, w_down, down_other)
         return keep, swapped(send)
 
-    def finish(where, rows, keep, got, dtype):
-        return expert_sums(where, rows, keep, got, pre, pre_other, w_up, up_other, dtype)
-
-    near_rows = [rows_own, rows_left, rows_right]
-    from_left, from_right = moved(rows_left, RIGHT[1:]), moved(rows_right, LEFT[1:])
-    near_keep, near_got = hidden(near, near_rows)
-    from_left, from_right, near_keep, up_send, pre_send = together(from_left, from_right, near_keep, up_send, pre)
+    def finish(where, rows, sums, dtype):
+        return expert_sums(where, rows, *sums, pre, pre_other, w_up, up_other, dtype)
 
     far, end = place(far_block), place(end_block)
     rows_far = jnp.where(me >= 2, from_left, from_right)
     rows_end = moved(rows_far, [(2, 3), (1, 0)])
-    up_other, pre_other = swapped(up_send), swapped(pre_send)
+    up_other = swapped(up_send)
+    near_rows = [rows_own, rows_left, rows_right]
+    keep, got = hidden(near, near_rows)
+    rows_end, rows_far, keep, up_other, conv_own = together(rows_end, rows_far, keep, up_other, conv_own)
+
+    conv_left, conv_right = moved(conv_own, RIGHT), moved(conv_own, LEFT)
+    end_hidden = hidden(end, [rows_end])
     far_keep, far_got = hidden(far, [rows_far])
-    next_head = moved(conv_own[:HEAD], [(2, 0), (3, 1)])
-    last_head = moved(conv_own[:HEAD], [(3, 0)])
-    rows_end, far_keep, up_other, pre_other, next_head, last_head, conv_own = together(
-        rows_end, far_keep, up_other, pre_other, next_head, last_head, conv_own
-    )
-
-    conv_left, conv_right = moved(conv_own, RIGHT), moved(conv_own, LEFT)
-    end_keep, end_got = hidden(end, [rows_end])
-    far_sums = finish(far, [rows_far], far_keep, far_got, F32)
-    end_sums = finish(end, [rows_end], end_keep, end_got, BF16)
-    conv_left, conv_right, end_sums, far_sums = together(conv_left, conv_right, end_sums, far_sums)
+    end_sums = finish(end, [rows_end], end_hidden, BF16)
+    conv_left, conv_right, end_sums, keep, far_keep = together(conv_left, conv_right, end_sums, keep, far_keep)
 
     from_left, from_right = moved(conv_left, RIGHT[1:]), moved(conv_right, LEFT[1:])
     back_end = moved(end_sums, [(0, 1), (3, 2)])
@@ -498,8 +498,9 @@
     near_proj, near_proj_got, tap_terms = proj(
         near, [conv_own, conv_left, conv_right], [conv_right, conv_own, next_head], conv_input[0]
     )
-    from_left, from_right, near_proj, conv_left, near_keep = together(
-        from_left, from_right, near_proj, conv_left, near_keep
+    far_sums = finish(far, [rows_far], (far_keep, far_got), F32)
+    from_left, from_right, near_proj, conv_left, keep, far_sums = together(
+        from_left, from_right, near_proj, conv_left, keep, far_sums
     )
 
     conv_far = jnp.where(me >= 2, from_left, from_right)
@@ -507,19 +508,15 @@
     conv_end = moved(conv_far, [(2, 3), (1, 0)])
     back = (far_sums + back_end.astype(F32)).astype(BF16)
     back_right, back_left = moved(back, RIGHT[:2]), moved(back, LEFT[:2])
-    far_head = jnp.where(me >= 2, conv_left[:HEAD], last_head)
-    near_sums = finish(near, near_rows, near_keep, near_got, F32)
-    near_sums, conv_far = together(near_sums, conv_far)
-    far_proj, far_proj_got = proj(far, [conv_far], [far_head])
-    conv_end, back_right, back_left, far_proj, near_sums = together(
-        conv_end, back_right, back_left, far_proj, near_sums
-    )
+    near_sums = finish(near, near_rows, (keep, got), F32)
+    conv_end, back_right, back_left, near_sums = together(conv_end, back_right, back_left, near_sums)
 
     to_right, to_left, own = combined(near, out_grad[0], near_sums, back_right, back_left, near_proj, near_proj_got)
     to_right, to_left, conv_end = together(to_right, to_left, conv_end)
     to_right, to_left = moved(to_right, RIGHT), moved(to_left, LEFT)
-    end_proj, end_proj_got = proj(end, [conv_end], [conv_far])
-    to_right, to_left, end_proj = together(to_right, to_left, end_proj)
+    far_head = jnp.where(me >= 2, conv_left[:HEAD], conv_end[:HEAD])
+    proj_keep, proj_got = proj(place(far_block, end_block), [conv_far, conv_end], [far_head, conv_far])
+    to_right, to_left, proj_keep = together(to_right, to_left, proj_keep)
 
     residual = (own + to_right.astype(F32) + to_left.astype(F32)).astype(BF16)
     sections, cores = lax.axis_size("section"), lax.axis_size("mp")
@@ -532,8 +529,8 @@
         return lax.ppermute((keep + got.astype(F32)).astype(BF16), ("section", "expert", "mp"), moves)
 
     residual = shifted(residual, "section", -1)
-    far_piece = deliver(far_proj, far_proj_got, [(e, (e + 2) % experts) for e in range(experts)])
-    end_piece = deliver(end_proj, end_proj_got, [(0, experts - 1), (experts - 1, 0)])
+    far_piece = deliver(proj_keep[:tok_rows], proj_got[:tok_rows], [(e, (e + 2) % experts) for e in range(experts)])
+    end_piece = deliver(proj_keep[tok_rows:], proj_got[tok_rows:], [(0, experts - 1), (experts - 1, 0)])
     tap_grads = doubling_sum(tap_terms, "expert")
     residual = final_sum(near, residual, far_piece, end_piece)
     return (residual[None], tap_grads[None])

time: 168 us -> 166 us (0.988)
  waiting for transfers between devices: 60.4 us -> 68.6 us
  Pallas kernels: 45.4 us -> 38.1 us
  starting transfers between devices: 44.6 us -> 40.1 us
    ppermute x17 -> x16, waiting for transfers between devices: 44.2 us -> 52.1 us  [moved(): return lax.ppermute(array, 'expert', pairs)]
    unnamed x34 -> x32, local copies, waits for them, and re-layouts: 4.26 us -> 8.07 us
    pallas_call x3, Pallas kernels: 14.7 us -> 11 us  [hidden_sums(): pl.pallas_call(functools.partial(hidden_kernel, count), grid_spec=pltpu.P...]
    ppermute x2, starting transfers between devices: 6.22 us -> 3.36 us  [doubling_sum(): lax.ppermute(array, axis, [(i, i ^ step) for i in range(size)])]
    pallas_call x3 -> x2, Pallas kernels: 12.1 us -> 10.1 us  [proj_sums(): pl.pallas_call(functools.partial(proj_kernel, count, with_taps), grid=(ha...]
    dynamic_slice x1, local copies, waits for them, and re-layouts: 3.24 us -> 1.47 us  [token_plan(): lax.dynamic_slice_in_dim(w_up, (1 - half) * half_width, half_width, 0)]
    ppermute x3 -> x2, starting transfers between devices: 3.86 us -> 2.58 us  [proj(): return (keep, lax.ppermute(send, ('expert', 'mp'), gather), *tap_terms)]
    ppermute x17 -> x16, starting transfers between devices: 30.2 us -> 29.7 us  [moved(): return lax.ppermute(array, 'expert', pairs)]
  transfers between devices with their start and end apart: 31 -> 29, of which waited for: 9 -> 9; matrix products, arithmetic and copies ran while one was open for 4% -> 4% of each run, Pallas kernels for 26% -> 22%
where the time goes in v7:
time: 166 us; the launch traced here: 165 us
  waiting for transfers between devices  68.6 us (41%)
  starting transfers between devices  40.1 us (24%)
  Pallas kernels  38.1 us (23%)
  local copies, waits for them, and re-layouts  13.1 us (8%)
  other arithmetic  4.21 us (3%)
    ppermute x16, waiting for transfers between devices, moved(): return lax.ppermute(array, 'expert', pairs)  52.1 us
    ppermute x16, starting transfers between devices, moved(): return lax.ppermute(array, 'expert', pairs)  29.7 us
    ppermute x1, waiting for transfers between devices, shifted(): return lax.ppermute(array, axis, pairs)  16.4 us
    pallas_call x3, Pallas kernels, expert_sums(): pl.pallas_call(functools.partial(finish_kernel, count), grid_spec=pltpu.P...  14.3 us
    pallas_call x3, Pallas kernels, hidden_sums(): pl.pallas_call(functools.partial(hidden_kernel, count), grid_spec=pltpu.P...  11 us
    pallas_call x2, Pallas kernels, proj_sums(): pl.pallas_call(functools.partial(proj_kernel, count, with_taps), grid=(ha...  10.1 us
    unnamed x32, local copies, waits for them, and re-layouts  8.07 us
    ppermute x2, starting transfers between devices, doubling_sum(): lax.ppermute(array, axis, [(i, i ^ step) for i in range(size)])  3.36 us
  transfers between devices with their start and end apart: 29, of which 9 were waited for; matrix products, arithmetic and copies ran while one was open for 4% of the time, Pallas kernels for 22%

profile of v7, /device:TPU:0, one launch (start us, length us, event | category | flops | bytes accessed | tf_op | source)
XLA Modules:
  0.0 165.3 jit_solution(3930851988393196272)
XLA Ops:
  0.6 0.7 convert_bitcast_fusion
  1.5 1.1 fusion.1.refs_0_.refs_3_
  2.6 5.0 %collective-permute-start = (bf16[128,2176]{1,0:T(8,128)(2,1)S(1)}, bf16[128,2176]{1,0:T(8,128)(2,1)S(1)}, u32[]{:S(2)}, u32[]{:S(2)}) collective-permute-start(bf16[128,2176]{1,0:T(8,128)(2,1)S(1)} %fusion.1.refs_0_.refs_3_), channel_id=1, source_target_pairs={{0,2},{2,4},{4,6},{1,3},{3,5},{5,7},{8,10},{10,12},{12,14},{9,11},... | collective-permute-start | bytes 1671176 | tf_op jit(solution)/shard_map/ppermute | solution.py:417
  7.5 1.3 collective-permute-start.1
  8.9 3.3 %dynamic-slice_bitcast_fusion.1 = bf16[512,2048]{1,0:T(8,128)(2,1)} fusion(bf16[1,1,512,4096]{3,2,1,0:T(8,128)(2,1)} %param.14, s32[]{:T(128)S(6)} %select_n.41), kind=kLoop, calls=%fused_computation.1 | loop fusion | bytes 4194308 | tf_op jit(solution)/shard_map/dynamic_slice | solution.py:456
  12.2 1.5 dynamic-slice_bitcast_fusion
  13.7 5.7 %collective-permute-done.refs_1_.refs_4_ = bf16[128,2176]{1,0:T(8,128)(2,1)S(1)} collective-permute-done((bf16[128,2176]{1,0:T(8,128)(2,1)S(1)}, bf16[128,2176]{1,0:T(8,128)(2,1)S(1)}, u32[]{:S(2)}, u32[]{:S(2)}) %collective-permute-start) | collective-permute-done | bytes 557088 | tf_op jit(solution)/shard_map/ppermute | solution.py:417
  19.4 4.1 %collective-permute-done.1.refs_2_.refs_5_ = bf16[128,2176]{1,0:T(8,128)(2,1)S(1)} collective-permute-done((bf16[128,2176]{1,0:T(8,128)(2,1)S(1)}, bf16[128,2176]{1,0:T(8,128)(2,1)S(1)}, u32[]{:S(2)}, u32[]{:S(2)}) %collective-permute-start.1) | collective-permute-done | bytes 557088 | tf_op jit(solution)/shard_map/ppermute | solution.py:417
  23.5 0.8 copy-done.11
  24.3 1.5 collective-permute-start.2
  25.8 1.3 collective-permute-start.3
  27.7 1.3 collective-permute-start.6
  29.0 20.3 %collective-permute-done.6.refs_5_ = bf16[16,2048]{1,0:T(8,128)(2,1)S(1)} collective-permute-done((bf16[16,2048]{1,0:T(8,128)(2,1)S(1)}, bf16[16,2048]{1,0:T(8,128)(2,1)S(1)}, u32[]{:S(2)}, u32[]{:S(2)}) %collective-permute-start.6) | collective-permute-done | bytes 65568 | tf_op jit(solution)/shard_map/ppermute | solution.py:417
  49.3 1.3 copy-done.6
  50.9 1.1 broadcast_select_fusion.refs_0_.refs_1_
  52.0 1.3 collective-permute-start.7
  53.3 2.2 %copy-done.1 = bf16[1,1,512,4096]{3,2,1,0:T(8,128)(2,1)S(1)} copy-done((bf16[1,1,512,4096]{3,2,1,0:T(8,128)(2,1)S(1)}, bf16[1,1,512,4096]{3,2,1,0:T(8,128)(2,1)}, u32[]{:S(2)}) %copy-start.1) | copy-done | bytes 4194328
  55.5 1.6 copy-done.7
  57.1 1.1 copy-done.9
  58.1 1.1 copy-done.12
  59.2 4.4 %hidden.3 = (bf16[384,1024]{1,0:T(8,128)(2,1)S(1)}, f32[384,1024]{1,0:T(8,128)S(1)}) custom-call(s32[5]{0:T(128)S(1)} %stack.43.place, bf16[128,2176]{1,0:T(8,128)(2,1)S(1)} %fusion.1.refs_0_.refs_3_, bf16[128,2176]{1,0:T(8,128)(2,1)S(1)} %copy-done.9, bf16[128,2176]{1,0:T(8,128)(2,1)S(1)} %copy-done.12, bf16[128,2176]{1,0:T(8,128)(2,1)S(1)} %fusion.1.refs_0_.refs_3_, ...), custom_call_target="tpu_custom_call" | custom-call | flops 12884901888 | bytes 46137344 | tf_op jit(solution)/shard_map/hidden/pallas_call | solution.py:199
  64.1 4.8 %collective-permute-done.7.refs_0_.refs_1_ = bf16[128,2176]{1,0:T(8,128)(2,1)S(1)} collective-permute-done((bf16[128,2176]{1,0:T(8,128)(2,1)S(1)}, bf16[128,2176]{1,0:T(8,128)(2,1)S(1)}, u32[]{:S(2)}, u32[]{:S(2)}) %collective-permute-start.7) | collective-permute-done | bytes 557088 | tf_op jit(solution)/shard_map/ppermute | solution.py:417
  68.9 1.5 collective-permute-start.9
  70.4 1.3 collective-permute-start.10
  71.7 3.3 %hidden.4 = (bf16[128,1024]{1,0:T(8,128)(2,1)S(1)}, f32[128,1024]{1,0:T(8,128)S(1)}) custom-call(s32[3]{0:T(128)S(1)} %get-tuple-element.112.place, bf16[128,2176]{1,0:T(8,128)(2,1)S(1)} %collective-permute-done.7.refs_0_.refs_1_, bf16[128,2176]{1,0:T(8,128)(2,1)S(1)} %collective-permute-done.7.refs_0_.refs_1_, bf16[512,4096]{1,0:T(8,128)(2,1)S(1)} %bitcast.30, ...), custom_call_target="tpu_custom_call" | custom-call | flops 4294967296 | bytes 37748736 | tf_op jit(solution)/shard_map/hidden/pallas_call | solution.py:199
  75.1 3.3 %hidden.5 = (bf16[128,1024]{1,0:T(8,128)(2,1)S(1)}, f32[128,1024]{1,0:T(8,128)S(1)}) custom-call(s32[3]{0:T(128)S(1)} %get-tuple-element.113.place, bf16[128,2176]{1,0:T(8,128)(2,1)S(1)} %broadcast_select_fusion.refs_0_.refs_1_, bf16[128,2176]{1,0:T(8,128)(2,1)S(1)} %broadcast_select_fusion.refs_0_.refs_1_, bf16[512,4096]{1,0:T(8,128)(2,1)S(1)} %bitcast.31, ...), custom_call_target="tpu_custom_call" | custom-call | flops 4294967296 | bytes 37748736 | tf_op jit(solution)/shard_map/hidden/pallas_call | solution.py:199
  79.0 4.6 %experts.3 = bf16[128,2048]{1,0:T(8,128)(2,1)S(1)} custom-call(s32[3]{0:T(128)S(1)} %get-tuple-element.112.place, bf16[128,2176]{1,0:T(8,128)(2,1)S(1)} %collective-permute-done.7.refs_0_.refs_1_, f32[128,1024]{1,0:T(8,128)S(1)} %get-tuple-element.69.refs_1_, bf16[128,1024]{1,0:T(8,128)(2,1)S(1)} %collective-permute-done.11.refs_2_, ...), custom_call_target="tpu_custom_call" | custom-call | flops 4294967296 | bytes 41943040 | tf_op jit(solution)/shard_map/experts/pallas_call | solution.py:254
  83.6 2.1 %collective-permute-done.10.refs_2_.refs_3_ = bf16[128,2048]{1,0:T(8,128)(2,1)S(1)} collective-permute-done((bf16[128,2048]{1,0:T(8,128)(2,1)S(1)}, bf16[128,2048]{1,0:T(8,128)(2,1)S(1)}, u32[]{:S(2)}, u32[]{:S(2)}) %collective-permute-start.10) | collective-permute-done | bytes 524320 | tf_op jit(solution)/shard_map/ppermute | solution.py:417
  86.4 1.3 collective-permute-start.13
  87.7 4.6 %collective-permute-start.15 = (bf16[128,2048]{1,0:T(8,128)(2,1)S(1)}, bf16[128,2048]{1,0:T(8,128)(2,1)S(1)}, u32[]{:S(2)}, u32[]{:S(2)}) collective-permute-start(bf16[128,2048]{1,0:T(8,128)(2,1)S(1)} %experts.3), channel_id=1, source_target_pairs={{0,2},{6,4},{1,3},{7,5},{8,10},{14,12},{9,11},{15,13},{16,18},{22,... | collective-permute-start | bytes 1572872 | tf_op jit(solution)/shard_map/ppermute | solution.py:417
  92.3 6.0 %projection.2 = (bf16[384,1024]{1,0:T(8,128)(2,1)S(1)}, f32[384,1024]{1,0:T(8,128)S(1)}, f32[4,2048]{1,0:T(4,128)S(1)}) custom-call(s32[5]{0:T(128)S(1)} %stack.43.place, bf16[128,2048]{1,0:T(8,128)(2,1)S(1)} %bitcast.37, bf16[128,2048]{1,0:T(8,128)(2,1)S(1)} %collective-permute-done.9.refs_1_, ...), custom_call_target="tpu_custom_call" | custom-call | flops 12884901888 | bytes 65011712 | tf_op jit(solution)/shard_map/projection/pallas_call | solution.py:336
  98.4 1.3 collective-permute-start.20
  99.7 4.3 %experts.4 = f32[128,2048]{1,0:T(8,128)S(1)} custom-call(s32[3]{0:T(128)S(1)} %get-tuple-element.113.place, bf16[128,2176]{1,0:T(8,128)(2,1)S(1)} %broadcast_select_fusion.refs_0_.refs_1_, f32[128,1024]{1,0:T(8,128)S(1)} %get-tuple-element.81.refs_1_, bf16[128,1024]{1,0:T(8,128)(2,1)S(1)} %collective-permute-done.14.refs_2_, ...), custom_call_target="tpu_custom_call" | custom-call | flops 4294967296 | bytes 41943040 | tf_op jit(solution)/shard_map/experts/pallas_call | solution.py:254
  104.3 4.1 %collective-permute-start.17 = (bf16[128,2048]{1,0:T(8,128)(2,1)S(1)}, bf16[128,2048]{1,0:T(8,128)(2,1)S(1)}, u32[]{:S(2)}, u32[]{:S(2)}) collective-permute-start(bf16[128,2048]{1,0:T(8,128)(2,1)S(1)} %add_convert_fusion.1), channel_id=1, source_target_pairs={{0,2},{2,4},{1,3},{3,5},{8,10},{10,12},{9,11},{11,13},{16,18},{18,... | collective-permute-start | bytes 1572872 | tf_op jit(solution)/shard_map/ppermute | solution.py:417
  109.1 1.3 collective-permute-start.16
  110.4 5.4 %experts.5.sums = f32[384,2048]{1,0:T(8,128)S(1)} custom-call(s32[5]{0:T(128)S(1)} %stack.43.place, bf16[128,2176]{1,0:T(8,128)(2,1)S(1)} %fusion.1.refs_0_.refs_3_, bf16[128,2176]{1,0:T(8,128)(2,1)S(1)} %copy-done.10, bf16[128,2176]{1,0:T(8,128)(2,1)S(1)} %copy-done.13, f32[384,1024]{1,0:T(8,128)S(1)} %get-tuple-element.89.refs_3_, ...), custom_call_target="tpu_custom_call" | custom-call | flops 12884901888 | bytes 58720256 | tf_op jit(solution)/shard_map/experts/pallas_call | solution.py:254
  115.9 9.6 %collective-permute-done.16.refs_1_ = bf16[128,2048]{1,0:T(8,128)(2,1)S(1)} collective-permute-done((bf16[128,2048]{1,0:T(8,128)(2,1)S(1)}, bf16[128,2048]{1,0:T(8,128)(2,1)S(1)}, u32[]{:S(2)}, u32[]{:S(2)}) %collective-permute-start.16) | collective-permute-done | bytes 524320 | tf_op jit(solution)/shard_map/ppermute | solution.py:417
  125.5 1.2 combine.1
  126.6 1.5 collective-permute-start.21
  128.1 1.3 collective-permute-start.22
  129.4 4.1 %projection.3 = (bf16[256,1024]{1,0:T(8,128)(2,1)S(1)}, f32[256,1024]{1,0:T(8,128)S(1)}) custom-call(s32[4]{0:T(128)S(1)} %pad_add_fusion.3.place, bf16[128,2048]{1,0:T(8,128)(2,1)S(1)} %broadcast_select_fusion.1.refs_0_.refs_3_, bf16[128,2048]{1,0:T(8,128)(2,1)S(1)} %collective-permute-done.16.refs_1_, bf16[16,2048]{1,0:T(8,128)(2,1)S(1)} %slice_select_fusion.refs_2_, ...), custom_call_target="tpu_custom_call" | custom-call | flops 8589934592 | bytes 54525952 | tf_op jit(solution)/shard_map/projection/pallas_call | solution.py:336
  133.6 1.3 collective-permute-start.24
  134.9 3.3 %collective-permute-start.28 = (f32[4,2048]{1,0:T(4,128)S(1)}, f32[4,2048]{1,0:T(4,128)S(1)}, u32[]{:S(2)}, u32[]{:S(2)}) collective-permute-start(f32[4,2048]{1,0:T(4,128)S(1)} %add.47), channel_id=1, source_target_pairs={{0,4},{2,6},{4,0},{6,2},{1,5},{3,7},{5,1},{7,3},{8,12},{10,14},{12... | collective-permute-start | bytes 98312 | tf_op jit(solution)/shard_map/ppermute | solution.py:139
  138.2 1.4 collective-permute-done.21
  139.6 4.2 %collective-permute-done.22 = bf16[128,2048]{1,0:T(8,128)(2,1)S(1)} collective-permute-done((bf16[128,2048]{1,0:T(8,128)(2,1)S(1)}, bf16[128,2048]{1,0:T(8,128)(2,1)S(1)}, u32[]{:S(2)}, u32[]{:S(2)}) %collective-permute-start.22) | collective-permute-done | bytes 524320 | tf_op jit(solution)/shard_map/ppermute | solution.py:417
  143.9 1.3 collective-permute-start.23
  147.4 16.4 %collective-permute-done.23.residual = bf16[128,2048]{1,0:T(8,128)(2,1)S(1)} collective-permute-done((bf16[128,2048]{1,0:T(8,128)(2,1)S(1)}, bf16[128,2048]{1,0:T(8,128)(2,1)S(1)}, u32[]{:S(2)}, u32[]{:S(2)}) %collective-permute-start.23) | collective-permute-done | bytes 524320 | tf_op jit(solution)/shard_map/ppermute | solution.py:14
  163.8 1.5 residual.1
  (70 shorter events, 6.2 us)
Async XLA Ops:
  2.6 16.8 %collective-permute-start = (bf16[128,2176]{1,0:T(8,128)(2,1)S(1)}, bf16[128,2176]{1,0:T(8,128)(2,1)S(1)}, u32[]{:S(2)}, u32[]{:S(2)}) collective-permute-start(bf16[128,2176]{1,0:T(8,128)(2,1)S(1)} %fusion.1.refs_0_.refs_3_), channel_id=1, source_target_pairs={{0,2},{2,4},{4,6},{1,3},{3,5},{5,7},{8,10},{10,12},{12,14},{9,11},... | collective-permute-start | bytes 1671176 | tf_op jit(solution)/shard_map/ppermute | solution.py:417
  7.5 16.0 %collective-permute-start.1 = (bf16[128,2176]{1,0:T(8,128)(2,1)S(1)}, bf16[128,2176]{1,0:T(8,128)(2,1)S(1)}, u32[]{:S(2)}, u32[]{:S(2)}) collective-permute-start(bf16[128,2176]{1,0:T(8,128)(2,1)S(1)} %fusion.1.refs_0_.refs_3_), channel_id=1, source_target_pairs={{6,4},{4,2},{2,0},{7,5},{5,3},{3,1},{14,12},{12,10},{10,8},{15,13}... | collective-permute-start | bytes 1671176 | tf_op jit(solution)/shard_map/ppermute | solution.py:417
  8.8 3.4 %copy-start.2 = (bf16[1,1,4096,512]{3,2,1,0:T(8,128)(2,1)S(1)}, bf16[1,1,4096,512]{3,2,1,0:T(8,128)(2,1)}, u32[]{:S(2)}) copy-start(bf16[1,1,4096,512]{3,2,1,0:T(8,128)(2,1)} %param.13) | copy-start | bytes 12582916
  12.2 1.5 copy-start.4
  19.4 4.2 %copy-start.8 = (bf16[128,2176]{1,0:T(8,128)(2,1)}, bf16[128,2176]{1,0:T(8,128)(2,1)S(1)}, u32[]{:S(2)}) copy-start(bf16[128,2176]{1,0:T(8,128)(2,1)S(1)} %collective-permute-done.refs_1_.refs_4_) | copy-start | bytes 1671172
  23.5 0.8 copy-start.11
  24.3 24.9 %collective-permute-start.4 = (bf16[512,2048]{1,0:T(8,128)(2,1)}, bf16[512,2048]{1,0:T(8,128)(2,1)S(1)}, u32[]{:S(2)}, u32[]{:S(2)}) collective-permute-start(bf16[512,2048]{1,0:T(8,128)(2,1)} %dynamic-slice_bitcast_fusion.1), channel_id=1, source_target_pairs={{0,1},{1,0},{2,3},{3,2},{4,5},{5,4},{6,7},{7,6},{8,9},{9,8},{10,11... | collective-permute-start | bytes 6291464 | tf_op jit(solution)/shard_map/ppermute | solution.py:129
  24.3 24.9 %collective-permute-start.2 = (bf16[128,2176]{1,0:T(8,128)(2,1)}, bf16[128,2176]{1,0:T(8,128)(2,1)}, u32[]{:S(2)}, u32[]{:S(2)}) collective-permute-start(bf16[128,2176]{1,0:T(8,128)(2,1)} %copy-done.8), channel_id=1, source_target_pairs={{2,4},{4,6},{3,5},{5,7},{10,12},{12,14},{11,13},{13,15},{18,20},{2... | collective-permute-start | bytes 1671176 | tf_op jit(solution)/shard_map/ppermute | solution.py:417
  25.8 23.5 %collective-permute-start.3 = (bf16[128,2176]{1,0:T(8,128)(2,1)}, bf16[128,2176]{1,0:T(8,128)(2,1)}, u32[]{:S(2)}, u32[]{:S(2)}) collective-permute-start(bf16[128,2176]{1,0:T(8,128)(2,1)} %copy-done.11), channel_id=1, source_target_pairs={{4,2},{2,0},{5,3},{3,1},{12,10},{10,8},{13,11},{11,9},{20,18},{18,... | collective-permute-start | bytes 1671176 | tf_op jit(solution)/shard_map/ppermute | solution.py:417
  27.1 22.2 %collective-permute-start.5 = (bf16[512,512]{1,0:T(8,128)(2,1)}, bf16[512,512]{1,0:T(8,128)(2,1)}, u32[]{:S(2)}, u32[]{:S(2)}) collective-permute-start(bf16[512,512]{1,0:T(8,128)(2,1)} %bitcast.9.refs_3_.refs_5_), channel_id=1, source_target_pairs={{0,1},{1,0},{2,3},{3,2},{4,5},{5,4},{6,7},{7,6},{8,9},{9,8},{10,11... | collective-permute-start | bytes 1572872 | tf_op jit(solution)/shard_map/ppermute | solution.py:129
  27.7 21.6 %collective-permute-start.6 = (bf16[16,2048]{1,0:T(8,128)(2,1)S(1)}, bf16[16,2048]{1,0:T(8,128)(2,1)S(1)}, u32[]{:S(2)}, u32[]{:S(2)}) collective-permute-start(bf16[16,2048]{1,0:T(8,128)(2,1)S(1)} %slice_bitcast_fusion), channel_id=1, source_target_pairs={{4,0},{6,2},{5,1},{7,3},{12,8},{14,10},{13,9},{15,11},{20,16},{22,... | collective-permute-start | bytes 196616 | tf_op jit(solution)/shard_map/ppermute | solution.py:417
  49.3 1.4 copy-start.6
  50.6 18.3 %collective-permute-start.8 = (bf16[2048,512]{1,0:T(8,128)(2,1)}, bf16[2048,512]{1,0:T(8,128)(2,1)S(1)}, u32[]{:S(2)}, u32[]{:S(2)}) collective-permute-start(bf16[2048,512]{1,0:T(8,128)(2,1)} %dynamic-slice_bitcast_fusion), channel_id=1, source_target_pairs={{0,1},{1,0},{2,3},{3,2},{4,5},{5,4},{6,7},{7,6},{8,9},{9,8},{10,11... | collective-permute-start | bytes 6291464 | tf_op jit(solution)/shard_map/ppermute | solution.py:129
  52.0 16.9 %collective-permute-start.7 = (bf16[128,2176]{1,0:T(8,128)(2,1)S(1)}, bf16[128,2176]{1,0:T(8,128)(2,1)S(1)}, u32[]{:S(2)}, u32[]{:S(2)}) collective-permute-start(bf16[128,2176]{1,0:T(8,128)(2,1)S(1)} %broadcast_select_fusion.refs_0_.refs_1_), channel_id=1, source_target_pairs={{4,6},{2,0},{5,7},{3,1},{12,14},{10,8},{13,15},{11,9},{20,22},{18,... | collective-permute-start | bytes 1671176 | tf_op jit(solution)/shard_map/ppermute | solution.py:417
  53.3 2.2 %copy-start.1 = (bf16[1,1,512,4096]{3,2,1,0:T(8,128)(2,1)S(1)}, bf16[1,1,512,4096]{3,2,1,0:T(8,128)(2,1)}, u32[]{:S(2)}) copy-start(bf16[1,1,512,4096]{3,2,1,0:T(8,128)(2,1)} %param.14) | copy-start | bytes 12582916
  55.5 1.6 copy-start.7
  57.1 1.1 copy-start.9
  58.1 1.1 copy-start.12
  63.6 45.5 %collective-permute-start.19 = (bf16[384,1024]{1,0:T(8,128)(2,1)S(1)}, bf16[384,1024]{1,0:T(8,128)(2,1)S(1)}, u32[]{:S(2)}, u32[]{:S(2)}) collective-permute-start(bf16[384,1024]{1,0:T(8,128)(2,1)S(1)} %get-tuple-element.90), channel_id=1, source_target_pairs={{0,1},{1,0},{2,3},{3,2},{4,5},{5,4},{6,7},{7,6},{8,9},{9,8},{10,11... | collective-permute-start | bytes 2359304 | tf_op jit(solution)/shard_map/ppermute | solution.py:129
  68.9 14.7 %collective-permute-start.9 = (bf16[128,2048]{1,0:T(8,128)(2,1)S(1)}, bf16[128,2048]{1,0:T(8,128)(2,1)S(1)}, u32[]{:S(2)}, u32[]{:S(2)}) collective-permute-start(bf16[128,2048]{1,0:T(8,128)(2,1)S(1)} %bitcast.35), channel_id=1, source_target_pairs={{0,2},{2,4},{4,6},{1,3},{3,5},{5,7},{8,10},{10,12},{12,14},{9,11},... | collective-permute-start | bytes 1572872 | tf_op jit(solution)/shard_map/ppermute | solution.py:417
  70.4 15.3 %collective-permute-start.10 = (bf16[128,2048]{1,0:T(8,128)(2,1)S(1)}, bf16[128,2048]{1,0:T(8,128)(2,1)S(1)}, u32[]{:S(2)}, u32[]{:S(2)}) collective-permute-start(bf16[128,2048]{1,0:T(8,128)(2,1)S(1)} %bitcast.36), channel_id=1, source_target_pairs={{6,4},{4,2},{2,0},{7,5},{5,3},{3,1},{14,12},{12,10},{10,8},{15,13}... | collective-permute-start | bytes 1572872 | tf_op jit(solution)/shard_map/ppermute | solution.py:417
  75.0 4.0 %collective-permute-start.11 = (bf16[128,1024]{1,0:T(8,128)(2,1)S(1)}, bf16[128,1024]{1,0:T(8,128)(2,1)S(1)}, u32[]{:S(2)}, u32[]{:S(2)}) collective-permute-start(bf16[128,1024]{1,0:T(8,128)(2,1)S(1)} %get-tuple-element.70), channel_id=1, source_target_pairs={{0,1},{1,0},{2,3},{3,2},{4,5},{5,4},{6,7},{7,6},{8,9},{9,8},{10,11... | collective-permute-start | bytes 786440 | tf_op jit(solution)/shard_map/ppermute | solution.py:129
  75.1 3.9 %copy-start.3 = (bf16[1,1,4096,512]{3,2,1,0:T(8,128)(2,1)S(1)}, bf16[1,1,4096,512]{3,2,1,0:T(8,128)(2,1)}, u32[]{:S(2)}) copy-start(bf16[1,1,4096,512]{3,2,1,0:T(8,128)(2,1)} %param.13) | copy-start | bytes 12582916
  78.4 19.9 %collective-permute-start.14 = (bf16[128,1024]{1,0:T(8,128)(2,1)S(1)}, bf16[128,1024]{1,0:T(8,128)(2,1)S(1)}, u32[]{:S(2)}, u32[]{:S(2)}) collective-permute-start(bf16[128,1024]{1,0:T(8,128)(2,1)S(1)} %get-tuple-element.82), channel_id=1, source_target_pairs={{0,1},{1,0},{2,3},{3,2},{4,5},{5,4},{6,7},{7,6},{8,9},{9,8},{10,11... | collective-permute-start | bytes 786440 | tf_op jit(solution)/shard_map/ppermute | solution.py:129
  79.0 13.3 %copy-start.5 = (bf16[1,1024,2048]{2,1,0:T(8,128)(2,1)S(1)}, bf16[1,1024,2048]{2,1,0:T(8,128)(2,1)}, u32[]{:S(2)}) copy-start(bf16[1,1024,2048]{2,1,0:T(8,128)(2,1)} %param.19) | copy-start | bytes 12582916
  79.0 13.3 %copy-start.14 = (bf16[1,128,2048]{2,1,0:T(8,128)(2,1)S(1)}, bf16[1,128,2048]{2,1,0:T(8,128)(2,1)}, u32[]{:S(2)}) copy-start(bf16[1,128,2048]{2,1,0:T(8,128)(2,1)} %param.17) | copy-start | bytes 1572868
  79.0 13.3 %copy-start.15 = (f32[1,4,2048]{2,1,0:T(4,128)S(1)}, f32[1,4,2048]{2,1,0:T(4,128)}, u32[]{:S(2)}) copy-start(f32[1,4,2048]{2,1,0:T(4,128)} %param.18) | copy-start | bytes 98308
  85.7 18.3 %collective-permute-start.12 = (bf16[128,2048]{1,0:T(8,128)(2,1)S(1)}, bf16[128,2048]{1,0:T(8,128)(2,1)S(1)}, u32[]{:S(2)}, u32[]{:S(2)}) collective-permute-start(bf16[128,2048]{1,0:T(8,128)(2,1)S(1)} %collective-permute-done.9.refs_1_), channel_id=1, source_target_pairs={{2,4},{4,6},{3,5},{5,7},{10,12},{12,14},{11,13},{13,15},{18,20},{2... | collective-permute-start | bytes 1572872 | tf_op jit(solution)/shard_map/ppermute | solution.py:417
  86.4 17.7 %collective-permute-start.13 = (bf16[128,2048]{1,0:T(8,128)(2,1)S(1)}, bf16[128,2048]{1,0:T(8,128)(2,1)S(1)}, u32[]{:S(2)}, u32[]{:S(2)}) collective-permute-start(bf16[128,2048]{1,0:T(8,128)(2,1)S(1)} %collective-permute-done.10.refs_2_.refs_3_), channel_id=1, source_target_pairs={{4,2},{2,0},{5,3},{3,1},{12,10},{10,8},{13,11},{11,9},{20,18},{18,... | collective-permute-start | bytes 1572872 | tf_op jit(solution)/shard_map/ppermute | solution.py:417
  87.7 16.5 %collective-permute-start.15 = (bf16[128,2048]{1,0:T(8,128)(2,1)S(1)}, bf16[128,2048]{1,0:T(8,128)(2,1)S(1)}, u32[]{:S(2)}, u32[]{:S(2)}) collective-permute-start(bf16[128,2048]{1,0:T(8,128)(2,1)S(1)} %experts.3), channel_id=1, source_target_pairs={{0,2},{6,4},{1,3},{7,5},{8,10},{14,12},{9,11},{15,13},{16,18},{22,... | collective-permute-start | bytes 1572872 | tf_op jit(solution)/shard_map/ppermute | solution.py:417
  98.4 27.1 %collective-permute-start.20 = (bf16[384,1024]{1,0:T(8,128)(2,1)S(1)}, bf16[384,1024]{1,0:T(8,128)(2,1)S(1)}, u32[]{:S(2)}, u32[]{:S(2)}) collective-permute-start(bf16[384,1024]{1,0:T(8,128)(2,1)S(1)} %get-tuple-element.95), channel_id=1, source_target_pairs={{1,0},{3,2},{4,5},{6,7},{9,8},{11,10},{12,13},{14,15},{17,16},{19,... | collective-permute-start | bytes 2359304 | tf_op jit(solution)/shard_map/ppermute | solution.py:496
  104.0 6.4 %copy-start.10 = (bf16[128,2176]{1,0:T(8,128)(2,1)S(1)}, bf16[128,2176]{1,0:T(8,128)(2,1)}, u32[]{:S(2)}) copy-start(bf16[128,2176]{1,0:T(8,128)(2,1)} %copy-done.8) | copy-start | bytes 1671172
  104.0 6.4 %copy-start.13 = (bf16[128,2176]{1,0:T(8,128)(2,1)S(1)}, bf16[128,2176]{1,0:T(8,128)(2,1)}, u32[]{:S(2)}) copy-start(bf16[128,2176]{1,0:T(8,128)(2,1)} %copy-done.11) | copy-start | bytes 1671172
  104.0 30.8 %collective-permute-start.27 = (f32[4,2048]{1,0:T(4,128)S(1)}, f32[4,2048]{1,0:T(4,128)S(1)}, u32[]{:S(2)}, u32[]{:S(2)}) collective-permute-start(f32[4,2048]{1,0:T(4,128)S(1)} %get-tuple-element.109), channel_id=1, source_target_pairs={{0,2},{2,0},{4,6},{6,4},{1,3},{3,1},{5,7},{7,5},{8,10},{10,8},{12,... | collective-permute-start | bytes 98312 | tf_op jit(solution)/shard_map/ppermute | solution.py:139
  104.3 21.2 %copy-start = (bf16[1,128,2048]{2,1,0:T(8,128)(2,1)S(1)}, bf16[1,128,2048]{2,1,0:T(8,128)(2,1)}, u32[]{:S(2)}) copy-start(bf16[1,128,2048]{2,1,0:T(8,128)(2,1)} %param.10) | copy-start | bytes 1572868
  104.3 21.1 %collective-permute-start.17 = (bf16[128,2048]{1,0:T(8,128)(2,1)S(1)}, bf16[128,2048]{1,0:T(8,128)(2,1)S(1)}, u32[]{:S(2)}, u32[]{:S(2)}) collective-permute-start(bf16[128,2048]{1,0:T(8,128)(2,1)S(1)} %add_convert_fusion.1), channel_id=1, source_target_pairs={{0,2},{2,4},{1,3},{3,5},{8,10},{10,12},{9,11},{11,13},{16,18},{18,... | collective-permute-start | bytes 1572872 | tf_op jit(solution)/shard_map/ppermute | solution.py:417
  108.4 17.1 %collective-permute-start.18 = (bf16[128,2048]{1,0:T(8,128)(2,1)S(1)}, bf16[128,2048]{1,0:T(8,128)(2,1)S(1)}, u32[]{:S(2)}, u32[]{:S(2)}) collective-permute-start(bf16[128,2048]{1,0:T(8,128)(2,1)S(1)} %add_convert_fusion.1), channel_id=1, source_target_pairs={{6,4},{4,2},{7,5},{5,3},{14,12},{12,10},{15,13},{13,11},{22,20},{2... | collective-permute-start | bytes 1572872 | tf_op jit(solution)/shard_map/ppermute | solution.py:417
  109.1 16.3 %collective-permute-start.16 = (bf16[128,2048]{1,0:T(8,128)(2,1)S(1)}, bf16[128,2048]{1,0:T(8,128)(2,1)S(1)}, u32[]{:S(2)}, u32[]{:S(2)}) collective-permute-start(bf16[128,2048]{1,0:T(8,128)(2,1)S(1)} %broadcast_select_fusion.1.refs_0_.refs_3_), channel_id=1, source_target_pairs={{4,6},{2,0},{5,7},{3,1},{12,14},{10,8},{13,15},{11,9},{20,22},{18,... | collective-permute-start | bytes 1572872 | tf_op jit(solution)/shard_map/ppermute | solution.py:417
  126.6 12.9 %collective-permute-start.21 = (bf16[128,2048]{1,0:T(8,128)(2,1)S(1)}, bf16[128,2048]{1,0:T(8,128)(2,1)S(1)}, u32[]{:S(2)}, u32[]{:S(2)}) collective-permute-start(bf16[128,2048]{1,0:T(8,128)(2,1)S(1)} %get-tuple-element.100), channel_id=1, source_target_pairs={{0,2},{2,4},{4,6},{1,3},{3,5},{5,7},{8,10},{10,12},{12,14},{9,11},... | collective-permute-start | bytes 1572872 | tf_op jit(solution)/shard_map/ppermute | solution.py:417
  128.1 15.6 %collective-permute-start.22 = (bf16[128,2048]{1,0:T(8,128)(2,1)S(1)}, bf16[128,2048]{1,0:T(8,128)(2,1)S(1)}, u32[]{:S(2)}, u32[]{:S(2)}) collective-permute-start(bf16[128,2048]{1,0:T(8,128)(2,1)S(1)} %get-tuple-element.101), channel_id=1, source_target_pairs={{6,4},{4,2},{2,0},{7,5},{5,3},{3,1},{14,12},{12,10},{10,8},{15,13}... | collective-permute-start | bytes 1572872 | tf_op jit(solution)/shard_map/ppermute | solution.py:417
  133.6 11.7 %collective-permute-start.24 = (bf16[256,1024]{1,0:T(8,128)(2,1)S(1)}, bf16[256,1024]{1,0:T(8,128)(2,1)S(1)}, u32[]{:S(2)}, u32[]{:S(2)}) collective-permute-start(bf16[256,1024]{1,0:T(8,128)(2,1)S(1)} %get-tuple-element.108), channel_id=1, source_target_pairs={{1,0},{3,2},{4,5},{6,7},{9,8},{11,10},{12,13},{14,15},{17,16},{19,... | collective-permute-start | bytes 1572872 | tf_op jit(solution)/shard_map/ppermute | solution.py:496
  134.9 11.9 %collective-permute-start.28 = (f32[4,2048]{1,0:T(4,128)S(1)}, f32[4,2048]{1,0:T(4,128)S(1)}, u32[]{:S(2)}, u32[]{:S(2)}) collective-permute-start(f32[4,2048]{1,0:T(4,128)S(1)} %add.47), channel_id=1, source_target_pairs={{0,4},{2,6},{4,0},{6,2},{1,5},{3,7},{5,1},{7,3},{8,12},{10,14},{12... | collective-permute-start | bytes 98312 | tf_op jit(solution)/shard_map/ppermute | solution.py:139
  143.9 19.9 %collective-permute-start.23 = (bf16[128,2048]{1,0:T(8,128)(2,1)S(1)}, bf16[128,2048]{1,0:T(8,128)(2,1)S(1)}, u32[]{:S(2)}, u32[]{:S(2)}) collective-permute-start(bf16[128,2048]{1,0:T(8,128)(2,1)S(1)} %add_convert_fusion), channel_id=1, source_target_pairs={{8,0},{16,8},{24,16},{9,1},{17,9},{25,17},{10,2},{18,10},{26,18},{... | collective-permute-start | bytes 1572872 | tf_op jit(solution)/shard_map/ppermute | solution.py:14
  145.4 2.0 %collective-permute-start.25 = (bf16[128,1024]{1,0:T(8,128)(2,1)S(1)}, bf16[128,1024]{1,0:T(8,128)(2,1)S(1)}, u32[]{:S(2)}, u32[]{:S(2)}) collective-permute-start(bf16[128,1024]{1,0:T(8,128)(2,1)S(1)} %get-tuple-element.111), channel_id=1, source_target_pairs={{8,4},{10,6},{13,1},{15,3},{16,12},{18,14},{21,9},{23,11},{24,20},... | collective-permute-start | bytes 786440 | tf_op jit(solution)/shard_map/ppermute | solution.py:529
  146.1 1.3 collective-permute-start.26

commit v8 on v7

--- a/solution.py
+++ b/solution.py
@@ -155,7 +155,7 @@
 
 
 def routing(columns, me):
-    values = columns[...].astype(F32)
+    values = columns.astype(F32)
     named = jnp.where(values[:, 0:2] == me.astype(F32), 1.0, 0.0)
     gate = jnp.sum(named * values[:, 2:4], axis=1, keepdims=True) / 256.0
     return jnp.sum(named, axis=1, keepdims=True), gate
@@ -163,7 +163,7 @@
 
 def hidden_kernel(count, place, *refs):
     routes, rows = refs[:count], refs[count : 2 * count]
-    down_own, down_other, send, keep, gates, scaled = refs[2 * count :]
+    down_own, down_other, send, keep, handed, gates, scaled = refs[2 * count :]
     tok_rows = rows[0].shape[0]
     units = down_own.shape[0]
     step = pl.program_id(0)
@@ -171,7 +171,9 @@
     @pl.when(step == 0)
     def _():
         for k in range(count):
-            gates[k * tok_rows : (k + 1) * tok_rows, :] = routing(routes[k], place[1])[1]
+            at = pl.ds(k * tok_rows, tok_rows)
+            gates[at, :] = routing(routes[k][...], place[1])[1]
+            handed[at, :] = routes[k][...]
         keep[...] = jnp.zeros_like(keep)
 
     for k in range(count):
@@ -207,19 +209,19 @@
                 pl.BlockSpec((units, chunk), lambda i, place: (0, 4 * place[0] + i)),
                 pl.BlockSpec((units, chunk), lambda i, place: (0, i)),
             ],
-            out_specs=[pl.BlockSpec((tokens, 2 * units), lambda i, place: (0, 0))] * 2,
+            out_specs=[pl.BlockSpec((tokens, 2 * units), lambda i, place: (0, 0))] * 2
+            + [pl.BlockSpec((tokens, LANES), lambda i, place: (0, 0))],
             scratch_shapes=[pltpu.VMEM((tokens, 1), F32), pltpu.VMEM((tokens, chunk), BF16)],
         ),
-        out_shape=[jax.ShapeDtypeStruct((tokens, 2 * units), dtype) for dtype in (BF16, F32)],
+        out_shape=[jax.ShapeDtypeStruct((tokens, 2 * units), dtype) for dtype in (BF16, F32)]
+        + [jax.ShapeDtypeStruct((tokens, LANES), BF16)],
         compiler_params=params(),
         cost_estimate=cost(4 * tokens * half_width * units, 4 * units * half_width + 2 * tokens * half_width),
         name="hidden",
     )(place, *rows, *rows, down, down_other)
 
 
-def finish_kernel(count, place, *refs):
-    routes = refs[:count]
-    keep, got, pre_own, pre_other, up_own, up_other, out, pre_grad = refs[count:]
+def finish_kernel(count, place, routes, keep, got, pre_own, pre_other, up_own, up_other, out, pre_grad):
     tok_rows = pre_grad.shape[0] // count
     units = pre_own.shape[1]
 
@@ -228,7 +230,7 @@
         row, column = square(tok_rows)
         for k in range(count):
             at = pl.ds(k * tok_rows, tok_rows)
-            named, _ = routing(routes[k], place[1])
+            named, _ = routing(routes[at, :], place[1])
             rank = jnp.sum(jnp.where(row < column, named, 0.0), axis=0, keepdims=True).astype(jnp.int32)
             named = jnp.sum(jnp.where(row == column, named, 0.0), axis=0, keepdims=True)
             pick = jnp.where(rank == row, named, 0.0).astype(BF16)
@@ -245,9 +247,9 @@
     out[...] = value.astype(out.dtype)
 
 
-def expert_sums(place, rows, keep, got, pre, pre_other, up, up_other, dtype):
-    count = len(rows)
-    tokens = count * rows[0].shape[0]
+def expert_sums(place, routes, keep, got, pre, pre_other, up, up_other, dtype):
+    tokens = keep.shape[0]
+    count = place.shape[0] - 2
     units = pre.shape[1]
     half_width = up_other.shape[0]
     chunk = half_width // 4
@@ -256,8 +258,7 @@
         grid_spec=pltpu.PrefetchScalarGridSpec(
             num_scalar_prefetch=1,
             grid=(4,),
-            in_specs=[route_columns(rows[0])] * count
-            + [whole()] * 4
+            in_specs=[whole()] * 5
             + [
                 pl.BlockSpec((chunk, units), lambda i, place: (4 * place[0] + i, 0)),
                 pl.BlockSpec((chunk, units), lambda i, place: (i, 0)),
@@ -269,7 +270,7 @@
         compiler_params=params(),
         cost_estimate=cost(4 * tokens * half_width * units, 4 * units * half_width + 4 * tokens * half_width),
         name="experts",
-    )(place, *rows, keep, got, pre, pre_other, up, up_other)
+    )(place, routes, keep, got, pre, pre_other, up, up_other)
 
 
 def proj_kernel(count, with_taps, place, *refs):
@@ -461,31 +462,35 @@
 
     from_left, from_right = moved(rows_left, RIGHT[1:]), moved(rows_right, LEFT[1:])
     down_other, pre_other = swapped(down_send), swapped(pre_send)
-    next_head = moved(head, [(2, 0), (3, 1)])
-    from_left, from_right, down_other, pre_other, up_send, next_head = together(
-        from_left, from_right, down_other, pre_other, up_send, next_head
+    from_left, from_right, down_other, pre_other, up_send, head = together(
+        from_left, from_right, down_other, pre_other, up_send, head
     )
 
     def hidden(where, rows):
-        send, keep = hidden_sums(where, rows, w_down, down_other)
-        return keep, swapped(send)
-
-    def finish(where, rows, sums, dtype):
-        return expert_sums(where, rows, *sums, pre, pre_other, w_up, up_other, dtype)
+        send, keep, routes = hidden_sums(where, rows, w_down, down_other)
+        return routes, keep, swapped(send)
+
+    def finish(where, sums, dtype):
+        return expert_sums(where, *sums, pre, pre_other, w_up, up_other, dtype)
 
     far, end = place(far_block), place(end_block)
     rows_far = jnp.where(me >= 2, from_left, from_right)
     rows_end = moved(rows_far, [(2, 3), (1, 0)])
     up_other = swapped(up_send)
-    near_rows = [rows_own, rows_left, rows_right]
-    keep, got = hidden(near, near_rows)
-    rows_end, rows_far, keep, up_other, conv_own = together(rows_end, rows_far, keep, up_other, conv_own)
+    routes, keep, got = hidden(near, [rows_own, rows_left, rows_right])
+    next_head = moved(head, LEFT[:2])
+    rows_end, rows_far, keep, up_other, conv_own, next_head = together(
+        rows_end, rows_far, keep, up_other, conv_own, next_head
+    )
 
     conv_left, conv_right = moved(conv_own, RIGHT), moved(conv_own, LEFT)
     end_hidden = hidden(end, [rows_end])
-    far_keep, far_got = hidden(far, [rows_far])
-    end_sums = finish(end, [rows_end], end_hidden, BF16)
-    conv_left, conv_right, end_sums, keep, far_keep = together(conv_left, conv_right, end_sums, keep, far_keep)
+    far_routes, far_keep, far_got = hidden(far, [rows_far])
+    end_sums = finish(end, end_hidden, BF16)
+    next_head = moved(next_head, LEFT[1:])
+    conv_left, conv_right, end_sums, keep, far_keep, next_head = together(
+        conv_left, conv_right, end_sums, keep, far_keep, next_head
+    )
 
     from_left, from_right = moved(conv_left, RIGHT[1:]), moved(conv_right, LEFT[1:])
     back_end = moved(end_sums, [(0, 1), (3, 2)])
@@ -498,7 +503,7 @@
     near_proj, near_proj_got, tap_terms = proj(
         near, [conv_own, conv_left, conv_right], [conv_right, conv_own, next_head], conv_input[0]
     )
-    far_sums = finish(far, [rows_far], (far_keep, far_got), F32)
+    far_sums = finish(far, (far_routes, far_keep, far_got), F32)
     from_left, from_right, near_proj, conv_left, keep, far_sums = together(
         from_left, from_right, near_proj, conv_left, keep, far_sums
     )
@@ -508,7 +513,7 @@
     conv_end = moved(conv_far, [(2, 3), (1, 0)])
     back = (far_sums + back_end.astype(F32)).astype(BF16)
     back_right, back_left = moved(back, RIGHT[:2]), moved(back, LEFT[:2])
-    near_sums = finish(near, near_rows, (keep, got), F32)
+    near_sums = finish(near, (routes, keep, got), F32)
     conv_end, back_right, back_left, near_sums = together(conv_end, back_right, back_left, near_sums)
 
     to_right, to_left, own = combined(near, out_grad[0], near_sums, back_right, back_left, near_proj, near_proj_got)

time: 166 us -> 165 us (level)
  waiting for transfers between devices: 68.6 us -> 66 us
  starting transfers between devices: 40.1 us -> 42.2 us
    ppermute x16 -> x17, waiting for transfers between devices: 52.1 us -> 47.7 us  [moved(): return lax.ppermute(array, 'expert', pairs)]
    ppermute x16 -> x17, starting transfers between devices: 29.7 us -> 31.8 us  [moved(): return lax.ppermute(array, 'expert', pairs)]
    ppermute x6, waiting for transfers between devices: 0.02 us -> 1.93 us  [rotated(): lax.ppermute(array, axis, [(i, (i + by) % size) for i in range(size)])]
    unnamed x32 -> x28, local copies, waits for them, and re-layouts: 8.07 us -> 8.07 us
  transfers between devices with their start and end apart: 29 -> 30, of which waited for: 9 -> 10; matrix products, arithmetic and copies ran while one was open for 4% -> 4% of each run, Pallas kernels for 22% -> 22%
where the time goes in v8:
time: 165 us; the launch traced here: 164 us
  waiting for transfers between devices  66 us (40%)
  starting transfers between devices  42.2 us (26%)
  Pallas kernels  37.7 us (23%)
  local copies, waits for them, and re-layouts  13.1 us (8%)
  other arithmetic  4.21 us (3%)
    ppermute x17, waiting for transfers between devices, moved(): return lax.ppermute(array, 'expert', pairs)  47.7 us
    ppermute x17, starting transfers between devices, moved(): return lax.ppermute(array, 'expert', pairs)  31.8 us
    ppermute x1, waiting for transfers between devices, shifted(): return lax.ppermute(array, axis, pairs)  16.3 us
    pallas_call x3, Pallas kernels, expert_sums(): pl.pallas_call(functools.partial(finish_kernel, count), grid_spec=pltpu.P...  14.2 us
    pallas_call x3, Pallas kernels, hidden_sums(): pl.pallas_call(functools.partial(hidden_kernel, count), grid_spec=pltpu.P...  10.9 us
    pallas_call x2, Pallas kernels, proj_sums(): pl.pallas_call(functools.partial(proj_kernel, count, with_taps), grid=(ha...  9.93 us
    unnamed x28, local copies, waits for them, and re-layouts  8.07 us
    ppermute x2, starting transfers between devices, doubling_sum(): lax.ppermute(array, axis, [(i, i ^ step) for i in range(size)])  3.4 us
  transfers between devices with their start and end apart: 30, of which 10 were waited for; matrix products, arithmetic and copies ran while one was open for 4% of the time, Pallas kernels for 22%

profile of v8, /device:TPU:0, one launch (start us, length us, event | category | flops | bytes accessed | tf_op | source)
XLA Modules:
  0.0 164.3 jit_solution(5004265684974487457)
XLA Ops:
  1.5 1.1 fusion.1.refs_0_.refs_3_
  2.6 5.0 %collective-permute-start = (bf16[128,2176]{1,0:T(8,128)(2,1)S(1)}, bf16[128,2176]{1,0:T(8,128)(2,1)S(1)}, u32[]{:S(2)}, u32[]{:S(2)}) collective-permute-start(bf16[128,2176]{1,0:T(8,128)(2,1)S(1)} %fusion.1.refs_0_.refs_3_), channel_id=1, source_target_pairs={{0,2},{2,4},{4,6},{1,3},{3,5},{5,7},{8,10},{10,12},{12,14},{9,11},... | collective-permute-start | bytes 1671176 | tf_op jit(solution)/shard_map/ppermute | solution.py:418
  7.5 1.3 collective-permute-start.1
  8.9 3.3 %dynamic-slice_bitcast_fusion.1 = bf16[512,2048]{1,0:T(8,128)(2,1)} fusion(bf16[1,1,512,4096]{3,2,1,0:T(8,128)(2,1)} %param.14, s32[]{:T(128)S(6)} %select_n.41), kind=kLoop, calls=%fused_computation.1 | loop fusion | bytes 4194308 | tf_op jit(solution)/shard_map/dynamic_slice | solution.py:457
  12.2 1.5 dynamic-slice_bitcast_fusion
  13.7 5.7 %collective-permute-done.refs_1_.refs_4_ = bf16[128,2176]{1,0:T(8,128)(2,1)S(1)} collective-permute-done((bf16[128,2176]{1,0:T(8,128)(2,1)S(1)}, bf16[128,2176]{1,0:T(8,128)(2,1)S(1)}, u32[]{:S(2)}, u32[]{:S(2)}) %collective-permute-start) | collective-permute-done | bytes 557088 | tf_op jit(solution)/shard_map/ppermute | solution.py:418
  19.4 4.1 %collective-permute-done.1.refs_2_.refs_5_ = bf16[128,2176]{1,0:T(8,128)(2,1)S(1)} collective-permute-done((bf16[128,2176]{1,0:T(8,128)(2,1)S(1)}, bf16[128,2176]{1,0:T(8,128)(2,1)S(1)}, u32[]{:S(2)}, u32[]{:S(2)}) %collective-permute-start.1) | collective-permute-done | bytes 557088 | tf_op jit(solution)/shard_map/ppermute | solution.py:418
  23.5 0.8 copy-done.10
  24.3 1.5 collective-permute-start.2
  25.8 1.3 collective-permute-start.3
  27.7 1.9 %collective-permute-done.5.pre_other = bf16[512,512]{1,0:T(8,128)(2,1)} collective-permute-done((bf16[512,512]{1,0:T(8,128)(2,1)}, bf16[512,512]{1,0:T(8,128)(2,1)}, u32[]{:S(2)}, u32[]{:S(2)}) %collective-permute-start.5) | collective-permute-done | bytes 524320 | tf_op jit(solution)/shard_map/ppermute | solution.py:129
  29.6 15.8 %collective-permute-done.3 = bf16[128,2176]{1,0:T(8,128)(2,1)} collective-permute-done((bf16[128,2176]{1,0:T(8,128)(2,1)}, bf16[128,2176]{1,0:T(8,128)(2,1)}, u32[]{:S(2)}, u32[]{:S(2)}) %collective-permute-start.3) | collective-permute-done | bytes 557088 | tf_op jit(solution)/shard_map/ppermute | solution.py:418
  45.4 1.3 copy-done.6
  47.0 1.1 broadcast_select_fusion.refs_0_.refs_1_
  48.1 1.3 collective-permute-start.6
  50.1 2.2 %copy-done.1 = bf16[1,1,512,4096]{3,2,1,0:T(8,128)(2,1)S(1)} copy-done((bf16[1,1,512,4096]{3,2,1,0:T(8,128)(2,1)S(1)}, bf16[1,1,512,4096]{3,2,1,0:T(8,128)(2,1)}, u32[]{:S(2)}) %copy-start.1) | copy-done | bytes 4194328
  52.3 1.6 copy-done.7
  53.9 1.1 copy-done.9
  54.9 1.1 copy-done.11
  56.0 4.3 %hidden.3 = (bf16[384,1024]{1,0:T(8,128)(2,1)S(1)}, f32[384,1024]{1,0:T(8,128)S(1)}, bf16[384,128]{1,0:T(8,128)(2,1)S(1)}) custom-call(s32[5]{0:T(128)S(1)} %stack.43.place, bf16[128,2176]{1,0:T(8,128)(2,1)S(1)} %fusion.1.refs_0_.refs_3_, bf16[128,2176]{1,0:T(8,128)(2,1)S(1)} %copy-done.9, bf16[128,2176]{1,0:T(8,128)(2,1)S(1)} %copy-done.11, ...), custom_call_target="tpu_custom_call" | custom-call | flops 12884901888 | bytes 46137344 | tf_op jit(solution)/shard_map/hidden/pallas_call | solution.py:201
  60.9 4.2 %collective-permute-done.6.refs_0_.refs_1_ = bf16[128,2176]{1,0:T(8,128)(2,1)S(1)} collective-permute-done((bf16[128,2176]{1,0:T(8,128)(2,1)S(1)}, bf16[128,2176]{1,0:T(8,128)(2,1)S(1)}, u32[]{:S(2)}, u32[]{:S(2)}) %collective-permute-start.6) | collective-permute-done | bytes 557088 | tf_op jit(solution)/shard_map/ppermute | solution.py:418
  65.0 1.5 collective-permute-start.9
  66.5 1.3 collective-permute-start.10
  67.8 3.3 %hidden.4 = (bf16[128,1024]{1,0:T(8,128)(2,1)S(1)}, f32[128,1024]{1,0:T(8,128)S(1)}, bf16[128,128]{1,0:T(8,128)(2,1)S(1)}) custom-call(s32[3]{0:T(128)S(1)} %get-tuple-element.122.place, bf16[128,2176]{1,0:T(8,128)(2,1)S(1)} %collective-permute-done.6.refs_0_.refs_1_, bf16[128,2176]{1,0:T(8,128)(2,1)S(1)} %collective-permute-done.6.refs_0_.refs_1_, ...), custom_call_target="tpu_custom_call" | custom-call | flops 4294967296 | bytes 37748736 | tf_op jit(solution)/shard_map/hidden/pallas_call | solution.py:201
  71.2 1.3 collective-permute-start.12
  72.5 3.3 %hidden.5 = (bf16[128,1024]{1,0:T(8,128)(2,1)S(1)}, f32[128,1024]{1,0:T(8,128)S(1)}, bf16[128,128]{1,0:T(8,128)(2,1)S(1)}) custom-call(s32[3]{0:T(128)S(1)} %get-tuple-element.123.place, bf16[128,2176]{1,0:T(8,128)(2,1)S(1)} %broadcast_select_fusion.refs_0_.refs_1_, bf16[128,2176]{1,0:T(8,128)(2,1)S(1)} %broadcast_select_fusion.refs_0_.refs_1_, ...), custom_call_target="tpu_custom_call" | custom-call | flops 4294967296 | bytes 37748736 | tf_op jit(solution)/shard_map/hidden/pallas_call | solution.py:201
  76.4 4.6 %experts.3 = bf16[128,2048]{1,0:T(8,128)(2,1)S(1)} custom-call(s32[3]{0:T(128)S(1)} %get-tuple-element.122.place, bf16[128,128]{1,0:T(8,128)(2,1)S(1)} %get-tuple-element.75.routes, f32[128,1024]{1,0:T(8,128)S(1)} %get-tuple-element.76.keep, bf16[128,1024]{1,0:T(8,128)(2,1)S(1)} %collective-permute-done.11.got, bf16[512,512]{1,0:T(8,128)(2,1)} %bitcast.9.pre_own, ...), custom_call_target="tpu_custom_call" | custom-call | flops 4294967296 | bytes 41943040 | tf_op jit(solution)/shard_map/experts/pallas_call | solution.py:256
  81.0 2.9 %collective-permute-done.12.refs_5_ = bf16[16,2048]{1,0:T(8,128)(2,1)S(1)} collective-permute-done((bf16[16,2048]{1,0:T(8,128)(2,1)S(1)}, bf16[16,2048]{1,0:T(8,128)(2,1)S(1)}, u32[]{:S(2)}, u32[]{:S(2)}) %collective-permute-start.12) | collective-permute-done | bytes 65568 | tf_op jit(solution)/shard_map/ppermute | solution.py:418
  84.6 1.3 collective-permute-start.14
  85.9 6.0 %collective-permute-start.16 = (bf16[128,2048]{1,0:T(8,128)(2,1)S(1)}, bf16[128,2048]{1,0:T(8,128)(2,1)S(1)}, u32[]{:S(2)}, u32[]{:S(2)}) collective-permute-start(bf16[128,2048]{1,0:T(8,128)(2,1)S(1)} %experts.3), channel_id=1, source_target_pairs={{0,2},{6,4},{1,3},{7,5},{8,10},{14,12},{9,11},{15,13},{16,18},{22,... | collective-permute-start | bytes 1572872 | tf_op jit(solution)/shard_map/ppermute | solution.py:418
  91.9 5.9 %projection.2 = (bf16[384,1024]{1,0:T(8,128)(2,1)S(1)}, f32[384,1024]{1,0:T(8,128)S(1)}, f32[4,2048]{1,0:T(4,128)S(1)}) custom-call(s32[5]{0:T(128)S(1)} %stack.43.place, bf16[128,2048]{1,0:T(8,128)(2,1)S(1)} %bitcast.37, bf16[128,2048]{1,0:T(8,128)(2,1)S(1)} %collective-permute-done.9.refs_1_, ...), custom_call_target="tpu_custom_call" | custom-call | flops 12884901888 | bytes 65011712 | tf_op jit(solution)/shard_map/projection/pallas_call | solution.py:337
  97.8 1.3 collective-permute-start.21
  99.1 4.3 %experts.4 = f32[128,2048]{1,0:T(8,128)S(1)} custom-call(s32[3]{0:T(128)S(1)} %get-tuple-element.123.place, bf16[128,128]{1,0:T(8,128)(2,1)S(1)} %get-tuple-element.89.routes, f32[128,1024]{1,0:T(8,128)S(1)} %get-tuple-element.90.keep, bf16[128,1024]{1,0:T(8,128)(2,1)S(1)} %collective-permute-done.15.got, bf16[512,512]{1,0:T(8,128)(2,1)} %bitcast.9.pre_own, ...), custom_call_target="tpu_custom_call" | custom-call | flops 4294967296 | bytes 41943040 | tf_op jit(solution)/shard_map/experts/pallas_call | solution.py:256
  103.7 4.0 %collective-permute-start.18 = (bf16[128,2048]{1,0:T(8,128)(2,1)S(1)}, bf16[128,2048]{1,0:T(8,128)(2,1)S(1)}, u32[]{:S(2)}, u32[]{:S(2)}) collective-permute-start(bf16[128,2048]{1,0:T(8,128)(2,1)S(1)} %add_convert_fusion.1), channel_id=1, source_target_pairs={{0,2},{2,4},{1,3},{3,5},{8,10},{10,12},{9,11},{11,13},{16,18},{18,... | collective-permute-start | bytes 1572872 | tf_op jit(solution)/shard_map/ppermute | solution.py:418
  108.4 1.3 collective-permute-start.17
  109.7 5.4 %experts.5.sums = f32[384,2048]{1,0:T(8,128)S(1)} custom-call(s32[5]{0:T(128)S(1)} %stack.43.place, bf16[384,128]{1,0:T(8,128)(2,1)S(1)} %get-tuple-element.98.routes, f32[384,1024]{1,0:T(8,128)S(1)} %get-tuple-element.99.keep, bf16[384,1024]{1,0:T(8,128)(2,1)S(1)} %collective-permute-done.20.got, bf16[512,512]{1,0:T(8,128)(2,1)} %bitcast.9.pre_own, ...), custom_call_target="tpu_custom_call" | custom-call | flops 12884901888 | bytes 58720256 | tf_op jit(solution)/shard_map/experts/pallas_call | solution.py:256
  115.1 9.6 %collective-permute-done.17.refs_1_ = bf16[128,2048]{1,0:T(8,128)(2,1)S(1)} collective-permute-done((bf16[128,2048]{1,0:T(8,128)(2,1)S(1)}, bf16[128,2048]{1,0:T(8,128)(2,1)S(1)}, u32[]{:S(2)}, u32[]{:S(2)}) %collective-permute-start.17) | collective-permute-done | bytes 524320 | tf_op jit(solution)/shard_map/ppermute | solution.py:418
  124.7 1.2 combine.1
  125.9 1.5 collective-permute-start.22
  127.4 1.3 collective-permute-start.23
  128.7 4.0 %projection.3 = (bf16[256,1024]{1,0:T(8,128)(2,1)S(1)}, f32[256,1024]{1,0:T(8,128)S(1)}) custom-call(s32[4]{0:T(128)S(1)} %pad_add_fusion.3.place, bf16[128,2048]{1,0:T(8,128)(2,1)S(1)} %broadcast_select_fusion.1.refs_0_.refs_3_, bf16[128,2048]{1,0:T(8,128)(2,1)S(1)} %collective-permute-done.17.refs_1_, bf16[16,2048]{1,0:T(8,128)(2,1)S(1)} %slice_select_fusion.refs_2_, ...), custom_call_target="tpu_custom_call" | custom-call | flops 8589934592 | bytes 54525952 | tf_op jit(solution)/shard_map/projection/pallas_call | solution.py:337
  132.7 1.3 collective-permute-start.25
  134.1 3.3 %collective-permute-start.29 = (f32[4,2048]{1,0:T(4,128)S(1)}, f32[4,2048]{1,0:T(4,128)S(1)}, u32[]{:S(2)}, u32[]{:S(2)}) collective-permute-start(f32[4,2048]{1,0:T(4,128)S(1)} %add.47), channel_id=1, source_target_pairs={{0,4},{2,6},{4,0},{6,2},{1,5},{3,7},{5,1},{7,3},{8,12},{10,14},{12... | collective-permute-start | bytes 98312 | tf_op jit(solution)/shard_map/ppermute | solution.py:139
  137.4 1.3 collective-permute-done.22
  138.7 4.2 %collective-permute-done.23 = bf16[128,2048]{1,0:T(8,128)(2,1)S(1)} collective-permute-done((bf16[128,2048]{1,0:T(8,128)(2,1)S(1)}, bf16[128,2048]{1,0:T(8,128)(2,1)S(1)}, u32[]{:S(2)}, u32[]{:S(2)}) %collective-permute-start.23) | collective-permute-done | bytes 524320 | tf_op jit(solution)/shard_map/ppermute | solution.py:418
  143.0 1.3 collective-permute-start.24
  146.5 16.3 %collective-permute-done.24.residual = bf16[128,2048]{1,0:T(8,128)(2,1)S(1)} collective-permute-done((bf16[128,2048]{1,0:T(8,128)(2,1)S(1)}, bf16[128,2048]{1,0:T(8,128)(2,1)S(1)}, u32[]{:S(2)}, u32[]{:S(2)}) %collective-permute-start.24) | collective-permute-done | bytes 524320 | tf_op jit(solution)/shard_map/ppermute | solution.py:14
  162.8 1.5 residual.1
  (68 shorter events, 7.6 us)
Async XLA Ops:
  2.6 16.8 %collective-permute-start = (bf16[128,2176]{1,0:T(8,128)(2,1)S(1)}, bf16[128,2176]{1,0:T(8,128)(2,1)S(1)}, u32[]{:S(2)}, u32[]{:S(2)}) collective-permute-start(bf16[128,2176]{1,0:T(8,128)(2,1)S(1)} %fusion.1.refs_0_.refs_3_), channel_id=1, source_target_pairs={{0,2},{2,4},{4,6},{1,3},{3,5},{5,7},{8,10},{10,12},{12,14},{9,11},... | collective-permute-start | bytes 1671176 | tf_op jit(solution)/shard_map/ppermute | solution.py:418
  7.5 16.0 %collective-permute-start.1 = (bf16[128,2176]{1,0:T(8,128)(2,1)S(1)}, bf16[128,2176]{1,0:T(8,128)(2,1)S(1)}, u32[]{:S(2)}, u32[]{:S(2)}) collective-permute-start(bf16[128,2176]{1,0:T(8,128)(2,1)S(1)} %fusion.1.refs_0_.refs_3_), channel_id=1, source_target_pairs={{6,4},{4,2},{2,0},{7,5},{5,3},{3,1},{14,12},{12,10},{10,8},{15,13}... | collective-permute-start | bytes 1671176 | tf_op jit(solution)/shard_map/ppermute | solution.py:418
  8.8 3.3 %copy-start.2 = (bf16[1,1,4096,512]{3,2,1,0:T(8,128)(2,1)S(1)}, bf16[1,1,4096,512]{3,2,1,0:T(8,128)(2,1)}, u32[]{:S(2)}) copy-start(bf16[1,1,4096,512]{3,2,1,0:T(8,128)(2,1)} %param.13) | copy-start | bytes 12582916
  12.2 1.5 copy-start.4
  19.4 4.2 %copy-start.8 = (bf16[128,2176]{1,0:T(8,128)(2,1)}, bf16[128,2176]{1,0:T(8,128)(2,1)S(1)}, u32[]{:S(2)}) copy-start(bf16[128,2176]{1,0:T(8,128)(2,1)S(1)} %collective-permute-done.refs_1_.refs_4_) | copy-start | bytes 1671172
  23.5 0.8 copy-start.10
  24.3 21.1 %collective-permute-start.4 = (bf16[512,2048]{1,0:T(8,128)(2,1)}, bf16[512,2048]{1,0:T(8,128)(2,1)S(1)}, u32[]{:S(2)}, u32[]{:S(2)}) collective-permute-start(bf16[512,2048]{1,0:T(8,128)(2,1)} %dynamic-slice_bitcast_fusion.1), channel_id=1, source_target_pairs={{0,1},{1,0},{2,3},{3,2},{4,5},{5,4},{6,7},{7,6},{8,9},{9,8},{10,11... | collective-permute-start | bytes 6291464 | tf_op jit(solution)/shard_map/ppermute | solution.py:129
  24.3 5.3 %collective-permute-start.2 = (bf16[128,2176]{1,0:T(8,128)(2,1)}, bf16[128,2176]{1,0:T(8,128)(2,1)}, u32[]{:S(2)}, u32[]{:S(2)}) collective-permute-start(bf16[128,2176]{1,0:T(8,128)(2,1)} %copy-done.8), channel_id=1, source_target_pairs={{2,4},{4,6},{3,5},{5,7},{10,12},{12,14},{11,13},{13,15},{18,20},{2... | collective-permute-start | bytes 1671176 | tf_op jit(solution)/shard_map/ppermute | solution.py:418
  25.8 19.6 %collective-permute-start.3 = (bf16[128,2176]{1,0:T(8,128)(2,1)}, bf16[128,2176]{1,0:T(8,128)(2,1)}, u32[]{:S(2)}, u32[]{:S(2)}) collective-permute-start(bf16[128,2176]{1,0:T(8,128)(2,1)} %copy-done.10), channel_id=1, source_target_pairs={{4,2},{2,0},{5,3},{3,1},{12,10},{10,8},{13,11},{11,9},{20,18},{18,... | collective-permute-start | bytes 1671176 | tf_op jit(solution)/shard_map/ppermute | solution.py:418
  27.1 2.5 %collective-permute-start.5 = (bf16[512,512]{1,0:T(8,128)(2,1)}, bf16[512,512]{1,0:T(8,128)(2,1)}, u32[]{:S(2)}, u32[]{:S(2)}) collective-permute-start(bf16[512,512]{1,0:T(8,128)(2,1)} %bitcast.9.pre_own), channel_id=1, source_target_pairs={{0,1},{1,0},{2,3},{3,2},{4,5},{5,4},{6,7},{7,6},{8,9},{9,8},{10,11... | collective-permute-start | bytes 1572872 | tf_op jit(solution)/shard_map/ppermute | solution.py:129
  45.4 1.3 copy-start.6
  46.7 18.3 %collective-permute-start.7 = (bf16[2048,512]{1,0:T(8,128)(2,1)}, bf16[2048,512]{1,0:T(8,128)(2,1)S(1)}, u32[]{:S(2)}, u32[]{:S(2)}) collective-permute-start(bf16[2048,512]{1,0:T(8,128)(2,1)} %dynamic-slice_bitcast_fusion), channel_id=1, source_target_pairs={{0,1},{1,0},{2,3},{3,2},{4,5},{5,4},{6,7},{7,6},{8,9},{9,8},{10,11... | collective-permute-start | bytes 6291464 | tf_op jit(solution)/shard_map/ppermute | solution.py:129
  48.1 16.9 %collective-permute-start.6 = (bf16[128,2176]{1,0:T(8,128)(2,1)S(1)}, bf16[128,2176]{1,0:T(8,128)(2,1)S(1)}, u32[]{:S(2)}, u32[]{:S(2)}) collective-permute-start(bf16[128,2176]{1,0:T(8,128)(2,1)S(1)} %broadcast_select_fusion.refs_0_.refs_1_), channel_id=1, source_target_pairs={{4,6},{2,0},{5,7},{3,1},{12,14},{10,8},{13,15},{11,9},{20,22},{18,... | collective-permute-start | bytes 1671176 | tf_op jit(solution)/shard_map/ppermute | solution.py:418
  49.4 11.5 %collective-permute-start.8 = (bf16[16,2048]{1,0:T(8,128)(2,1)S(1)}, bf16[16,2048]{1,0:T(8,128)(2,1)S(1)}, u32[]{:S(2)}, u32[]{:S(2)}) collective-permute-start(bf16[16,2048]{1,0:T(8,128)(2,1)S(1)} %slice_bitcast_fusion), channel_id=1, source_target_pairs={{6,4},{4,2},{7,5},{5,3},{14,12},{12,10},{15,13},{13,11},{22,20},{2... | collective-permute-start | bytes 196616 | tf_op jit(solution)/shard_map/ppermute | solution.py:418
  50.1 2.2 %copy-start.1 = (bf16[1,1,512,4096]{3,2,1,0:T(8,128)(2,1)S(1)}, bf16[1,1,512,4096]{3,2,1,0:T(8,128)(2,1)}, u32[]{:S(2)}) copy-start(bf16[1,1,512,4096]{3,2,1,0:T(8,128)(2,1)} %param.14) | copy-start | bytes 12582916
  52.3 1.6 copy-start.7
  53.9 1.1 copy-start.9
  54.9 1.1 copy-start.11
  60.3 48.1 %collective-permute-start.20 = (bf16[384,1024]{1,0:T(8,128)(2,1)S(1)}, bf16[384,1024]{1,0:T(8,128)(2,1)S(1)}, u32[]{:S(2)}, u32[]{:S(2)}) collective-permute-start(bf16[384,1024]{1,0:T(8,128)(2,1)S(1)} %get-tuple-element.100), channel_id=1, source_target_pairs={{0,1},{1,0},{2,3},{3,2},{4,5},{5,4},{6,7},{7,6},{8,9},{9,8},{10,11... | collective-permute-start | bytes 2359304 | tf_op jit(solution)/shard_map/ppermute | solution.py:129
  65.0 18.8 %collective-permute-start.9 = (bf16[128,2048]{1,0:T(8,128)(2,1)S(1)}, bf16[128,2048]{1,0:T(8,128)(2,1)S(1)}, u32[]{:S(2)}, u32[]{:S(2)}) collective-permute-start(bf16[128,2048]{1,0:T(8,128)(2,1)S(1)} %bitcast.35), channel_id=1, source_target_pairs={{0,2},{2,4},{4,6},{1,3},{3,5},{5,7},{8,10},{10,12},{12,14},{9,11},... | collective-permute-start | bytes 1572872 | tf_op jit(solution)/shard_map/ppermute | solution.py:418
  66.5 17.3 %collective-permute-start.10 = (bf16[128,2048]{1,0:T(8,128)(2,1)S(1)}, bf16[128,2048]{1,0:T(8,128)(2,1)S(1)}, u32[]{:S(2)}, u32[]{:S(2)}) collective-permute-start(bf16[128,2048]{1,0:T(8,128)(2,1)S(1)} %bitcast.36), channel_id=1, source_target_pairs={{6,4},{4,2},{2,0},{7,5},{5,3},{3,1},{14,12},{12,10},{10,8},{15,13}... | collective-permute-start | bytes 1572872 | tf_op jit(solution)/shard_map/ppermute | solution.py:418
  71.1 4.7 %collective-permute-start.11 = (bf16[128,1024]{1,0:T(8,128)(2,1)S(1)}, bf16[128,1024]{1,0:T(8,128)(2,1)S(1)}, u32[]{:S(2)}, u32[]{:S(2)}) collective-permute-start(bf16[128,1024]{1,0:T(8,128)(2,1)S(1)} %get-tuple-element.77), channel_id=1, source_target_pairs={{0,1},{1,0},{2,3},{3,2},{4,5},{5,4},{6,7},{7,6},{8,9},{9,8},{10,11... | collective-permute-start | bytes 786440 | tf_op jit(solution)/shard_map/ppermute | solution.py:129
  71.2 12.7 %collective-permute-start.12 = (bf16[16,2048]{1,0:T(8,128)(2,1)S(1)}, bf16[16,2048]{1,0:T(8,128)(2,1)S(1)}, u32[]{:S(2)}, u32[]{:S(2)}) collective-permute-start(bf16[16,2048]{1,0:T(8,128)(2,1)S(1)} %collective-permute-done.8), channel_id=1, source_target_pairs={{4,2},{2,0},{5,3},{3,1},{12,10},{10,8},{13,11},{11,9},{20,18},{18,... | collective-permute-start | bytes 196616 | tf_op jit(solution)/shard_map/ppermute | solution.py:418
  72.5 3.9 %copy-start.3 = (bf16[1,1,4096,512]{3,2,1,0:T(8,128)(2,1)S(1)}, bf16[1,1,4096,512]{3,2,1,0:T(8,128)(2,1)}, u32[]{:S(2)}) copy-start(bf16[1,1,4096,512]{3,2,1,0:T(8,128)(2,1)} %param.13) | copy-start | bytes 12582916
  75.8 22.0 %collective-permute-start.15 = (bf16[128,1024]{1,0:T(8,128)(2,1)S(1)}, bf16[128,1024]{1,0:T(8,128)(2,1)S(1)}, u32[]{:S(2)}, u32[]{:S(2)}) collective-permute-start(bf16[128,1024]{1,0:T(8,128)(2,1)S(1)} %get-tuple-element.91), channel_id=1, source_target_pairs={{0,1},{1,0},{2,3},{3,2},{4,5},{5,4},{6,7},{7,6},{8,9},{9,8},{10,11... | collective-permute-start | bytes 786440 | tf_op jit(solution)/shard_map/ppermute | solution.py:129
  76.4 15.4 %copy-start.5 = (bf16[1,1024,2048]{2,1,0:T(8,128)(2,1)S(1)}, bf16[1,1024,2048]{2,1,0:T(8,128)(2,1)}, u32[]{:S(2)}) copy-start(bf16[1,1024,2048]{2,1,0:T(8,128)(2,1)} %param.19) | copy-start | bytes 12582916
  76.4 15.5 %copy-start.12 = (bf16[1,128,2048]{2,1,0:T(8,128)(2,1)S(1)}, bf16[1,128,2048]{2,1,0:T(8,128)(2,1)}, u32[]{:S(2)}) copy-start(bf16[1,128,2048]{2,1,0:T(8,128)(2,1)} %param.17) | copy-start | bytes 1572868
  76.4 15.5 %copy-start.13 = (f32[1,4,2048]{2,1,0:T(4,128)S(1)}, f32[1,4,2048]{2,1,0:T(4,128)}, u32[]{:S(2)}) copy-start(f32[1,4,2048]{2,1,0:T(4,128)} %param.18) | copy-start | bytes 98308
  83.9 19.5 %collective-permute-start.13 = (bf16[128,2048]{1,0:T(8,128)(2,1)S(1)}, bf16[128,2048]{1,0:T(8,128)(2,1)S(1)}, u32[]{:S(2)}, u32[]{:S(2)}) collective-permute-start(bf16[128,2048]{1,0:T(8,128)(2,1)S(1)} %collective-permute-done.9.refs_1_), channel_id=1, source_target_pairs={{2,4},{4,6},{3,5},{5,7},{10,12},{12,14},{11,13},{13,15},{18,20},{2... | collective-permute-start | bytes 1572872 | tf_op jit(solution)/shard_map/ppermute | solution.py:418
  84.6 18.9 %collective-permute-start.14 = (bf16[128,2048]{1,0:T(8,128)(2,1)S(1)}, bf16[128,2048]{1,0:T(8,128)(2,1)S(1)}, u32[]{:S(2)}, u32[]{:S(2)}) collective-permute-start(bf16[128,2048]{1,0:T(8,128)(2,1)S(1)} %collective-permute-done.10.refs_2_.refs_3_), channel_id=1, source_target_pairs={{4,2},{2,0},{5,3},{3,1},{12,10},{10,8},{13,11},{11,9},{20,18},{18,... | collective-permute-start | bytes 1572872 | tf_op jit(solution)/shard_map/ppermute | solution.py:418
  85.9 17.7 %collective-permute-start.16 = (bf16[128,2048]{1,0:T(8,128)(2,1)S(1)}, bf16[128,2048]{1,0:T(8,128)(2,1)S(1)}, u32[]{:S(2)}, u32[]{:S(2)}) collective-permute-start(bf16[128,2048]{1,0:T(8,128)(2,1)S(1)} %experts.3), channel_id=1, source_target_pairs={{0,2},{6,4},{1,3},{7,5},{8,10},{14,12},{9,11},{15,13},{16,18},{22,... | collective-permute-start | bytes 1572872 | tf_op jit(solution)/shard_map/ppermute | solution.py:418
  97.8 26.9 %collective-permute-start.21 = (bf16[384,1024]{1,0:T(8,128)(2,1)S(1)}, bf16[384,1024]{1,0:T(8,128)(2,1)S(1)}, u32[]{:S(2)}, u32[]{:S(2)}) collective-permute-start(bf16[384,1024]{1,0:T(8,128)(2,1)S(1)} %get-tuple-element.105), channel_id=1, source_target_pairs={{1,0},{3,2},{4,5},{6,7},{9,8},{11,10},{12,13},{14,15},{17,16},{19,... | collective-permute-start | bytes 2359304 | tf_op jit(solution)/shard_map/ppermute | solution.py:501
  103.4 30.6 %collective-permute-start.28 = (f32[4,2048]{1,0:T(4,128)S(1)}, f32[4,2048]{1,0:T(4,128)S(1)}, u32[]{:S(2)}, u32[]{:S(2)}) collective-permute-start(f32[4,2048]{1,0:T(4,128)S(1)} %get-tuple-element.119), channel_id=1, source_target_pairs={{0,2},{2,0},{4,6},{6,4},{1,3},{3,1},{5,7},{7,5},{8,10},{10,8},{12,... | collective-permute-start | bytes 98312 | tf_op jit(solution)/shard_map/ppermute | solution.py:139
  103.7 21.0 %collective-permute-start.18 = (bf16[128,2048]{1,0:T(8,128)(2,1)S(1)}, bf16[128,2048]{1,0:T(8,128)(2,1)S(1)}, u32[]{:S(2)}, u32[]{:S(2)}) collective-permute-start(bf16[128,2048]{1,0:T(8,128)(2,1)S(1)} %add_convert_fusion.1), channel_id=1, source_target_pairs={{0,2},{2,4},{1,3},{3,5},{8,10},{10,12},{9,11},{11,13},{16,18},{18,... | collective-permute-start | bytes 1572872 | tf_op jit(solution)/shard_map/ppermute | solution.py:418
  107.7 17.0 %collective-permute-start.19 = (bf16[128,2048]{1,0:T(8,128)(2,1)S(1)}, bf16[128,2048]{1,0:T(8,128)(2,1)S(1)}, u32[]{:S(2)}, u32[]{:S(2)}) collective-permute-start(bf16[128,2048]{1,0:T(8,128)(2,1)S(1)} %add_convert_fusion.1), channel_id=1, source_target_pairs={{6,4},{4,2},{7,5},{5,3},{14,12},{12,10},{15,13},{13,11},{22,20},{2... | collective-permute-start | bytes 1572872 | tf_op jit(solution)/shard_map/ppermute | solution.py:418
  108.4 16.3 %collective-permute-start.17 = (bf16[128,2048]{1,0:T(8,128)(2,1)S(1)}, bf16[128,2048]{1,0:T(8,128)(2,1)S(1)}, u32[]{:S(2)}, u32[]{:S(2)}) collective-permute-start(bf16[128,2048]{1,0:T(8,128)(2,1)S(1)} %broadcast_select_fusion.1.refs_0_.refs_3_), channel_id=1, source_target_pairs={{4,6},{2,0},{5,7},{3,1},{12,14},{10,8},{13,15},{11,9},{20,22},{18,... | collective-permute-start | bytes 1572872 | tf_op jit(solution)/shard_map/ppermute | solution.py:418
  109.7 15.0 %copy-start = (bf16[1,128,2048]{2,1,0:T(8,128)(2,1)S(1)}, bf16[1,128,2048]{2,1,0:T(8,128)(2,1)}, u32[]{:S(2)}) copy-start(bf16[1,128,2048]{2,1,0:T(8,128)(2,1)} %param.10) | copy-start | bytes 1572868
  125.9 12.8 %collective-permute-start.22 = (bf16[128,2048]{1,0:T(8,128)(2,1)S(1)}, bf16[128,2048]{1,0:T(8,128)(2,1)S(1)}, u32[]{:S(2)}, u32[]{:S(2)}) collective-permute-start(bf16[128,2048]{1,0:T(8,128)(2,1)S(1)} %get-tuple-element.110), channel_id=1, source_target_pairs={{0,2},{2,4},{4,6},{1,3},{3,5},{5,7},{8,10},{10,12},{12,14},{9,11},... | collective-permute-start | bytes 1572872 | tf_op jit(solution)/shard_map/ppermute | solution.py:418
  127.4 15.4 %collective-permute-start.23 = (bf16[128,2048]{1,0:T(8,128)(2,1)S(1)}, bf16[128,2048]{1,0:T(8,128)(2,1)S(1)}, u32[]{:S(2)}, u32[]{:S(2)}) collective-permute-start(bf16[128,2048]{1,0:T(8,128)(2,1)S(1)} %get-tuple-element.111), channel_id=1, source_target_pairs={{6,4},{4,2},{2,0},{7,5},{5,3},{3,1},{14,12},{12,10},{10,8},{15,13}... | collective-permute-start | bytes 1572872 | tf_op jit(solution)/shard_map/ppermute | solution.py:418
  132.7 11.6 %collective-permute-start.25 = (bf16[256,1024]{1,0:T(8,128)(2,1)S(1)}, bf16[256,1024]{1,0:T(8,128)(2,1)S(1)}, u32[]{:S(2)}, u32[]{:S(2)}) collective-permute-start(bf16[256,1024]{1,0:T(8,128)(2,1)S(1)} %get-tuple-element.118), channel_id=1, source_target_pairs={{1,0},{3,2},{4,5},{6,7},{9,8},{11,10},{12,13},{14,15},{17,16},{19,... | collective-permute-start | bytes 1572872 | tf_op jit(solution)/shard_map/ppermute | solution.py:501
  134.1 11.8 %collective-permute-start.29 = (f32[4,2048]{1,0:T(4,128)S(1)}, f32[4,2048]{1,0:T(4,128)S(1)}, u32[]{:S(2)}, u32[]{:S(2)}) collective-permute-start(f32[4,2048]{1,0:T(4,128)S(1)} %add.47), channel_id=1, source_target_pairs={{0,4},{2,6},{4,0},{6,2},{1,5},{3,7},{5,1},{7,3},{8,12},{10,14},{12... | collective-permute-start | bytes 98312 | tf_op jit(solution)/shard_map/ppermute | solution.py:139
  143.0 19.8 %collective-permute-start.24 = (bf16[128,2048]{1,0:T(8,128)(2,1)S(1)}, bf16[128,2048]{1,0:T(8,128)(2,1)S(1)}, u32[]{:S(2)}, u32[]{:S(2)}) collective-permute-start(bf16[128,2048]{1,0:T(8,128)(2,1)S(1)} %add_convert_fusion), channel_id=1, source_target_pairs={{8,0},{16,8},{24,16},{9,1},{17,9},{25,17},{10,2},{18,10},{26,18},{... | collective-permute-start | bytes 1572872 | tf_op jit(solution)/shard_map/ppermute | solution.py:14
  144.5 2.0 %collective-permute-start.26 = (bf16[128,1024]{1,0:T(8,128)(2,1)S(1)}, bf16[128,1024]{1,0:T(8,128)(2,1)S(1)}, u32[]{:S(2)}, u32[]{:S(2)}) collective-permute-start(bf16[128,1024]{1,0:T(8,128)(2,1)S(1)} %get-tuple-element.121), channel_id=1, source_target_pairs={{8,4},{10,6},{13,1},{15,3},{16,12},{18,14},{21,9},{23,11},{24,20},... | collective-permute-start | bytes 786440 | tf_op jit(solution)/shard_map/ppermute | solution.py:534
  145.2 1.3 collective-permute-start.27

commit v9 on v8

--- a/solution.py
+++ b/solution.py
@@ -488,9 +488,7 @@
     far_routes, far_keep, far_got = hidden(far, [rows_far])
     end_sums = finish(end, end_hidden, BF16)
     next_head = moved(next_head, LEFT[1:])
-    conv_left, conv_right, end_sums, keep, far_keep, next_head = together(
-        conv_left, conv_right, end_sums, keep, far_keep, next_head
-    )
+    conv_right, end_sums, keep, far_keep, next_head = together(conv_right, end_sums, keep, far_keep, next_head)
 
     from_left, from_right = moved(conv_left, RIGHT[1:]), moved(conv_right, LEFT[1:])
     back_end = moved(end_sums, [(0, 1), (3, 2)])

time: 165 us -> 162 us (0.982)
  waiting for transfers between devices: 66 us -> 63.3 us
    ppermute x17, starting transfers between devices: 31.8 us -> 28.6 us  [moved(): return lax.ppermute(array, 'expert', pairs)]
    ppermute x2, starting transfers between devices: 3.4 us -> 5.62 us  [doubling_sum(): lax.ppermute(array, axis, [(i, i ^ step) for i in range(size)])]
    ppermute x1, waiting for transfers between devices: 16.3 us -> 14.5 us  [shifted(): return lax.ppermute(array, axis, pairs)]
  transfers between devices with their start and end apart: 30 -> 30, of which waited for: 10 -> 10; matrix products, arithmetic and copies ran while one was open for 4% -> 5% of each run, Pallas kernels for 22% -> 23%
where the time goes in v9:
time: 162 us; the launch traced here: 161 us
  waiting for transfers between devices  63.3 us (39%)
  starting transfers between devices  41.1 us (25%)
  Pallas kernels  38.1 us (24%)
  local copies, waits for them, and re-layouts  13.1 us (8%)
  other arithmetic  4.29 us (3%)
    ppermute x17, waiting for transfers between devices, moved(): return lax.ppermute(array, 'expert', pairs)  46.9 us
    ppermute x17, starting transfers between devices, moved(): return lax.ppermute(array, 'expert', pairs)  28.6 us
    ppermute x1, waiting for transfers between devices, shifted(): return lax.ppermute(array, axis, pairs)  14.5 us
    pallas_call x3, Pallas kernels, expert_sums(): pl.pallas_call(functools.partial(finish_kernel, count), grid_spec=pltpu.P...  14.3 us
    pallas_call x3, Pallas kernels, hidden_sums(): pl.pallas_call(functools.partial(hidden_kernel, count), grid_spec=pltpu.P...  11 us
    pallas_call x2, Pallas kernels, proj_sums(): pl.pallas_call(functools.partial(proj_kernel, count, with_taps), grid=(ha...  10.1 us
    unnamed x28, local copies, waits for them, and re-layouts  8.07 us
    ppermute x2, starting transfers between devices, doubling_sum(): lax.ppermute(array, axis, [(i, i ^ step) for i in range(size)])  5.62 us
  transfers between devices with their start and end apart: 30, of which 10 were waited for; matrix products, arithmetic and copies ran while one was open for 5% of the time, Pallas kernels for 23%

profile of v9, /device:TPU:0, one launch (start us, length us, event | category | flops | bytes accessed | tf_op | source)
XLA Modules:
  0.0 160.9 jit_solution(10947655023600636946)
XLA Ops:
  1.5 1.1 fusion.1.refs_0_.refs_3_
  2.6 5.0 %collective-permute-start = (bf16[128,2176]{1,0:T(8,128)(2,1)S(1)}, bf16[128,2176]{1,0:T(8,128)(2,1)S(1)}, u32[]{:S(2)}, u32[]{:S(2)}) collective-permute-start(bf16[128,2176]{1,0:T(8,128)(2,1)S(1)} %fusion.1.refs_0_.refs_3_), channel_id=1, source_target_pairs={{0,2},{2,4},{4,6},{1,3},{3,5},{5,7},{8,10},{10,12},{12,14},{9,11},... | collective-permute-start | bytes 1671176 | tf_op jit(solution)/shard_map/ppermute | solution.py:418
  7.5 1.3 collective-permute-start.1
  8.9 3.3 %dynamic-slice_bitcast_fusion.1 = bf16[512,2048]{1,0:T(8,128)(2,1)} fusion(bf16[1,1,512,4096]{3,2,1,0:T(8,128)(2,1)} %param.14, s32[]{:T(128)S(6)} %select_n.41), kind=kLoop, calls=%fused_computation.1 | loop fusion | bytes 4194308 | tf_op jit(solution)/shard_map/dynamic_slice | solution.py:457
  12.2 1.5 dynamic-slice_bitcast_fusion
  13.7 5.7 %collective-permute-done.refs_1_.refs_4_ = bf16[128,2176]{1,0:T(8,128)(2,1)S(1)} collective-permute-done((bf16[128,2176]{1,0:T(8,128)(2,1)S(1)}, bf16[128,2176]{1,0:T(8,128)(2,1)S(1)}, u32[]{:S(2)}, u32[]{:S(2)}) %collective-permute-start) | collective-permute-done | bytes 557088 | tf_op jit(solution)/shard_map/ppermute | solution.py:418
  19.4 4.1 %collective-permute-done.1.refs_2_.refs_5_ = bf16[128,2176]{1,0:T(8,128)(2,1)S(1)} collective-permute-done((bf16[128,2176]{1,0:T(8,128)(2,1)S(1)}, bf16[128,2176]{1,0:T(8,128)(2,1)S(1)}, u32[]{:S(2)}, u32[]{:S(2)}) %collective-permute-start.1) | collective-permute-done | bytes 557088 | tf_op jit(solution)/shard_map/ppermute | solution.py:418
  23.5 0.8 copy-done.10
  24.3 1.5 collective-permute-start.2
  25.8 1.3 collective-permute-start.3
  27.8 1.8 %collective-permute-done.5.pre_other = bf16[512,512]{1,0:T(8,128)(2,1)} collective-permute-done((bf16[512,512]{1,0:T(8,128)(2,1)}, bf16[512,512]{1,0:T(8,128)(2,1)}, u32[]{:S(2)}, u32[]{:S(2)}) %collective-permute-start.5) | collective-permute-done | bytes 524320 | tf_op jit(solution)/shard_map/ppermute | solution.py:129
  29.6 15.8 %collective-permute-done.3 = bf16[128,2176]{1,0:T(8,128)(2,1)} collective-permute-done((bf16[128,2176]{1,0:T(8,128)(2,1)}, bf16[128,2176]{1,0:T(8,128)(2,1)}, u32[]{:S(2)}, u32[]{:S(2)}) %collective-permute-start.3) | collective-permute-done | bytes 557088 | tf_op jit(solution)/shard_map/ppermute | solution.py:418
  45.4 1.3 copy-done.6
  47.0 1.1 broadcast_select_fusion.refs_0_.refs_1_
  48.1 1.3 collective-permute-start.6
  50.1 2.2 %copy-done.1 = bf16[1,1,512,4096]{3,2,1,0:T(8,128)(2,1)S(1)} copy-done((bf16[1,1,512,4096]{3,2,1,0:T(8,128)(2,1)S(1)}, bf16[1,1,512,4096]{3,2,1,0:T(8,128)(2,1)}, u32[]{:S(2)}) %copy-start.1) | copy-done | bytes 4194328
  52.3 1.6 copy-done.7
  53.9 1.1 copy-done.9
  54.9 1.1 copy-done.11
  56.0 4.3 %hidden.3 = (bf16[384,1024]{1,0:T(8,128)(2,1)S(1)}, f32[384,1024]{1,0:T(8,128)S(1)}, bf16[384,128]{1,0:T(8,128)(2,1)S(1)}) custom-call(s32[5]{0:T(128)S(1)} %stack.43.place, bf16[128,2176]{1,0:T(8,128)(2,1)S(1)} %fusion.1.refs_0_.refs_3_, bf16[128,2176]{1,0:T(8,128)(2,1)S(1)} %copy-done.9, bf16[128,2176]{1,0:T(8,128)(2,1)S(1)} %copy-done.11, ...), custom_call_target="tpu_custom_call" | custom-call | flops 12884901888 | bytes 46137344 | tf_op jit(solution)/shard_map/hidden/pallas_call | solution.py:201
  60.9 4.1 %collective-permute-done.6.refs_0_.refs_1_ = bf16[128,2176]{1,0:T(8,128)(2,1)S(1)} collective-permute-done((bf16[128,2176]{1,0:T(8,128)(2,1)S(1)}, bf16[128,2176]{1,0:T(8,128)(2,1)S(1)}, u32[]{:S(2)}, u32[]{:S(2)}) %collective-permute-start.6) | collective-permute-done | bytes 557088 | tf_op jit(solution)/shard_map/ppermute | solution.py:418
  65.1 1.5 collective-permute-start.9
  66.5 1.3 collective-permute-start.11
  67.8 3.3 %hidden.4 = (bf16[128,1024]{1,0:T(8,128)(2,1)S(1)}, f32[128,1024]{1,0:T(8,128)S(1)}, bf16[128,128]{1,0:T(8,128)(2,1)S(1)}) custom-call(s32[3]{0:T(128)S(1)} %pad_add_fusion.place, bf16[128,2176]{1,0:T(8,128)(2,1)S(1)} %collective-permute-done.6.refs_0_.refs_1_, bf16[128,2176]{1,0:T(8,128)(2,1)S(1)} %collective-permute-done.6.refs_0_.refs_1_, ...), custom_call_target="tpu_custom_call" | custom-call | flops 4294967296 | bytes 37748736 | tf_op jit(solution)/shard_map/hidden/pallas_call | solution.py:201
  71.2 1.6 collective-permute-start.13
  72.8 3.3 %hidden.5 = (bf16[128,1024]{1,0:T(8,128)(2,1)S(1)}, f32[128,1024]{1,0:T(8,128)S(1)}, bf16[128,128]{1,0:T(8,128)(2,1)S(1)}) custom-call(s32[3]{0:T(128)S(1)} %pad_add_fusion.2.place, bf16[128,2176]{1,0:T(8,128)(2,1)S(1)} %broadcast_select_fusion.refs_0_.refs_1_, bf16[128,2176]{1,0:T(8,128)(2,1)S(1)} %broadcast_select_fusion.refs_0_.refs_1_, ...), custom_call_target="tpu_custom_call" | custom-call | flops 4294967296 | bytes 37748736 | tf_op jit(solution)/shard_map/hidden/pallas_call | solution.py:201
  76.6 4.6 %experts.3 = bf16[128,2048]{1,0:T(8,128)(2,1)S(1)} custom-call(s32[3]{0:T(128)S(1)} %pad_add_fusion.place, bf16[128,128]{1,0:T(8,128)(2,1)S(1)} %get-tuple-element.74.routes, f32[128,1024]{1,0:T(8,128)S(1)} %get-tuple-element.75.keep, bf16[128,1024]{1,0:T(8,128)(2,1)S(1)} %collective-permute-done.12.got, bf16[512,512]{1,0:T(8,128)(2,1)} %bitcast.9.pre_own, ...), custom_call_target="tpu_custom_call" | custom-call | flops 4294967296 | bytes 41943040 | tf_op jit(solution)/shard_map/experts/pallas_call | solution.py:256
  81.2 2.7 %collective-permute-done.13.refs_5_ = bf16[16,2048]{1,0:T(8,128)(2,1)S(1)} collective-permute-done((bf16[16,2048]{1,0:T(8,128)(2,1)S(1)}, bf16[16,2048]{1,0:T(8,128)(2,1)S(1)}, u32[]{:S(2)}, u32[]{:S(2)}) %collective-permute-start.13) | collective-permute-done | bytes 65568 | tf_op jit(solution)/shard_map/ppermute | solution.py:418
  83.9 1.3 collective-permute-start.14
  85.2 4.6 %collective-permute-start.16 = (bf16[128,2048]{1,0:T(8,128)(2,1)S(1)}, bf16[128,2048]{1,0:T(8,128)(2,1)S(1)}, u32[]{:S(2)}, u32[]{:S(2)}) collective-permute-start(bf16[128,2048]{1,0:T(8,128)(2,1)S(1)} %experts.3), channel_id=1, source_target_pairs={{0,2},{6,4},{1,3},{7,5},{8,10},{14,12},{9,11},{15,13},{16,18},{22,... | collective-permute-start | bytes 1572872 | tf_op jit(solution)/shard_map/ppermute | solution.py:418
  90.5 6.0 %projection.2 = (bf16[384,1024]{1,0:T(8,128)(2,1)S(1)}, f32[384,1024]{1,0:T(8,128)S(1)}, f32[4,2048]{1,0:T(4,128)S(1)}) custom-call(s32[5]{0:T(128)S(1)} %stack.43.place, bf16[128,2048]{1,0:T(8,128)(2,1)S(1)} %bitcast.37, bf16[128,2048]{1,0:T(8,128)(2,1)S(1)} %collective-permute-done.9.refs_1_, ...), custom_call_target="tpu_custom_call" | custom-call | flops 12884901888 | bytes 65011712 | tf_op jit(solution)/shard_map/projection/pallas_call | solution.py:337
  96.5 1.3 collective-permute-start.21
  97.8 4.3 %experts.4 = f32[128,2048]{1,0:T(8,128)S(1)} custom-call(s32[3]{0:T(128)S(1)} %pad_add_fusion.2.place, bf16[128,128]{1,0:T(8,128)(2,1)S(1)} %get-tuple-element.87.routes, f32[128,1024]{1,0:T(8,128)S(1)} %get-tuple-element.88.keep, bf16[128,1024]{1,0:T(8,128)(2,1)S(1)} %collective-permute-done.15.got, bf16[512,512]{1,0:T(8,128)(2,1)} %bitcast.9.pre_own, ...), custom_call_target="tpu_custom_call" | custom-call | flops 4294967296 | bytes 41943040 | tf_op jit(solution)/shard_map/experts/pallas_call | solution.py:256
  102.2 2.4 %collective-permute-start.28 = (f32[4,2048]{1,0:T(4,128)S(1)}, f32[4,2048]{1,0:T(4,128)S(1)}, u32[]{:S(2)}, u32[]{:S(2)}) collective-permute-start(f32[4,2048]{1,0:T(4,128)S(1)} %get-tuple-element.117), channel_id=1, source_target_pairs={{0,2},{2,0},{4,6},{6,4},{1,3},{3,1},{5,7},{7,5},{8,10},{10,8},{12,... | collective-permute-start | bytes 98312 | tf_op jit(solution)/shard_map/ppermute | solution.py:139
  104.8 2.0 %collective-permute-start.18 = (bf16[128,2048]{1,0:T(8,128)(2,1)S(1)}, bf16[128,2048]{1,0:T(8,128)(2,1)S(1)}, u32[]{:S(2)}, u32[]{:S(2)}) collective-permute-start(bf16[128,2048]{1,0:T(8,128)(2,1)S(1)} %add_convert_fusion.1), channel_id=1, source_target_pairs={{0,2},{2,4},{1,3},{3,5},{8,10},{10,12},{9,11},{11,13},{16,18},{18,... | collective-permute-start | bytes 1572872 | tf_op jit(solution)/shard_map/ppermute | solution.py:418
  107.5 1.3 collective-permute-start.17
  108.8 5.4 %experts.5.sums = f32[384,2048]{1,0:T(8,128)S(1)} custom-call(s32[5]{0:T(128)S(1)} %stack.43.place, bf16[384,128]{1,0:T(8,128)(2,1)S(1)} %get-tuple-element.96.routes, f32[384,1024]{1,0:T(8,128)S(1)} %get-tuple-element.97.keep, bf16[384,1024]{1,0:T(8,128)(2,1)S(1)} %collective-permute-done.20.got, bf16[512,512]{1,0:T(8,128)(2,1)} %bitcast.9.pre_own, ...), custom_call_target="tpu_custom_call" | custom-call | flops 12884901888 | bytes 58720256 | tf_op jit(solution)/shard_map/experts/pallas_call | solution.py:256
  114.2 9.9 %collective-permute-done.17.refs_1_ = bf16[128,2048]{1,0:T(8,128)(2,1)S(1)} collective-permute-done((bf16[128,2048]{1,0:T(8,128)(2,1)S(1)}, bf16[128,2048]{1,0:T(8,128)(2,1)S(1)}, u32[]{:S(2)}, u32[]{:S(2)}) %collective-permute-start.17) | collective-permute-done | bytes 524320 | tf_op jit(solution)/shard_map/ppermute | solution.py:418
  124.1 1.3 combine.1
  125.4 1.5 collective-permute-start.22
  126.9 1.3 collective-permute-start.23
  128.2 4.1 %projection.3 = (bf16[256,1024]{1,0:T(8,128)(2,1)S(1)}, f32[256,1024]{1,0:T(8,128)S(1)}) custom-call(s32[4]{0:T(128)S(1)} %pad_add_fusion.3.place, bf16[128,2048]{1,0:T(8,128)(2,1)S(1)} %broadcast_select_fusion.1.refs_0_.refs_3_, bf16[128,2048]{1,0:T(8,128)(2,1)S(1)} %collective-permute-done.17.refs_1_, bf16[16,2048]{1,0:T(8,128)(2,1)S(1)} %slice_select_fusion.refs_2_, ...), custom_call_target="tpu_custom_call" | custom-call | flops 8589934592 | bytes 54525952 | tf_op jit(solution)/shard_map/projection/pallas_call | solution.py:337
  132.3 1.3 collective-permute-start.25
  133.6 3.2 %collective-permute-start.29 = (f32[4,2048]{1,0:T(4,128)S(1)}, f32[4,2048]{1,0:T(4,128)S(1)}, u32[]{:S(2)}, u32[]{:S(2)}) collective-permute-start(f32[4,2048]{1,0:T(4,128)S(1)} %add.47), channel_id=1, source_target_pairs={{0,4},{2,6},{4,0},{6,2},{1,5},{3,7},{5,1},{7,3},{8,12},{10,14},{12... | collective-permute-start | bytes 98312 | tf_op jit(solution)/shard_map/ppermute | solution.py:139
  136.9 4.3 %collective-permute-done.23 = bf16[128,2048]{1,0:T(8,128)(2,1)S(1)} collective-permute-done((bf16[128,2048]{1,0:T(8,128)(2,1)S(1)}, bf16[128,2048]{1,0:T(8,128)(2,1)S(1)}, u32[]{:S(2)}, u32[]{:S(2)}) %collective-permute-start.23) | collective-permute-done | bytes 524320 | tf_op jit(solution)/shard_map/ppermute | solution.py:418
  141.5 1.3 collective-permute-start.24
  144.9 14.5 %collective-permute-done.24.residual = bf16[128,2048]{1,0:T(8,128)(2,1)S(1)} collective-permute-done((bf16[128,2048]{1,0:T(8,128)(2,1)S(1)}, bf16[128,2048]{1,0:T(8,128)(2,1)S(1)}, u32[]{:S(2)}, u32[]{:S(2)}) %collective-permute-start.24) | collective-permute-done | bytes 524320 | tf_op jit(solution)/shard_map/ppermute | solution.py:14
  159.4 1.5 residual.1
  (69 shorter events, 7.6 us)
Async XLA Ops:
  2.6 16.8 %collective-permute-start = (bf16[128,2176]{1,0:T(8,128)(2,1)S(1)}, bf16[128,2176]{1,0:T(8,128)(2,1)S(1)}, u32[]{:S(2)}, u32[]{:S(2)}) collective-permute-start(bf16[128,2176]{1,0:T(8,128)(2,1)S(1)} %fusion.1.refs_0_.refs_3_), channel_id=1, source_target_pairs={{0,2},{2,4},{4,6},{1,3},{3,5},{5,7},{8,10},{10,12},{12,14},{9,11},... | collective-permute-start | bytes 1671176 | tf_op jit(solution)/shard_map/ppermute | solution.py:418
  7.5 16.0 %collective-permute-start.1 = (bf16[128,2176]{1,0:T(8,128)(2,1)S(1)}, bf16[128,2176]{1,0:T(8,128)(2,1)S(1)}, u32[]{:S(2)}, u32[]{:S(2)}) collective-permute-start(bf16[128,2176]{1,0:T(8,128)(2,1)S(1)} %fusion.1.refs_0_.refs_3_), channel_id=1, source_target_pairs={{6,4},{4,2},{2,0},{7,5},{5,3},{3,1},{14,12},{12,10},{10,8},{15,13}... | collective-permute-start | bytes 1671176 | tf_op jit(solution)/shard_map/ppermute | solution.py:418
  8.8 3.4 %copy-start.2 = (bf16[1,1,4096,512]{3,2,1,0:T(8,128)(2,1)S(1)}, bf16[1,1,4096,512]{3,2,1,0:T(8,128)(2,1)}, u32[]{:S(2)}) copy-start(bf16[1,1,4096,512]{3,2,1,0:T(8,128)(2,1)} %param.13) | copy-start | bytes 12582916
  12.2 1.5 copy-start.4
  19.4 4.2 %copy-start.8 = (bf16[128,2176]{1,0:T(8,128)(2,1)}, bf16[128,2176]{1,0:T(8,128)(2,1)S(1)}, u32[]{:S(2)}) copy-start(bf16[128,2176]{1,0:T(8,128)(2,1)S(1)} %collective-permute-done.refs_1_.refs_4_) | copy-start | bytes 1671172
  23.5 0.8 copy-start.10
  24.3 21.1 %collective-permute-start.4 = (bf16[512,2048]{1,0:T(8,128)(2,1)}, bf16[512,2048]{1,0:T(8,128)(2,1)S(1)}, u32[]{:S(2)}, u32[]{:S(2)}) collective-permute-start(bf16[512,2048]{1,0:T(8,128)(2,1)} %dynamic-slice_bitcast_fusion.1), channel_id=1, source_target_pairs={{0,1},{1,0},{2,3},{3,2},{4,5},{5,4},{6,7},{7,6},{8,9},{9,8},{10,11... | collective-permute-start | bytes 6291464 | tf_op jit(solution)/shard_map/ppermute | solution.py:129
  24.3 5.3 %collective-permute-start.2 = (bf16[128,2176]{1,0:T(8,128)(2,1)}, bf16[128,2176]{1,0:T(8,128)(2,1)}, u32[]{:S(2)}, u32[]{:S(2)}) collective-permute-start(bf16[128,2176]{1,0:T(8,128)(2,1)} %copy-done.8), channel_id=1, source_target_pairs={{2,4},{4,6},{3,5},{5,7},{10,12},{12,14},{11,13},{13,15},{18,20},{2... | collective-permute-start | bytes 1671176 | tf_op jit(solution)/shard_map/ppermute | solution.py:418
  25.8 19.6 %collective-permute-start.3 = (bf16[128,2176]{1,0:T(8,128)(2,1)}, bf16[128,2176]{1,0:T(8,128)(2,1)}, u32[]{:S(2)}, u32[]{:S(2)}) collective-permute-start(bf16[128,2176]{1,0:T(8,128)(2,1)} %copy-done.10), channel_id=1, source_target_pairs={{4,2},{2,0},{5,3},{3,1},{12,10},{10,8},{13,11},{11,9},{20,18},{18,... | collective-permute-start | bytes 1671176 | tf_op jit(solution)/shard_map/ppermute | solution.py:418
  27.1 2.5 %collective-permute-start.5 = (bf16[512,512]{1,0:T(8,128)(2,1)}, bf16[512,512]{1,0:T(8,128)(2,1)}, u32[]{:S(2)}, u32[]{:S(2)}) collective-permute-start(bf16[512,512]{1,0:T(8,128)(2,1)} %bitcast.9.pre_own), channel_id=1, source_target_pairs={{0,1},{1,0},{2,3},{3,2},{4,5},{5,4},{6,7},{7,6},{8,9},{9,8},{10,11... | collective-permute-start | bytes 1572872 | tf_op jit(solution)/shard_map/ppermute | solution.py:129
  45.4 1.3 copy-start.6
  46.8 18.3 %collective-permute-start.7 = (bf16[2048,512]{1,0:T(8,128)(2,1)}, bf16[2048,512]{1,0:T(8,128)(2,1)S(1)}, u32[]{:S(2)}, u32[]{:S(2)}) collective-permute-start(bf16[2048,512]{1,0:T(8,128)(2,1)} %dynamic-slice_bitcast_fusion), channel_id=1, source_target_pairs={{0,1},{1,0},{2,3},{3,2},{4,5},{5,4},{6,7},{7,6},{8,9},{9,8},{10,11... | collective-permute-start | bytes 6291464 | tf_op jit(solution)/shard_map/ppermute | solution.py:129
  48.1 16.9 %collective-permute-start.6 = (bf16[128,2176]{1,0:T(8,128)(2,1)S(1)}, bf16[128,2176]{1,0:T(8,128)(2,1)S(1)}, u32[]{:S(2)}, u32[]{:S(2)}) collective-permute-start(bf16[128,2176]{1,0:T(8,128)(2,1)S(1)} %broadcast_select_fusion.refs_0_.refs_1_), channel_id=1, source_target_pairs={{4,6},{2,0},{5,7},{3,1},{12,14},{10,8},{13,15},{11,9},{20,22},{18,... | collective-permute-start | bytes 1671176 | tf_op jit(solution)/shard_map/ppermute | solution.py:418
  49.4 11.5 %collective-permute-start.8 = (bf16[16,2048]{1,0:T(8,128)(2,1)S(1)}, bf16[16,2048]{1,0:T(8,128)(2,1)S(1)}, u32[]{:S(2)}, u32[]{:S(2)}) collective-permute-start(bf16[16,2048]{1,0:T(8,128)(2,1)S(1)} %slice_bitcast_fusion), channel_id=1, source_target_pairs={{6,4},{4,2},{7,5},{5,3},{14,12},{12,10},{15,13},{13,11},{22,20},{2... | collective-permute-start | bytes 196616 | tf_op jit(solution)/shard_map/ppermute | solution.py:418
  50.1 2.2 %copy-start.1 = (bf16[1,1,512,4096]{3,2,1,0:T(8,128)(2,1)S(1)}, bf16[1,1,512,4096]{3,2,1,0:T(8,128)(2,1)}, u32[]{:S(2)}) copy-start(bf16[1,1,512,4096]{3,2,1,0:T(8,128)(2,1)} %param.14) | copy-start | bytes 12582916
  52.3 1.6 copy-start.7
  53.9 1.1 copy-start.9
  54.9 1.1 copy-start.11
  60.3 47.1 %collective-permute-start.20 = (bf16[384,1024]{1,0:T(8,128)(2,1)S(1)}, bf16[384,1024]{1,0:T(8,128)(2,1)S(1)}, u32[]{:S(2)}, u32[]{:S(2)}) collective-permute-start(bf16[384,1024]{1,0:T(8,128)(2,1)S(1)} %get-tuple-element.98), channel_id=1, source_target_pairs={{0,1},{1,0},{2,3},{3,2},{4,5},{5,4},{6,7},{7,6},{8,9},{9,8},{10,11... | collective-permute-start | bytes 2359304 | tf_op jit(solution)/shard_map/ppermute | solution.py:129
  65.1 24.7 %collective-permute-start.9 = (bf16[128,2048]{1,0:T(8,128)(2,1)S(1)}, bf16[128,2048]{1,0:T(8,128)(2,1)S(1)}, u32[]{:S(2)}, u32[]{:S(2)}) collective-permute-start(bf16[128,2048]{1,0:T(8,128)(2,1)S(1)} %bitcast.35), channel_id=1, source_target_pairs={{0,2},{2,4},{4,6},{1,3},{3,5},{5,7},{8,10},{10,12},{12,14},{9,11},... | collective-permute-start | bytes 1572872 | tf_op jit(solution)/shard_map/ppermute | solution.py:418
  66.5 17.4 %collective-permute-start.11 = (bf16[128,2048]{1,0:T(8,128)(2,1)S(1)}, bf16[128,2048]{1,0:T(8,128)(2,1)S(1)}, u32[]{:S(2)}, u32[]{:S(2)}) collective-permute-start(bf16[128,2048]{1,0:T(8,128)(2,1)S(1)} %bitcast.36), channel_id=1, source_target_pairs={{6,4},{4,2},{2,0},{7,5},{5,3},{3,1},{14,12},{12,10},{10,8},{15,13}... | collective-permute-start | bytes 1572872 | tf_op jit(solution)/shard_map/ppermute | solution.py:418
  71.2 5.4 %copy-start.3 = (bf16[1,1,4096,512]{3,2,1,0:T(8,128)(2,1)S(1)}, bf16[1,1,4096,512]{3,2,1,0:T(8,128)(2,1)}, u32[]{:S(2)}) copy-start(bf16[1,1,4096,512]{3,2,1,0:T(8,128)(2,1)} %param.13) | copy-start | bytes 12582916
  71.2 5.0 %collective-permute-start.12 = (bf16[128,1024]{1,0:T(8,128)(2,1)S(1)}, bf16[128,1024]{1,0:T(8,128)(2,1)S(1)}, u32[]{:S(2)}, u32[]{:S(2)}) collective-permute-start(bf16[128,1024]{1,0:T(8,128)(2,1)S(1)} %get-tuple-element.76), channel_id=1, source_target_pairs={{0,1},{1,0},{2,3},{3,2},{4,5},{5,4},{6,7},{7,6},{8,9},{9,8},{10,11... | collective-permute-start | bytes 786440 | tf_op jit(solution)/shard_map/ppermute | solution.py:129
  71.2 12.6 %collective-permute-start.13 = (bf16[16,2048]{1,0:T(8,128)(2,1)S(1)}, bf16[16,2048]{1,0:T(8,128)(2,1)S(1)}, u32[]{:S(2)}, u32[]{:S(2)}) collective-permute-start(bf16[16,2048]{1,0:T(8,128)(2,1)S(1)} %collective-permute-done.8), channel_id=1, source_target_pairs={{4,2},{2,0},{5,3},{3,1},{12,10},{10,8},{13,11},{11,9},{20,18},{18,... | collective-permute-start | bytes 196616 | tf_op jit(solution)/shard_map/ppermute | solution.py:418
  76.1 20.4 %collective-permute-start.15 = (bf16[128,1024]{1,0:T(8,128)(2,1)S(1)}, bf16[128,1024]{1,0:T(8,128)(2,1)S(1)}, u32[]{:S(2)}, u32[]{:S(2)}) collective-permute-start(bf16[128,1024]{1,0:T(8,128)(2,1)S(1)} %get-tuple-element.89), channel_id=1, source_target_pairs={{0,1},{1,0},{2,3},{3,2},{4,5},{5,4},{6,7},{7,6},{8,9},{9,8},{10,11... | collective-permute-start | bytes 786440 | tf_op jit(solution)/shard_map/ppermute | solution.py:129
  76.6 13.9 %copy-start.5 = (bf16[1,1024,2048]{2,1,0:T(8,128)(2,1)S(1)}, bf16[1,1024,2048]{2,1,0:T(8,128)(2,1)}, u32[]{:S(2)}) copy-start(bf16[1,1024,2048]{2,1,0:T(8,128)(2,1)} %param.19) | copy-start | bytes 12582916
  76.6 13.9 %copy-start.12 = (bf16[1,128,2048]{2,1,0:T(8,128)(2,1)S(1)}, bf16[1,128,2048]{2,1,0:T(8,128)(2,1)}, u32[]{:S(2)}) copy-start(bf16[1,128,2048]{2,1,0:T(8,128)(2,1)} %param.17) | copy-start | bytes 1572868
  76.6 13.9 %copy-start.13 = (f32[1,4,2048]{2,1,0:T(4,128)S(1)}, f32[1,4,2048]{2,1,0:T(4,128)}, u32[]{:S(2)}) copy-start(f32[1,4,2048]{2,1,0:T(4,128)} %param.18) | copy-start | bytes 98308
  83.9 20.7 %collective-permute-start.14 = (bf16[128,2048]{1,0:T(8,128)(2,1)S(1)}, bf16[128,2048]{1,0:T(8,128)(2,1)S(1)}, u32[]{:S(2)}, u32[]{:S(2)}) collective-permute-start(bf16[128,2048]{1,0:T(8,128)(2,1)S(1)} %collective-permute-done.11.refs_2_.refs_3_), channel_id=1, source_target_pairs={{4,2},{2,0},{5,3},{3,1},{12,10},{10,8},{13,11},{11,9},{20,18},{18,... | collective-permute-start | bytes 1572872 | tf_op jit(solution)/shard_map/ppermute | solution.py:418
  85.2 19.5 %collective-permute-start.16 = (bf16[128,2048]{1,0:T(8,128)(2,1)S(1)}, bf16[128,2048]{1,0:T(8,128)(2,1)S(1)}, u32[]{:S(2)}, u32[]{:S(2)}) collective-permute-start(bf16[128,2048]{1,0:T(8,128)(2,1)S(1)} %experts.3), channel_id=1, source_target_pairs={{0,2},{6,4},{1,3},{7,5},{8,10},{14,12},{9,11},{15,13},{16,18},{22,... | collective-permute-start | bytes 1572872 | tf_op jit(solution)/shard_map/ppermute | solution.py:418
  89.8 12.4 %collective-permute-start.10 = (bf16[128,2048]{1,0:T(8,128)(2,1)S(1)}, bf16[128,2048]{1,0:T(8,128)(2,1)S(1)}, u32[]{:S(2)}, u32[]{:S(2)}) collective-permute-start(bf16[128,2048]{1,0:T(8,128)(2,1)S(1)} %collective-permute-done.9.refs_1_), channel_id=1, source_target_pairs={{2,4},{4,6},{3,5},{5,7},{10,12},{12,14},{11,13},{13,15},{18,20},{2... | collective-permute-start | bytes 1572872 | tf_op jit(solution)/shard_map/ppermute | solution.py:418
  96.5 27.5 %collective-permute-start.21 = (bf16[384,1024]{1,0:T(8,128)(2,1)S(1)}, bf16[384,1024]{1,0:T(8,128)(2,1)S(1)}, u32[]{:S(2)}, u32[]{:S(2)}) collective-permute-start(bf16[384,1024]{1,0:T(8,128)(2,1)S(1)} %get-tuple-element.103), channel_id=1, source_target_pairs={{1,0},{3,2},{4,5},{6,7},{9,8},{11,10},{12,13},{14,15},{17,16},{19,... | collective-permute-start | bytes 2359304 | tf_op jit(solution)/shard_map/ppermute | solution.py:499
  102.2 31.4 %collective-permute-start.28 = (f32[4,2048]{1,0:T(4,128)S(1)}, f32[4,2048]{1,0:T(4,128)S(1)}, u32[]{:S(2)}, u32[]{:S(2)}) collective-permute-start(f32[4,2048]{1,0:T(4,128)S(1)} %get-tuple-element.117), channel_id=1, source_target_pairs={{0,2},{2,0},{4,6},{6,4},{1,3},{3,1},{5,7},{7,5},{8,10},{10,8},{12,... | collective-permute-start | bytes 98312 | tf_op jit(solution)/shard_map/ppermute | solution.py:139
  104.8 19.3 %collective-permute-start.18 = (bf16[128,2048]{1,0:T(8,128)(2,1)S(1)}, bf16[128,2048]{1,0:T(8,128)(2,1)S(1)}, u32[]{:S(2)}, u32[]{:S(2)}) collective-permute-start(bf16[128,2048]{1,0:T(8,128)(2,1)S(1)} %add_convert_fusion.1), channel_id=1, source_target_pairs={{0,2},{2,4},{1,3},{3,5},{8,10},{10,12},{9,11},{11,13},{16,18},{18,... | collective-permute-start | bytes 1572872 | tf_op jit(solution)/shard_map/ppermute | solution.py:418
  106.8 17.3 %collective-permute-start.19 = (bf16[128,2048]{1,0:T(8,128)(2,1)S(1)}, bf16[128,2048]{1,0:T(8,128)(2,1)S(1)}, u32[]{:S(2)}, u32[]{:S(2)}) collective-permute-start(bf16[128,2048]{1,0:T(8,128)(2,1)S(1)} %add_convert_fusion.1), channel_id=1, source_target_pairs={{6,4},{4,2},{7,5},{5,3},{14,12},{12,10},{15,13},{13,11},{22,20},{2... | collective-permute-start | bytes 1572872 | tf_op jit(solution)/shard_map/ppermute | solution.py:418
  107.5 16.6 %collective-permute-start.17 = (bf16[128,2048]{1,0:T(8,128)(2,1)S(1)}, bf16[128,2048]{1,0:T(8,128)(2,1)S(1)}, u32[]{:S(2)}, u32[]{:S(2)}) collective-permute-start(bf16[128,2048]{1,0:T(8,128)(2,1)S(1)} %broadcast_select_fusion.1.refs_0_.refs_3_), channel_id=1, source_target_pairs={{4,6},{2,0},{5,7},{3,1},{12,14},{10,8},{13,15},{11,9},{20,22},{18,... | collective-permute-start | bytes 1572872 | tf_op jit(solution)/shard_map/ppermute | solution.py:418
  108.8 15.3 %copy-start = (bf16[1,128,2048]{2,1,0:T(8,128)(2,1)S(1)}, bf16[1,128,2048]{2,1,0:T(8,128)(2,1)}, u32[]{:S(2)}) copy-start(bf16[1,128,2048]{2,1,0:T(8,128)(2,1)} %param.10) | copy-start | bytes 1572868
  125.4 11.5 %collective-permute-start.22 = (bf16[128,2048]{1,0:T(8,128)(2,1)S(1)}, bf16[128,2048]{1,0:T(8,128)(2,1)S(1)}, u32[]{:S(2)}, u32[]{:S(2)}) collective-permute-start(bf16[128,2048]{1,0:T(8,128)(2,1)S(1)} %get-tuple-element.108), channel_id=1, source_target_pairs={{0,2},{2,4},{4,6},{1,3},{3,5},{5,7},{8,10},{10,12},{12,14},{9,11},... | collective-permute-start | bytes 1572872 | tf_op jit(solution)/shard_map/ppermute | solution.py:418
  126.9 14.4 %collective-permute-start.23 = (bf16[128,2048]{1,0:T(8,128)(2,1)S(1)}, bf16[128,2048]{1,0:T(8,128)(2,1)S(1)}, u32[]{:S(2)}, u32[]{:S(2)}) collective-permute-start(bf16[128,2048]{1,0:T(8,128)(2,1)S(1)} %get-tuple-element.109), channel_id=1, source_target_pairs={{6,4},{4,2},{2,0},{7,5},{5,3},{3,1},{14,12},{12,10},{10,8},{15,13}... | collective-permute-start | bytes 1572872 | tf_op jit(solution)/shard_map/ppermute | solution.py:418
  132.3 10.5 %collective-permute-start.25 = (bf16[256,1024]{1,0:T(8,128)(2,1)S(1)}, bf16[256,1024]{1,0:T(8,128)(2,1)S(1)}, u32[]{:S(2)}, u32[]{:S(2)}) collective-permute-start(bf16[256,1024]{1,0:T(8,128)(2,1)S(1)} %get-tuple-element.116), channel_id=1, source_target_pairs={{1,0},{3,2},{4,5},{6,7},{9,8},{11,10},{12,13},{14,15},{17,16},{19,... | collective-permute-start | bytes 1572872 | tf_op jit(solution)/shard_map/ppermute | solution.py:499
  133.6 10.7 %collective-permute-start.29 = (f32[4,2048]{1,0:T(4,128)S(1)}, f32[4,2048]{1,0:T(4,128)S(1)}, u32[]{:S(2)}, u32[]{:S(2)}) collective-permute-start(f32[4,2048]{1,0:T(4,128)S(1)} %add.47), channel_id=1, source_target_pairs={{0,4},{2,6},{4,0},{6,2},{1,5},{3,7},{5,1},{7,3},{8,12},{10,14},{12... | collective-permute-start | bytes 98312 | tf_op jit(solution)/shard_map/ppermute | solution.py:139
  141.5 18.0 %collective-permute-start.24 = (bf16[128,2048]{1,0:T(8,128)(2,1)S(1)}, bf16[128,2048]{1,0:T(8,128)(2,1)S(1)}, u32[]{:S(2)}, u32[]{:S(2)}) collective-permute-start(bf16[128,2048]{1,0:T(8,128)(2,1)S(1)} %add_convert_fusion), channel_id=1, source_target_pairs={{8,0},{16,8},{24,16},{9,1},{17,9},{25,17},{10,2},{18,10},{26,18},{... | collective-permute-start | bytes 1572872 | tf_op jit(solution)/shard_map/ppermute | solution.py:14
  142.9 2.0 %collective-permute-start.26 = (bf16[128,1024]{1,0:T(8,128)(2,1)S(1)}, bf16[128,1024]{1,0:T(8,128)(2,1)S(1)}, u32[]{:S(2)}, u32[]{:S(2)}) collective-permute-start(bf16[128,1024]{1,0:T(8,128)(2,1)S(1)} %get-tuple-element.119), channel_id=1, source_target_pairs={{8,4},{10,6},{13,1},{15,3},{16,12},{18,14},{21,9},{23,11},{24,20},... | collective-permute-start | bytes 786440 | tf_op jit(solution)/shard_map/ppermute | solution.py:532
  143.6 1.3 collective-permute-start.27

commit v10 on v9

--- a/solution.py
+++ b/solution.py
@@ -512,10 +512,10 @@
     back = (far_sums + back_end.astype(F32)).astype(BF16)
     back_right, back_left = moved(back, RIGHT[:2]), moved(back, LEFT[:2])
     near_sums = finish(near, (routes, keep, got), F32)
-    conv_end, back_right, back_left, near_sums = together(conv_end, back_right, back_left, near_sums)
+    back_right, back_left, near_sums = together(back_right, back_left, near_sums)
 
     to_right, to_left, own = combined(near, out_grad[0], near_sums, back_right, back_left, near_proj, near_proj_got)
-    to_right, to_left, conv_end = together(to_right, to_left, conv_end)
+    to_right, to_left, conv_far = together(to_right, to_left, conv_far)
     to_right, to_left = moved(to_right, RIGHT), moved(to_left, LEFT)
     far_head = jnp.where(me >= 2, conv_left[:HEAD], conv_end[:HEAD])
     proj_keep, proj_got = proj(place(far_block, end_block), [conv_far, conv_end], [far_head, conv_far])

time: 162 us -> 160 us (0.988)
  waiting for transfers between devices: 63.3 us -> 57.7 us
  starting transfers between devices: 41.1 us -> 45.3 us
    ppermute x17, starting transfers between devices: 28.6 us -> 33.8 us  [moved(): return lax.ppermute(array, 'expert', pairs)]
    ppermute x17, waiting for transfers between devices: 46.9 us -> 42 us  [moved(): return lax.ppermute(array, 'expert', pairs)]
where the time goes in v10:
time: 160 us
  waiting for transfers between devices  57.7 us (36%)
  starting transfers between devices  45.3 us (28%)
  Pallas kernels  38.1 us (24%)
  local copies, waits for them, and re-layouts  13.1 us (8%)
  other arithmetic  4.29 us (3%)
    ppermute x17, waiting for transfers between devices, moved(): return lax.ppermute(array, 'expert', pairs)  42 us
    ppermute x17, starting transfers between devices, moved(): return lax.ppermute(array, 'expert', pairs)  33.8 us
    pallas_call x3, Pallas kernels, expert_sums(): pl.pallas_call(functools.partial(finish_kernel, count), grid_spec=pltpu.P...  14.3 us
    ppermute x1, waiting for transfers between devices, shifted(): return lax.ppermute(array, axis, pairs)  13.8 us
    pallas_call x3, Pallas kernels, hidden_sums(): pl.pallas_call(functools.partial(hidden_kernel, count), grid_spec=pltpu.P...  11 us
    pallas_call x2, Pallas kernels, proj_sums(): pl.pallas_call(functools.partial(proj_kernel, count, with_taps), grid=(ha...  10.1 us
    unnamed x28, local copies, waits for them, and re-layouts  8.07 us
    ppermute x2, starting transfers between devices, doubling_sum(): lax.ppermute(array, axis, [(i, i ^ step) for i in range(size)])  4.59 us
  transfers between devices with their start and end apart: 30, of which 10 were waited for; matrix products, arithmetic and copies ran while one was open for 5% of the time, Pallas kernels for 23%

profile of v10, /device:TPU:0, one launch (start us, length us, event | category | flops | bytes accessed | tf_op | source)
XLA Modules:
  0.0 159.5 jit_solution(3983196060226617112)
XLA Ops:
  1.5 1.1 fusion.1.refs_0_.refs_3_
  2.6 5.0 %collective-permute-start = (bf16[128,2176]{1,0:T(8,128)(2,1)S(1)}, bf16[128,2176]{1,0:T(8,128)(2,1)S(1)}, u32[]{:S(2)}, u32[]{:S(2)}) collective-permute-start(bf16[128,2176]{1,0:T(8,128)(2,1)S(1)} %fusion.1.refs_0_.refs_3_), channel_id=1, source_target_pairs={{0,2},{2,4},{4,6},{1,3},{3,5},{5,7},{8,10},{10,12},{12,14},{9,11},... | collective-permute-start | bytes 1671176 | tf_op jit(solution)/shard_map/ppermute | solution.py:418
  7.5 1.3 collective-permute-start.1
  8.9 3.3 %dynamic-slice_bitcast_fusion.1 = bf16[512,2048]{1,0:T(8,128)(2,1)} fusion(bf16[1,1,512,4096]{3,2,1,0:T(8,128)(2,1)} %param.14, s32[]{:T(128)S(6)} %select_n.40), kind=kLoop, calls=%fused_computation.1 | loop fusion | bytes 4194308 | tf_op jit(solution)/shard_map/dynamic_slice | solution.py:457
  12.2 1.5 dynamic-slice_bitcast_fusion
  13.7 5.7 %collective-permute-done.refs_1_.refs_4_ = bf16[128,2176]{1,0:T(8,128)(2,1)S(1)} collective-permute-done((bf16[128,2176]{1,0:T(8,128)(2,1)S(1)}, bf16[128,2176]{1,0:T(8,128)(2,1)S(1)}, u32[]{:S(2)}, u32[]{:S(2)}) %collective-permute-start) | collective-permute-done | bytes 557088 | tf_op jit(solution)/shard_map/ppermute | solution.py:418
  19.4 4.1 %collective-permute-done.1.refs_2_.refs_5_ = bf16[128,2176]{1,0:T(8,128)(2,1)S(1)} collective-permute-done((bf16[128,2176]{1,0:T(8,128)(2,1)S(1)}, bf16[128,2176]{1,0:T(8,128)(2,1)S(1)}, u32[]{:S(2)}, u32[]{:S(2)}) %collective-permute-start.1) | collective-permute-done | bytes 557088 | tf_op jit(solution)/shard_map/ppermute | solution.py:418
  23.5 0.8 copy-done.10
  24.3 1.5 collective-permute-start.2
  25.8 1.3 collective-permute-start.3
  27.8 1.8 %collective-permute-done.5.pre_other = bf16[512,512]{1,0:T(8,128)(2,1)} collective-permute-done((bf16[512,512]{1,0:T(8,128)(2,1)}, bf16[512,512]{1,0:T(8,128)(2,1)}, u32[]{:S(2)}, u32[]{:S(2)}) %collective-permute-start.5) | collective-permute-done | bytes 524320 | tf_op jit(solution)/shard_map/ppermute | solution.py:129
  29.6 15.8 %collective-permute-done.3 = bf16[128,2176]{1,0:T(8,128)(2,1)} collective-permute-done((bf16[128,2176]{1,0:T(8,128)(2,1)}, bf16[128,2176]{1,0:T(8,128)(2,1)}, u32[]{:S(2)}, u32[]{:S(2)}) %collective-permute-start.3) | collective-permute-done | bytes 557088 | tf_op jit(solution)/shard_map/ppermute | solution.py:418
  45.4 1.3 copy-done.6
  47.0 1.1 broadcast_select_fusion.refs_0_.refs_1_
  48.1 1.3 collective-permute-start.6
  50.1 2.2 %copy-done.1 = bf16[1,1,512,4096]{3,2,1,0:T(8,128)(2,1)S(1)} copy-done((bf16[1,1,512,4096]{3,2,1,0:T(8,128)(2,1)S(1)}, bf16[1,1,512,4096]{3,2,1,0:T(8,128)(2,1)}, u32[]{:S(2)}) %copy-start.1) | copy-done | bytes 4194328
  52.3 1.6 copy-done.7
  53.9 1.1 copy-done.9
  54.9 1.1 copy-done.11
  56.0 4.3 %hidden.3 = (bf16[384,1024]{1,0:T(8,128)(2,1)S(1)}, f32[384,1024]{1,0:T(8,128)S(1)}, bf16[384,128]{1,0:T(8,128)(2,1)S(1)}) custom-call(s32[5]{0:T(128)S(1)} %stack.43.place, bf16[128,2176]{1,0:T(8,128)(2,1)S(1)} %fusion.1.refs_0_.refs_3_, bf16[128,2176]{1,0:T(8,128)(2,1)S(1)} %copy-done.9, bf16[128,2176]{1,0:T(8,128)(2,1)S(1)} %copy-done.11, ...), custom_call_target="tpu_custom_call" | custom-call | flops 12884901888 | bytes 46137344 | tf_op jit(solution)/shard_map/hidden/pallas_call | solution.py:201
  60.9 4.1 %collective-permute-done.6.refs_0_.refs_1_ = bf16[128,2176]{1,0:T(8,128)(2,1)S(1)} collective-permute-done((bf16[128,2176]{1,0:T(8,128)(2,1)S(1)}, bf16[128,2176]{1,0:T(8,128)(2,1)S(1)}, u32[]{:S(2)}, u32[]{:S(2)}) %collective-permute-start.6) | collective-permute-done | bytes 557088 | tf_op jit(solution)/shard_map/ppermute | solution.py:418
  65.1 1.5 collective-permute-start.9
  66.5 1.3 collective-permute-start.11
  67.8 3.3 %hidden.4 = (bf16[128,1024]{1,0:T(8,128)(2,1)S(1)}, f32[128,1024]{1,0:T(8,128)S(1)}, bf16[128,128]{1,0:T(8,128)(2,1)S(1)}) custom-call(s32[3]{0:T(128)S(1)} %pad_add_fusion.place, bf16[128,2176]{1,0:T(8,128)(2,1)S(1)} %collective-permute-done.6.refs_0_.refs_1_, bf16[128,2176]{1,0:T(8,128)(2,1)S(1)} %collective-permute-done.6.refs_0_.refs_1_, ...), custom_call_target="tpu_custom_call" | custom-call | flops 4294967296 | bytes 37748736 | tf_op jit(solution)/shard_map/hidden/pallas_call | solution.py:201
  71.2 1.6 collective-permute-start.13
  72.8 3.3 %hidden.5 = (bf16[128,1024]{1,0:T(8,128)(2,1)S(1)}, f32[128,1024]{1,0:T(8,128)S(1)}, bf16[128,128]{1,0:T(8,128)(2,1)S(1)}) custom-call(s32[3]{0:T(128)S(1)} %pad_add_fusion.2.place, bf16[128,2176]{1,0:T(8,128)(2,1)S(1)} %broadcast_select_fusion.refs_0_.refs_1_, bf16[128,2176]{1,0:T(8,128)(2,1)S(1)} %broadcast_select_fusion.refs_0_.refs_1_, ...), custom_call_target="tpu_custom_call" | custom-call | flops 4294967296 | bytes 37748736 | tf_op jit(solution)/shard_map/hidden/pallas_call | solution.py:201
  76.6 4.6 %experts.3 = bf16[128,2048]{1,0:T(8,128)(2,1)S(1)} custom-call(s32[3]{0:T(128)S(1)} %pad_add_fusion.place, bf16[128,128]{1,0:T(8,128)(2,1)S(1)} %get-tuple-element.73.routes, f32[128,1024]{1,0:T(8,128)S(1)} %get-tuple-element.74.keep, bf16[128,1024]{1,0:T(8,128)(2,1)S(1)} %collective-permute-done.12.got, bf16[512,512]{1,0:T(8,128)(2,1)} %bitcast.9.pre_own, ...), custom_call_target="tpu_custom_call" | custom-call | flops 4294967296 | bytes 41943040 | tf_op jit(solution)/shard_map/experts/pallas_call | solution.py:256
  81.2 2.7 %collective-permute-done.13.refs_5_ = bf16[16,2048]{1,0:T(8,128)(2,1)S(1)} collective-permute-done((bf16[16,2048]{1,0:T(8,128)(2,1)S(1)}, bf16[16,2048]{1,0:T(8,128)(2,1)S(1)}, u32[]{:S(2)}, u32[]{:S(2)}) %collective-permute-start.13) | collective-permute-done | bytes 65568 | tf_op jit(solution)/shard_map/ppermute | solution.py:418
  83.9 1.3 collective-permute-start.14
  85.2 4.6 %collective-permute-start.16 = (bf16[128,2048]{1,0:T(8,128)(2,1)S(1)}, bf16[128,2048]{1,0:T(8,128)(2,1)S(1)}, u32[]{:S(2)}, u32[]{:S(2)}) collective-permute-start(bf16[128,2048]{1,0:T(8,128)(2,1)S(1)} %experts.3), channel_id=1, source_target_pairs={{0,2},{6,4},{1,3},{7,5},{8,10},{14,12},{9,11},{15,13},{16,18},{22,... | collective-permute-start | bytes 1572872 | tf_op jit(solution)/shard_map/ppermute | solution.py:418
  90.5 6.0 %projection.2 = (bf16[384,1024]{1,0:T(8,128)(2,1)S(1)}, f32[384,1024]{1,0:T(8,128)S(1)}, f32[4,2048]{1,0:T(4,128)S(1)}) custom-call(s32[5]{0:T(128)S(1)} %stack.43.place, bf16[128,2048]{1,0:T(8,128)(2,1)S(1)} %bitcast.37, bf16[128,2048]{1,0:T(8,128)(2,1)S(1)} %collective-permute-done.9.refs_1_, ...), custom_call_target="tpu_custom_call" | custom-call | flops 12884901888 | bytes 65011712 | tf_op jit(solution)/shard_map/projection/pallas_call | solution.py:337
  96.5 1.3 collective-permute-start.20
  97.8 4.3 %experts.4 = f32[128,2048]{1,0:T(8,128)S(1)} custom-call(s32[3]{0:T(128)S(1)} %pad_add_fusion.2.place, bf16[128,128]{1,0:T(8,128)(2,1)S(1)} %get-tuple-element.86.routes, f32[128,1024]{1,0:T(8,128)S(1)} %get-tuple-element.87.keep, bf16[128,1024]{1,0:T(8,128)(2,1)S(1)} %collective-permute-done.15.got, bf16[512,512]{1,0:T(8,128)(2,1)} %bitcast.9.pre_own, ...), custom_call_target="tpu_custom_call" | custom-call | flops 4294967296 | bytes 41943040 | tf_op jit(solution)/shard_map/experts/pallas_call | solution.py:256
  102.2 2.4 %collective-permute-start.28 = (f32[4,2048]{1,0:T(4,128)S(1)}, f32[4,2048]{1,0:T(4,128)S(1)}, u32[]{:S(2)}, u32[]{:S(2)}) collective-permute-start(f32[4,2048]{1,0:T(4,128)S(1)} %get-tuple-element.115), channel_id=1, source_target_pairs={{0,2},{2,0},{4,6},{6,4},{1,3},{3,1},{5,7},{7,5},{8,10},{10,8},{12,... | collective-permute-start | bytes 98312 | tf_op jit(solution)/shard_map/ppermute | solution.py:139
  104.8 2.0 %collective-permute-start.17 = (bf16[128,2048]{1,0:T(8,128)(2,1)S(1)}, bf16[128,2048]{1,0:T(8,128)(2,1)S(1)}, u32[]{:S(2)}, u32[]{:S(2)}) collective-permute-start(bf16[128,2048]{1,0:T(8,128)(2,1)S(1)} %add_convert_fusion.1), channel_id=1, source_target_pairs={{0,2},{2,4},{1,3},{3,5},{8,10},{10,12},{9,11},{11,13},{16,18},{18,... | collective-permute-start | bytes 1572872 | tf_op jit(solution)/shard_map/ppermute | solution.py:418
  107.5 1.3 collective-permute-start.23
  108.8 5.4 %experts.5.sums = f32[384,2048]{1,0:T(8,128)S(1)} custom-call(s32[5]{0:T(128)S(1)} %stack.43.place, bf16[384,128]{1,0:T(8,128)(2,1)S(1)} %get-tuple-element.94.routes, f32[384,1024]{1,0:T(8,128)S(1)} %get-tuple-element.95.keep, bf16[384,1024]{1,0:T(8,128)(2,1)S(1)} %collective-permute-done.19.got, bf16[512,512]{1,0:T(8,128)(2,1)} %bitcast.9.pre_own, ...), custom_call_target="tpu_custom_call" | custom-call | flops 12884901888 | bytes 58720256 | tf_op jit(solution)/shard_map/experts/pallas_call | solution.py:256
  114.2 4.7 %collective-permute-done.17.back_right = bf16[128,2048]{1,0:T(8,128)(2,1)S(1)} collective-permute-done((bf16[128,2048]{1,0:T(8,128)(2,1)S(1)}, bf16[128,2048]{1,0:T(8,128)(2,1)S(1)}, u32[]{:S(2)}, u32[]{:S(2)}) %collective-permute-start.17) | collective-permute-done | bytes 524320 | tf_op jit(solution)/shard_map/ppermute | solution.py:418
  118.8 1.3 combine.1
  120.1 6.7 %collective-permute-start.21 = (bf16[128,2048]{1,0:T(8,128)(2,1)S(1)}, bf16[128,2048]{1,0:T(8,128)(2,1)S(1)}, u32[]{:S(2)}, u32[]{:S(2)}) collective-permute-start(bf16[128,2048]{1,0:T(8,128)(2,1)S(1)} %get-tuple-element.106), channel_id=1, source_target_pairs={{0,2},{2,4},{4,6},{1,3},{3,5},{5,7},{8,10},{10,12},{12,14},{9,11},... | collective-permute-start | bytes 1572872 | tf_op jit(solution)/shard_map/ppermute | solution.py:418
  126.9 1.3 collective-permute-start.22
  128.2 4.1 %projection.3 = (bf16[256,1024]{1,0:T(8,128)(2,1)S(1)}, f32[256,1024]{1,0:T(8,128)S(1)}) custom-call(s32[4]{0:T(128)S(1)} %pad_add_fusion.3.place, bf16[128,2048]{1,0:T(8,128)(2,1)S(1)} %broadcast_select_fusion.1.refs_0_.refs_3_, bf16[128,2048]{1,0:T(8,128)(2,1)S(1)} %collective-permute-done.23.refs_1_, bf16[16,2048]{1,0:T(8,128)(2,1)S(1)} %slice_select_fusion.refs_2_, ...), custom_call_target="tpu_custom_call" | custom-call | flops 8589934592 | bytes 54525952 | tf_op jit(solution)/shard_map/projection/pallas_call | solution.py:337
  132.3 1.3 collective-permute-start.25
  133.6 2.2 %collective-permute-start.29 = (f32[4,2048]{1,0:T(4,128)S(1)}, f32[4,2048]{1,0:T(4,128)S(1)}, u32[]{:S(2)}, u32[]{:S(2)}) collective-permute-start(f32[4,2048]{1,0:T(4,128)S(1)} %add.47), channel_id=1, source_target_pairs={{0,4},{2,6},{4,0},{6,2},{1,5},{3,7},{5,1},{7,3},{8,12},{10,14},{12... | collective-permute-start | bytes 98312 | tf_op jit(solution)/shard_map/ppermute | solution.py:139
  136.2 4.4 %collective-permute-done.22 = bf16[128,2048]{1,0:T(8,128)(2,1)S(1)} collective-permute-done((bf16[128,2048]{1,0:T(8,128)(2,1)S(1)}, bf16[128,2048]{1,0:T(8,128)(2,1)S(1)}, u32[]{:S(2)}, u32[]{:S(2)}) %collective-permute-start.22) | collective-permute-done | bytes 524320 | tf_op jit(solution)/shard_map/ppermute | solution.py:418
  140.8 1.3 collective-permute-start.24
  144.3 13.8 %collective-permute-done.24.residual = bf16[128,2048]{1,0:T(8,128)(2,1)S(1)} collective-permute-done((bf16[128,2048]{1,0:T(8,128)(2,1)S(1)}, bf16[128,2048]{1,0:T(8,128)(2,1)S(1)}, u32[]{:S(2)}, u32[]{:S(2)}) %collective-permute-start.24) | collective-permute-done | bytes 524320 | tf_op jit(solution)/shard_map/ppermute | solution.py:14
  158.1 1.5 residual.1
  (69 shorter events, 7.9 us)
Async XLA Ops:
  2.6 16.8 %collective-permute-start = (bf16[128,2176]{1,0:T(8,128)(2,1)S(1)}, bf16[128,2176]{1,0:T(8,128)(2,1)S(1)}, u32[]{:S(2)}, u32[]{:S(2)}) collective-permute-start(bf16[128,2176]{1,0:T(8,128)(2,1)S(1)} %fusion.1.refs_0_.refs_3_), channel_id=1, source_target_pairs={{0,2},{2,4},{4,6},{1,3},{3,5},{5,7},{8,10},{10,12},{12,14},{9,11},... | collective-permute-start | bytes 1671176 | tf_op jit(solution)/shard_map/ppermute | solution.py:418
  7.5 16.0 %collective-permute-start.1 = (bf16[128,2176]{1,0:T(8,128)(2,1)S(1)}, bf16[128,2176]{1,0:T(8,128)(2,1)S(1)}, u32[]{:S(2)}, u32[]{:S(2)}) collective-permute-start(bf16[128,2176]{1,0:T(8,128)(2,1)S(1)} %fusion.1.refs_0_.refs_3_), channel_id=1, source_target_pairs={{6,4},{4,2},{2,0},{7,5},{5,3},{3,1},{14,12},{12,10},{10,8},{15,13}... | collective-permute-start | bytes 1671176 | tf_op jit(solution)/shard_map/ppermute | solution.py:418
  8.8 3.4 %copy-start.2 = (bf16[1,1,4096,512]{3,2,1,0:T(8,128)(2,1)S(1)}, bf16[1,1,4096,512]{3,2,1,0:T(8,128)(2,1)}, u32[]{:S(2)}) copy-start(bf16[1,1,4096,512]{3,2,1,0:T(8,128)(2,1)} %param.13) | copy-start | bytes 12582916
  12.2 1.5 copy-start.4
  19.4 4.2 %copy-start.8 = (bf16[128,2176]{1,0:T(8,128)(2,1)}, bf16[128,2176]{1,0:T(8,128)(2,1)S(1)}, u32[]{:S(2)}) copy-start(bf16[128,2176]{1,0:T(8,128)(2,1)S(1)} %collective-permute-done.refs_1_.refs_4_) | copy-start | bytes 1671172
  23.5 0.8 copy-start.10
  24.3 21.1 %collective-permute-start.4 = (bf16[512,2048]{1,0:T(8,128)(2,1)}, bf16[512,2048]{1,0:T(8,128)(2,1)S(1)}, u32[]{:S(2)}, u32[]{:S(2)}) collective-permute-start(bf16[512,2048]{1,0:T(8,128)(2,1)} %dynamic-slice_bitcast_fusion.1), channel_id=1, source_target_pairs={{0,1},{1,0},{2,3},{3,2},{4,5},{5,4},{6,7},{7,6},{8,9},{9,8},{10,11... | collective-permute-start | bytes 6291464 | tf_op jit(solution)/shard_map/ppermute | solution.py:129
  24.3 5.3 %collective-permute-start.2 = (bf16[128,2176]{1,0:T(8,128)(2,1)}, bf16[128,2176]{1,0:T(8,128)(2,1)}, u32[]{:S(2)}, u32[]{:S(2)}) collective-permute-start(bf16[128,2176]{1,0:T(8,128)(2,1)} %copy-done.8), channel_id=1, source_target_pairs={{2,4},{4,6},{3,5},{5,7},{10,12},{12,14},{11,13},{13,15},{18,20},{2... | collective-permute-start | bytes 1671176 | tf_op jit(solution)/shard_map/ppermute | solution.py:418
  25.8 19.6 %collective-permute-start.3 = (bf16[128,2176]{1,0:T(8,128)(2,1)}, bf16[128,2176]{1,0:T(8,128)(2,1)}, u32[]{:S(2)}, u32[]{:S(2)}) collective-permute-start(bf16[128,2176]{1,0:T(8,128)(2,1)} %copy-done.10), channel_id=1, source_target_pairs={{4,2},{2,0},{5,3},{3,1},{12,10},{10,8},{13,11},{11,9},{20,18},{18,... | collective-permute-start | bytes 1671176 | tf_op jit(solution)/shard_map/ppermute | solution.py:418
  27.1 2.5 %collective-permute-start.5 = (bf16[512,512]{1,0:T(8,128)(2,1)}, bf16[512,512]{1,0:T(8,128)(2,1)}, u32[]{:S(2)}, u32[]{:S(2)}) collective-permute-start(bf16[512,512]{1,0:T(8,128)(2,1)} %bitcast.9.pre_own), channel_id=1, source_target_pairs={{0,1},{1,0},{2,3},{3,2},{4,5},{5,4},{6,7},{7,6},{8,9},{9,8},{10,11... | collective-permute-start | bytes 1572872 | tf_op jit(solution)/shard_map/ppermute | solution.py:129
  45.4 1.3 copy-start.6
  46.8 18.3 %collective-permute-start.7 = (bf16[2048,512]{1,0:T(8,128)(2,1)}, bf16[2048,512]{1,0:T(8,128)(2,1)S(1)}, u32[]{:S(2)}, u32[]{:S(2)}) collective-permute-start(bf16[2048,512]{1,0:T(8,128)(2,1)} %dynamic-slice_bitcast_fusion), channel_id=1, source_target_pairs={{0,1},{1,0},{2,3},{3,2},{4,5},{5,4},{6,7},{7,6},{8,9},{9,8},{10,11... | collective-permute-start | bytes 6291464 | tf_op jit(solution)/shard_map/ppermute | solution.py:129
  48.1 16.9 %collective-permute-start.6 = (bf16[128,2176]{1,0:T(8,128)(2,1)S(1)}, bf16[128,2176]{1,0:T(8,128)(2,1)S(1)}, u32[]{:S(2)}, u32[]{:S(2)}) collective-permute-start(bf16[128,2176]{1,0:T(8,128)(2,1)S(1)} %broadcast_select_fusion.refs_0_.refs_1_), channel_id=1, source_target_pairs={{4,6},{2,0},{5,7},{3,1},{12,14},{10,8},{13,15},{11,9},{20,22},{18,... | collective-permute-start | bytes 1671176 | tf_op jit(solution)/shard_map/ppermute | solution.py:418
  49.4 11.5 %collective-permute-start.8 = (bf16[16,2048]{1,0:T(8,128)(2,1)S(1)}, bf16[16,2048]{1,0:T(8,128)(2,1)S(1)}, u32[]{:S(2)}, u32[]{:S(2)}) collective-permute-start(bf16[16,2048]{1,0:T(8,128)(2,1)S(1)} %slice_bitcast_fusion), channel_id=1, source_target_pairs={{6,4},{4,2},{7,5},{5,3},{14,12},{12,10},{15,13},{13,11},{22,20},{2... | collective-permute-start | bytes 196616 | tf_op jit(solution)/shard_map/ppermute | solution.py:418
  50.1 2.2 %copy-start.1 = (bf16[1,1,512,4096]{3,2,1,0:T(8,128)(2,1)S(1)}, bf16[1,1,512,4096]{3,2,1,0:T(8,128)(2,1)}, u32[]{:S(2)}) copy-start(bf16[1,1,512,4096]{3,2,1,0:T(8,128)(2,1)} %param.14) | copy-start | bytes 12582916
  52.3 1.6 copy-start.7
  53.9 1.1 copy-start.9
  54.9 1.1 copy-start.11
  60.3 47.1 %collective-permute-start.19 = (bf16[384,1024]{1,0:T(8,128)(2,1)S(1)}, bf16[384,1024]{1,0:T(8,128)(2,1)S(1)}, u32[]{:S(2)}, u32[]{:S(2)}) collective-permute-start(bf16[384,1024]{1,0:T(8,128)(2,1)S(1)} %get-tuple-element.96), channel_id=1, source_target_pairs={{0,1},{1,0},{2,3},{3,2},{4,5},{5,4},{6,7},{7,6},{8,9},{9,8},{10,11... | collective-permute-start | bytes 2359304 | tf_op jit(solution)/shard_map/ppermute | solution.py:129
  65.1 24.7 %collective-permute-start.9 = (bf16[128,2048]{1,0:T(8,128)(2,1)S(1)}, bf16[128,2048]{1,0:T(8,128)(2,1)S(1)}, u32[]{:S(2)}, u32[]{:S(2)}) collective-permute-start(bf16[128,2048]{1,0:T(8,128)(2,1)S(1)} %bitcast.35), channel_id=1, source_target_pairs={{0,2},{2,4},{4,6},{1,3},{3,5},{5,7},{8,10},{10,12},{12,14},{9,11},... | collective-permute-start | bytes 1572872 | tf_op jit(solution)/shard_map/ppermute | solution.py:418
  66.5 17.4 %collective-permute-start.11 = (bf16[128,2048]{1,0:T(8,128)(2,1)S(1)}, bf16[128,2048]{1,0:T(8,128)(2,1)S(1)}, u32[]{:S(2)}, u32[]{:S(2)}) collective-permute-start(bf16[128,2048]{1,0:T(8,128)(2,1)S(1)} %bitcast.36), channel_id=1, source_target_pairs={{6,4},{4,2},{2,0},{7,5},{5,3},{3,1},{14,12},{12,10},{10,8},{15,13}... | collective-permute-start | bytes 1572872 | tf_op jit(solution)/shard_map/ppermute | solution.py:418
  71.2 5.4 %copy-start.3 = (bf16[1,1,4096,512]{3,2,1,0:T(8,128)(2,1)S(1)}, bf16[1,1,4096,512]{3,2,1,0:T(8,128)(2,1)}, u32[]{:S(2)}) copy-start(bf16[1,1,4096,512]{3,2,1,0:T(8,128)(2,1)} %param.13) | copy-start | bytes 12582916
  71.2 5.0 %collective-permute-start.12 = (bf16[128,1024]{1,0:T(8,128)(2,1)S(1)}, bf16[128,1024]{1,0:T(8,128)(2,1)S(1)}, u32[]{:S(2)}, u32[]{:S(2)}) collective-permute-start(bf16[128,1024]{1,0:T(8,128)(2,1)S(1)} %get-tuple-element.75), channel_id=1, source_target_pairs={{0,1},{1,0},{2,3},{3,2},{4,5},{5,4},{6,7},{7,6},{8,9},{9,8},{10,11... | collective-permute-start | bytes 786440 | tf_op jit(solution)/shard_map/ppermute | solution.py:129
  71.2 12.6 %collective-permute-start.13 = (bf16[16,2048]{1,0:T(8,128)(2,1)S(1)}, bf16[16,2048]{1,0:T(8,128)(2,1)S(1)}, u32[]{:S(2)}, u32[]{:S(2)}) collective-permute-start(bf16[16,2048]{1,0:T(8,128)(2,1)S(1)} %collective-permute-done.8), channel_id=1, source_target_pairs={{4,2},{2,0},{5,3},{3,1},{12,10},{10,8},{13,11},{11,9},{20,18},{18,... | collective-permute-start | bytes 196616 | tf_op jit(solution)/shard_map/ppermute | solution.py:418
  76.1 20.4 %collective-permute-start.15 = (bf16[128,1024]{1,0:T(8,128)(2,1)S(1)}, bf16[128,1024]{1,0:T(8,128)(2,1)S(1)}, u32[]{:S(2)}, u32[]{:S(2)}) collective-permute-start(bf16[128,1024]{1,0:T(8,128)(2,1)S(1)} %get-tuple-element.88), channel_id=1, source_target_pairs={{0,1},{1,0},{2,3},{3,2},{4,5},{5,4},{6,7},{7,6},{8,9},{9,8},{10,11... | collective-permute-start | bytes 786440 | tf_op jit(solution)/shard_map/ppermute | solution.py:129
  76.6 13.9 %copy-start.5 = (bf16[1,1024,2048]{2,1,0:T(8,128)(2,1)S(1)}, bf16[1,1024,2048]{2,1,0:T(8,128)(2,1)}, u32[]{:S(2)}) copy-start(bf16[1,1024,2048]{2,1,0:T(8,128)(2,1)} %param.19) | copy-start | bytes 12582916
  76.6 13.9 %copy-start.12 = (bf16[1,128,2048]{2,1,0:T(8,128)(2,1)S(1)}, bf16[1,128,2048]{2,1,0:T(8,128)(2,1)}, u32[]{:S(2)}) copy-start(bf16[1,128,2048]{2,1,0:T(8,128)(2,1)} %param.17) | copy-start | bytes 1572868
  76.6 13.9 %copy-start.13 = (f32[1,4,2048]{2,1,0:T(4,128)S(1)}, f32[1,4,2048]{2,1,0:T(4,128)}, u32[]{:S(2)}) copy-start(f32[1,4,2048]{2,1,0:T(4,128)} %param.18) | copy-start | bytes 98308
  83.9 20.7 %collective-permute-start.14 = (bf16[128,2048]{1,0:T(8,128)(2,1)S(1)}, bf16[128,2048]{1,0:T(8,128)(2,1)S(1)}, u32[]{:S(2)}, u32[]{:S(2)}) collective-permute-start(bf16[128,2048]{1,0:T(8,128)(2,1)S(1)} %collective-permute-done.11.refs_2_.refs_3_), channel_id=1, source_target_pairs={{4,2},{2,0},{5,3},{3,1},{12,10},{10,8},{13,11},{11,9},{20,18},{18,... | collective-permute-start | bytes 1572872 | tf_op jit(solution)/shard_map/ppermute | solution.py:418
  85.2 19.5 %collective-permute-start.16 = (bf16[128,2048]{1,0:T(8,128)(2,1)S(1)}, bf16[128,2048]{1,0:T(8,128)(2,1)S(1)}, u32[]{:S(2)}, u32[]{:S(2)}) collective-permute-start(bf16[128,2048]{1,0:T(8,128)(2,1)S(1)} %experts.3), channel_id=1, source_target_pairs={{0,2},{6,4},{1,3},{7,5},{8,10},{14,12},{9,11},{15,13},{16,18},{22,... | collective-permute-start | bytes 1572872 | tf_op jit(solution)/shard_map/ppermute | solution.py:418
  89.8 12.4 %collective-permute-start.10 = (bf16[128,2048]{1,0:T(8,128)(2,1)S(1)}, bf16[128,2048]{1,0:T(8,128)(2,1)S(1)}, u32[]{:S(2)}, u32[]{:S(2)}) collective-permute-start(bf16[128,2048]{1,0:T(8,128)(2,1)S(1)} %collective-permute-done.9.refs_1_), channel_id=1, source_target_pairs={{2,4},{4,6},{3,5},{5,7},{10,12},{12,14},{11,13},{13,15},{18,20},{2... | collective-permute-start | bytes 1572872 | tf_op jit(solution)/shard_map/ppermute | solution.py:418
  96.5 22.3 %collective-permute-start.20 = (bf16[384,1024]{1,0:T(8,128)(2,1)S(1)}, bf16[384,1024]{1,0:T(8,128)(2,1)S(1)}, u32[]{:S(2)}, u32[]{:S(2)}) collective-permute-start(bf16[384,1024]{1,0:T(8,128)(2,1)S(1)} %get-tuple-element.101), channel_id=1, source_target_pairs={{1,0},{3,2},{4,5},{6,7},{9,8},{11,10},{12,13},{14,15},{17,16},{19,... | collective-permute-start | bytes 2359304 | tf_op jit(solution)/shard_map/ppermute | solution.py:499
  102.2 31.4 %collective-permute-start.28 = (f32[4,2048]{1,0:T(4,128)S(1)}, f32[4,2048]{1,0:T(4,128)S(1)}, u32[]{:S(2)}, u32[]{:S(2)}) collective-permute-start(f32[4,2048]{1,0:T(4,128)S(1)} %get-tuple-element.115), channel_id=1, source_target_pairs={{0,2},{2,0},{4,6},{6,4},{1,3},{3,1},{5,7},{7,5},{8,10},{10,8},{12,... | collective-permute-start | bytes 98312 | tf_op jit(solution)/shard_map/ppermute | solution.py:139
  104.8 14.0 %collective-permute-start.17 = (bf16[128,2048]{1,0:T(8,128)(2,1)S(1)}, bf16[128,2048]{1,0:T(8,128)(2,1)S(1)}, u32[]{:S(2)}, u32[]{:S(2)}) collective-permute-start(bf16[128,2048]{1,0:T(8,128)(2,1)S(1)} %add_convert_fusion.1), channel_id=1, source_target_pairs={{0,2},{2,4},{1,3},{3,5},{8,10},{10,12},{9,11},{11,13},{16,18},{18,... | collective-permute-start | bytes 1572872 | tf_op jit(solution)/shard_map/ppermute | solution.py:418
  106.8 12.1 %collective-permute-start.18 = (bf16[128,2048]{1,0:T(8,128)(2,1)S(1)}, bf16[128,2048]{1,0:T(8,128)(2,1)S(1)}, u32[]{:S(2)}, u32[]{:S(2)}) collective-permute-start(bf16[128,2048]{1,0:T(8,128)(2,1)S(1)} %add_convert_fusion.1), channel_id=1, source_target_pairs={{6,4},{4,2},{7,5},{5,3},{14,12},{12,10},{15,13},{13,11},{22,20},{2... | collective-permute-start | bytes 1572872 | tf_op jit(solution)/shard_map/ppermute | solution.py:418
  107.5 20.7 %collective-permute-start.23 = (bf16[128,2048]{1,0:T(8,128)(2,1)S(1)}, bf16[128,2048]{1,0:T(8,128)(2,1)S(1)}, u32[]{:S(2)}, u32[]{:S(2)}) collective-permute-start(bf16[128,2048]{1,0:T(8,128)(2,1)S(1)} %broadcast_select_fusion.1.refs_0_.refs_3_), channel_id=1, source_target_pairs={{4,6},{2,0},{5,7},{3,1},{12,14},{10,8},{13,15},{11,9},{20,22},{18,... | collective-permute-start | bytes 1572872 | tf_op jit(solution)/shard_map/ppermute | solution.py:418
  108.8 10.1 %copy-start = (bf16[1,128,2048]{2,1,0:T(8,128)(2,1)S(1)}, bf16[1,128,2048]{2,1,0:T(8,128)(2,1)}, u32[]{:S(2)}) copy-start(bf16[1,128,2048]{2,1,0:T(8,128)(2,1)} %param.10) | copy-start | bytes 1572868
  120.1 16.1 %collective-permute-start.21 = (bf16[128,2048]{1,0:T(8,128)(2,1)S(1)}, bf16[128,2048]{1,0:T(8,128)(2,1)S(1)}, u32[]{:S(2)}, u32[]{:S(2)}) collective-permute-start(bf16[128,2048]{1,0:T(8,128)(2,1)S(1)} %get-tuple-element.106), channel_id=1, source_target_pairs={{0,2},{2,4},{4,6},{1,3},{3,5},{5,7},{8,10},{10,12},{12,14},{9,11},... | collective-permute-start | bytes 1572872 | tf_op jit(solution)/shard_map/ppermute | solution.py:418
  126.9 13.8 %collective-permute-start.22 = (bf16[128,2048]{1,0:T(8,128)(2,1)S(1)}, bf16[128,2048]{1,0:T(8,128)(2,1)S(1)}, u32[]{:S(2)}, u32[]{:S(2)}) collective-permute-start(bf16[128,2048]{1,0:T(8,128)(2,1)S(1)} %get-tuple-element.107), channel_id=1, source_target_pairs={{6,4},{4,2},{2,0},{7,5},{5,3},{3,1},{14,12},{12,10},{10,8},{15,13}... | collective-permute-start | bytes 1572872 | tf_op jit(solution)/shard_map/ppermute | solution.py:418
  132.3 9.8 %collective-permute-start.25 = (bf16[256,1024]{1,0:T(8,128)(2,1)S(1)}, bf16[256,1024]{1,0:T(8,128)(2,1)S(1)}, u32[]{:S(2)}, u32[]{:S(2)}) collective-permute-start(bf16[256,1024]{1,0:T(8,128)(2,1)S(1)} %get-tuple-element.114), channel_id=1, source_target_pairs={{1,0},{3,2},{4,5},{6,7},{9,8},{11,10},{12,13},{14,15},{17,16},{19,... | collective-permute-start | bytes 1572872 | tf_op jit(solution)/shard_map/ppermute | solution.py:499
  133.6 10.0 %collective-permute-start.29 = (f32[4,2048]{1,0:T(4,128)S(1)}, f32[4,2048]{1,0:T(4,128)S(1)}, u32[]{:S(2)}, u32[]{:S(2)}) collective-permute-start(f32[4,2048]{1,0:T(4,128)S(1)} %add.47), channel_id=1, source_target_pairs={{0,4},{2,6},{4,0},{6,2},{1,5},{3,7},{5,1},{7,3},{8,12},{10,14},{12... | collective-permute-start | bytes 98312 | tf_op jit(solution)/shard_map/ppermute | solution.py:139
  140.8 17.2 %collective-permute-start.24 = (bf16[128,2048]{1,0:T(8,128)(2,1)S(1)}, bf16[128,2048]{1,0:T(8,128)(2,1)S(1)}, u32[]{:S(2)}, u32[]{:S(2)}) collective-permute-start(bf16[128,2048]{1,0:T(8,128)(2,1)S(1)} %add_convert_fusion), channel_id=1, source_target_pairs={{8,0},{16,8},{24,16},{9,1},{17,9},{25,17},{10,2},{18,10},{26,18},{... | collective-permute-start | bytes 1572872 | tf_op jit(solution)/shard_map/ppermute | solution.py:14
  142.3 2.0 %collective-permute-start.26 = (bf16[128,1024]{1,0:T(8,128)(2,1)S(1)}, bf16[128,1024]{1,0:T(8,128)(2,1)S(1)}, u32[]{:S(2)}, u32[]{:S(2)}) collective-permute-start(bf16[128,1024]{1,0:T(8,128)(2,1)S(1)} %get-tuple-element.117), channel_id=1, source_target_pairs={{8,4},{10,6},{13,1},{15,3},{16,12},{18,14},{21,9},{23,11},{24,20},... | collective-permute-start | bytes 786440 | tf_op jit(solution)/shard_map/ppermute | solution.py:532
  143.0 1.3 collective-permute-start.27
